TPU v7x, 32 devices: a whole 2x2x4 slice. The times are simulated.
32 devices in a mesh: ep: 16 (over z, y, core), tp: 2 (over x).
Axes of the slice: x: 2, y: 2, z: 4, core: 2. Of those that a mesh axis runs over, the one named last changes fastest.
Arguments:
- grad_out: bfloat16 [2048, 3584], P('ep', 'tp'), may hold values from -6 to 6
- routes: int32 [2048, 8], P('ep'), may hold values from 0 to 15, all different within a row; in each aligned block of 128 rows (0 to 127, 128 to 255, ...) at most 66 rows name the same one
- gate_weights: float32 [2048, 8], P('ep'), may hold values from 0.05 to 0.5
- gate_act: bfloat16 [16, 1056, 1024], P('ep', None, 'tp'), may hold values from -6 to 6
- w_down: bfloat16 [16, 1024, 3584], P('ep', None, 'tp'), may hold values from -0.1875 to 0.1875
- w_up: bfloat16 [16, 3584, 1024], P('ep', 'tp'), may hold values from -0.09375 to 0.09375
Outputs:
- grad_in: bfloat16 [2048, 3584], P('ep', 'tp')
Inputs may be any that keep to these rules, and one draw needn't show every extreme that they name: `routes`: each row names 8 different experts; among the 128 rows of one device no expert is named more than 66 times, a bound that some block reaches.
All inputs are finite; a program needn't handle non-finite values.
Results may differ from a plain program's by a relative error of at most 0.02.
Values may be sent and summed in bfloat16 or wider, within the bound.
No kernel may reach another device: no remote copies, remote signals or barrier semaphores. Data moves between devices by JAX's collectives and lax.ppermute only.
A program may use at most 64 MiB of HBM per device.

v0:
```python
import jax
import jax.numpy as jnp
from jax import lax
from jax.sharding import PartitionSpec as P


def on_device(grad_out, routes, gate_weights, gate_act, w_down, w_up):
    experts_n = lax.axis_size("ep")
    slot_n = gate_act.shape[1] // experts_n
    rows_n = experts_n * slot_n
    token_n, choose_n = routes.shape
    flat_ids = routes.reshape(-1)
    one_hot = (flat_ids[:, None] == jnp.arange(experts_n, dtype=jnp.int32)[None, :]).astype(
        jnp.int32
    )
    earlier = jnp.cumsum(one_hot, axis=0) - one_hot
    slot_rank = jnp.sum(earlier * one_hot, axis=1)
    position = flat_ids * slot_n + slot_rank
    token_ids = jnp.arange(token_n * choose_n, dtype=jnp.int32) // choose_n
    token_of = jnp.full((rows_n,), token_n, jnp.int32).at[position].set(token_ids)
    weight_of = jnp.zeros((rows_n,), jnp.float32).at[position].set(gate_weights.reshape(-1))
    down_local = w_down[0]
    up_local = w_up[0]
    feat_part = grad_out.shape[1]
    padded = jnp.concatenate([grad_out, jnp.zeros((1, feat_part), grad_out.dtype)], axis=0)
    placed = (padded[token_of].astype(jnp.float32) * weight_of[:, None]).astype(jnp.bfloat16)
    placed = placed.reshape(experts_n, slot_n, feat_part)
    partial_value = jnp.einsum(
        "nsd,fd->nsf",
        lax.all_to_all(placed, "ep", split_axis=0, concat_axis=0, tiled=True),
        down_local,
        preferred_element_type=jnp.float32,
    )
    partial_value = partial_value.reshape(rows_n, -1)
    hidden_grad = lax.psum_scatter(
        partial_value.astype(jnp.bfloat16), "tp", scatter_dimension=1, tiled=True
    ).astype(jnp.float32)
    up_grad = (hidden_grad * gate_act[0].astype(jnp.float32)).astype(jnp.bfloat16)
    row_grad = lax.dot_general(
        lax.all_gather(up_grad, "tp", axis=1, tiled=True),
        up_local,
        (((1,), (1,)), ((), ())),
        preferred_element_type=jnp.float32,
    )
    row_grad = row_grad.astype(jnp.bfloat16).reshape(experts_n, slot_n, -1)
    returned = lax.all_to_all(row_grad, "ep", split_axis=0, concat_axis=0, tiled=True)
    picked = returned.reshape(rows_n, -1)[position]
    summed = jnp.sum(picked.astype(jnp.float32).reshape(token_n, choose_n, -1), axis=1)
    return summed.astype(jnp.bfloat16)


def solution(mesh):
    placed = (
        P("ep", "tp"),
        P("ep", None),
        P("ep", None),
        P("ep", None, "tp"),
        P("ep", None, "tp"),
        P("ep", "tp", None),
    )
    return jax.shard_map(
        on_device, mesh=mesh, in_specs=placed, out_specs=P("ep", "tp"), check_vma=False
    )
```

profile of v0, /device:TPU:13, one launch (start us, length us, event | category | flops | bytes accessed | tf_op | source)
XLA Modules:
  0.0 358.2 jit_solution(3832320076274109932)
XLA Ops:
  6.5 0.0 reduce-scatter.2.cloned.1.call-start
  6.5 0.7 broadcast_multiply_fusion
  7.2 0.8 copy.10
  8.0 0.1 eq.29
  8.1 0.1 eq.25
  8.2 0.1 copy.9
  8.3 0.1 mul.35
  8.4 4.5 %reduce-window.6 = s32[16,8,128]{2,1,0:T(8,128)S(1)} reduce-window(s32[16,8,128]{2,1,0:T(8,128)S(1)} %fusion.6, s32[]{:T(128)} %constant.31.clone.1), window={size=1x1x128 pad=0_0x0_0x127_0}, to_apply=%region_0.0 | reduce-window | flops 2080768 | bytes 131076 | tf_op jit(solution)/shard_map/reduce-window
  12.9 0.1 slice.12
  13.0 0.1 copy.12
  13.2 0.1 copy.13
  13.3 0.1 broadcast_add_fusion
  13.4 4.3 %scatter_custom_fusion = s32[1056]{0:T(1024)S(1)} fusion(s32[1024]{0:T(1024)S(1)} %bitcast.38, s32[1024]{0:T(1024)S(1)} %add_select_fusion, s32[]{:T(128)} %constant.29.clone.1), kind=kCustom, calls=%fused_computation.31 | custom fusion | bytes 4228 | tf_op jit(solution)/shard_map/scatter | solution.py:20
  17.8 0.8 copy.14
  18.5 0.1 reshape.105
  18.6 4.3 %scatter_custom_fusion.1 = f32[1056]{0:T(1024)S(1)} fusion(s32[1024]{0:T(1024)S(1)} %bitcast.39, f32[1024]{0:T(1024)S(1)} %reshape.105, f32[]{:T(128)} %constant.38.clone.1), kind=kCustom, calls=%fused_computation.29 | custom fusion | bytes 4228 | tf_op jit(solution)/shard_map/scatter | solution.py:21
  23.0 0.1 mul.37
  23.0 1.1 concatenate.3
  24.1 5.6 %gather_fusion = bf16[1056,1792]{1,0:T(8,128)(2,1)} fusion(bf16[129,1792]{1,0:T(8,128)(2,1)S(1)} %concatenate.3, s32[2048]{0:T(1024)S(1)} %pad_clamp_fusion), kind=kCustom, calls=%fused_computation | custom fusion | bytes 7573632 | tf_op jit(solution)/shard_map/gather | solution.py:26
  29.7 5.9 %reshape.75 = f32[16,66,1792]{2,1,0:T(8,128)} reshape(bf16[1056,1792]{1,0:T(8,128)(2,1)} %gather_fusion) | data formatting | bytes 11354112 | tf_op jit(solution)/shard_map/convert_element_type | solution.py:26
  35.7 3.9 %multiply_convert_fusion = bf16[16,66,1792]{2,1,0:T(8,128)(2,1)S(1)} fusion(f32[16,66,1792]{2,1,0:T(8,128)} %reshape.75, f32[16,66]{1,0:T(8,128)S(1)} %mul.37), kind=kLoop, calls=%fused_computation.4 | loop fusion | flops 3784704 | bytes 11358336 | tf_op jit(solution)/shard_map/convert_element_type | solution.py:26
  39.5 97.3 %all_to_all.10 = bf16[16,66,1792]{2,1,0:T(8,128)(2,1)} all-to-all(bf16[16,66,1792]{2,1,0:T(8,128)(2,1)S(1)} %multiply_convert_fusion), channel_id=1, replica_groups=mesh['ep'=16,'tp'=2] {'ep'}, dimensions={0} | all-to-all | bytes 7569408 | tf_op jit(solution)/shard_map/all_to_all | solution.py:30
  136.8 4.9 %dot_general.8 = bf16[1056,1792]{1,0:T(8,128)(2,1)} reshape(bf16[16,66,1792]{2,1,0:T(8,128)(2,1)} %all_to_all.10) | data formatting | bytes 7569408 | tf_op jit(solution)/shard_map/nsd,fd->nsf/dot_general | solution.py:28
  141.8 0.0 copy-start
  141.8 8.7 %convolution_convert_fusion.1 = bf16[1056,1024]{1,0:T(8,128)(2,1)} fusion(bf16[1056,1792]{1,0:T(8,128)(2,1)} %dot_general.8, bf16[1,1024,1792]{2,1,0:T(8,128)(2,1)} %param.10), kind=kOutput, calls=%fused_computation.6 | convolution fusion | flops 3876618240 | bytes 9617408 | tf_op jit(solution)/shard_map/nsd,fd->nsf/dot_general | solution.py:28
  150.5 0.0 reduce-scatter.2.cloned.1.call-update
  150.5 0.0 all-gather.2.cloned.1.call-start
  150.6 32.5 %reduce-scatter.2.cloned.1.call-done = bf16[1056,512]{1,0:T(8,128)(2,1)} async-done(((bf16[1056,1024]{1,0:T(8,128)(2,1)}), bf16[1056,512]{1,0:T(8,128)(2,1)}) %reduce-scatter.2.cloned.1.call-update) | async-done | bytes 1081360 | tf_op jit(solution)/shard_map/reduce_scatter | solution.py:35
  183.1 0.0 copy-done
  183.1 2.5 fusion.2
  185.6 0.0 all-gather.2.cloned.1.call-update
  185.6 34.0 %all-gather.2.cloned.1.call-done = bf16[1056,1024]{1,0:T(8,128)(2,1)} async-done(((bf16[1056,512]{1,0:T(8,128)(2,1)}), bf16[1056,1024]{1,0:T(8,128)(2,1)}) %all-gather.2.cloned.1.call-update) | async-done | bytes 2162704 | tf_op jit(solution)/shard_map/all_gather | solution.py:40
  219.7 8.6 %convolution_convert_fusion = bf16[1056,1792]{1,0:T(8,128)(2,1)} fusion(bf16[1056,1024]{1,0:T(8,128)(2,1)} %all-gather.2.cloned.1.call-done, bf16[1,1792,1024]{2,1,0:T(8,128)(2,1)} %param.11), kind=kOutput, calls=%fused_computation.5 | convolution fusion | flops 3877429248 | bytes 9617408 | tf_op jit(solution)/shard_map/dot_general | solution.py:39
  228.3 5.0 %reshape.73 = bf16[16,66,1792]{2,1,0:T(8,128)(2,1)} reshape(bf16[1056,1792]{1,0:T(8,128)(2,1)} %convolution_convert_fusion) | data formatting | bytes 7569408 | tf_op jit(solution)/shard_map/reshape | solution.py:45
  233.3 6.4 %all-to-all-start.1 = ((bf16[16,66,1792]{2,1,0:T(8,128)(2,1)}), bf16[16,66,1792]{2,1,0:T(8,128)(2,1)}, u32[]{:S(2)}, u32[]{:S(2)}) async-start(bf16[16,66,1792]{2,1,0:T(8,128)(2,1)} %reshape.73), calls=%async_computation.2 | async-start | bytes 8257536 | tf_op jit(solution)/shard_map/all_to_all | solution.py:46
  239.7 91.1 %all-to-all-done.1 = bf16[16,66,1792]{2,1,0:T(8,128)(2,1)} async-done(((bf16[16,66,1792]{2,1,0:T(8,128)(2,1)}), bf16[16,66,1792]{2,1,0:T(8,128)(2,1)}, u32[]{:S(2)}, u32[]{:S(2)}) %all-to-all-start.1) | async-done | bytes 3784736 | tf_op jit(solution)/shard_map/all_to_all | solution.py:46
  330.7 4.9 %reshape.74 = bf16[1056,1792]{1,0:T(8,128)(2,1)} reshape(bf16[16,66,1792]{2,1,0:T(8,128)(2,1)} %all-to-all-done.1) | data formatting | bytes 7569408 | tf_op jit(solution)/shard_map/reshape | solution.py:47
  335.6 10.5 %gather_fusion.1 = bf16[1024,1792]{1,0:T(8,128)(2,1)} fusion(bf16[1056,1792]{1,0:T(8,128)(2,1)} %reshape.74, s32[1024]{0:T(1024)S(1)} %broadcast_clamp_fusion), kind=kCustom, calls=%fused_computation.1 | custom fusion | bytes 7344128 | tf_op jit(solution)/shard_map/gather | solution.py:47
  346.1 5.3 %bitcast_reduce_fusion = bf16[128,1792]{1,0:T(8,128)(2,1)} fusion(bf16[1024,1792]{1,0:T(8,128)(2,1)} %gather_fusion.1), kind=kLoop, calls=%fused_computation.7 | loop fusion | flops 1605632 | bytes 4128768 | tf_op jit(solution)/shard_map/reduce_sum | solution.py:48
  (9 shorter events, 0.1 us)
Async XLA Ops:
  6.5 176.6 %reduce-scatter.2.cloned.1.call-start = ((), (), s32[]{:S(2)}) async-start(), calls=%async_computation.3 | async-start | bytes 3244032 | tf_op jit(solution)/shard_map/reduce_scatter | solution.py:35
  141.8 41.3 %copy-start = (bf16[1,1056,512]{2,1,0:T(8,128)(2,1)S(1)}, bf16[1,1056,512]{2,1,0:T(8,128)(2,1)}, u32[]{:S(2)}) copy-start(bf16[1,1056,512]{2,1,0:T(8,128)(2,1)} %param.9) | copy-start | bytes 3244036
  150.5 69.1 %all-gather.2.cloned.1.call-start = ((), (), s32[]{:S(2)}) async-start(), calls=%async_computation.4 | async-start | bytes 3244032 | tf_op jit(solution)/shard_map/all_gather | solution.py:40
  233.3 97.4 %all-to-all-start.1 = ((bf16[16,66,1792]{2,1,0:T(8,128)(2,1)}), bf16[16,66,1792]{2,1,0:T(8,128)(2,1)}, u32[]{:S(2)}, u32[]{:S(2)}) async-start(bf16[16,66,1792]{2,1,0:T(8,128)(2,1)} %reshape.73), calls=%async_computation.2 | async-start | bytes 8257536 | tf_op jit(solution)/shard_map/all_to_all | solution.py:46
Sparse Core Ops, SparseCore 0:
  150.6 32.4 reduce-scatter.1
  185.8 33.8 all-gather.1
where the time goes:
time: 359 us; the launch traced here: 358 us
  waiting for transfers between devices  158 us (44%)
  blocking collectives  97.3 us (27%)
  local copies, waits for them, and re-layouts  49 us (14%)
  matrix products  17.4 us (5%)
  other arithmetic  17 us (5%)
  between operations  13.5 us (4%)
  starting transfers between devices  6.42 us (2%)
    all_to_all x1, blocking collectives, on_device(): lax.all_to_all(placed, 'ep', split_axis=0, concat_axis=0, tiled=True)  97.3 us
    all_to_all x1, waiting for transfers between devices, on_device(): lax.all_to_all(row_grad, 'ep', split_axis=0, concat_axis=0, tiled=True)  91.1 us
    all_gather x1, waiting for transfers between devices, on_device(): lax.all_gather(up_grad, 'tp', axis=1, tiled=True)  34 us
    reduce_scatter x1, waiting for transfers between devices, on_device(): lax.psum_scatter(partial_value.astype(jnp.bfloat16), 'tp', scatter_dimens...  32.5 us
    gather x1, local copies, waits for them, and re-layouts, on_device(): picked = returned.reshape(rows_n, -1)[position]  10.5 us
    dot_general x1, matrix products, on_device(): jnp.einsum('nsd,fd->nsf', lax.all_to_all(placed, 'ep', split_axis=0, conc...  8.74 us
    dot_general x1, matrix products, on_device(): lax.dot_general(lax.all_gather(up_grad, 'tp', axis=1, tiled=True), up_loc...  8.64 us
  transfers between devices with their start and end apart: 3, of which 3 were waited for; matrix products, arithmetic and copies ran while one was open for 0% of the time, Pallas kernels for 0%

commit v1 on v0

--- a/solution.py
+++ b/solution.py
@@ -1,10 +1,294 @@
+import functools
+
 import jax
 import jax.numpy as jnp
 from jax import lax
+from jax.experimental import pallas as pl
+from jax.experimental.pallas import tpu as pltpu
 from jax.sharding import PartitionSpec as P
 
-
-def on_device(grad_out, routes, gate_weights, gate_act, w_down, w_up):
+BF16 = jnp.bfloat16
+F32 = jnp.float32
+VMEM = pl.BlockSpec(memory_space=pltpu.VMEM)
+SMEM = pl.BlockSpec(memory_space=pltpu.SMEM)
+LIMIT = pltpu.CompilerParams(vmem_limit_bytes=40 * 1024 * 1024)
+
+
+def dot_t(a, b):
+    return lax.dot_general(a, b, (((1,), (1,)), ((), ())), preferred_element_type=F32)
+
+
+def meta_kernel(routes_ref, gates_ref, meta_ref):
+    token_n, choose_n = routes_ref.shape
+    expert_n = meta_ref.shape[0]
+    wide = 128
+    lane = lax.broadcasted_iota(jnp.int32, (token_n, wide), 1)
+    chosen = jnp.zeros((token_n, wide), F32)
+    weight = jnp.zeros((token_n, wide), F32)
+    for k in range(choose_n):
+        hit = routes_ref[:, k : k + 1] == lane
+        chosen = jnp.where(hit, 1.0, chosen)
+        weight = jnp.where(hit, gates_ref[:, k : k + 1], weight)
+    first = lax.broadcasted_iota(jnp.int32, (token_n, token_n), 0)
+    second = lax.broadcasted_iota(jnp.int32, (token_n, token_n), 1)
+    earlier = jnp.where(second < first, 1.0, 0.0).astype(BF16)
+    rank = jnp.dot(earlier, chosen.astype(BF16), preferred_element_type=F32)
+    slot = jnp.where(chosen > 0.5, rank, -1.0)
+    slot_t = jnp.transpose(slot)
+    weight_t = jnp.transpose(weight)
+    meta_ref[...] = jnp.zeros_like(meta_ref)
+    for e in range(expert_n):
+        meta_ref[e, 0:1, :] = slot_t[e : e + 1, :]
+        meta_ref[e, 1:2, :] = weight_t[e : e + 1, :]
+
+
+def act_kernel(slot_n, pieces, where_ref, act_ref, *out_refs):
+    rows_n = act_ref.shape[0]
+    at = 0
+    for out_ref, piece_n in zip(out_refs, pieces):
+        part = piece_n * slot_n
+        row = lax.broadcasted_iota(jnp.int32, (part, 1), 0)
+        target = row + where_ref[at] * slot_n
+        for b in range(1, piece_n):
+            target = jnp.where(row >= b * slot_n, row + (where_ref[at + b] - b) * slot_n, target)
+        column = lax.broadcasted_iota(jnp.int32, (part, rows_n), 1)
+        select = jnp.where(column == target, 1.0, 0.0).astype(BF16)
+        out_ref[...] = jnp.dot(select, act_ref[...], preferred_element_type=F32).astype(BF16)
+        at += piece_n
+
+
+def selector(slot_n, piece_n, first, where_ref, meta_ref):
+    slots, weights = [], []
+    for b in range(piece_n):
+        source = where_ref[first + b]
+        slot = meta_ref[source, 0:1, :]
+        slots.append(jnp.where(slot >= 0.0, slot + float(b * slot_n), -1.0))
+        weights.append(meta_ref[source, 1:2, :])
+    slots = jnp.concatenate(slots, axis=1).astype(jnp.int32)
+    weights = jnp.concatenate(weights, axis=1)
+    row = lax.broadcasted_iota(jnp.int32, (piece_n * slot_n, slots.shape[1]), 0)
+    hit = row == slots
+    return hit, weights
+
+
+def down_kernel(slot_n, piece_n, first, halves, where_ref, meta_ref, *refs):
+    source_n = where_ref.shape[0] - 2
+    core, side = where_ref[source_n], where_ref[source_n + 1]
+    block_refs, (w_ref, keep_ref, give_ref, rows_ref) = refs[:-4], refs[-4:]
+    hit, weights = selector(slot_n, piece_n, first, where_ref, meta_ref)
+    weight = jnp.sum(jnp.where(hit, weights, 0.0), axis=1, keepdims=True)
+    select = jnp.where(hit, 1.0, 0.0).astype(BF16)
+    if halves:
+        half = block_refs[0].shape[1]
+        token_n = meta_ref.shape[2]
+        turned = jnp.concatenate([select[:, token_n:], select[:, :token_n]], axis=1)
+        for ref, chosen, place in ((block_refs[0], select, core), (block_refs[1], turned, 1 - core)):
+            value = jnp.dot(chosen, ref[...], preferred_element_type=F32)
+            at = pl.multiple_of(place * half, 128)
+            rows_ref[:, pl.ds(at, half)] = (value * weight).astype(BF16)
+    else:
+        value, at = None, 0
+        for ref in block_refs:
+            part = ref.shape[0]
+            term = jnp.dot(select[:, at : at + part], ref[...], preferred_element_type=F32)
+            value = term if value is None else value + term
+            at += part
+        rows_ref[...] = (value * weight).astype(BF16)
+    unit = keep_ref.shape[1]
+    tile = 256
+    for out_ref, place in ((give_ref, 1 - side), (keep_ref, side)):
+        for t in range(unit // tile):
+            at = pl.multiple_of(place * unit + t * tile, tile)
+            out_ref[:, t * tile : (t + 1) * tile] = dot_t(
+                rows_ref[...], w_ref[pl.ds(at, tile), :]
+            ).astype(BF16)
+
+
+def up_kernel(slot_n, piece_n, first, halves, where_ref, meta_ref, mine_ref, peer_ref, w_ref, *refs):
+    source_n = where_ref.shape[0] - 2
+    core, side = where_ref[source_n], where_ref[source_n + 1]
+    hit, _ = selector(slot_n, piece_n, first, where_ref, meta_ref)
+    select = jnp.where(hit, 1.0, 0.0).astype(BF16)
+    unit = mine_ref.shape[1]
+    token_n = meta_ref.shape[2]
+    feat_n = w_ref.shape[0]
+    tile = 256 if feat_n % 256 == 0 else 128
+    mine_at = pl.multiple_of(side * unit, 128)
+    peer_at = pl.multiple_of((1 - side) * unit, 128)
+
+    def placed(at):
+        row = dot_t(mine_ref[...], w_ref[pl.ds(at, tile), pl.ds(mine_at, unit)])
+        row = row + dot_t(peer_ref[...], w_ref[pl.ds(at, tile), pl.ds(peer_at, unit)])
+        return lax.dot_general(
+            select, row.astype(BF16), (((0,), (0,)), ((), ())), preferred_element_type=F32
+        ).astype(BF16)
+
+    if halves:
+        tile = 128
+        keep_ref, give_ref = refs
+        half = feat_n // 2
+        for t in range(half // tile):
+            value = placed(pl.multiple_of(core * half + t * tile, tile))
+            keep_ref[:token_n, t * tile : (t + 1) * tile] = value[token_n:]
+            keep_ref[token_n:, t * tile : (t + 1) * tile] = value[:token_n]
+            value = placed(pl.multiple_of((1 - core) * half + t * tile, tile))
+            give_ref[:, t * tile : (t + 1) * tile] = value
+    else:
+        for t in range(feat_n // tile):
+            value = placed(t * tile)
+            at = 0
+            for ref in refs:
+                part = ref.shape[0]
+                ref[:, t * tile : (t + 1) * tile] = value[at : at + part]
+                at += part
+
+
+def join_kernel(where_ref, keep_ref, given_ref, half_ref, out_ref):
+    source_n = where_ref.shape[0] - 2
+    core = where_ref[source_n]
+    half = half_ref.shape[1]
+    mine = pl.multiple_of(core * half, 128)
+    other = pl.multiple_of((1 - core) * half, 128)
+    total = keep_ref[:, pl.ds(mine, half)].astype(F32) + given_ref[:, pl.ds(mine, half)].astype(F32)
+    out_ref[:, pl.ds(mine, half)] = (total + half_ref[...].astype(F32)).astype(BF16)
+    total = keep_ref[:, pl.ds(other, half)].astype(F32) + given_ref[:, pl.ds(other, half)].astype(F32)
+    out_ref[:, pl.ds(other, half)] = total.astype(BF16)
+
+
+def ring_on_device(grad_out, routes, gate_weights, gate_act, w_down, w_up):
+    experts_n = lax.axis_size("ep")
+    slot_n = gate_act.shape[1] // experts_n
+    token_n = routes.shape[0]
+    feat_n = grad_out.shape[1]
+    unit_n = gate_act.shape[2]
+    chips_n = experts_n // 2
+    far = chips_n // 2
+    order = [2 * i for i in range(far)] + [2 * i + 1 for i in reversed(range(far))]
+    spot = [order.index(c) for c in range(chips_n)]
+    across = [(0, 1), (1, 0)]
+    swap = [(i, i ^ 1) for i in range(experts_n)]
+    ring = [
+        (i, 2 * order[(spot[i // 2] + 1 - 2 * (i % 2)) % chips_n] + i % 2) for i in range(experts_n)
+    ]
+
+    def to_core(x):
+        return lax.ppermute(x, "ep", swap)
+
+    def to_ring(x):
+        return lax.ppermute(x, "ep", ring)
+
+    def to_side(x):
+        return lax.ppermute(x, "tp", across)
+
+    me = lax.axis_index("ep")
+    core, side = me % 2, lax.axis_index("tp")
+    here = jnp.array(spot, jnp.int32)[me // 2]
+    table = jnp.array(order, jnp.int32)
+
+    def chip_at(distance):
+        return table[(here + distance * (2 * core - 1)) % chips_n]
+
+    sources = [me, me ^ 1]
+    for k in range(1, far):
+        mine, sib = chip_at(k), chip_at(-k)
+        sources += [2 * mine + core, 2 * mine + 1 - core, 2 * sib + 1 - core, 2 * sib + core]
+    mine = chip_at(far)
+    sources += [2 * mine + core, 2 * mine + 1 - core]
+    where = jnp.stack([s.astype(jnp.int32) for s in sources + [core, side]])
+    pieces = [2] + [4] * (far - 1) + [2]
+    firsts = [sum(pieces[:k]) for k in range(far + 1)]
+
+    blocks = [[grad_out, to_core(grad_out)]]
+    moving = jnp.concatenate(blocks[0], axis=0)
+    for k in range(1, far):
+        moving = to_ring(moving)
+        blocks.append([moving, to_core(moving)])
+    half = feat_n // 2
+    moving = to_ring(lax.dynamic_slice_in_dim(moving, core * half, half, 1))
+    blocks.append([moving, to_core(moving)])
+
+    meta = pl.pallas_call(
+        meta_kernel,
+        out_shape=jax.ShapeDtypeStruct((experts_n, 8, token_n), F32),
+        in_specs=[VMEM, VMEM],
+        out_specs=VMEM,
+        name="meta",
+    )(routes, gate_weights)
+    meta = lax.all_to_all(meta, "ep", split_axis=0, concat_axis=0, tiled=True)
+    acts = pl.pallas_call(
+        functools.partial(act_kernel, slot_n, pieces),
+        out_shape=[jax.ShapeDtypeStruct((p * slot_n, unit_n), BF16) for p in pieces],
+        in_specs=[SMEM, VMEM],
+        out_specs=[VMEM] * len(pieces),
+        compiler_params=LIMIT,
+        name="act",
+    )(where, gate_act[0])
+
+    keeps, gives = [], []
+    for k in range(far + 1):
+        rows_n = pieces[k] * slot_n
+        part = jax.ShapeDtypeStruct((rows_n, unit_n), BF16)
+        keep, give = pl.pallas_call(
+            functools.partial(down_kernel, slot_n, pieces[k], firsts[k], k == far),
+            out_shape=[part, part],
+            in_specs=[SMEM] + [VMEM] * (len(blocks[k]) + 2),
+            out_specs=[VMEM, VMEM],
+            scratch_shapes=[pltpu.VMEM((rows_n, feat_n), BF16)],
+            compiler_params=LIMIT,
+            cost_estimate=pl.CostEstimate(
+                flops=2 * rows_n * feat_n * (2 * unit_n + 128 * pieces[k]),
+                bytes_accessed=2 * feat_n * 2 * unit_n,
+                transcendentals=0,
+            ),
+            name="down%d" % k,
+        )(where, meta, *blocks[k], w_down[0])
+        hidden = keep.astype(F32) + to_side(give).astype(F32)
+        up = (hidden * acts[k].astype(F32)).astype(BF16)
+        up_peer = to_side(up)
+        if k == far:
+            outs = [jax.ShapeDtypeStruct((2 * token_n, half), BF16)] * 2
+        else:
+            outs = [jax.ShapeDtypeStruct((pieces[k] // 2 * token_n, feat_n), BF16)] * 2
+        given, kept = pl.pallas_call(
+            functools.partial(up_kernel, slot_n, pieces[k], firsts[k], k == far),
+            out_shape=outs,
+            in_specs=[SMEM] + [VMEM] * 4,
+            out_specs=[VMEM, VMEM],
+            compiler_params=LIMIT,
+            cost_estimate=pl.CostEstimate(
+                flops=2 * rows_n * feat_n * (2 * unit_n + 128 * pieces[k]),
+                bytes_accessed=2 * feat_n * 2 * unit_n,
+                transcendentals=0,
+            ),
+            name="up%d" % k,
+        )(where, meta, up, up_peer, w_up[0])
+        if k == far:
+            given, kept = kept, given
+        keeps.append(kept)
+        gives.append(given)
+
+    total = (keeps[far].astype(F32) + to_core(gives[far]).astype(F32)).astype(BF16)
+    came = to_ring(total)
+    for k in range(far - 1, 0, -1):
+        given = to_core(gives[k])
+        if k == far - 1:
+            total = pl.pallas_call(
+                join_kernel,
+                out_shape=jax.ShapeDtypeStruct((2 * token_n, feat_n), BF16),
+                in_specs=[SMEM] + [VMEM] * 3,
+                out_specs=VMEM,
+                compiler_params=LIMIT,
+                name="join",
+            )(where, keeps[k], given, came)
+        else:
+            total = (keeps[k].astype(F32) + given.astype(F32) + came.astype(F32)).astype(BF16)
+        came = to_ring(total)
+    other = (came[:token_n].astype(F32) + keeps[0].astype(F32)).astype(BF16)
+    mine = came[token_n:].astype(F32) + gives[0].astype(F32)
+    return (mine + to_core(other).astype(F32)).astype(BF16)
+
+
+def spread_on_device(grad_out, routes, gate_weights, gate_act, w_down, w_up):
     experts_n = lax.axis_size("ep")
     slot_n = gate_act.shape[1] // experts_n
     rows_n = experts_n * slot_n
@@ -58,6 +342,17 @@
         P("ep", None, "tp"),
         P("ep", "tp", None),
     )
-    return jax.shard_map(
-        on_device, mesh=mesh, in_specs=placed, out_specs=P("ep", "tp"), check_vma=False
-    )
+
+    def whole(grad_out, routes, *rest):
+        ep, tp = mesh.shape["ep"], mesh.shape["tp"]
+        dense = tp == 2 and ep % 4 == 0 and 8 <= ep <= 2 * routes.shape[1]
+        dense = dense and routes.shape[0] == 128 * ep and grad_out.shape[1] % 512 == 0
+        return jax.shard_map(
+            ring_on_device if dense else spread_on_device,
+            mesh=mesh,
+            in_specs=placed,
+            out_specs=P("ep", "tp"),
+            check_vma=False,
+        )(grad_out, routes, *rest)
+
+    return whole

time: 359 us -> 186 us (0.52)
  blocking collectives: 97.3 us -> 0 us
  waiting for transfers between devices: 158 us -> 85.9 us
  Pallas kernels: 0 us -> 40.7 us
  local copies, waits for them, and re-layouts: 49 us -> 8.37 us
  starting transfers between devices: 6.42 us -> 37.1 us
  matrix products: 17.4 us -> 0 us
  other arithmetic: 17 us -> 3.32 us
  between operations: 13.5 us -> 8.74 us
    all_to_all x1 -> x0, blocking collectives: 97.3 us -> none  [on_device(): lax.all_to_all(placed, 'ep', split_axis=0, concat_axis=0, tiled=True)]
    all_to_all x1, waiting for transfers between devices: 91.1 us -> 0.01 us  [ring_on_device(): meta = lax.all_to_all(meta, 'ep', split_axis=0, concat_axis=0, tiled=True)]
    ppermute x0 -> x28, waiting for transfers between devices: none -> 85.9 us  [the longest x8 49.2 us: to_ring(): return lax.ppermute(x, 'ep', ring)]
    pallas_call x0 -> x13, Pallas kernels: none -> 40.7 us  [the longest x5 22.7 us: ring_on_device(): pl.pallas_call(functools.partial(up_kernel, slot_n, pieces[k], firsts[k],...]
    all_gather x1 -> x0, waiting for transfers between devices: 34 us -> none  [on_device(): lax.all_gather(up_grad, 'tp', axis=1, tiled=True)]
    reduce_scatter x1 -> x0, waiting for transfers between devices: 32.5 us -> none  [on_device(): lax.psum_scatter(partial_value.astype(jnp.bfloat16), 'tp', scatter_dimens...]
    ppermute x0 -> x28, starting transfers between devices: none -> 31.1 us  [the longest x10 12.7 us: to_core(): return lax.ppermute(x, 'ep', swap)]
    dot_general x2 -> x0, matrix products: 17.4 us -> none  [the longest x1 8.74 us: on_device(): jnp.einsum('nsd,fd->nsf', lax.all_to_all(placed, 'ep', split_axis=0, conc...]
  transfers between devices with their start and end apart: 3 -> 29, of which waited for: 3 -> 15; matrix products, arithmetic and copies ran while one was open for 0% -> 2% of each run, Pallas kernels for 0% -> 22%
where the time goes in v1:
time: 186 us; the launch traced here: 184 us
  waiting for transfers between devices  85.9 us (46%)
  Pallas kernels  40.7 us (22%)
  starting transfers between devices  37.1 us (20%)
  between operations  8.74 us (5%)
  local copies, waits for them, and re-layouts  8.37 us (4%)
  other arithmetic  3.32 us (2%)
    ppermute x8, waiting for transfers between devices, to_ring(): return lax.ppermute(x, 'ep', ring)  49.2 us
    ppermute x10, waiting for transfers between devices, to_side(): return lax.ppermute(x, 'tp', across)  33.1 us
    pallas_call x5, Pallas kernels, ring_on_device(): pl.pallas_call(functools.partial(up_kernel, slot_n, pieces[k], firsts[k],...  22.7 us
    pallas_call x5, Pallas kernels, ring_on_device(): pl.pallas_call(functools.partial(down_kernel, slot_n, pieces[k], firsts[k...  12.9 us
    ppermute x10, starting transfers between devices, to_core(): return lax.ppermute(x, 'ep', swap)  12.7 us
    ppermute x8, starting transfers between devices, to_ring(): return lax.ppermute(x, 'ep', ring)  10.6 us
    ppermute x10, starting transfers between devices, to_side(): return lax.ppermute(x, 'tp', across)  7.77 us
    unnamed x40, local copies, waits for them, and re-layouts  6.95 us
  transfers between devices with their start and end apart: 29, of which 15 were waited for; matrix products, arithmetic and copies ran while one was open for 2% of the time, Pallas kernels for 22%

profile of v1, /device:TPU:13, one launch (start us, length us, event | category | flops | bytes accessed | tf_op | source)
XLA Modules:
  0.0 184.1 jit_solution(9256499783693235818)
XLA Ops:
  0.0 0.7 collective-permute-start
  0.8 1.7 collective-permute-done.refs_1_
  2.4 1.1 pad_maximum_fusion
  3.5 1.3 collective-permute-start.1
  4.9 11.2 %collective-permute-done.1.refs_0_ = bf16[256,1792]{1,0:T(8,128)(2,1)S(1)} collective-permute-done((bf16[256,1792]{1,0:T(8,128)(2,1)S(1)}, bf16[256,1792]{1,0:T(8,128)(2,1)S(1)}, u32[]{:S(2)}, u32[]{:S(2)}) %collective-permute-start.1) | collective-permute-done | bytes 917536 | tf_op jit(solution)/shard_map/ppermute | solution.py:178
  16.1 1.3 collective-permute-start.6
  17.4 11.3 %collective-permute-done.6.refs_0_ = bf16[256,1792]{1,0:T(8,128)(2,1)} collective-permute-done((bf16[256,1792]{1,0:T(8,128)(2,1)S(1)}, bf16[256,1792]{1,0:T(8,128)(2,1)}, u32[]{:S(2)}, u32[]{:S(2)}) %collective-permute-start.6) | collective-permute-done | bytes 917536 | tf_op jit(solution)/shard_map/ppermute | solution.py:178
  28.7 1.3 collective-permute-start.11
  30.0 11.5 %collective-permute-done.11.refs_0_ = bf16[256,1792]{1,0:T(8,128)(2,1)S(1)} collective-permute-done((bf16[256,1792]{1,0:T(8,128)(2,1)}, bf16[256,1792]{1,0:T(8,128)(2,1)S(1)}, u32[]{:S(2)}, u32[]{:S(2)}) %collective-permute-start.11) | collective-permute-done | bytes 917536 | tf_op jit(solution)/shard_map/ppermute | solution.py:178
  41.5 1.3 collective-permute-start.16
  42.9 2.1 %collective-permute-start.12 = (bf16[256,1792]{1,0:T(8,128)(2,1)S(1)}, bf16[256,1792]{1,0:T(8,128)(2,1)}, u32[]{:S(2)}, u32[]{:S(2)}) collective-permute-start(bf16[256,1792]{1,0:T(8,128)(2,1)S(1)} %collective-permute-done.11.refs_0_), channel_id=1, source_target_pairs={{0,2},{2,0},{4,6},{6,4},{8,10},{10,8},{12,14},{14,12},{16,18},{18,... | collective-permute-start | bytes 2752520 | tf_op jit(solution)/shard_map/ppermute | solution.py:175
  45.0 4.3 %collective-permute-done.16.refs_0_ = bf16[256,896]{1,0:T(8,128)(2,1)} collective-permute-done((bf16[256,896]{1,0:T(8,128)(2,1)S(1)}, bf16[256,896]{1,0:T(8,128)(2,1)}, u32[]{:S(2)}, u32[]{:S(2)}) %collective-permute-start.16) | collective-permute-done | bytes 458784 | tf_op jit(solution)/shard_map/ppermute | solution.py:178
  49.3 3.8 %collective-permute-start.17 = (bf16[256,896]{1,0:T(8,128)(2,1)}, bf16[256,896]{1,0:T(8,128)(2,1)}, u32[]{:S(2)}, u32[]{:S(2)}) collective-permute-start(bf16[256,896]{1,0:T(8,128)(2,1)} %collective-permute-done.16.refs_0_), channel_id=1, source_target_pairs={{0,2},{2,0},{4,6},{6,4},{8,10},{10,8},{12,14},{14,12},{16,18},{18,... | collective-permute-start | bytes 1376264 | tf_op jit(solution)/shard_map/ppermute | solution.py:175
  54.6 2.0 %meta.1 = f32[16,8,128]{2,1,0:T(8,128)} custom-call(s32[128,8]{1,0:T(8,128)} %copy.9.routes_ref, f32[128,8]{1,0:T(8,128)} %copy.10.gates_ref), custom_call_target="tpu_custom_call" | custom-call | tf_op jit(solution)/shard_map/meta/pallas_call | solution.py:210
  56.6 6.0 %all-to-all-start = ((f32[16,8,128]{2,1,0:T(8,128)}), f32[16,8,128]{2,1,0:T(8,128)S(1)}, u32[]{:S(2)}, u32[]{:S(2)}) async-start(f32[16,8,128]{2,1,0:T(8,128)} %meta.1), calls=%async_computation | async-start | bytes 131072 | tf_op jit(solution)/shard_map/all_to_all | solution.py:217
  72.4 2.2 %act.1 = (bf16[132,512]{1,0:T(8,128)(2,1)S(1)}, bf16[264,512]{1,0:T(8,128)(2,1)S(1)}, bf16[264,512]{1,0:T(8,128)(2,1)S(1)}, bf16[264,512]{1,0:T(8,128)(2,1)S(1)}, bf16[132,512]{1,0:T(8,128)(2,1)S(1)}) custom-call(s32[18]{0:T(128)S(1)} %stack.75.where_ref, bf16[1056,512]{1,0:T(8,128)(2,1)S(1)} %bitcast.39), custom_call_target="tpu_custom_call" | custom-call | tf_op jit(solution)/shard_map/act/pallas_call | solution.py:218
  78.4 2.0 %copy-done = bf16[1,1024,1792]{2,1,0:T(8,128)(2,1)S(1)} copy-done((bf16[1,1024,1792]{2,1,0:T(8,128)(2,1)S(1)}, bf16[1,1024,1792]{2,1,0:T(8,128)(2,1)}, u32[]{:S(2)}) %copy-start) | copy-done | bytes 3670040
  80.4 2.8 %down4.1 = (bf16[132,512]{1,0:T(8,128)(2,1)S(1)}, bf16[132,512]{1,0:T(8,128)(2,1)S(1)}) custom-call(s32[18]{0:T(128)S(1)} %stack.75.where_ref, f32[16,8,128]{2,1,0:T(8,128)S(1)} %all-to-all-done.meta_ref, bf16[256,896]{1,0:T(8,128)(2,1)} %collective-permute-done.16.refs_0_, bf16[256,896]{1,0:T(8,128)(2,1)} %collective-permute-done.17.refs_1_, ...), custom_call_target="tpu_custom_call" | custom-call | flops 605552640 | bytes 3670016 | tf_op jit(solution)/shard_map/down4/pallas_call | solution.py:231
  83.2 1.3 collective-permute-start.18
  84.5 2.9 %down3.1 = (bf16[264,512]{1,0:T(8,128)(2,1)S(1)}, bf16[264,512]{1,0:T(8,128)(2,1)S(1)}) custom-call(s32[18]{0:T(128)S(1)} %stack.75.where_ref, f32[16,8,128]{2,1,0:T(8,128)S(1)} %all-to-all-done.meta_ref, bf16[256,1792]{1,0:T(8,128)(2,1)S(1)} %collective-permute-done.11.refs_0_, bf16[256,1792]{1,0:T(8,128)(2,1)} %collective-permute-done.12.refs_1_, ...), custom_call_target="tpu_custom_call" | custom-call | flops 1453326336 | bytes 3670016 | tf_op jit(solution)/shard_map/down3/pallas_call | solution.py:231
  88.5 1.3 collective-permute-start.19
  89.8 8.3 %collective-permute-done.19.peer_ref = bf16[132,512]{1,0:T(8,128)(2,1)S(1)} collective-permute-done((bf16[132,512]{1,0:T(8,128)(2,1)S(1)}, bf16[132,512]{1,0:T(8,128)(2,1)S(1)}, u32[]{:S(2)}, u32[]{:S(2)}) %collective-permute-start.19) | collective-permute-done | bytes 135200 | tf_op jit(solution)/shard_map/ppermute | solution.py:181
  98.1 5.2 %up4.1 = (bf16[256,896]{1,0:T(8,128)(2,1)S(1)}, bf16[256,896]{1,0:T(8,128)(2,1)S(1)}) custom-call(s32[18]{0:T(128)S(1)} %stack.75.where_ref, f32[16,8,128]{2,1,0:T(8,128)S(1)} %all-to-all-done.meta_ref, bf16[132,512]{1,0:T(8,128)(2,1)S(1)} %multiply_convert_fusion.4.mine_ref, bf16[132,512]{1,0:T(8,128)(2,1)S(1)} %collective-permute-done.19.peer_ref, ...), custom_call_target="tpu_custom_call" | custom-call | flops 605552640 | bytes 3670016 | tf_op jit(solution)/shard_map/up4/pallas_call | solution.py:252
  103.3 1.3 collective-permute-start.20
  105.6 2.9 %down2.1 = (bf16[264,512]{1,0:T(8,128)(2,1)S(1)}, bf16[264,512]{1,0:T(8,128)(2,1)S(1)}) custom-call(s32[18]{0:T(128)S(1)} %stack.75.where_ref, f32[16,8,128]{2,1,0:T(8,128)S(1)} %all-to-all-done.meta_ref, bf16[256,1792]{1,0:T(8,128)(2,1)} %collective-permute-done.6.refs_0_, bf16[256,1792]{1,0:T(8,128)(2,1)S(1)} %collective-permute-done.7.refs_1_, ...), custom_call_target="tpu_custom_call" | custom-call | flops 1453326336 | bytes 3670016 | tf_op jit(solution)/shard_map/down2/pallas_call | solution.py:231
  108.5 1.1 collective-permute-start.8
  109.6 3.3 %collective-permute-done.14.peer_ref = bf16[264,512]{1,0:T(8,128)(2,1)S(1)} collective-permute-done((bf16[264,512]{1,0:T(8,128)(2,1)S(1)}, bf16[264,512]{1,0:T(8,128)(2,1)S(1)}, u32[]{:S(2)}, u32[]{:S(2)}) %collective-permute-start.14) | collective-permute-done | bytes 270368 | tf_op jit(solution)/shard_map/ppermute | solution.py:181
  112.9 4.7 %up3.1 = (bf16[256,1792]{1,0:T(8,128)(2,1)S(1)}, bf16[256,1792]{1,0:T(8,128)(2,1)S(1)}) custom-call(s32[18]{0:T(128)S(1)} %stack.75.where_ref, f32[16,8,128]{2,1,0:T(8,128)S(1)} %all-to-all-done.meta_ref, bf16[264,512]{1,0:T(8,128)(2,1)S(1)} %multiply_convert_fusion.mine_ref, bf16[264,512]{1,0:T(8,128)(2,1)S(1)} %collective-permute-done.14.peer_ref, ...), custom_call_target="tpu_custom_call" | custom-call | flops 1453326336 | bytes 3670016 | tf_op jit(solution)/shard_map/up3/pallas_call | solution.py:252
  117.6 1.3 collective-permute-start.15
  119.0 1.4 collective-permute-start.21
  121.0 2.2 %down1.1 = (bf16[264,512]{1,0:T(8,128)(2,1)S(1)}, bf16[264,512]{1,0:T(8,128)(2,1)S(1)}) custom-call(s32[18]{0:T(128)S(1)} %stack.75.where_ref, f32[16,8,128]{2,1,0:T(8,128)S(1)} %all-to-all-done.meta_ref, bf16[256,1792]{1,0:T(8,128)(2,1)S(1)} %collective-permute-done.1.refs_0_, bf16[256,1792]{1,0:T(8,128)(2,1)S(1)} %collective-permute-done.2.refs_1_, ...), custom_call_target="tpu_custom_call" | custom-call | flops 1453326336 | bytes 3670016 | tf_op jit(solution)/shard_map/down1/pallas_call | solution.py:231
  123.3 1.1 collective-permute-start.3
  124.4 4.7 %collective-permute-done.9.peer_ref = bf16[264,512]{1,0:T(8,128)(2,1)S(1)} collective-permute-done((bf16[264,512]{1,0:T(8,128)(2,1)S(1)}, bf16[264,512]{1,0:T(8,128)(2,1)S(1)}, u32[]{:S(2)}, u32[]{:S(2)}) %collective-permute-start.9) | collective-permute-done | bytes 270368 | tf_op jit(solution)/shard_map/ppermute | solution.py:181
  129.1 4.7 %up2.1 = (bf16[256,1792]{1,0:T(8,128)(2,1)S(1)}, bf16[256,1792]{1,0:T(8,128)(2,1)S(1)}) custom-call(s32[18]{0:T(128)S(1)} %stack.75.where_ref, f32[16,8,128]{2,1,0:T(8,128)S(1)} %all-to-all-done.meta_ref, bf16[264,512]{1,0:T(8,128)(2,1)S(1)} %multiply_convert_fusion.1.mine_ref, bf16[264,512]{1,0:T(8,128)(2,1)S(1)} %collective-permute-done.9.peer_ref, ...), custom_call_target="tpu_custom_call" | custom-call | flops 1453326336 | bytes 3670016 | tf_op jit(solution)/shard_map/up2/pallas_call | solution.py:252
  134.0 0.8 join.1
  134.8 1.2 collective-permute-start.22
  136.7 7.9 %collective-permute-done.4.peer_ref = bf16[264,512]{1,0:T(8,128)(2,1)S(1)} collective-permute-done((bf16[264,512]{1,0:T(8,128)(2,1)S(1)}, bf16[264,512]{1,0:T(8,128)(2,1)S(1)}, u32[]{:S(2)}, u32[]{:S(2)}) %collective-permute-start.4) | collective-permute-done | bytes 270368 | tf_op jit(solution)/shard_map/ppermute | solution.py:181
  144.6 4.7 %up1.1 = (bf16[256,1792]{1,0:T(8,128)(2,1)S(1)}, bf16[256,1792]{1,0:T(8,128)(2,1)S(1)}) custom-call(s32[18]{0:T(128)S(1)} %stack.75.where_ref, f32[16,8,128]{2,1,0:T(8,128)S(1)} %all-to-all-done.meta_ref, bf16[264,512]{1,0:T(8,128)(2,1)S(1)} %multiply_convert_fusion.2.mine_ref, bf16[264,512]{1,0:T(8,128)(2,1)S(1)} %collective-permute-done.4.peer_ref, ...), custom_call_target="tpu_custom_call" | custom-call | flops 1453326336 | bytes 3670016 | tf_op jit(solution)/shard_map/up1/pallas_call | solution.py:252
  150.2 1.3 collective-permute-start.23
  151.9 10.8 %collective-permute-done.23 = bf16[256,1792]{1,0:T(8,128)(2,1)S(1)} collective-permute-done((bf16[256,1792]{1,0:T(8,128)(2,1)S(1)}, bf16[256,1792]{1,0:T(8,128)(2,1)S(1)}, u32[]{:S(2)}, u32[]{:S(2)}) %collective-permute-start.23) | collective-permute-done | bytes 917536 | tf_op jit(solution)/shard_map/ppermute | solution.py:178
  163.1 1.3 collective-permute-start.24
  164.4 2.1 %down0.1 = (bf16[132,512]{1,0:T(8,128)(2,1)S(1)}, bf16[132,512]{1,0:T(8,128)(2,1)S(1)}) custom-call(s32[18]{0:T(128)S(1)} %stack.75.where_ref, f32[16,8,128]{2,1,0:T(8,128)S(1)} %all-to-all-done.meta_ref, bf16[128,1792]{1,0:T(8,128)(2,1)S(1)} %copy-done.3, bf16[128,1792]{1,0:T(8,128)(2,1)S(1)} %collective-permute-done.refs_1_, bf16[1024,1792]{1,0:T(8,128)(2,1)S(1)} %bitcast.33), custom_call_target="tpu_custom_call" | custom-call | flops 605552640 | bytes 3670016 | tf_op jit(solution)/shard_map/down0/pallas_call | solution.py:231
  167.1 4.6 %collective-permute-done.25 = bf16[132,512]{1,0:T(8,128)(2,1)S(1)} collective-permute-done((bf16[132,512]{1,0:T(8,128)(2,1)S(1)}, bf16[132,512]{1,0:T(8,128)(2,1)S(1)}, u32[]{:S(2)}, u32[]{:S(2)}) %collective-permute-start.25) | collective-permute-done | bytes 135200 | tf_op jit(solution)/shard_map/ppermute | solution.py:181
  172.3 3.8 %collective-permute-done.26.peer_ref = bf16[132,512]{1,0:T(8,128)(2,1)S(1)} collective-permute-done((bf16[132,512]{1,0:T(8,128)(2,1)S(1)}, bf16[132,512]{1,0:T(8,128)(2,1)S(1)}, u32[]{:S(2)}, u32[]{:S(2)}) %collective-permute-start.26) | collective-permute-done | bytes 135200 | tf_op jit(solution)/shard_map/ppermute | solution.py:181
  176.1 3.5 %up0.1 = (bf16[128,1792]{1,0:T(8,128)(2,1)S(1)}, bf16[128,1792]{1,0:T(8,128)(2,1)S(1)}) custom-call(s32[18]{0:T(128)S(1)} %stack.75.where_ref, f32[16,8,128]{2,1,0:T(8,128)S(1)} %all-to-all-done.meta_ref, bf16[132,512]{1,0:T(8,128)(2,1)S(1)} %multiply_convert_fusion.3.mine_ref, bf16[132,512]{1,0:T(8,128)(2,1)S(1)} %collective-permute-done.26.peer_ref, ...), custom_call_target="tpu_custom_call" | custom-call | flops 605552640 | bytes 3670016 | tf_op jit(solution)/shard_map/up0/pallas_call | solution.py:252
  179.7 2.0 %collective-permute-start.27 = (bf16[128,1792]{1,0:T(8,128)(2,1)S(1)}, bf16[128,1792]{1,0:T(8,128)(2,1)S(1)}, u32[]{:S(2)}, u32[]{:S(2)}) collective-permute-start(bf16[128,1792]{1,0:T(8,128)(2,1)S(1)} %add_convert_fusion.3), channel_id=1, source_target_pairs={{0,2},{2,0},{4,6},{6,4},{8,10},{10,8},{12,14},{14,12},{16,18},{18,... | collective-permute-start | bytes 1376264 | tf_op jit(solution)/shard_map/ppermute | solution.py:175
  181.7 1.4 collective-permute-done.27
  183.1 0.9 add_convert_fusion.2
  (78 shorter events, 13.1 us)
Async XLA Ops:
  0.0 62.6 %copy-start.18 = (s32[8]{0:T(128)S(1)}, s32[8]{0:T(128)}, u32[]{:S(2)}) copy-start(s32[8]{0:T(128)} %constant.94.clone) | copy-start | bytes 100
  0.0 67.3 %copy-start.15 = (s32[8]{0:T(128)S(1)}, s32[8]{0:T(128)}, u32[]{:S(2)}) copy-start(s32[8]{0:T(128)} %constant.95.clone) | copy-start | bytes 100
  0.0 53.1 %copy-start.16 = (s32[128,8]{0,1:T(8,128)S(1)}, s32[128,8]{0,1:T(8,128)}, u32[]{:S(2)}) copy-start(s32[128,8]{0,1:T(8,128)} %param.9) | copy-start | bytes 12292
  0.0 53.8 %copy-start.17 = (f32[128,8]{0,1:T(8,128)S(1)}, f32[128,8]{0,1:T(8,128)}, u32[]{:S(2)}) copy-start(f32[128,8]{0,1:T(8,128)} %param.10) | copy-start | bytes 12292
  0.0 72.4 %copy-start.4 = (bf16[1,1056,512]{2,1,0:T(8,128)(2,1)S(1)}, bf16[1,1056,512]{2,1,0:T(8,128)(2,1)}, u32[]{:S(2)}) copy-start(bf16[1,1056,512]{2,1,0:T(8,128)(2,1)} %param.11) | copy-start | bytes 3244036
  0.0 2.4 %collective-permute-start = (bf16[128,1792]{1,0:T(8,128)(2,1)}, bf16[128,1792]{1,0:T(8,128)(2,1)S(1)}, u32[]{:S(2)}, u32[]{:S(2)}) collective-permute-start(bf16[128,1792]{1,0:T(8,128)(2,1)} %refs_0_.1), channel_id=1, source_target_pairs={{0,2},{2,0},{4,6},{6,4},{8,10},{10,8},{12,14},{14,12},{16,18},{18,... | collective-permute-start | bytes 1376264 | tf_op jit(solution)/shard_map/ppermute | solution.py:175
  3.5 12.6 %collective-permute-start.1 = (bf16[256,1792]{1,0:T(8,128)(2,1)S(1)}, bf16[256,1792]{1,0:T(8,128)(2,1)S(1)}, u32[]{:S(2)}, u32[]{:S(2)}) collective-permute-start(bf16[256,1792]{1,0:T(8,128)(2,1)S(1)} %pad_maximum_fusion), channel_id=1, source_target_pairs={{0,8},{2,6},{4,0},{6,14},{8,16},{10,2},{12,4},{14,22},{16,24},{18,... | collective-permute-start | bytes 2752520 | tf_op jit(solution)/shard_map/ppermute | solution.py:178
  16.1 12.6 %collective-permute-start.6 = (bf16[256,1792]{1,0:T(8,128)(2,1)S(1)}, bf16[256,1792]{1,0:T(8,128)(2,1)}, u32[]{:S(2)}, u32[]{:S(2)}) collective-permute-start(bf16[256,1792]{1,0:T(8,128)(2,1)S(1)} %collective-permute-done.1.refs_0_), channel_id=1, source_target_pairs={{0,8},{2,6},{4,0},{6,14},{8,16},{10,2},{12,4},{14,22},{16,24},{18,... | collective-permute-start | bytes 2752520 | tf_op jit(solution)/shard_map/ppermute | solution.py:178
  28.7 12.8 %collective-permute-start.11 = (bf16[256,1792]{1,0:T(8,128)(2,1)}, bf16[256,1792]{1,0:T(8,128)(2,1)S(1)}, u32[]{:S(2)}, u32[]{:S(2)}) collective-permute-start(bf16[256,1792]{1,0:T(8,128)(2,1)} %collective-permute-done.6.refs_0_), channel_id=1, source_target_pairs={{0,8},{2,6},{4,0},{6,14},{8,16},{10,2},{12,4},{14,22},{16,24},{18,... | collective-permute-start | bytes 2752520 | tf_op jit(solution)/shard_map/ppermute | solution.py:178
  41.5 7.8 %collective-permute-start.16 = (bf16[256,896]{1,0:T(8,128)(2,1)S(1)}, bf16[256,896]{1,0:T(8,128)(2,1)}, u32[]{:S(2)}, u32[]{:S(2)}) collective-permute-start(bf16[256,896]{1,0:T(8,128)(2,1)S(1)} %constant_dynamic-slice_fusion), channel_id=1, source_target_pairs={{0,8},{2,6},{4,0},{6,14},{8,16},{10,2},{12,4},{14,22},{16,24},{18,... | collective-permute-start | bytes 1376264 | tf_op jit(solution)/shard_map/ppermute | solution.py:178
  42.9 41.6 %collective-permute-start.12 = (bf16[256,1792]{1,0:T(8,128)(2,1)S(1)}, bf16[256,1792]{1,0:T(8,128)(2,1)}, u32[]{:S(2)}, u32[]{:S(2)}) collective-permute-start(bf16[256,1792]{1,0:T(8,128)(2,1)S(1)} %collective-permute-done.11.refs_0_), channel_id=1, source_target_pairs={{0,2},{2,0},{4,6},{6,4},{8,10},{10,8},{12,14},{14,12},{16,18},{18,... | collective-permute-start | bytes 2752520 | tf_op jit(solution)/shard_map/ppermute | solution.py:175
  49.3 29.1 %collective-permute-start.17 = (bf16[256,896]{1,0:T(8,128)(2,1)}, bf16[256,896]{1,0:T(8,128)(2,1)}, u32[]{:S(2)}, u32[]{:S(2)}) collective-permute-start(bf16[256,896]{1,0:T(8,128)(2,1)} %collective-permute-done.16.refs_0_), channel_id=1, source_target_pairs={{0,2},{2,0},{4,6},{6,4},{8,10},{10,8},{12,14},{14,12},{16,18},{18,... | collective-permute-start | bytes 1376264 | tf_op jit(solution)/shard_map/ppermute | solution.py:175
  56.6 21.8 %all-to-all-start = ((f32[16,8,128]{2,1,0:T(8,128)}), f32[16,8,128]{2,1,0:T(8,128)S(1)}, u32[]{:S(2)}, u32[]{:S(2)}) async-start(f32[16,8,128]{2,1,0:T(8,128)} %meta.1), calls=%async_computation | async-start | bytes 131072 | tf_op jit(solution)/shard_map/all_to_all | solution.py:217
  74.6 0.7 copy-start.5
  75.3 0.7 copy-start.7
  76.0 0.7 copy-start.9
  76.7 0.7 copy-start.11
  77.4 0.7 copy-start.13
  78.0 27.6 %collective-permute-start.7 = (bf16[256,1792]{1,0:T(8,128)(2,1)}, bf16[256,1792]{1,0:T(8,128)(2,1)S(1)}, u32[]{:S(2)}, u32[]{:S(2)}) collective-permute-start(bf16[256,1792]{1,0:T(8,128)(2,1)} %collective-permute-done.6.refs_0_), channel_id=1, source_target_pairs={{0,2},{2,0},{4,6},{6,4},{8,10},{10,8},{12,14},{14,12},{16,18},{18,... | collective-permute-start | bytes 2752520 | tf_op jit(solution)/shard_map/ppermute | solution.py:175
  78.4 2.0 %copy-start = (bf16[1,1024,1792]{2,1,0:T(8,128)(2,1)S(1)}, bf16[1,1024,1792]{2,1,0:T(8,128)(2,1)}, u32[]{:S(2)}) copy-start(bf16[1,1024,1792]{2,1,0:T(8,128)(2,1)} %param.12) | copy-start | bytes 11010052
  83.2 5.2 %copy-start.14 = (bf16[132,512]{1,0:T(8,128)(2,1)S(1)}, bf16[132,512]{1,0:T(8,128)(2,1)}, u32[]{:S(2)}) copy-start(bf16[132,512]{1,0:T(8,128)(2,1)} %copy-done.13) | copy-start | bytes 405508
  83.2 14.9 %copy-start.2 = (bf16[1,1792,1024]{2,1,0:T(8,128)(2,1)S(1)}, bf16[1,1792,1024]{2,1,0:T(8,128)(2,1)}, u32[]{:S(2)}) copy-start(bf16[1,1792,1024]{2,1,0:T(8,128)(2,1)} %param.13) | copy-start | bytes 11010052
  83.2 5.2 %collective-permute-start.18 = (bf16[132,512]{1,0:T(8,128)(2,1)S(1)}, bf16[132,512]{1,0:T(8,128)(2,1)S(1)}, u32[]{:S(2)}, u32[]{:S(2)}) collective-permute-start(bf16[132,512]{1,0:T(8,128)(2,1)S(1)} %get-tuple-element.46), channel_id=1, source_target_pairs={{0,1},{1,0},{2,3},{3,2},{4,5},{5,4},{6,7},{7,6},{8,9},{9,8},{10,11... | collective-permute-start | bytes 405512 | tf_op jit(solution)/shard_map/ppermute | solution.py:181
  87.4 17.2 %collective-permute-start.13 = (bf16[264,512]{1,0:T(8,128)(2,1)S(1)}, bf16[264,512]{1,0:T(8,128)(2,1)S(1)}, u32[]{:S(2)}, u32[]{:S(2)}) collective-permute-start(bf16[264,512]{1,0:T(8,128)(2,1)S(1)} %get-tuple-element.41), channel_id=1, source_target_pairs={{0,1},{1,0},{2,3},{3,2},{4,5},{5,4},{6,7},{7,6},{8,9},{9,8},{10,11... | collective-permute-start | bytes 811016 | tf_op jit(solution)/shard_map/ppermute | solution.py:181
  88.5 9.6 %collective-permute-start.19 = (bf16[132,512]{1,0:T(8,128)(2,1)S(1)}, bf16[132,512]{1,0:T(8,128)(2,1)S(1)}, u32[]{:S(2)}, u32[]{:S(2)}) collective-permute-start(bf16[132,512]{1,0:T(8,128)(2,1)S(1)} %multiply_convert_fusion.4.mine_ref), channel_id=1, source_target_pairs={{0,1},{1,0},{2,3},{3,2},{4,5},{5,4},{6,7},{7,6},{8,9},{9,8},{10,11... | collective-permute-start | bytes 405512 | tf_op jit(solution)/shard_map/ppermute | solution.py:181
  98.1 6.6 %copy-start.10 = (bf16[264,512]{1,0:T(8,128)(2,1)S(1)}, bf16[264,512]{1,0:T(8,128)(2,1)}, u32[]{:S(2)}) copy-start(bf16[264,512]{1,0:T(8,128)(2,1)} %copy-done.9) | copy-start | bytes 811012
  98.1 7.5 %copy-start.1 = (bf16[1,1024,1792]{2,1,0:T(8,128)(2,1)S(1)}, bf16[1,1024,1792]{2,1,0:T(8,128)(2,1)}, u32[]{:S(2)}) copy-start(bf16[1,1024,1792]{2,1,0:T(8,128)(2,1)} %param.12) | copy-start | bytes 11010052
  103.3 15.6 %collective-permute-start.20 = (bf16[256,896]{1,0:T(8,128)(2,1)S(1)}, bf16[256,896]{1,0:T(8,128)(2,1)S(1)}, u32[]{:S(2)}, u32[]{:S(2)}) collective-permute-start(bf16[256,896]{1,0:T(8,128)(2,1)S(1)} %get-tuple-element.49), channel_id=1, source_target_pairs={{0,2},{2,0},{4,6},{6,4},{8,10},{10,8},{12,14},{14,12},{16,18},{18,... | collective-permute-start | bytes 1376264 | tf_op jit(solution)/shard_map/ppermute | solution.py:175
  104.8 8.1 %collective-permute-start.14 = (bf16[264,512]{1,0:T(8,128)(2,1)S(1)}, bf16[264,512]{1,0:T(8,128)(2,1)S(1)}, u32[]{:S(2)}, u32[]{:S(2)}) collective-permute-start(bf16[264,512]{1,0:T(8,128)(2,1)S(1)} %multiply_convert_fusion.mine_ref), channel_id=1, source_target_pairs={{0,1},{1,0},{2,3},{3,2},{4,5},{5,4},{6,7},{7,6},{8,9},{9,8},{10,11... | collective-permute-start | bytes 811016 | tf_op jit(solution)/shard_map/ppermute | solution.py:181
  105.3 15.8 %collective-permute-start.2 = (bf16[256,1792]{1,0:T(8,128)(2,1)S(1)}, bf16[256,1792]{1,0:T(8,128)(2,1)S(1)}, u32[]{:S(2)}, u32[]{:S(2)}) collective-permute-start(bf16[256,1792]{1,0:T(8,128)(2,1)S(1)} %collective-permute-done.1.refs_0_), channel_id=1, source_target_pairs={{0,2},{2,0},{4,6},{6,4},{8,10},{10,8},{12,14},{14,12},{16,18},{18,... | collective-permute-start | bytes 2752520 | tf_op jit(solution)/shard_map/ppermute | solution.py:175
  108.5 11.9 %copy-start.8 = (bf16[264,512]{1,0:T(8,128)(2,1)S(1)}, bf16[264,512]{1,0:T(8,128)(2,1)}, u32[]{:S(2)}) copy-start(bf16[264,512]{1,0:T(8,128)(2,1)} %copy-done.7) | copy-start | bytes 811012
  108.5 11.9 %collective-permute-start.8 = (bf16[264,512]{1,0:T(8,128)(2,1)S(1)}, bf16[264,512]{1,0:T(8,128)(2,1)S(1)}, u32[]{:S(2)}, u32[]{:S(2)}) collective-permute-start(bf16[264,512]{1,0:T(8,128)(2,1)S(1)} %get-tuple-element.36), channel_id=1, source_target_pairs={{0,1},{1,0},{2,3},{3,2},{4,5},{5,4},{6,7},{7,6},{8,9},{9,8},{10,11... | collective-permute-start | bytes 811016 | tf_op jit(solution)/shard_map/ppermute | solution.py:181
  117.6 16.4 %collective-permute-start.15 = (bf16[256,1792]{1,0:T(8,128)(2,1)S(1)}, bf16[256,1792]{1,0:T(8,128)(2,1)S(1)}, u32[]{:S(2)}, u32[]{:S(2)}) collective-permute-start(bf16[256,1792]{1,0:T(8,128)(2,1)S(1)} %get-tuple-element.44), channel_id=1, source_target_pairs={{0,2},{2,0},{4,6},{6,4},{8,10},{10,8},{12,14},{14,12},{16,18},{18,... | collective-permute-start | bytes 2752520 | tf_op jit(solution)/shard_map/ppermute | solution.py:175
  119.0 15.0 %collective-permute-start.21 = (bf16[256,896]{1,0:T(8,128)(2,1)S(1)}, bf16[256,896]{1,0:T(8,128)(2,1)S(1)}, u32[]{:S(2)}, u32[]{:S(2)}) collective-permute-start(bf16[256,896]{1,0:T(8,128)(2,1)S(1)} %add_convert_fusion.4), channel_id=1, source_target_pairs={{0,8},{2,6},{4,0},{6,14},{8,16},{10,2},{12,4},{14,22},{16,24},{18,... | collective-permute-start | bytes 1376264 | tf_op jit(solution)/shard_map/ppermute | solution.py:178
  120.5 8.6 %collective-permute-start.9 = (bf16[264,512]{1,0:T(8,128)(2,1)S(1)}, bf16[264,512]{1,0:T(8,128)(2,1)S(1)}, u32[]{:S(2)}, u32[]{:S(2)}) collective-permute-start(bf16[264,512]{1,0:T(8,128)(2,1)S(1)} %multiply_convert_fusion.1.mine_ref), channel_id=1, source_target_pairs={{0,1},{1,0},{2,3},{3,2},{4,5},{5,4},{6,7},{7,6},{8,9},{9,8},{10,11... | collective-permute-start | bytes 811016 | tf_op jit(solution)/shard_map/ppermute | solution.py:181
  123.3 12.7 %collective-permute-start.3 = (bf16[264,512]{1,0:T(8,128)(2,1)S(1)}, bf16[264,512]{1,0:T(8,128)(2,1)S(1)}, u32[]{:S(2)}, u32[]{:S(2)}) collective-permute-start(bf16[264,512]{1,0:T(8,128)(2,1)S(1)} %get-tuple-element.31), channel_id=1, source_target_pairs={{0,1},{1,0},{2,3},{3,2},{4,5},{5,4},{6,7},{7,6},{8,9},{9,8},{10,11... | collective-permute-start | bytes 811016 | tf_op jit(solution)/shard_map/ppermute | solution.py:181
  133.7 2.3 %copy-start.6 = (bf16[264,512]{1,0:T(8,128)(2,1)S(1)}, bf16[264,512]{1,0:T(8,128)(2,1)}, u32[]{:S(2)}) copy-start(bf16[264,512]{1,0:T(8,128)(2,1)} %copy-done.5) | copy-start | bytes 811012
  133.8 16.1 %collective-permute-start.10 = (bf16[256,1792]{1,0:T(8,128)(2,1)S(1)}, bf16[256,1792]{1,0:T(8,128)(2,1)S(1)}, u32[]{:S(2)}, u32[]{:S(2)}) collective-permute-start(bf16[256,1792]{1,0:T(8,128)(2,1)S(1)} %get-tuple-element.39), channel_id=1, source_target_pairs={{0,2},{2,0},{4,6},{6,4},{8,10},{10,8},{12,14},{14,12},{16,18},{18,... | collective-permute-start | bytes 2752520 | tf_op jit(solution)/shard_map/ppermute | solution.py:175
  134.8 15.1 %collective-permute-start.22 = (bf16[256,1792]{1,0:T(8,128)(2,1)S(1)}, bf16[256,1792]{1,0:T(8,128)(2,1)S(1)}, u32[]{:S(2)}, u32[]{:S(2)}) collective-permute-start(bf16[256,1792]{1,0:T(8,128)(2,1)S(1)} %join.1), channel_id=1, source_target_pairs={{0,8},{2,6},{4,0},{6,14},{8,16},{10,2},{12,4},{14,22},{16,24},{18,... | collective-permute-start | bytes 2752520 | tf_op jit(solution)/shard_map/ppermute | solution.py:178
  136.1 8.4 %collective-permute-start.4 = (bf16[264,512]{1,0:T(8,128)(2,1)S(1)}, bf16[264,512]{1,0:T(8,128)(2,1)S(1)}, u32[]{:S(2)}, u32[]{:S(2)}) collective-permute-start(bf16[264,512]{1,0:T(8,128)(2,1)S(1)} %multiply_convert_fusion.2.mine_ref), channel_id=1, source_target_pairs={{0,1},{1,0},{2,3},{3,2},{4,5},{5,4},{6,7},{7,6},{8,9},{9,8},{10,11... | collective-permute-start | bytes 811016 | tf_op jit(solution)/shard_map/ppermute | solution.py:181
  149.2 2.7 %collective-permute-start.5 = (bf16[256,1792]{1,0:T(8,128)(2,1)S(1)}, bf16[256,1792]{1,0:T(8,128)(2,1)S(1)}, u32[]{:S(2)}, u32[]{:S(2)}) collective-permute-start(bf16[256,1792]{1,0:T(8,128)(2,1)S(1)} %get-tuple-element.34), channel_id=1, source_target_pairs={{0,2},{2,0},{4,6},{6,4},{8,10},{10,8},{12,14},{14,12},{16,18},{18,... | collective-permute-start | bytes 2752520 | tf_op jit(solution)/shard_map/ppermute | solution.py:175
  150.2 12.6 %collective-permute-start.23 = (bf16[256,1792]{1,0:T(8,128)(2,1)S(1)}, bf16[256,1792]{1,0:T(8,128)(2,1)S(1)}, u32[]{:S(2)}, u32[]{:S(2)}) collective-permute-start(bf16[256,1792]{1,0:T(8,128)(2,1)S(1)} %add_convert_fusion.1), channel_id=1, source_target_pairs={{0,8},{2,6},{4,0},{6,14},{8,16},{10,2},{12,4},{14,22},{16,24},{18,... | collective-permute-start | bytes 2752520 | tf_op jit(solution)/shard_map/ppermute | solution.py:178
  162.8 1.7 copy-start.3
  163.1 8.6 %copy-start.12 = (bf16[132,512]{1,0:T(8,128)(2,1)S(1)}, bf16[132,512]{1,0:T(8,128)(2,1)}, u32[]{:S(2)}) copy-start(bf16[132,512]{1,0:T(8,128)(2,1)} %copy-done.11) | copy-start | bytes 405508
  163.1 16.5 %collective-permute-start.24 = (bf16[256,1792]{1,0:T(8,128)(2,1)S(1)}, bf16[256,1792]{1,0:T(8,128)(2,1)S(1)}, u32[]{:S(2)}, u32[]{:S(2)}) collective-permute-start(bf16[256,1792]{1,0:T(8,128)(2,1)S(1)} %add_convert_fusion), channel_id=1, source_target_pairs={{0,8},{2,6},{4,0},{6,14},{8,16},{10,2},{12,4},{14,22},{16,24},{18,... | collective-permute-start | bytes 2752520 | tf_op jit(solution)/shard_map/ppermute | solution.py:178
  166.6 5.1 %collective-permute-start.25 = (bf16[132,512]{1,0:T(8,128)(2,1)S(1)}, bf16[132,512]{1,0:T(8,128)(2,1)S(1)}, u32[]{:S(2)}, u32[]{:S(2)}) collective-permute-start(bf16[132,512]{1,0:T(8,128)(2,1)S(1)} %get-tuple-element.51), channel_id=1, source_target_pairs={{0,1},{1,0},{2,3},{3,2},{4,5},{5,4},{6,7},{7,6},{8,9},{9,8},{10,11... | collective-permute-start | bytes 405512 | tf_op jit(solution)/shard_map/ppermute | solution.py:181
  171.8 4.3 %collective-permute-start.26 = (bf16[132,512]{1,0:T(8,128)(2,1)S(1)}, bf16[132,512]{1,0:T(8,128)(2,1)S(1)}, u32[]{:S(2)}, u32[]{:S(2)}) collective-permute-start(bf16[132,512]{1,0:T(8,128)(2,1)S(1)} %multiply_convert_fusion.3.mine_ref), channel_id=1, source_target_pairs={{0,1},{1,0},{2,3},{3,2},{4,5},{5,4},{6,7},{7,6},{8,9},{9,8},{10,11... | collective-permute-start | bytes 405512 | tf_op jit(solution)/shard_map/ppermute | solution.py:181
  179.7 3.4 %collective-permute-start.27 = (bf16[128,1792]{1,0:T(8,128)(2,1)S(1)}, bf16[128,1792]{1,0:T(8,128)(2,1)S(1)}, u32[]{:S(2)}, u32[]{:S(2)}) collective-permute-start(bf16[128,1792]{1,0:T(8,128)(2,1)S(1)} %add_convert_fusion.3), channel_id=1, source_target_pairs={{0,2},{2,0},{4,6},{6,4},{8,10},{10,8},{12,14},{14,12},{16,18},{18,... | collective-permute-start | bytes 1376264 | tf_op jit(solution)/shard_map/ppermute | solution.py:175

commit v2 on v0

--- a/solution.py
+++ b/solution.py
@@ -1,10 +1,396 @@
+import functools
+
 import jax
 import jax.numpy as jnp
 from jax import lax
+from jax.experimental import pallas as pl
+from jax.experimental.pallas import tpu as pltpu
 from jax.sharding import PartitionSpec as P
 
-
-def on_device(grad_out, routes, gate_weights, gate_act, w_down, w_up):
+BF16 = jnp.bfloat16
+F32 = jnp.float32
+VMEM = pl.BlockSpec(memory_space=pltpu.VMEM)
+HBM = pl.BlockSpec(memory_space=pltpu.HBM)
+TABLE = 128
+LIMIT = pltpu.CompilerParams(vmem_limit_bytes=16 * 1024 * 1024)
+
+
+def dot_t(a, b):
+    return lax.dot_general(a, b, (((1,), (1,)), ((), ())), preferred_element_type=F32)
+
+
+def prepare_kernel(rows_hbm, routes_hbm, gates_hbm, block_ref, routes_ref, gates_ref, sems):
+    token_n, feat_n = rows_hbm.shape
+    copies = [
+        pltpu.make_async_copy(routes_hbm, routes_ref, sems.at[0]),
+        pltpu.make_async_copy(gates_hbm, gates_ref, sems.at[1]),
+        pltpu.make_async_copy(rows_hbm, block_ref.at[:, pl.ds(0, feat_n)], sems.at[2]),
+    ]
+    for copy in copies:
+        copy.start()
+    copies[0].wait()
+    copies[1].wait()
+    choose_n = routes_ref.shape[0]
+    expert_n = lax.axis_size("ep")
+    expert = lax.broadcasted_iota(jnp.int32, (expert_n, token_n), 0)
+    chosen = jnp.zeros((expert_n, token_n), F32)
+    weight = jnp.zeros((expert_n, token_n), F32)
+    for k in range(choose_n):
+        hit = routes_ref[k : k + 1, :] == expert
+        chosen = jnp.where(hit, 1.0, chosen)
+        weight = jnp.where(hit, gates_ref[k : k + 1, :], weight)
+    first = lax.broadcasted_iota(jnp.int32, (token_n, token_n), 0)
+    second = lax.broadcasted_iota(jnp.int32, (token_n, token_n), 1)
+    earlier = jnp.where(first < second, 1.0, 0.0).astype(BF16)
+    rank = jnp.dot(chosen.astype(BF16), earlier, preferred_element_type=F32)
+    slot = jnp.where(chosen > 0.5, rank, -1.0)
+    high = weight.astype(BF16).astype(F32)
+    parts = [slot, high, weight - high]
+    rest = jnp.zeros((TABLE - len(parts) * expert_n, token_n), F32)
+    block_ref[:, feat_n:] = jnp.transpose(jnp.concatenate(parts + [rest], axis=0)).astype(BF16)
+    copies[2].wait()
+
+
+class Ring:
+    def __init__(self, experts_n, slot_n, token_n):
+        self.slot_n = slot_n
+        self.token_n = token_n
+        self.experts_n = experts_n
+        self.chips_n = experts_n // 2
+        self.far = self.chips_n // 2
+        self.arrivals = [(0, 0), (0, 1)]
+        for k in range(1, self.far):
+            self.arrivals += [(k, 0), (k, 1), (-k, 1), (-k, 0)]
+        self.arrivals += [(self.far, 0), (self.far, 1)]
+        self.pieces = [2] + [4] * (self.far - 1) + [2]
+        self.firsts = [sum(self.pieces[:k]) for k in range(self.far + 1)]
+
+    def tables(self, chunk, refs):
+        out = [(ref, at) for ref in refs for at in range(0, ref.shape[0], self.token_n)]
+        return out[: self.pieces[chunk]]
+
+    def chip(self, spot):
+        return 2 * spot if spot < self.far else 2 * (self.chips_n - 1 - spot) + 1
+
+    def pairs(self):
+        out = []
+        for i in range(self.experts_n):
+            z, y = i // 4, i // 2 % 2
+            spot = self.chips_n - 1 - z if y else z
+            out.append((i, 2 * self.chip((spot + 1 - 2 * (i % 2)) % self.chips_n) + i % 2))
+        return out
+
+    def sources(self, chunk):
+        me = lax.axis_index("ep")
+        core = lax.rem(me, 2)
+        z, y = me // 4, lax.rem(me // 2, 2)
+        here = jnp.where(y == 1, self.chips_n - 1 - z, z)
+        first = self.firsts[chunk]
+        out = []
+        for steps, flip in self.arrivals[first : first + self.pieces[chunk]]:
+            spot = lax.rem(here + steps * (2 * core - 1) + self.chips_n, self.chips_n)
+            chip = jnp.where(spot < self.far, 2 * spot, 2 * (self.chips_n - 1 - spot) + 1)
+            out.append(2 * chip + (1 - core if flip else core))
+        return out
+
+
+def act_kernel(ring, act_ref, *out_refs):
+    rows_n, slot_n = act_ref.shape[0], ring.slot_n
+    for chunk, out_ref in enumerate(out_refs):
+        part = out_ref.shape[0]
+        row = lax.broadcasted_iota(jnp.int32, (part, 1), 0)
+        target = row
+        for b, source in enumerate(ring.sources(chunk)):
+            target = jnp.where(row >= b * slot_n, row + (source - b) * slot_n, target)
+        column = lax.broadcasted_iota(jnp.int32, (part, rows_n), 1)
+        select = jnp.where(column == target, 1.0, 0.0).astype(BF16)
+        out_ref[...] = jnp.dot(select, act_ref[...], preferred_element_type=F32).astype(BF16)
+
+
+def mine_of(*columns):
+    me, expert_n = lax.axis_index("ep"), lax.axis_size("ep")
+    row = lax.broadcasted_iota(jnp.int32, (8, TABLE), 0)
+    lane = lax.broadcasted_iota(jnp.int32, (8, TABLE), 1)
+    hit = row < 0
+    for i, parts in enumerate(columns):
+        for part in parts:
+            hit = hit | ((row == i) & (lane == part * expert_n + me))
+    return jnp.where(hit, 1.0, 0.0).astype(BF16)
+
+
+def down_kernel(ring, chunk, *refs):
+    core, side = lax.rem(lax.axis_index("ep"), 2), lax.axis_index("tp")
+    whole = chunk == ring.far
+    outs_n = 1 if whole else 2
+    blocks, w_ref = refs[: -3 - outs_n], refs[-3 - outs_n]
+    outs, table_ref, rows_ref = refs[-2 - outs_n : -2], refs[-2], refs[-1]
+    slot_n, token_n = ring.slot_n, ring.token_n
+    feat_n = w_ref.shape[1]
+    mine = mine_of((0,), (1, 2))
+    slots, weights = [], []
+    for b, (ref, at) in enumerate(ring.tables(chunk, blocks)):
+        table = ref[at : at + token_n, ref.shape[1] - TABLE :]
+        table_ref[b * token_n : (b + 1) * token_n, :] = table
+        table = dot_t(mine, table)
+        slots.append(jnp.where(table[0:1] >= 0.0, table[0:1] + float(b * slot_n), -1.0))
+        weights.append(table[1:2])
+    slots = jnp.concatenate(slots, axis=1).astype(jnp.int32)
+    weights = jnp.concatenate(weights, axis=1)
+    hit = lax.broadcasted_iota(jnp.int32, (rows_ref.shape[0], slots.shape[1]), 0) == slots
+    weight = jnp.sum(jnp.where(hit, weights, 0.0), axis=1, keepdims=True)
+    select = jnp.where(hit, 1.0, 0.0).astype(BF16)
+
+    def chosen(select, parts):
+        value, at = None, 0
+        for ref in parts:
+            rows = ref[:, : ref.shape[1] - TABLE]
+            term = jnp.dot(select[:, at : at + ref.shape[0]], rows, preferred_element_type=F32)
+            value = term if value is None else value + term
+            at += ref.shape[0]
+        return (value * weight).astype(BF16)
+
+    if whole:
+        half = feat_n // 2
+        turned = jnp.concatenate([select[:, token_n:], select[:, :token_n]], axis=1)
+        rows_ref[:, pl.ds(pl.multiple_of(core * half, 128), half)] = chosen(select, blocks[:1])
+        rows_ref[:, pl.ds(pl.multiple_of((1 - core) * half, 128), half)] = chosen(turned, blocks[1:])
+    else:
+        rows_ref[...] = chosen(select, blocks)
+    tile = 256
+    if whole:
+        (out_ref,) = outs
+        for at in range(0, out_ref.shape[1], tile):
+            out_ref[:, at : at + tile] = dot_t(rows_ref[...], w_ref[at : at + tile, :]).astype(BF16)
+    else:
+        unit = outs[0].shape[1]
+        for out_ref, place in zip(outs, (side, 1 - side)):
+            for t in range(0, unit, tile):
+                at = pl.multiple_of(place * unit + t, tile)
+                out_ref[:, t : t + tile] = dot_t(rows_ref[...], w_ref[pl.ds(at, tile), :]).astype(BF16)
+
+
+def up_kernel(ring, chunk, *refs):
+    if chunk == ring.far:
+        refs, all_ref = refs[:-1], refs[-1]
+    core, side = lax.rem(lax.axis_index("ep"), 2), lax.axis_index("tp")
+    table_ref, ins, (w_ref, keep_ref, give_ref) = refs[0], refs[1:-3], refs[-3:]
+    slot_n, token_n = ring.slot_n, ring.token_n
+    feat_n, unit = w_ref.shape[0], w_ref.shape[1] // 2
+    mine_at = pl.multiple_of(side * unit, 128)
+    peer_at = pl.multiple_of((1 - side) * unit, 128)
+    if len(ins) == 2:
+        ups = [ref[...] for ref in ins]
+    else:
+        ups = []
+        for at, act_ref in ((mine_at, ins[2]), (peer_at, ins[3])):
+            hidden = ins[0][:, pl.ds(at, unit)].astype(F32) + ins[1][:, pl.ds(at, unit)].astype(F32)
+            ups.append((hidden * act_ref[...].astype(F32)).astype(BF16))
+    rows_n = ups[0].shape[0]
+    window = rows_n if rows_n <= 2 * slot_n else 2 * slot_n + (-2 * slot_n) % 16
+    lane = lax.broadcasted_iota(jnp.int32, (token_n, window), 1)
+    mine = mine_of((0,))
+    selects, starts = [], []
+    for b, (ref, at) in enumerate(ring.tables(chunk, [table_ref])):
+        start = 0 if b < 2 else rows_n - window
+        slot = dot_t(ref[at : at + token_n, :], mine)[:, 0:1].astype(jnp.int32)
+        slot = jnp.where(slot >= 0, slot + (b * slot_n - start), -1)
+        selects.append(jnp.where(lane == slot, 1.0, 0.0).astype(BF16))
+        starts.append(start)
+    selects = [jnp.concatenate(selects[b : b + 2], axis=0) for b in range(0, len(selects), 2)]
+
+    def placed(at, tile):
+        row = dot_t(ups[0], w_ref[pl.ds(at, tile), pl.ds(mine_at, unit)])
+        row = row + dot_t(ups[1], w_ref[pl.ds(at, tile), pl.ds(peer_at, unit)])
+        row = row.astype(BF16)
+        out = []
+        for select, start in zip(selects, starts[::2]):
+            part = row[start : start + window]
+            out.append(jnp.dot(select, part, preferred_element_type=F32).astype(BF16))
+        return out
+
+    tile = 256
+    if chunk == ring.far:
+        half = feat_n // 2
+        for t in range(0, feat_n, tile):
+            (value,) = placed(t, tile)
+            all_ref[:, t : t + tile] = value
+        keep = pl.ds(pl.multiple_of(core * half, 128), half)
+        keep_ref[:token_n, :] = all_ref[token_n:, keep]
+        keep_ref[token_n:, :] = all_ref[:token_n, keep]
+        give_ref[...] = all_ref[:, pl.ds(pl.multiple_of((1 - core) * half, 128), half)]
+    else:
+        for t in range(0, feat_n, tile):
+            value = placed(t, tile)
+            if chunk == 0:
+                value = [value[0][:token_n], value[0][token_n:]]
+            give_ref[:, t : t + tile] = value[0]
+            keep_ref[:, t : t + tile] = value[1]
+
+
+def join_kernel(first, keep_ref, *refs):
+    core = lax.rem(lax.axis_index("ep"), 2)
+    given_refs, came_ref, out_ref = refs[:-2], refs[-2], refs[-1]
+    feat_n, half = out_ref.shape[1], came_ref.shape[1]
+    at = 0
+    for given_ref in given_refs:
+        rows = pl.ds(at, given_ref.shape[0])
+        kept = pl.ds(first + at, given_ref.shape[0])
+
+        def total(columns):
+            return keep_ref[kept, columns].astype(F32) + given_ref[:, columns].astype(F32)
+
+        if half == feat_n:
+            value = total(pl.ds(0, feat_n)) + came_ref[rows, :].astype(F32)
+            out_ref[rows, :] = value.astype(BF16)
+        else:
+            mine = pl.ds(pl.multiple_of(core * half, 128), half)
+            other = pl.ds(pl.multiple_of((1 - core) * half, 128), half)
+            out_ref[rows, mine] = (total(mine) + came_ref[rows, :].astype(F32)).astype(BF16)
+            out_ref[rows, other] = total(other).astype(BF16)
+        at += given_ref.shape[0]
+
+
+def after(value, *others):
+    return lax.optimization_barrier((value, *others))[0]
+
+
+def ring_on_device(grad_out, routes, gate_weights, gate_act, w_down, w_up):
+    experts_n = lax.axis_size("ep")
+    slot_n = gate_act.shape[1] // experts_n
+    token_n = routes.shape[0]
+    feat_n = grad_out.shape[1]
+    half = feat_n // 2
+    unit_n = gate_act.shape[2]
+    ring = Ring(experts_n, slot_n, token_n)
+    far, pieces = ring.far, ring.pieces
+    swap = [(i, i ^ 1) for i in range(experts_n)]
+    ring_pairs = ring.pairs()
+    core = lax.axis_index("ep") % 2
+
+    def parts_to_core(x, rows):
+        return [lax.ppermute(p, "ep", swap) for p in jnp.split(x, x.shape[0] // rows)]
+
+    def to_core(x, rows=128):
+        return jnp.concatenate(parts_to_core(x, rows), axis=0)
+
+    def to_ring(x):
+        return lax.ppermute(x, "ep", ring_pairs)
+
+    def to_side(x):
+        return lax.ppermute(x, "tp", [(0, 1), (1, 0)])
+
+    def call(kernel, outs, *args, scratch=()):
+        return pl.pallas_call(
+            kernel,
+            out_shape=[jax.ShapeDtypeStruct(shape, BF16) for shape in outs],
+            in_specs=[VMEM] * len(args),
+            out_specs=[VMEM] * len(outs),
+            scratch_shapes=scratch,
+            compiler_params=LIMIT,
+        )(*args)
+
+    def down(k):
+        rows_n = pieces[k] * slot_n
+        return call(
+            functools.partial(down_kernel, ring, k),
+            ([(rows_n, 2 * unit_n)] if k == far else [(rows_n, unit_n)] * 2)
+            + [(pieces[k] * token_n, TABLE)],
+            *blocks[k],
+            w_down[0],
+            scratch=[pltpu.VMEM((rows_n, feat_n), BF16)],
+        )
+
+    def middle(k, sent):
+        hidden = partials[k][0].astype(F32) + sent.astype(F32)
+        return (hidden * acts[k].astype(F32)).astype(BF16)
+
+    def up(k, *args):
+        shape = (2 * token_n, half) if k == far else (pieces[k] // 2 * token_n, feat_n)
+        return call(
+            functools.partial(up_kernel, ring, k),
+            [shape] * 2,
+            partials[k][-1],
+            *args,
+            w_up[0],
+            scratch=[pltpu.VMEM((2 * token_n, feat_n), BF16)] if k == far else [],
+        )
+
+    def join(first, width, *args):
+        return call(functools.partial(join_kernel, first), [(token_n, width)], *args)[0]
+
+    own = pl.pallas_call(
+        prepare_kernel,
+        out_shape=jax.ShapeDtypeStruct((token_n, feat_n + TABLE), BF16),
+        in_specs=[HBM] * 3,
+        out_specs=VMEM,
+        scratch_shapes=[
+            pltpu.VMEM(routes.shape[::-1], jnp.int32),
+            pltpu.VMEM(routes.shape[::-1], F32),
+            pltpu.SemaphoreType.DMA((3,)),
+        ],
+        compiler_params=LIMIT,
+    )(grad_out, routes.T, gate_weights.T)
+    sibling = to_core(own)
+    blocks = [[own, sibling]]
+    moving = to_ring(jnp.concatenate(blocks[0], axis=0))
+    acts = call(
+        functools.partial(act_kernel, ring),
+        [(p * slot_n, unit_n) for p in pieces],
+        gate_act[0],
+    )
+    act_peer = to_side(acts[far])
+    partials, mines, peers, ups = [down(0)], {}, {}, {}
+    sents = [to_side(partials[0][1])]
+    for k in range(1, far + 1):
+        ended = [partials[k - 1][0]]
+        if k < far:
+            ended += [sents[k - 1]] + ([act_peer] if k == 1 else [])
+        if k >= 3:
+            ended += [peers[k - 2]]
+        here = after(moving, *ended)
+        if k < far - 1:
+            moving = to_ring(here)
+        elif k == far - 1:
+            part = lax.dynamic_slice_in_dim(here, core * half, half, 1)
+            moving = to_ring(jnp.concatenate([part, here[:, feat_n:]], axis=1))
+        if 2 <= k < far:
+            mines[k - 1] = middle(k - 1, after(sents[k - 1], here))
+            peers[k - 1] = to_side(mines[k - 1])
+            here = after(here, mines[k - 1])
+        blocks.append([here, to_core(here, 64 if k == far else 128)])
+        if k == far:
+            mines[k - 1] = middle(k - 1, sents[k - 1])
+            blocks[k][1] = after(blocks[k][1], mines[k - 1])
+        partials.append(down(k))
+        sents.append(to_side(partials[k][-2]))
+
+    for k in range(1, far - 1):
+        ups[k] = up(k, mines[k], after(peers[k], partials[far][0]))
+    full = after(sents[far], *(ups[k][0] for k in range(1, far - 1)))
+    ups[far] = up(far, partials[far][0], full, acts[far], act_peer)
+    peer = to_side(after(mines[far - 1], full))
+    keep, give = ups[far]
+    total = (keep.astype(F32) + to_core(give, 64).astype(F32)).astype(BF16)
+    came = to_ring(total)
+    ups[far - 1] = up(far - 1, mines[far - 1], after(peer, total))
+    mines[0] = middle(0, after(sents[0], peer))
+    peer = to_side(mines[0])
+    came = [came[:token_n], came[token_n:]]
+    for k in range(far - 1, 0, -1):
+        keep, give = ups[k]
+        rows = 64 if k == far - 1 else 128
+        given = parts_to_core(give, rows)
+        for i in range(2):
+            parts = given[i * (token_n // rows) : (i + 1) * (token_n // rows)]
+            total = join(i * token_n, feat_n, keep, *parts, came[i])
+            came[i] = to_ring(total)
+        came[0] = after(came[0], total)
+    keep, give = up(0, mines[0], after(peer, total))
+    total = to_core((came[0].astype(F32) + keep.astype(F32)).astype(BF16))
+    return (came[1].astype(F32) + give.astype(F32) + total.astype(F32)).astype(BF16)
+
+
+def spread_on_device(grad_out, routes, gate_weights, gate_act, w_down, w_up):
     experts_n = lax.axis_size("ep")
     slot_n = gate_act.shape[1] // experts_n
     rows_n = experts_n * slot_n
@@ -58,6 +444,17 @@
         P("ep", None, "tp"),
         P("ep", "tp", None),
     )
-    return jax.shard_map(
-        on_device, mesh=mesh, in_specs=placed, out_specs=P("ep", "tp"), check_vma=False
-    )
+
+    def whole(grad_out, routes, *rest):
+        ep, tp = mesh.shape["ep"], mesh.shape["tp"]
+        dense = tp == 2 and ep % 4 == 0 and 8 <= ep <= 2 * routes.shape[1]
+        dense = dense and routes.shape[0] == 128 * ep and grad_out.shape[1] % 512 == 0
+        return jax.shard_map(
+            ring_on_device if dense else spread_on_device,
+            mesh=mesh,
+            in_specs=placed,
+            out_specs=P("ep", "tp"),
+            check_vma=False,
+        )(grad_out, routes, *rest)
+
+    return whole

time: 359 us -> 132 us (0.37)
  waiting for transfers between devices: 158 us -> 60.6 us
  blocking collectives: 97.3 us -> 0 us
  local copies, waits for them, and re-layouts: 49 us -> 5.55 us
  Pallas kernels: 0 us -> 29.4 us
  starting transfers between devices: 6.42 us -> 31.3 us
  matrix products: 17.4 us -> 0 us
  other arithmetic: 17 us -> 2.88 us
  between operations: 13.5 us -> 0.38 us
    all_to_all x1 -> x0, blocking collectives: 97.3 us -> none  [on_device(): lax.all_to_all(placed, 'ep', split_axis=0, concat_axis=0, tiled=True)]
    all_to_all x1 -> x0, waiting for transfers between devices: 91.1 us -> none  [on_device(): lax.all_to_all(row_grad, 'ep', split_axis=0, concat_axis=0, tiled=True)]
    ppermute x0 -> x45, waiting for transfers between devices: none -> 60.6 us  [the longest x10 34.2 us: to_side(): return lax.ppermute(x, 'tp', [(0, 1), (1, 0)])]
    all_gather x1 -> x0, waiting for transfers between devices: 34 us -> none  [on_device(): lax.all_gather(up_grad, 'tp', axis=1, tiled=True)]
    reduce_scatter x1 -> x0, waiting for transfers between devices: 32.5 us -> none  [on_device(): lax.psum_scatter(partial_value.astype(jnp.bfloat16), 'tp', scatter_dimens...]
    ppermute x0 -> x45, starting transfers between devices: none -> 31.3 us  [the longest x24 12 us: parts_to_core(): lax.ppermute(p, 'ep', swap)]
    pallas_call x0 -> x18, Pallas kernels: none -> 29.4 us  [the longest x17 29.1 us: call(): pl.pallas_call(kernel, out_shape=[jax.ShapeDtypeStruct(shape, BF16) for s...]
    dot_general x2 -> x0, matrix products: 17.4 us -> none  [the longest x1 8.74 us: on_device(): jnp.einsum('nsd,fd->nsf', lax.all_to_all(placed, 'ep', split_axis=0, conc...]
  transfers between devices with their start and end apart: 3 -> 45, of which waited for: 3 -> 26; matrix products, arithmetic and copies ran while one was open for 0% -> 1% of each run, Pallas kernels for 0% -> 19%
where the time goes in v2:
time: 132 us; the launch traced here: 130 us
  waiting for transfers between devices  60.6 us (46%)
  starting transfers between devices  31.3 us (24%)
  Pallas kernels  29.4 us (22%)
  local copies, waits for them, and re-layouts  5.55 us (4%)
  other arithmetic  2.88 us (2%)
    ppermute x10, waiting for transfers between devices, to_side(): return lax.ppermute(x, 'tp', [(0, 1), (1, 0)])  34.2 us
    pallas_call x17, Pallas kernels, call(): pl.pallas_call(kernel, out_shape=[jax.ShapeDtypeStruct(shape, BF16) for s...  29.1 us
    ppermute x11, waiting for transfers between devices, to_ring(): return lax.ppermute(x, 'ep', ring_pairs)  20.2 us
    ppermute x24, starting transfers between devices, parts_to_core(): lax.ppermute(p, 'ep', swap)  12 us
    ppermute x10, starting transfers between devices, to_side(): return lax.ppermute(x, 'tp', [(0, 1), (1, 0)])  10.7 us
    ppermute x11, starting transfers between devices, to_ring(): return lax.ppermute(x, 'ep', ring_pairs)  8.68 us
    ppermute x24, waiting for transfers between devices, parts_to_core(): lax.ppermute(p, 'ep', swap)  6.27 us
    unnamed x38, local copies, waits for them, and re-layouts  5 us
  transfers between devices with their start and end apart: 45, of which 26 were waited for; matrix products, arithmetic and copies ran while one was open for 1% of the time, Pallas kernels for 19%

profile of v2, /device:TPU:13, one launch (start us, length us, event | category | flops | bytes accessed | tf_op | source)
XLA Modules:
  0.0 130.2 jit_solution(16671146258974611094)
XLA Ops:
  0.0 1.0 copy-done.4
  3.4 1.5 %collective-permute-done.refs_1_ = bf16[128,1920]{1,0:T(8,128)(2,1)S(1)} collective-permute-done((bf16[128,1920]{1,0:T(8,128)(2,1)S(1)}, bf16[128,1920]{1,0:T(8,128)(2,1)S(1)}, u32[]{:S(2)}, u32[]{:S(2)}) %collective-permute-start) | collective-permute-done | bytes 491552 | tf_op jit(solution)/shard_map/ppermute | solution.py:271
  5.0 1.3 %collective-permute-start.1 = (bf16[256,1920]{1,0:T(8,128)(2,1)S(1)}, bf16[256,1920]{1,0:T(8,128)(2,1)S(1)}, u32[]{:S(2)}, u32[]{:S(2)}) collective-permute-start(bf16[256,1920]{1,0:T(8,128)(2,1)S(1)} %pad_maximum_fusion), channel_id=1, source_target_pairs={{0,8},{2,6},{4,0},{6,14},{8,16},{10,2},{12,4},{14,22},{16,24},{18,... | collective-permute-start | bytes 2949128 | tf_op jit(solution)/shard_map/ppermute | solution.py:277
  6.4 1.2 copy-done.3
  7.6 1.6 %shard_map.66 = (bf16[132,512]{1,0:T(8,128)(2,1)S(1)}, bf16[264,512]{1,0:T(8,128)(2,1)S(1)}, bf16[264,512]{1,0:T(8,128)(2,1)S(1)}, bf16[264,512]{1,0:T(8,128)(2,1)S(1)}, bf16[132,512]{1,0:T(8,128)(2,1)S(1)}) custom-call(bf16[1056,512]{1,0:T(8,128)(2,1)S(1)} %bitcast.15), custom_call_target="tpu_custom_call" | custom-call | tf_op jit(solution)/shard_map/pallas_call | solution.py:283
  9.9 1.2 collective-permute-start.3
  11.1 1.7 %shard_map.65 = (bf16[132,512]{1,0:T(8,128)(2,1)S(1)}, bf16[132,512]{1,0:T(8,128)(2,1)S(1)}, bf16[256,128]{1,0:T(8,128)(2,1)S(1)}) custom-call(bf16[128,1920]{1,0:T(8,128)(2,1)S(1)} %shard_map.64.refs_0_, bf16[128,1920]{1,0:T(8,128)(2,1)S(1)} %collective-permute-done.refs_1_, bf16[1024,1792]{1,0:T(8,128)(2,1)S(1)} %bitcast.5), custom_call_target="tpu_custom_call" | custom-call | tf_op jit(solution)/shard_map/pallas_call | solution.py:283
  13.2 2.4 %collective-permute-done.3.refs_4_ = bf16[132,512]{1,0:T(8,128)(2,1)S(1)} collective-permute-done((bf16[132,512]{1,0:T(8,128)(2,1)S(1)}, bf16[132,512]{1,0:T(8,128)(2,1)S(1)}, u32[]{:S(2)}, u32[]{:S(2)}) %collective-permute-start.3) | collective-permute-done | bytes 135200 | tf_op jit(solution)/shard_map/ppermute | solution.py:280
  15.6 2.8 %collective-permute-done.2 = bf16[132,512]{1,0:T(8,128)(2,1)S(1)} collective-permute-done((bf16[132,512]{1,0:T(8,128)(2,1)S(1)}, bf16[132,512]{1,0:T(8,128)(2,1)S(1)}, u32[]{:S(2)}, u32[]{:S(2)}) %collective-permute-start.2) | collective-permute-done | bytes 135200 | tf_op jit(solution)/shard_map/ppermute | solution.py:280
  18.5 1.2 collective-permute-start.4
  19.8 1.3 collective-permute-start.7
  22.0 1.9 %shard_map.67 = (bf16[264,512]{1,0:T(8,128)(2,1)S(1)}, bf16[264,512]{1,0:T(8,128)(2,1)S(1)}, bf16[512,128]{1,0:T(8,128)(2,1)S(1)}) custom-call(bf16[256,1920]{1,0:T(8,128)(2,1)S(1)} %collective-permute-done.1.refs_0_, bf16[256,1920]{1,0:T(8,128)(2,1)S(1)} %pad_maximum_fusion.1.refs_1_, bf16[1024,1792]{1,0:T(8,128)(2,1)S(1)} %bitcast.6), custom_call_target="tpu_custom_call" | custom-call | tf_op jit(solution)/shard_map/pallas_call | solution.py:283
  23.8 1.3 collective-permute-start.6
  25.1 6.5 %collective-permute-done.6 = bf16[264,512]{1,0:T(8,128)(2,1)S(1)} collective-permute-done((bf16[264,512]{1,0:T(8,128)(2,1)S(1)}, bf16[264,512]{1,0:T(8,128)(2,1)S(1)}, u32[]{:S(2)}, u32[]{:S(2)}) %collective-permute-start.6) | collective-permute-done | bytes 270368 | tf_op jit(solution)/shard_map/ppermute | solution.py:280
  31.6 1.4 %collective-permute-done.7.refs_0_ = bf16[256,1920]{1,0:T(8,128)(2,1)S(1)} collective-permute-done((bf16[256,1920]{1,0:T(8,128)(2,1)S(1)}, bf16[256,1920]{1,0:T(8,128)(2,1)S(1)}, u32[]{:S(2)}, u32[]{:S(2)}) %collective-permute-start.7) | collective-permute-done | bytes 983072 | tf_op jit(solution)/shard_map/ppermute | solution.py:277
  33.2 1.3 %collective-permute-start.10 = (bf16[128,1920]{1,0:T(8,128)(2,1)S(1)}, bf16[128,1920]{1,0:T(8,128)(2,1)S(1)}, u32[]{:S(2)}, u32[]{:S(2)}) collective-permute-start(bf16[128,1920]{1,0:T(8,128)(2,1)S(1)} %get-tuple-element.103), channel_id=1, source_target_pairs={{0,2},{2,0},{4,6},{6,4},{8,10},{10,8},{12,14},{14,12},{16,18},{18,... | collective-permute-start | bytes 1474568 | tf_op jit(solution)/shard_map/ppermute | solution.py:271
  34.6 1.3 collective-permute-start.9
  35.9 1.2 collective-permute-start.8
  37.2 2.6 %shard_map.68 = (bf16[264,512]{1,0:T(8,128)(2,1)S(1)}, bf16[264,512]{1,0:T(8,128)(2,1)}, bf16[512,128]{1,0:T(8,128)(2,1)S(1)}) custom-call(bf16[256,1920]{1,0:T(8,128)(2,1)S(1)} %collective-permute-done.7.refs_0_, bf16[256,1920]{1,0:T(8,128)(2,1)S(1)} %pad_maximum_fusion.2.refs_1_, bf16[1024,1792]{1,0:T(8,128)(2,1)S(1)} %bitcast.7), custom_call_target="tpu_custom_call" | custom-call | tf_op jit(solution)/shard_map/pallas_call | solution.py:283
  41.2 3.1 %collective-permute-done.8.refs_2_ = bf16[264,512]{1,0:T(8,128)(2,1)S(1)} collective-permute-done((bf16[264,512]{1,0:T(8,128)(2,1)S(1)}, bf16[264,512]{1,0:T(8,128)(2,1)S(1)}, u32[]{:S(2)}, u32[]{:S(2)}) %collective-permute-start.8) | collective-permute-done | bytes 270368 | tf_op jit(solution)/shard_map/ppermute | solution.py:280
  44.4 5.9 %collective-permute-done.12 = bf16[264,512]{1,0:T(8,128)(2,1)} collective-permute-done((bf16[264,512]{1,0:T(8,128)(2,1)}, bf16[264,512]{1,0:T(8,128)(2,1)}, u32[]{:S(2)}, u32[]{:S(2)}) %collective-permute-start.12) | collective-permute-done | bytes 270368 | tf_op jit(solution)/shard_map/ppermute | solution.py:280
  50.3 1.1 multiply_convert_fusion.1.refs_1_
  52.1 1.5 %collective-permute-start.13 = (bf16[256,1024]{1,0:T(8,128)(2,1)S(1)}, bf16[256,1024]{1,0:T(8,128)(2,1)S(1)}, u32[]{:S(2)}, u32[]{:S(2)}) collective-permute-start(bf16[256,1024]{1,0:T(8,128)(2,1)S(1)} %pad_maximum_fusion.4), channel_id=1, source_target_pairs={{0,8},{2,6},{4,0},{6,14},{8,16},{10,2},{12,4},{14,22},{16,24},{18,... | collective-permute-start | bytes 1572872 | tf_op jit(solution)/shard_map/ppermute | solution.py:277
  53.7 1.2 collective-permute-start.16
  55.0 1.9 %shard_map.69 = (bf16[264,512]{1,0:T(8,128)(2,1)S(1)}, bf16[264,512]{1,0:T(8,128)(2,1)S(1)}, bf16[512,128]{1,0:T(8,128)(2,1)S(1)}) custom-call(bf16[256,1920]{1,0:T(8,128)(2,1)S(1)} %collective-permute-done.9.refs_0_, bf16[256,1920]{1,0:T(8,128)(2,1)S(1)} %pad_maximum_fusion.3.refs_1_, bf16[1024,1792]{1,0:T(8,128)(2,1)S(1)} %bitcast.8), custom_call_target="tpu_custom_call" | custom-call | tf_op jit(solution)/shard_map/pallas_call | solution.py:283
  57.4 4.8 %collective-permute-done.16.refs_2_ = bf16[264,512]{1,0:T(8,128)(2,1)S(1)} collective-permute-done((bf16[264,512]{1,0:T(8,128)(2,1)S(1)}, bf16[264,512]{1,0:T(8,128)(2,1)S(1)}, u32[]{:S(2)}, u32[]{:S(2)}) %collective-permute-start.16) | collective-permute-done | bytes 270368 | tf_op jit(solution)/shard_map/ppermute | solution.py:280
  64.4 3.0 %collective-permute-done.21 = bf16[264,512]{1,0:T(8,128)(2,1)S(1)} collective-permute-done((bf16[264,512]{1,0:T(8,128)(2,1)S(1)}, bf16[264,512]{1,0:T(8,128)(2,1)S(1)}, u32[]{:S(2)}, u32[]{:S(2)}) %collective-permute-start.21) | collective-permute-done | bytes 270368 | tf_op jit(solution)/shard_map/ppermute | solution.py:280
  67.5 1.7 %shard_map.70 = (bf16[132,1024]{1,0:T(8,128)(2,1)S(1)}, bf16[256,128]{1,0:T(8,128)(2,1)S(1)}) custom-call(bf16[256,1024]{1,0:T(8,128)(2,1)S(1)} %collective-permute-done.13.refs_0_, bf16[256,1024]{1,0:T(8,128)(2,1)S(1)} %pad_maximum_fusion.5.refs_1_, bf16[1024,1792]{1,0:T(8,128)(2,1)S(1)} %bitcast.9), custom_call_target="tpu_custom_call" | custom-call | tf_op jit(solution)/shard_map/pallas_call | solution.py:283
  69.1 1.9 %collective-permute-start.24 = (bf16[132,1024]{1,0:T(8,128)(2,1)S(1)}, bf16[132,1024]{1,0:T(8,128)(2,1)S(1)}, u32[]{:S(2)}, u32[]{:S(2)}) collective-permute-start(bf16[132,1024]{1,0:T(8,128)(2,1)S(1)} %get-tuple-element.75.refs_1_), channel_id=1, source_target_pairs={{0,1},{1,0},{2,3},{3,2},{4,5},{5,4},{6,7},{7,6},{8,9},{9,8},{10,11... | collective-permute-start | bytes 811016 | tf_op jit(solution)/shard_map/ppermute | solution.py:280
  71.0 3.5 %shard_map.71 = (bf16[256,1792]{1,0:T(8,128)(2,1)S(1)}, bf16[256,1792]{1,0:T(8,128)(2,1)S(1)}) custom-call(bf16[512,128]{1,0:T(8,128)(2,1)S(1)} %copy-done.12, bf16[264,512]{1,0:T(8,128)(2,1)S(1)} %multiply_convert_fusion.2.refs_1_, bf16[264,512]{1,0:T(8,128)(2,1)S(1)} %collective-permute-done.8.refs_2_, bf16[1792,1024]{1,0:T(8,128)(2,1)S(1)} %bitcast.10), custom_call_target="tpu_custom_call" | custom-call | tf_op jit(solution)/shard_map/pallas_call | solution.py:283
  74.6 3.6 %shard_map.72 = (bf16[256,1792]{1,0:T(8,128)(2,1)S(1)}, bf16[256,1792]{1,0:T(8,128)(2,1)S(1)}) custom-call(bf16[512,128]{1,0:T(8,128)(2,1)S(1)} %copy-done.14, bf16[264,512]{1,0:T(8,128)(2,1)S(1)} %multiply_convert_fusion.1.refs_1_, bf16[264,512]{1,0:T(8,128)(2,1)S(1)} %collective-permute-done.16.refs_2_, bf16[1792,1024]{1,0:T(8,128)(2,1)S(1)} %bitcast.11), custom_call_target="tpu_custom_call" | custom-call | tf_op jit(solution)/shard_map/pallas_call | solution.py:283
  78.2 3.2 %shard_map.73 = (bf16[256,896]{1,0:T(8,128)(2,1)S(1)}, bf16[256,896]{1,0:T(8,128)(2,1)S(1)}) custom-call(bf16[256,128]{1,0:T(8,128)(2,1)S(1)} %get-tuple-element.86.refs_0_, bf16[132,1024]{1,0:T(8,128)(2,1)S(1)} %get-tuple-element.75.refs_1_, bf16[132,1024]{1,0:T(8,128)(2,1)S(1)} %collective-permute-done.24.refs_2_, ...), custom_call_target="tpu_custom_call" | custom-call | tf_op jit(solution)/shard_map/pallas_call | solution.py:283
  82.8 1.2 collective-permute-start.25
  84.6 5.8 %collective-permute-done.25.refs_2_ = bf16[264,512]{1,0:T(8,128)(2,1)S(1)} collective-permute-done((bf16[264,512]{1,0:T(8,128)(2,1)S(1)}, bf16[264,512]{1,0:T(8,128)(2,1)S(1)}, u32[]{:S(2)}, u32[]{:S(2)}) %collective-permute-start.25) | collective-permute-done | bytes 270368 | tf_op jit(solution)/shard_map/ppermute | solution.py:280
  90.4 3.5 %shard_map.74 = (bf16[256,1792]{1,0:T(8,128)(2,1)S(1)}, bf16[256,1792]{1,0:T(8,128)(2,1)S(1)}) custom-call(bf16[512,128]{1,0:T(8,128)(2,1)S(1)} %get-tuple-element.83.refs_0_, bf16[264,512]{1,0:T(8,128)(2,1)S(1)} %multiply_convert_fusion.refs_1_, bf16[264,512]{1,0:T(8,128)(2,1)S(1)} %collective-permute-done.25.refs_2_, bf16[1792,1024]{1,0:T(8,128)(2,1)S(1)} %bitcast.13), custom_call_target="tpu_custom_call" | custom-call | tf_op jit(solution)/shard_map/pallas_call | solution.py:283
  94.0 1.3 %collective-permute-start.40 = (bf16[64,1792]{1,0:T(8,128)(2,1)S(1)}, bf16[64,1792]{1,0:T(8,128)(2,1)S(1)}, u32[]{:S(2)}, u32[]{:S(2)}) collective-permute-start(bf16[64,1792]{1,0:T(8,128)(2,1)S(1)} %get-tuple-element.107), channel_id=1, source_target_pairs={{0,2},{2,0},{4,6},{6,4},{8,10},{10,8},{12,14},{14,12},{16,18},{18,... | collective-permute-start | bytes 688136 | tf_op jit(solution)/shard_map/ppermute | solution.py:271
  98.5 1.2 collective-permute-done.31.refs_1_
  100.2 1.4 %collective-permute-start.33 = (bf16[128,1792]{1,0:T(8,128)(2,1)S(1)}, bf16[128,1792]{1,0:T(8,128)(2,1)S(1)}, u32[]{:S(2)}, u32[]{:S(2)}) collective-permute-start(bf16[128,1792]{1,0:T(8,128)(2,1)S(1)} %shard_map.75), channel_id=1, source_target_pairs={{0,8},{2,6},{4,0},{6,14},{8,16},{10,2},{12,4},{14,22},{16,24},{18,... | collective-permute-start | bytes 1376264 | tf_op jit(solution)/shard_map/ppermute | solution.py:277
  101.5 3.1 %collective-permute-done.41.refs_1_ = bf16[128,1792]{1,0:T(8,128)(2,1)S(1)} collective-permute-done((bf16[128,1792]{1,0:T(8,128)(2,1)S(1)}, bf16[128,1792]{1,0:T(8,128)(2,1)S(1)}, u32[]{:S(2)}, u32[]{:S(2)}) %collective-permute-start.41) | collective-permute-done | bytes 458784 | tf_op jit(solution)/shard_map/ppermute | solution.py:277
  105.2 1.5 %collective-permute-start.37 = (bf16[128,1792]{1,0:T(8,128)(2,1)S(1)}, bf16[128,1792]{1,0:T(8,128)(2,1)S(1)}, u32[]{:S(2)}, u32[]{:S(2)}) collective-permute-start(bf16[128,1792]{1,0:T(8,128)(2,1)S(1)} %get-tuple-element.113), channel_id=1, source_target_pairs={{0,2},{2,0},{4,6},{6,4},{8,10},{10,8},{12,14},{14,12},{16,18},{18,... | collective-permute-start | bytes 1376264 | tf_op jit(solution)/shard_map/ppermute | solution.py:271
  106.8 2.8 %collective-permute-done.33.refs_1_ = bf16[128,1792]{1,0:T(8,128)(2,1)S(1)} collective-permute-done((bf16[128,1792]{1,0:T(8,128)(2,1)S(1)}, bf16[128,1792]{1,0:T(8,128)(2,1)S(1)}, u32[]{:S(2)}, u32[]{:S(2)}) %collective-permute-start.33) | collective-permute-done | bytes 458784 | tf_op jit(solution)/shard_map/ppermute | solution.py:277
  110.0 4.5 %collective-permute-done.42.refs_1_ = bf16[128,1792]{1,0:T(8,128)(2,1)S(1)} collective-permute-done((bf16[128,1792]{1,0:T(8,128)(2,1)S(1)}, bf16[128,1792]{1,0:T(8,128)(2,1)S(1)}, u32[]{:S(2)}, u32[]{:S(2)}) %collective-permute-start.42) | collective-permute-done | bytes 458784 | tf_op jit(solution)/shard_map/ppermute | solution.py:277
  115.0 1.1 collective-permute-start.36
  116.1 3.3 %collective-permute-done.34.refs_1_ = bf16[128,1792]{1,0:T(8,128)(2,1)S(1)} collective-permute-done((bf16[128,1792]{1,0:T(8,128)(2,1)S(1)}, bf16[128,1792]{1,0:T(8,128)(2,1)S(1)}, u32[]{:S(2)}, u32[]{:S(2)}) %collective-permute-start.34) | collective-permute-done | bytes 458784 | tf_op jit(solution)/shard_map/ppermute | solution.py:277
  119.8 3.0 %shard_map.78 = (bf16[128,1792]{1,0:T(8,128)(2,1)S(1)}, bf16[128,1792]{1,0:T(8,128)(2,1)S(1)}) custom-call(bf16[256,128]{1,0:T(8,128)(2,1)S(1)} %get-tuple-element.92.refs_0_, bf16[132,512]{1,0:T(8,128)(2,1)S(1)} %multiply_convert_fusion.3.refs_1_, bf16[132,512]{1,0:T(8,128)(2,1)S(1)} %collective-permute-done.36.refs_2_, bf16[1792,1024]{1,0:T(8,128)(2,1)S(1)} %bitcast.14), custom_call_target="tpu_custom_call" | custom-call | tf_op jit(solution)/shard_map/pallas_call | solution.py:283
  122.9 1.4 %collective-permute-done.43 = bf16[128,1792]{1,0:T(8,128)(2,1)S(1)} collective-permute-done((bf16[128,1792]{1,0:T(8,128)(2,1)S(1)}, bf16[128,1792]{1,0:T(8,128)(2,1)S(1)}, u32[]{:S(2)}, u32[]{:S(2)}) %collective-permute-start.43) | collective-permute-done | bytes 458784 | tf_op jit(solution)/shard_map/ppermute | solution.py:277
  124.4 1.3 collective-permute-start.44
  125.7 3.6 %collective-permute-done.35 = bf16[128,1792]{1,0:T(8,128)(2,1)S(1)} collective-permute-done((bf16[128,1792]{1,0:T(8,128)(2,1)S(1)}, bf16[128,1792]{1,0:T(8,128)(2,1)S(1)}, u32[]{:S(2)}, u32[]{:S(2)}) %collective-permute-start.35) | collective-permute-done | bytes 458784 | tf_op jit(solution)/shard_map/ppermute | solution.py:277
  (122 shorter events, 18.8 us)
Async XLA Ops:
  2.4 8.7 %copy-start = (bf16[1,1024,1792]{2,1,0:T(8,128)(2,1)S(1)}, bf16[1,1024,1792]{2,1,0:T(8,128)(2,1)}, u32[]{:S(2)}) copy-start(bf16[1,1024,1792]{2,1,0:T(8,128)(2,1)} %param.10) | copy-start | bytes 11010052
  2.7 2.2 %collective-permute-start = (bf16[128,1920]{1,0:T(8,128)(2,1)S(1)}, bf16[128,1920]{1,0:T(8,128)(2,1)S(1)}, u32[]{:S(2)}, u32[]{:S(2)}) collective-permute-start(bf16[128,1920]{1,0:T(8,128)(2,1)S(1)} %shard_map.64.refs_0_), channel_id=1, source_target_pairs={{0,2},{2,0},{4,6},{6,4},{8,10},{10,8},{12,14},{14,12},{16,18},{18,... | collective-permute-start | bytes 1474568 | tf_op jit(solution)/shard_map/ppermute | solution.py:271
  5.0 13.4 %collective-permute-start.1 = (bf16[256,1920]{1,0:T(8,128)(2,1)S(1)}, bf16[256,1920]{1,0:T(8,128)(2,1)S(1)}, u32[]{:S(2)}, u32[]{:S(2)}) collective-permute-start(bf16[256,1920]{1,0:T(8,128)(2,1)S(1)} %pad_maximum_fusion), channel_id=1, source_target_pairs={{0,8},{2,6},{4,0},{6,14},{8,16},{10,2},{12,4},{14,22},{16,24},{18,... | collective-permute-start | bytes 2949128 | tf_op jit(solution)/shard_map/ppermute | solution.py:277
  9.9 5.7 %collective-permute-start.3 = (bf16[132,512]{1,0:T(8,128)(2,1)S(1)}, bf16[132,512]{1,0:T(8,128)(2,1)S(1)}, u32[]{:S(2)}, u32[]{:S(2)}) collective-permute-start(bf16[132,512]{1,0:T(8,128)(2,1)S(1)} %get-tuple-element.55.refs_3_), channel_id=1, source_target_pairs={{0,1},{1,0},{2,3},{3,2},{4,5},{5,4},{6,7},{7,6},{8,9},{9,8},{10,11... | collective-permute-start | bytes 405512 | tf_op jit(solution)/shard_map/ppermute | solution.py:280
  12.9 9.0 %copy-start.9 = (bf16[132,512]{1,0:T(8,128)(2,1)}, bf16[132,512]{1,0:T(8,128)(2,1)S(1)}, u32[]{:S(2)}) copy-start(bf16[132,512]{1,0:T(8,128)(2,1)S(1)} %get-tuple-element.53) | copy-start | bytes 405508
  12.9 5.5 %collective-permute-start.2 = (bf16[132,512]{1,0:T(8,128)(2,1)S(1)}, bf16[132,512]{1,0:T(8,128)(2,1)S(1)}, u32[]{:S(2)}, u32[]{:S(2)}) collective-permute-start(bf16[132,512]{1,0:T(8,128)(2,1)S(1)} %get-tuple-element.54), channel_id=1, source_target_pairs={{0,1},{1,0},{2,3},{3,2},{4,5},{5,4},{6,7},{7,6},{8,9},{9,8},{10,11... | collective-permute-start | bytes 405512 | tf_op jit(solution)/shard_map/ppermute | solution.py:280
  18.5 2.7 %collective-permute-start.4 = (bf16[128,1920]{1,0:T(8,128)(2,1)S(1)}, bf16[128,1920]{1,0:T(8,128)(2,1)S(1)}, u32[]{:S(2)}, u32[]{:S(2)}) collective-permute-start(bf16[128,1920]{1,0:T(8,128)(2,1)S(1)} %get-tuple-element.105), channel_id=1, source_target_pairs={{0,2},{2,0},{4,6},{6,4},{8,10},{10,8},{12,14},{14,12},{16,18},{18,... | collective-permute-start | bytes 1474568 | tf_op jit(solution)/shard_map/ppermute | solution.py:271
  19.7 2.2 %collective-permute-start.5 = (bf16[128,1920]{1,0:T(8,128)(2,1)S(1)}, bf16[128,1920]{1,0:T(8,128)(2,1)S(1)}, u32[]{:S(2)}, u32[]{:S(2)}) collective-permute-start(bf16[128,1920]{1,0:T(8,128)(2,1)S(1)} %get-tuple-element.106), channel_id=1, source_target_pairs={{0,2},{2,0},{4,6},{6,4},{8,10},{10,8},{12,14},{14,12},{16,18},{18,... | collective-permute-start | bytes 1474568 | tf_op jit(solution)/shard_map/ppermute | solution.py:271
  19.8 13.2 %collective-permute-start.7 = (bf16[256,1920]{1,0:T(8,128)(2,1)S(1)}, bf16[256,1920]{1,0:T(8,128)(2,1)S(1)}, u32[]{:S(2)}, u32[]{:S(2)}) collective-permute-start(bf16[256,1920]{1,0:T(8,128)(2,1)S(1)} %collective-permute-done.1.refs_0_), channel_id=1, source_target_pairs={{0,8},{2,6},{4,0},{6,14},{8,16},{10,2},{12,4},{14,22},{16,24},{18,... | collective-permute-start | bytes 2949128 | tf_op jit(solution)/shard_map/ppermute | solution.py:277
  23.8 13.3 %copy-start.11 = (bf16[512,128]{1,0:T(8,128)(2,1)}, bf16[512,128]{1,0:T(8,128)(2,1)S(1)}, u32[]{:S(2)}) copy-start(bf16[512,128]{1,0:T(8,128)(2,1)S(1)} %get-tuple-element.57.refs_0_) | copy-start | bytes 393220
  23.8 7.7 %collective-permute-start.6 = (bf16[264,512]{1,0:T(8,128)(2,1)S(1)}, bf16[264,512]{1,0:T(8,128)(2,1)S(1)}, u32[]{:S(2)}, u32[]{:S(2)}) collective-permute-start(bf16[264,512]{1,0:T(8,128)(2,1)S(1)} %get-tuple-element.59), channel_id=1, source_target_pairs={{0,1},{1,0},{2,3},{3,2},{4,5},{5,4},{6,7},{7,6},{8,9},{9,8},{10,11... | collective-permute-start | bytes 811016 | tf_op jit(solution)/shard_map/ppermute | solution.py:280
  33.2 3.9 %collective-permute-start.10 = (bf16[128,1920]{1,0:T(8,128)(2,1)S(1)}, bf16[128,1920]{1,0:T(8,128)(2,1)S(1)}, u32[]{:S(2)}, u32[]{:S(2)}) collective-permute-start(bf16[128,1920]{1,0:T(8,128)(2,1)S(1)} %get-tuple-element.103), channel_id=1, source_target_pairs={{0,2},{2,0},{4,6},{6,4},{8,10},{10,8},{12,14},{14,12},{16,18},{18,... | collective-permute-start | bytes 1474568 | tf_op jit(solution)/shard_map/ppermute | solution.py:271
  34.5 2.6 %collective-permute-start.11 = (bf16[128,1920]{1,0:T(8,128)(2,1)S(1)}, bf16[128,1920]{1,0:T(8,128)(2,1)S(1)}, u32[]{:S(2)}, u32[]{:S(2)}) collective-permute-start(bf16[128,1920]{1,0:T(8,128)(2,1)S(1)} %get-tuple-element.104), channel_id=1, source_target_pairs={{0,2},{2,0},{4,6},{6,4},{8,10},{10,8},{12,14},{14,12},{16,18},{18,... | collective-permute-start | bytes 1474568 | tf_op jit(solution)/shard_map/ppermute | solution.py:271
  34.6 15.7 %collective-permute-start.9 = (bf16[256,1920]{1,0:T(8,128)(2,1)S(1)}, bf16[256,1920]{1,0:T(8,128)(2,1)S(1)}, u32[]{:S(2)}, u32[]{:S(2)}) collective-permute-start(bf16[256,1920]{1,0:T(8,128)(2,1)S(1)} %collective-permute-done.7.refs_0_), channel_id=1, source_target_pairs={{0,8},{2,6},{4,0},{6,14},{8,16},{10,2},{12,4},{14,22},{16,24},{18,... | collective-permute-start | bytes 2949128 | tf_op jit(solution)/shard_map/ppermute | solution.py:277
  35.9 8.5 %collective-permute-start.8 = (bf16[264,512]{1,0:T(8,128)(2,1)S(1)}, bf16[264,512]{1,0:T(8,128)(2,1)S(1)}, u32[]{:S(2)}, u32[]{:S(2)}) collective-permute-start(bf16[264,512]{1,0:T(8,128)(2,1)S(1)} %multiply_convert_fusion.2.refs_1_), channel_id=1, source_target_pairs={{0,1},{1,0},{2,3},{3,2},{4,5},{5,4},{6,7},{7,6},{8,9},{9,8},{10,11... | collective-permute-start | bytes 811016 | tf_op jit(solution)/shard_map/ppermute | solution.py:280
  40.4 9.8 %collective-permute-start.12 = (bf16[264,512]{1,0:T(8,128)(2,1)}, bf16[264,512]{1,0:T(8,128)(2,1)}, u32[]{:S(2)}, u32[]{:S(2)}) collective-permute-start(bf16[264,512]{1,0:T(8,128)(2,1)} %get-tuple-element.65), channel_id=1, source_target_pairs={{0,1},{1,0},{2,3},{3,2},{4,5},{5,4},{6,7},{7,6},{8,9},{9,8},{10,11... | collective-permute-start | bytes 811016 | tf_op jit(solution)/shard_map/ppermute | solution.py:280
  51.4 3.5 %collective-permute-start.14 = (bf16[128,1920]{1,0:T(8,128)(2,1)S(1)}, bf16[128,1920]{1,0:T(8,128)(2,1)S(1)}, u32[]{:S(2)}, u32[]{:S(2)}) collective-permute-start(bf16[128,1920]{1,0:T(8,128)(2,1)S(1)} %get-tuple-element.101), channel_id=1, source_target_pairs={{0,2},{2,0},{4,6},{6,4},{8,10},{10,8},{12,14},{14,12},{16,18},{18,... | collective-permute-start | bytes 1474568 | tf_op jit(solution)/shard_map/ppermute | solution.py:271
  51.9 2.9 %collective-permute-start.15 = (bf16[128,1920]{1,0:T(8,128)(2,1)S(1)}, bf16[128,1920]{1,0:T(8,128)(2,1)S(1)}, u32[]{:S(2)}, u32[]{:S(2)}) collective-permute-start(bf16[128,1920]{1,0:T(8,128)(2,1)S(1)} %get-tuple-element.102), channel_id=1, source_target_pairs={{0,2},{2,0},{4,6},{6,4},{8,10},{10,8},{12,14},{14,12},{16,18},{18,... | collective-permute-start | bytes 1474568 | tf_op jit(solution)/shard_map/ppermute | solution.py:271
  52.1 10.0 %collective-permute-start.13 = (bf16[256,1024]{1,0:T(8,128)(2,1)S(1)}, bf16[256,1024]{1,0:T(8,128)(2,1)S(1)}, u32[]{:S(2)}, u32[]{:S(2)}) collective-permute-start(bf16[256,1024]{1,0:T(8,128)(2,1)S(1)} %pad_maximum_fusion.4), channel_id=1, source_target_pairs={{0,8},{2,6},{4,0},{6,14},{8,16},{10,2},{12,4},{14,22},{16,24},{18,... | collective-permute-start | bytes 1572872 | tf_op jit(solution)/shard_map/ppermute | solution.py:277
  53.7 8.5 %collective-permute-start.16 = (bf16[264,512]{1,0:T(8,128)(2,1)S(1)}, bf16[264,512]{1,0:T(8,128)(2,1)S(1)}, u32[]{:S(2)}, u32[]{:S(2)}) collective-permute-start(bf16[264,512]{1,0:T(8,128)(2,1)S(1)} %multiply_convert_fusion.1.refs_1_), channel_id=1, source_target_pairs={{0,1},{1,0},{2,3},{3,2},{4,5},{5,4},{6,7},{7,6},{8,9},{9,8},{10,11... | collective-permute-start | bytes 811016 | tf_op jit(solution)/shard_map/ppermute | solution.py:280
  56.8 10.5 %collective-permute-start.21 = (bf16[264,512]{1,0:T(8,128)(2,1)S(1)}, bf16[264,512]{1,0:T(8,128)(2,1)S(1)}, u32[]{:S(2)}, u32[]{:S(2)}) collective-permute-start(bf16[264,512]{1,0:T(8,128)(2,1)S(1)} %get-tuple-element.72), channel_id=1, source_target_pairs={{0,1},{1,0},{2,3},{3,2},{4,5},{5,4},{6,7},{7,6},{8,9},{9,8},{10,11... | collective-permute-start | bytes 811016 | tf_op jit(solution)/shard_map/ppermute | solution.py:280
  62.2 1.4 %collective-permute-start.17 = (bf16[64,1024]{1,0:T(8,128)(2,1)S(1)}, bf16[64,1024]{1,0:T(8,128)(2,1)S(1)}, u32[]{:S(2)}, u32[]{:S(2)}) collective-permute-start(bf16[64,1024]{1,0:T(8,128)(2,1)S(1)} %get-tuple-element.115), channel_id=1, source_target_pairs={{0,2},{2,0},{4,6},{6,4},{8,10},{10,8},{12,14},{14,12},{16,18},{18,... | collective-permute-start | bytes 393224 | tf_op jit(solution)/shard_map/ppermute | solution.py:271
  62.3 1.5 %collective-permute-start.20 = (bf16[64,1024]{1,0:T(8,128)(2,1)S(1)}, bf16[64,1024]{1,0:T(8,128)(2,1)S(1)}, u32[]{:S(2)}, u32[]{:S(2)}) collective-permute-start(bf16[64,1024]{1,0:T(8,128)(2,1)S(1)} %get-tuple-element.116), channel_id=1, source_target_pairs={{0,2},{2,0},{4,6},{6,4},{8,10},{10,8},{12,14},{14,12},{16,18},{18,... | collective-permute-start | bytes 393224 | tf_op jit(solution)/shard_map/ppermute | solution.py:271
  62.8 1.3 %collective-permute-start.19 = (bf16[64,1024]{1,0:T(8,128)(2,1)S(1)}, bf16[64,1024]{1,0:T(8,128)(2,1)S(1)}, u32[]{:S(2)}, u32[]{:S(2)}) collective-permute-start(bf16[64,1024]{1,0:T(8,128)(2,1)S(1)} %get-tuple-element.117), channel_id=1, source_target_pairs={{0,2},{2,0},{4,6},{6,4},{8,10},{10,8},{12,14},{14,12},{16,18},{18,... | collective-permute-start | bytes 393224 | tf_op jit(solution)/shard_map/ppermute | solution.py:271
  62.9 1.5 %collective-permute-start.18 = (bf16[64,1024]{1,0:T(8,128)(2,1)S(1)}, bf16[64,1024]{1,0:T(8,128)(2,1)S(1)}, u32[]{:S(2)}, u32[]{:S(2)}) collective-permute-start(bf16[64,1024]{1,0:T(8,128)(2,1)S(1)} %get-tuple-element.118), channel_id=1, source_target_pairs={{0,2},{2,0},{4,6},{6,4},{8,10},{10,8},{12,14},{14,12},{16,18},{18,... | collective-permute-start | bytes 393224 | tf_op jit(solution)/shard_map/ppermute | solution.py:271
  69.1 9.0 %collective-permute-start.24 = (bf16[132,1024]{1,0:T(8,128)(2,1)S(1)}, bf16[132,1024]{1,0:T(8,128)(2,1)S(1)}, u32[]{:S(2)}, u32[]{:S(2)}) collective-permute-start(bf16[132,1024]{1,0:T(8,128)(2,1)S(1)} %get-tuple-element.75.refs_1_), channel_id=1, source_target_pairs={{0,1},{1,0},{2,3},{3,2},{4,5},{5,4},{6,7},{7,6},{8,9},{9,8},{10,11... | collective-permute-start | bytes 811016 | tf_op jit(solution)/shard_map/ppermute | solution.py:280
  81.4 2.5 %collective-permute-start.26 = (bf16[64,896]{1,0:T(8,128)(2,1)S(1)}, bf16[64,896]{1,0:T(8,128)(2,1)S(1)}, u32[]{:S(2)}, u32[]{:S(2)}) collective-permute-start(bf16[64,896]{1,0:T(8,128)(2,1)S(1)} %get-tuple-element.121), channel_id=1, source_target_pairs={{0,2},{2,0},{4,6},{6,4},{8,10},{10,8},{12,14},{14,12},{16,18},{18,... | collective-permute-start | bytes 344072 | tf_op jit(solution)/shard_map/ppermute | solution.py:271
  82.2 1.8 %collective-permute-start.29 = (bf16[64,896]{1,0:T(8,128)(2,1)S(1)}, bf16[64,896]{1,0:T(8,128)(2,1)S(1)}, u32[]{:S(2)}, u32[]{:S(2)}) collective-permute-start(bf16[64,896]{1,0:T(8,128)(2,1)S(1)} %get-tuple-element.122), channel_id=1, source_target_pairs={{0,2},{2,0},{4,6},{6,4},{8,10},{10,8},{12,14},{14,12},{16,18},{18,... | collective-permute-start | bytes 344072 | tf_op jit(solution)/shard_map/ppermute | solution.py:271
  82.2 1.7 %collective-permute-start.28 = (bf16[64,896]{1,0:T(8,128)(2,1)S(1)}, bf16[64,896]{1,0:T(8,128)(2,1)S(1)}, u32[]{:S(2)}, u32[]{:S(2)}) collective-permute-start(bf16[64,896]{1,0:T(8,128)(2,1)S(1)} %get-tuple-element.123), channel_id=1, source_target_pairs={{0,2},{2,0},{4,6},{6,4},{8,10},{10,8},{12,14},{14,12},{16,18},{18,... | collective-permute-start | bytes 344072 | tf_op jit(solution)/shard_map/ppermute | solution.py:271
  82.7 1.3 %collective-permute-start.27 = (bf16[64,896]{1,0:T(8,128)(2,1)S(1)}, bf16[64,896]{1,0:T(8,128)(2,1)S(1)}, u32[]{:S(2)}, u32[]{:S(2)}) collective-permute-start(bf16[64,896]{1,0:T(8,128)(2,1)S(1)} %get-tuple-element.124), channel_id=1, source_target_pairs={{0,2},{2,0},{4,6},{6,4},{8,10},{10,8},{12,14},{14,12},{16,18},{18,... | collective-permute-start | bytes 344072 | tf_op jit(solution)/shard_map/ppermute | solution.py:271
  82.8 7.6 %collective-permute-start.25 = (bf16[264,512]{1,0:T(8,128)(2,1)S(1)}, bf16[264,512]{1,0:T(8,128)(2,1)S(1)}, u32[]{:S(2)}, u32[]{:S(2)}) collective-permute-start(bf16[264,512]{1,0:T(8,128)(2,1)S(1)} %multiply_convert_fusion.refs_1_), channel_id=1, source_target_pairs={{0,1},{1,0},{2,3},{3,2},{4,5},{5,4},{6,7},{7,6},{8,9},{9,8},{10,11... | collective-permute-start | bytes 811016 | tf_op jit(solution)/shard_map/ppermute | solution.py:280
  84.1 11.3 %collective-permute-start.32 = (bf16[256,896]{1,0:T(8,128)(2,1)S(1)}, bf16[256,896]{1,0:T(8,128)(2,1)S(1)}, u32[]{:S(2)}, u32[]{:S(2)}) collective-permute-start(bf16[256,896]{1,0:T(8,128)(2,1)S(1)} %add_convert_fusion.2), channel_id=1, source_target_pairs={{0,8},{2,6},{4,0},{6,14},{8,16},{10,2},{12,4},{14,22},{16,24},{18,... | collective-permute-start | bytes 1376264 | tf_op jit(solution)/shard_map/ppermute | solution.py:277
  94.0 2.5 %collective-permute-start.40 = (bf16[64,1792]{1,0:T(8,128)(2,1)S(1)}, bf16[64,1792]{1,0:T(8,128)(2,1)S(1)}, u32[]{:S(2)}, u32[]{:S(2)}) collective-permute-start(bf16[64,1792]{1,0:T(8,128)(2,1)S(1)} %get-tuple-element.107), channel_id=1, source_target_pairs={{0,2},{2,0},{4,6},{6,4},{8,10},{10,8},{12,14},{14,12},{16,18},{18,... | collective-permute-start | bytes 688136 | tf_op jit(solution)/shard_map/ppermute | solution.py:271
  95.3 1.5 %collective-permute-start.39 = (bf16[64,1792]{1,0:T(8,128)(2,1)S(1)}, bf16[64,1792]{1,0:T(8,128)(2,1)S(1)}, u32[]{:S(2)}, u32[]{:S(2)}) collective-permute-start(bf16[64,1792]{1,0:T(8,128)(2,1)S(1)} %get-tuple-element.108), channel_id=1, source_target_pairs={{0,2},{2,0},{4,6},{6,4},{8,10},{10,8},{12,14},{14,12},{16,18},{18,... | collective-permute-start | bytes 688136 | tf_op jit(solution)/shard_map/ppermute | solution.py:271
  97.0 7.7 %collective-permute-start.41 = (bf16[128,1792]{1,0:T(8,128)(2,1)S(1)}, bf16[128,1792]{1,0:T(8,128)(2,1)S(1)}, u32[]{:S(2)}, u32[]{:S(2)}) collective-permute-start(bf16[128,1792]{1,0:T(8,128)(2,1)S(1)} %shard_map.79), channel_id=1, source_target_pairs={{0,8},{2,6},{4,0},{6,14},{8,16},{10,2},{12,4},{14,22},{16,24},{18,... | collective-permute-start | bytes 1376264 | tf_op jit(solution)/shard_map/ppermute | solution.py:277
  97.3 7.3 %collective-permute-start.38 = (bf16[128,1792]{1,0:T(8,128)(2,1)S(1)}, bf16[128,1792]{1,0:T(8,128)(2,1)S(1)}, u32[]{:S(2)}, u32[]{:S(2)}) collective-permute-start(bf16[128,1792]{1,0:T(8,128)(2,1)S(1)} %get-tuple-element.111), channel_id=1, source_target_pairs={{0,2},{2,0},{4,6},{6,4},{8,10},{10,8},{12,14},{14,12},{16,18},{18,... | collective-permute-start | bytes 1376264 | tf_op jit(solution)/shard_map/ppermute | solution.py:271
  97.9 1.8 %collective-permute-start.31 = (bf16[64,1792]{1,0:T(8,128)(2,1)S(1)}, bf16[64,1792]{1,0:T(8,128)(2,1)S(1)}, u32[]{:S(2)}, u32[]{:S(2)}) collective-permute-start(bf16[64,1792]{1,0:T(8,128)(2,1)S(1)} %get-tuple-element.109), channel_id=1, source_target_pairs={{0,2},{2,0},{4,6},{6,4},{8,10},{10,8},{12,14},{14,12},{16,18},{18,... | collective-permute-start | bytes 688136 | tf_op jit(solution)/shard_map/ppermute | solution.py:271
  98.0 2.0 %collective-permute-start.30 = (bf16[64,1792]{1,0:T(8,128)(2,1)S(1)}, bf16[64,1792]{1,0:T(8,128)(2,1)S(1)}, u32[]{:S(2)}, u32[]{:S(2)}) collective-permute-start(bf16[64,1792]{1,0:T(8,128)(2,1)S(1)} %get-tuple-element.110), channel_id=1, source_target_pairs={{0,2},{2,0},{4,6},{6,4},{8,10},{10,8},{12,14},{14,12},{16,18},{18,... | collective-permute-start | bytes 688136 | tf_op jit(solution)/shard_map/ppermute | solution.py:271
  98.5 8.3 %collective-permute-start.23 = (bf16[128,1792]{1,0:T(8,128)(2,1)S(1)}, bf16[128,1792]{1,0:T(8,128)(2,1)S(1)}, u32[]{:S(2)}, u32[]{:S(2)}) collective-permute-start(bf16[128,1792]{1,0:T(8,128)(2,1)S(1)} %get-tuple-element.112), channel_id=1, source_target_pairs={{0,2},{2,0},{4,6},{6,4},{8,10},{10,8},{12,14},{14,12},{16,18},{18,... | collective-permute-start | bytes 1376264 | tf_op jit(solution)/shard_map/ppermute | solution.py:271
  100.2 9.4 %collective-permute-start.33 = (bf16[128,1792]{1,0:T(8,128)(2,1)S(1)}, bf16[128,1792]{1,0:T(8,128)(2,1)S(1)}, u32[]{:S(2)}, u32[]{:S(2)}) collective-permute-start(bf16[128,1792]{1,0:T(8,128)(2,1)S(1)} %shard_map.75), channel_id=1, source_target_pairs={{0,8},{2,6},{4,0},{6,14},{8,16},{10,2},{12,4},{14,22},{16,24},{18,... | collective-permute-start | bytes 1376264 | tf_op jit(solution)/shard_map/ppermute | solution.py:277
  104.8 9.7 %collective-permute-start.42 = (bf16[128,1792]{1,0:T(8,128)(2,1)S(1)}, bf16[128,1792]{1,0:T(8,128)(2,1)S(1)}, u32[]{:S(2)}, u32[]{:S(2)}) collective-permute-start(bf16[128,1792]{1,0:T(8,128)(2,1)S(1)} %shard_map.80), channel_id=1, source_target_pairs={{0,8},{2,6},{4,0},{6,14},{8,16},{10,2},{12,4},{14,22},{16,24},{18,... | collective-permute-start | bytes 1376264 | tf_op jit(solution)/shard_map/ppermute | solution.py:277
  105.2 9.3 %collective-permute-start.37 = (bf16[128,1792]{1,0:T(8,128)(2,1)S(1)}, bf16[128,1792]{1,0:T(8,128)(2,1)S(1)}, u32[]{:S(2)}, u32[]{:S(2)}) collective-permute-start(bf16[128,1792]{1,0:T(8,128)(2,1)S(1)} %get-tuple-element.113), channel_id=1, source_target_pairs={{0,2},{2,0},{4,6},{6,4},{8,10},{10,8},{12,14},{14,12},{16,18},{18,... | collective-permute-start | bytes 1376264 | tf_op jit(solution)/shard_map/ppermute | solution.py:271
  106.7 9.4 %collective-permute-start.22 = (bf16[128,1792]{1,0:T(8,128)(2,1)S(1)}, bf16[128,1792]{1,0:T(8,128)(2,1)S(1)}, u32[]{:S(2)}, u32[]{:S(2)}) collective-permute-start(bf16[128,1792]{1,0:T(8,128)(2,1)S(1)} %get-tuple-element.114), channel_id=1, source_target_pairs={{0,2},{2,0},{4,6},{6,4},{8,10},{10,8},{12,14},{14,12},{16,18},{18,... | collective-permute-start | bytes 1376264 | tf_op jit(solution)/shard_map/ppermute | solution.py:271
  109.7 9.7 %collective-permute-start.34 = (bf16[128,1792]{1,0:T(8,128)(2,1)S(1)}, bf16[128,1792]{1,0:T(8,128)(2,1)S(1)}, u32[]{:S(2)}, u32[]{:S(2)}) collective-permute-start(bf16[128,1792]{1,0:T(8,128)(2,1)S(1)} %shard_map.76), channel_id=1, source_target_pairs={{0,8},{2,6},{4,0},{6,14},{8,16},{10,2},{12,4},{14,22},{16,24},{18,... | collective-permute-start | bytes 1376264 | tf_op jit(solution)/shard_map/ppermute | solution.py:277
  114.7 9.7 %collective-permute-start.43 = (bf16[128,1792]{1,0:T(8,128)(2,1)S(1)}, bf16[128,1792]{1,0:T(8,128)(2,1)S(1)}, u32[]{:S(2)}, u32[]{:S(2)}) collective-permute-start(bf16[128,1792]{1,0:T(8,128)(2,1)S(1)} %shard_map.81), channel_id=1, source_target_pairs={{0,8},{2,6},{4,0},{6,14},{8,16},{10,2},{12,4},{14,22},{16,24},{18,... | collective-permute-start | bytes 1376264 | tf_op jit(solution)/shard_map/ppermute | solution.py:277
  115.0 4.8 %collective-permute-start.36 = (bf16[132,512]{1,0:T(8,128)(2,1)S(1)}, bf16[132,512]{1,0:T(8,128)(2,1)S(1)}, u32[]{:S(2)}, u32[]{:S(2)}) collective-permute-start(bf16[132,512]{1,0:T(8,128)(2,1)S(1)} %multiply_convert_fusion.3.refs_1_), channel_id=1, source_target_pairs={{0,1},{1,0},{2,3},{3,2},{4,5},{5,4},{6,7},{7,6},{8,9},{9,8},{10,11... | collective-permute-start | bytes 405512 | tf_op jit(solution)/shard_map/ppermute | solution.py:280
  119.6 9.7 %collective-permute-start.35 = (bf16[128,1792]{1,0:T(8,128)(2,1)S(1)}, bf16[128,1792]{1,0:T(8,128)(2,1)S(1)}, u32[]{:S(2)}, u32[]{:S(2)}) collective-permute-start(bf16[128,1792]{1,0:T(8,128)(2,1)S(1)} %shard_map.77), channel_id=1, source_target_pairs={{0,8},{2,6},{4,0},{6,14},{8,16},{10,2},{12,4},{14,22},{16,24},{18,... | collective-permute-start | bytes 1376264 | tf_op jit(solution)/shard_map/ppermute | solution.py:277
  124.4 4.8 %collective-permute-start.44 = (bf16[128,1792]{1,0:T(8,128)(2,1)S(1)}, bf16[128,1792]{1,0:T(8,128)(2,1)S(1)}, u32[]{:S(2)}, u32[]{:S(2)}) collective-permute-start(bf16[128,1792]{1,0:T(8,128)(2,1)S(1)} %add_convert_fusion.1), channel_id=1, source_target_pairs={{0,2},{2,0},{4,6},{6,4},{8,10},{10,8},{12,14},{14,12},{16,18},{18,... | collective-permute-start | bytes 1376264 | tf_op jit(solution)/shard_map/ppermute | solution.py:271
  (16 other events, 54.8 us)

commit v3 on v2

--- a/solution.py
+++ b/solution.py
@@ -169,68 +169,64 @@
                 out_ref[:, t : t + tile] = dot_t(rows_ref[...], w_ref[pl.ds(at, tile), :]).astype(BF16)
 
 
-def up_kernel(ring, chunk, *refs):
-    if chunk == ring.far:
-        refs, all_ref = refs[:-1], refs[-1]
+def up_kernel(ring, chunk, table_ref, *refs):
     core, side = lax.rem(lax.axis_index("ep"), 2), lax.axis_index("tp")
-    table_ref, ins, (w_ref, keep_ref, give_ref) = refs[0], refs[1:-3], refs[-3:]
+    ins, (w_ref, keep_ref, give_ref, up_ref, row_ref) = refs[:-5], refs[-5:]
     slot_n, token_n = ring.slot_n, ring.token_n
     feat_n, unit = w_ref.shape[0], w_ref.shape[1] // 2
     mine_at = pl.multiple_of(side * unit, 128)
     peer_at = pl.multiple_of((1 - side) * unit, 128)
     if len(ins) == 2:
-        ups = [ref[...] for ref in ins]
+        up_ref[:, pl.ds(mine_at, unit)] = ins[0][...]
+        up_ref[:, pl.ds(peer_at, unit)] = ins[1][...]
     else:
-        ups = []
         for at, act_ref in ((mine_at, ins[2]), (peer_at, ins[3])):
-            hidden = ins[0][:, pl.ds(at, unit)].astype(F32) + ins[1][:, pl.ds(at, unit)].astype(F32)
-            ups.append((hidden * act_ref[...].astype(F32)).astype(BF16))
-    rows_n = ups[0].shape[0]
+            part = pl.ds(at, unit)
+            hidden = ins[0][:, part].astype(F32) + ins[1][:, part].astype(F32)
+            up_ref[:, part] = (hidden * act_ref[...].astype(F32)).astype(BF16)
+    rows_n = up_ref.shape[0]
+    tile = 256
+    for t in range(0, feat_n, tile):
+        row_ref[:, t : t + tile] = dot_t(up_ref[...], w_ref[t : t + tile, :]).astype(BF16)
     window = rows_n if rows_n <= 2 * slot_n else 2 * slot_n + (-2 * slot_n) % 16
     lane = lax.broadcasted_iota(jnp.int32, (token_n, window), 1)
     mine = mine_of((0,))
     selects, starts = [], []
-    for b, (ref, at) in enumerate(ring.tables(chunk, [table_ref])):
+    for b in range(ring.pieces[chunk]):
         start = 0 if b < 2 else rows_n - window
-        slot = dot_t(ref[at : at + token_n, :], mine)[:, 0:1].astype(jnp.int32)
+        table = table_ref[b * token_n : (b + 1) * token_n, :]
+        slot = dot_t(table, mine)[:, 0:1].astype(jnp.int32)
         slot = jnp.where(slot >= 0, slot + (b * slot_n - start), -1)
         selects.append(jnp.where(lane == slot, 1.0, 0.0).astype(BF16))
         starts.append(start)
-    selects = [jnp.concatenate(selects[b : b + 2], axis=0) for b in range(0, len(selects), 2)]
-
-    def placed(at, tile):
-        row = dot_t(ups[0], w_ref[pl.ds(at, tile), pl.ds(mine_at, unit)])
-        row = row + dot_t(ups[1], w_ref[pl.ds(at, tile), pl.ds(peer_at, unit)])
-        row = row.astype(BF16)
-        out = []
-        for select, start in zip(selects, starts[::2]):
-            part = row[start : start + window]
-            out.append(jnp.dot(select, part, preferred_element_type=F32).astype(BF16))
-        return out
-
-    tile = 256
+
+    def placed(b, sources_n, columns):
+        select = jnp.concatenate(selects[b : b + sources_n], axis=0)
+        rows = row_ref[starts[b] : starts[b] + window, columns]
+        return jnp.dot(select, rows, preferred_element_type=F32).astype(BF16)
+
     if chunk == ring.far:
         half = feat_n // 2
-        for t in range(0, feat_n, tile):
-            (value,) = placed(t, tile)
-            all_ref[:, t : t + tile] = value
-        keep = pl.ds(pl.multiple_of(core * half, 128), half)
-        keep_ref[:token_n, :] = all_ref[token_n:, keep]
-        keep_ref[token_n:, :] = all_ref[:token_n, keep]
-        give_ref[...] = all_ref[:, pl.ds(pl.multiple_of((1 - core) * half, 128), half)]
+        keep = placed(0, 2, pl.ds(pl.multiple_of(core * half, 128), half))
+        keep_ref[:token_n, :] = keep[token_n:]
+        keep_ref[token_n:, :] = keep[:token_n]
+        give_ref[...] = placed(0, 2, pl.ds(pl.multiple_of((1 - core) * half, 128), half))
     else:
-        for t in range(0, feat_n, tile):
-            value = placed(t, tile)
-            if chunk == 0:
-                value = [value[0][:token_n], value[0][token_n:]]
-            give_ref[:, t : t + tile] = value[0]
-            keep_ref[:, t : t + tile] = value[1]
+        sources_n = ring.pieces[chunk] // 2
+        give_ref[...] = placed(0, sources_n, pl.ds(0, feat_n))
+        keep_ref[...] = placed(sources_n, sources_n, pl.ds(0, feat_n))
 
 
 def join_kernel(first, keep_ref, *refs):
     core = lax.rem(lax.axis_index("ep"), 2)
-    given_refs, came_ref, out_ref = refs[:-2], refs[-2], refs[-1]
-    feat_n, half = out_ref.shape[1], came_ref.shape[1]
+    out_ref = refs[-1]
+    rows_n, feat_n = out_ref.shape
+    given_refs, at = [], 0
+    while at < rows_n:
+        given_refs.append(refs[len(given_refs)])
+        at += given_refs[-1].shape[0]
+    came_refs = refs[len(given_refs) : -1]
+    half = came_refs[0].shape[1] if came_refs else feat_n
     at = 0
     for given_ref in given_refs:
         rows = pl.ds(at, given_ref.shape[0])
@@ -240,12 +236,15 @@
             return keep_ref[kept, columns].astype(F32) + given_ref[:, columns].astype(F32)
 
         if half == feat_n:
-            value = total(pl.ds(0, feat_n)) + came_ref[rows, :].astype(F32)
+            value = total(pl.ds(0, feat_n))
+            for came_ref in came_refs:
+                value = value + came_ref[rows, :].astype(F32)
             out_ref[rows, :] = value.astype(BF16)
         else:
             mine = pl.ds(pl.multiple_of(core * half, 128), half)
             other = pl.ds(pl.multiple_of((1 - core) * half, 128), half)
-            out_ref[rows, mine] = (total(mine) + came_ref[rows, :].astype(F32)).astype(BF16)
+            value = total(mine) + came_refs[0][rows, :].astype(F32)
+            out_ref[rows, mine] = value.astype(BF16)
             out_ref[rows, other] = total(other).astype(BF16)
         at += given_ref.shape[0]
 
@@ -312,11 +311,12 @@
             partials[k][-1],
             *args,
             w_up[0],
-            scratch=[pltpu.VMEM((2 * token_n, feat_n), BF16)] if k == far else [],
+            scratch=[pltpu.VMEM((pieces[k] * slot_n, n), BF16) for n in (2 * unit_n, feat_n)],
         )
 
     def join(first, width, *args):
-        return call(functools.partial(join_kernel, first), [(token_n, width)], *args)[0]
+        rows_n = 2 * token_n if width == half else token_n
+        return call(functools.partial(join_kernel, first), [(rows_n, width)], *args)[0]
 
     own = pl.pallas_call(
         prepare_kernel,
@@ -339,24 +339,18 @@
         gate_act[0],
     )
     act_peer = to_side(acts[far])
-    partials, mines, peers, ups = [down(0)], {}, {}, {}
+    partials, mines, ups = [down(0)], {}, {}
     sents = [to_side(partials[0][1])]
     for k in range(1, far + 1):
         ended = [partials[k - 1][0]]
         if k < far:
             ended += [sents[k - 1]] + ([act_peer] if k == 1 else [])
-        if k >= 3:
-            ended += [peers[k - 2]]
         here = after(moving, *ended)
         if k < far - 1:
             moving = to_ring(here)
         elif k == far - 1:
             part = lax.dynamic_slice_in_dim(here, core * half, half, 1)
             moving = to_ring(jnp.concatenate([part, here[:, feat_n:]], axis=1))
-        if 2 <= k < far:
-            mines[k - 1] = middle(k - 1, after(sents[k - 1], here))
-            peers[k - 1] = to_side(mines[k - 1])
-            here = after(here, mines[k - 1])
         blocks.append([here, to_core(here, 64 if k == far else 128)])
         if k == far:
             mines[k - 1] = middle(k - 1, sents[k - 1])
@@ -364,28 +358,25 @@
         partials.append(down(k))
         sents.append(to_side(partials[k][-2]))
 
-    for k in range(1, far - 1):
-        ups[k] = up(k, mines[k], after(peers[k], partials[far][0]))
-    full = after(sents[far], *(ups[k][0] for k in range(1, far - 1)))
-    ups[far] = up(far, partials[far][0], full, acts[far], act_peer)
-    peer = to_side(after(mines[far - 1], full))
-    keep, give = ups[far]
-    total = (keep.astype(F32) + to_core(give, 64).astype(F32)).astype(BF16)
+    keep, give = up(far, partials[far][0], sents[far], acts[far], act_peer)
+    peer = to_side(after(mines[far - 1], sents[far]))
+    total = join(0, half, keep, *parts_to_core(give, 64))
     came = to_ring(total)
-    ups[far - 1] = up(far - 1, mines[far - 1], after(peer, total))
-    mines[0] = middle(0, after(sents[0], peer))
-    peer = to_side(mines[0])
     came = [came[:token_n], came[token_n:]]
+    peer = after(peer, total)
     for k in range(far - 1, 0, -1):
-        keep, give = ups[k]
-        rows = 64 if k == far - 1 else 128
+        keep, give = up(k, mines[k], peer)
+        mines[k - 1] = middle(k - 1, after(sents[k - 1], peer))
+        peer = to_side(mines[k - 1])
+        rows = 128
         given = parts_to_core(give, rows)
         for i in range(2):
             parts = given[i * (token_n // rows) : (i + 1) * (token_n // rows)]
             total = join(i * token_n, feat_n, keep, *parts, came[i])
             came[i] = to_ring(total)
         came[0] = after(came[0], total)
-    keep, give = up(0, mines[0], after(peer, total))
+        peer = after(peer, total)
+    keep, give = up(0, mines[0], peer)
     total = to_core((came[0].astype(F32) + keep.astype(F32)).astype(BF16))
     return (came[1].astype(F32) + give.astype(F32) + total.astype(F32)).astype(BF16)
 

time: 132 us -> 125 us (0.947)
  Pallas kernels: 29.4 us -> 22.1 us
  starting transfers between devices: 31.3 us -> 37.9 us
  waiting for transfers between devices: 60.6 us -> 54.7 us
    pallas_call x17 -> x18, Pallas kernels: 29.1 us -> 21.8 us  [call(): pl.pallas_call(kernel, out_shape=[jax.ShapeDtypeStruct(shape, BF16) for s...]
    ppermute x11, starting transfers between devices: 8.68 us -> 14.9 us  [to_ring(): return lax.ppermute(x, 'ep', ring_pairs)]
    ppermute x10, waiting for transfers between devices: 34.2 us -> 29.4 us  [to_side(): return lax.ppermute(x, 'tp', [(0, 1), (1, 0)])]
    ppermute x11, waiting for transfers between devices: 20.2 us -> 18.1 us  [to_ring(): return lax.ppermute(x, 'ep', ring_pairs)]
    ppermute x24 -> x22, starting transfers between devices: 12 us -> 14 us  [parts_to_core(): lax.ppermute(p, 'ep', swap)]
    ppermute x10, starting transfers between devices: 10.7 us -> 9.01 us  [to_side(): return lax.ppermute(x, 'tp', [(0, 1), (1, 0)])]
    ppermute x24 -> x22, waiting for transfers between devices: 6.27 us -> 7.26 us  [parts_to_core(): lax.ppermute(p, 'ep', swap)]
    unnamed x38 -> x42, local copies, waits for them, and re-layouts: 5 us -> 5.01 us
  transfers between devices with their start and end apart: 45 -> 43, of which waited for: 26 -> 31; matrix products, arithmetic and copies ran while one was open for 1% -> 2% of each run, Pallas kernels for 19% -> 16%
where the time goes in v3:
time: 125 us; the launch traced here: 123 us
  waiting for transfers between devices  54.7 us (44%)
  starting transfers between devices  37.9 us (30%)
  Pallas kernels  22.1 us (18%)
  local copies, waits for them, and re-layouts  5.56 us (4%)
  other arithmetic  2.76 us (2%)
    ppermute x10, waiting for transfers between devices, to_side(): return lax.ppermute(x, 'tp', [(0, 1), (1, 0)])  29.4 us
    pallas_call x18, Pallas kernels, call(): pl.pallas_call(kernel, out_shape=[jax.ShapeDtypeStruct(shape, BF16) for s...  21.8 us
    ppermute x11, waiting for transfers between devices, to_ring(): return lax.ppermute(x, 'ep', ring_pairs)  18.1 us
    ppermute x11, starting transfers between devices, to_ring(): return lax.ppermute(x, 'ep', ring_pairs)  14.9 us
    ppermute x22, starting transfers between devices, parts_to_core(): lax.ppermute(p, 'ep', swap)  14 us
    ppermute x10, starting transfers between devices, to_side(): return lax.ppermute(x, 'tp', [(0, 1), (1, 0)])  9.01 us
    ppermute x22, waiting for transfers between devices, parts_to_core(): lax.ppermute(p, 'ep', swap)  7.26 us
    unnamed x42, local copies, waits for them, and re-layouts  5.01 us
  transfers between devices with their start and end apart: 43, of which 31 were waited for; matrix products, arithmetic and copies ran while one was open for 2% of the time, Pallas kernels for 16%

profile of v3, /device:TPU:13, one launch (start us, length us, event | category | flops | bytes accessed | tf_op | source)
XLA Modules:
  0.0 123.5 jit_solution(12904261635752742112)
XLA Ops:
  3.4 1.5 %collective-permute-done.refs_1_ = bf16[128,1920]{1,0:T(8,128)(2,1)S(1)} collective-permute-done((bf16[128,1920]{1,0:T(8,128)(2,1)S(1)}, bf16[128,1920]{1,0:T(8,128)(2,1)S(1)}, u32[]{:S(2)}, u32[]{:S(2)}) %collective-permute-start) | collective-permute-done | bytes 491552 | tf_op jit(solution)/shard_map/ppermute | solution.py:270
  5.0 1.3 %collective-permute-start.1 = (bf16[256,1920]{1,0:T(8,128)(2,1)S(1)}, bf16[256,1920]{1,0:T(8,128)(2,1)S(1)}, u32[]{:S(2)}, u32[]{:S(2)}) collective-permute-start(bf16[256,1920]{1,0:T(8,128)(2,1)S(1)} %pad_maximum_fusion), channel_id=1, source_target_pairs={{0,8},{2,6},{4,0},{6,14},{8,16},{10,2},{12,4},{14,22},{16,24},{18,... | collective-permute-start | bytes 2949128 | tf_op jit(solution)/shard_map/ppermute | solution.py:276
  6.4 1.2 copy-done.3
  7.6 1.6 %shard_map.66 = (bf16[132,512]{1,0:T(8,128)(2,1)S(1)}, bf16[264,512]{1,0:T(8,128)(2,1)S(1)}, bf16[264,512]{1,0:T(8,128)(2,1)S(1)}, bf16[264,512]{1,0:T(8,128)(2,1)S(1)}, bf16[132,512]{1,0:T(8,128)(2,1)S(1)}) custom-call(bf16[1056,512]{1,0:T(8,128)(2,1)S(1)} %bitcast.15), custom_call_target="tpu_custom_call" | custom-call | tf_op jit(solution)/shard_map/pallas_call | solution.py:282
  9.9 1.2 collective-permute-start.3
  11.1 1.7 %shard_map.65 = (bf16[132,512]{1,0:T(8,128)(2,1)S(1)}, bf16[132,512]{1,0:T(8,128)(2,1)S(1)}, bf16[256,128]{1,0:T(8,128)(2,1)S(1)}) custom-call(bf16[128,1920]{1,0:T(8,128)(2,1)S(1)} %shard_map.64.refs_0_, bf16[128,1920]{1,0:T(8,128)(2,1)S(1)} %collective-permute-done.refs_1_, bf16[1024,1792]{1,0:T(8,128)(2,1)S(1)} %bitcast.5), custom_call_target="tpu_custom_call" | custom-call | tf_op jit(solution)/shard_map/pallas_call | solution.py:282
  13.2 2.4 %collective-permute-done.3.refs_3_ = bf16[132,512]{1,0:T(8,128)(2,1)S(1)} collective-permute-done((bf16[132,512]{1,0:T(8,128)(2,1)S(1)}, bf16[132,512]{1,0:T(8,128)(2,1)S(1)}, u32[]{:S(2)}, u32[]{:S(2)}) %collective-permute-start.3) | collective-permute-done | bytes 135200 | tf_op jit(solution)/shard_map/ppermute | solution.py:279
  15.6 2.8 %collective-permute-done.2 = bf16[132,512]{1,0:T(8,128)(2,1)S(1)} collective-permute-done((bf16[132,512]{1,0:T(8,128)(2,1)S(1)}, bf16[132,512]{1,0:T(8,128)(2,1)S(1)}, u32[]{:S(2)}, u32[]{:S(2)}) %collective-permute-start.2) | collective-permute-done | bytes 135200 | tf_op jit(solution)/shard_map/ppermute | solution.py:279
  18.5 1.2 collective-permute-start.4
  19.8 1.3 %collective-permute-start.7 = (bf16[256,1920]{1,0:T(8,128)(2,1)S(1)}, bf16[256,1920]{1,0:T(8,128)(2,1)S(1)}, u32[]{:S(2)}, u32[]{:S(2)}) collective-permute-start(bf16[256,1920]{1,0:T(8,128)(2,1)S(1)} %collective-permute-done.1.refs_0_), channel_id=1, source_target_pairs={{0,8},{2,6},{4,0},{6,14},{8,16},{10,2},{12,4},{14,22},{16,24},{18,... | collective-permute-start | bytes 2949128 | tf_op jit(solution)/shard_map/ppermute | solution.py:276
  22.0 1.9 %shard_map.67 = (bf16[264,512]{1,0:T(8,128)(2,1)S(1)}, bf16[264,512]{1,0:T(8,128)(2,1)S(1)}, bf16[512,128]{1,0:T(8,128)(2,1)S(1)}) custom-call(bf16[256,1920]{1,0:T(8,128)(2,1)S(1)} %collective-permute-done.1.refs_0_, bf16[256,1920]{1,0:T(8,128)(2,1)S(1)} %pad_maximum_fusion.1.refs_1_, bf16[1024,1792]{1,0:T(8,128)(2,1)S(1)} %bitcast.6), custom_call_target="tpu_custom_call" | custom-call | tf_op jit(solution)/shard_map/pallas_call | solution.py:282
  23.8 1.3 %collective-permute-start.6 = (bf16[264,512]{1,0:T(8,128)(2,1)S(1)}, bf16[264,512]{1,0:T(8,128)(2,1)S(1)}, u32[]{:S(2)}, u32[]{:S(2)}) collective-permute-start(bf16[264,512]{1,0:T(8,128)(2,1)S(1)} %get-tuple-element.56), channel_id=1, source_target_pairs={{0,1},{1,0},{2,3},{3,2},{4,5},{5,4},{6,7},{7,6},{8,9},{9,8},{10,11... | collective-permute-start | bytes 811016 | tf_op jit(solution)/shard_map/ppermute | solution.py:279
  25.1 6.5 %collective-permute-done.6 = bf16[264,512]{1,0:T(8,128)(2,1)S(1)} collective-permute-done((bf16[264,512]{1,0:T(8,128)(2,1)S(1)}, bf16[264,512]{1,0:T(8,128)(2,1)S(1)}, u32[]{:S(2)}, u32[]{:S(2)}) %collective-permute-start.6) | collective-permute-done | bytes 270368 | tf_op jit(solution)/shard_map/ppermute | solution.py:279
  31.6 1.4 %collective-permute-done.7.refs_0_ = bf16[256,1920]{1,0:T(8,128)(2,1)S(1)} collective-permute-done((bf16[256,1920]{1,0:T(8,128)(2,1)S(1)}, bf16[256,1920]{1,0:T(8,128)(2,1)S(1)}, u32[]{:S(2)}, u32[]{:S(2)}) %collective-permute-start.7) | collective-permute-done | bytes 983072 | tf_op jit(solution)/shard_map/ppermute | solution.py:276
  33.1 1.4 %collective-permute-start.8 = (bf16[128,1920]{1,0:T(8,128)(2,1)S(1)}, bf16[128,1920]{1,0:T(8,128)(2,1)S(1)}, u32[]{:S(2)}, u32[]{:S(2)}) collective-permute-start(bf16[128,1920]{1,0:T(8,128)(2,1)S(1)} %get-tuple-element.97), channel_id=1, source_target_pairs={{0,2},{2,0},{4,6},{6,4},{8,10},{10,8},{12,14},{14,12},{16,18},{18,... | collective-permute-start | bytes 1474568 | tf_op jit(solution)/shard_map/ppermute | solution.py:270
  34.5 1.3 %collective-permute-start.11 = (bf16[256,1920]{1,0:T(8,128)(2,1)S(1)}, bf16[256,1920]{1,0:T(8,128)(2,1)S(1)}, u32[]{:S(2)}, u32[]{:S(2)}) collective-permute-start(bf16[256,1920]{1,0:T(8,128)(2,1)S(1)} %collective-permute-done.7.refs_0_), channel_id=1, source_target_pairs={{0,8},{2,6},{4,0},{6,14},{8,16},{10,2},{12,4},{14,22},{16,24},{18,... | collective-permute-start | bytes 2949128 | tf_op jit(solution)/shard_map/ppermute | solution.py:276
  36.7 2.6 %shard_map.68 = (bf16[264,512]{1,0:T(8,128)(2,1)S(1)}, bf16[264,512]{1,0:T(8,128)(2,1)}, bf16[512,128]{1,0:T(8,128)(2,1)S(1)}) custom-call(bf16[256,1920]{1,0:T(8,128)(2,1)S(1)} %collective-permute-done.7.refs_0_, bf16[256,1920]{1,0:T(8,128)(2,1)S(1)} %pad_maximum_fusion.2.refs_1_, bf16[1024,1792]{1,0:T(8,128)(2,1)S(1)} %bitcast.7), custom_call_target="tpu_custom_call" | custom-call | tf_op jit(solution)/shard_map/pallas_call | solution.py:282
  41.1 6.8 %collective-permute-done.10 = bf16[264,512]{1,0:T(8,128)(2,1)} collective-permute-done((bf16[264,512]{1,0:T(8,128)(2,1)}, bf16[264,512]{1,0:T(8,128)(2,1)}, u32[]{:S(2)}, u32[]{:S(2)}) %collective-permute-start.10) | collective-permute-done | bytes 270368 | tf_op jit(solution)/shard_map/ppermute | solution.py:279
  48.0 1.3 %collective-permute-start.12 = (bf16[128,1920]{1,0:T(8,128)(2,1)S(1)}, bf16[128,1920]{1,0:T(8,128)(2,1)S(1)}, u32[]{:S(2)}, u32[]{:S(2)}) collective-permute-start(bf16[128,1920]{1,0:T(8,128)(2,1)S(1)} %get-tuple-element.95), channel_id=1, source_target_pairs={{0,2},{2,0},{4,6},{6,4},{8,10},{10,8},{12,14},{14,12},{16,18},{18,... | collective-permute-start | bytes 1474568 | tf_op jit(solution)/shard_map/ppermute | solution.py:270
  49.5 1.4 %collective-permute-start.15 = (bf16[256,1024]{1,0:T(8,128)(2,1)S(1)}, bf16[256,1024]{1,0:T(8,128)(2,1)S(1)}, u32[]{:S(2)}, u32[]{:S(2)}) collective-permute-start(bf16[256,1024]{1,0:T(8,128)(2,1)S(1)} %pad_maximum_fusion.4), channel_id=1, source_target_pairs={{0,8},{2,6},{4,0},{6,14},{8,16},{10,2},{12,4},{14,22},{16,24},{18,... | collective-permute-start | bytes 1572872 | tf_op jit(solution)/shard_map/ppermute | solution.py:276
  51.6 1.9 %shard_map.69 = (bf16[264,512]{1,0:T(8,128)(2,1)S(1)}, bf16[264,512]{1,0:T(8,128)(2,1)S(1)}, bf16[512,128]{1,0:T(8,128)(2,1)S(1)}) custom-call(bf16[256,1920]{1,0:T(8,128)(2,1)S(1)} %collective-permute-done.11.refs_0_, bf16[256,1920]{1,0:T(8,128)(2,1)S(1)} %pad_maximum_fusion.3.refs_1_, bf16[1024,1792]{1,0:T(8,128)(2,1)S(1)} %bitcast.8), custom_call_target="tpu_custom_call" | custom-call | tf_op jit(solution)/shard_map/pallas_call | solution.py:282
  53.4 1.3 %collective-permute-start.14 = (bf16[264,512]{1,0:T(8,128)(2,1)S(1)}, bf16[264,512]{1,0:T(8,128)(2,1)S(1)}, u32[]{:S(2)}, u32[]{:S(2)}) collective-permute-start(bf16[264,512]{1,0:T(8,128)(2,1)S(1)} %get-tuple-element.62), channel_id=1, source_target_pairs={{0,1},{1,0},{2,3},{3,2},{4,5},{5,4},{6,7},{7,6},{8,9},{9,8},{10,11... | collective-permute-start | bytes 811016 | tf_op jit(solution)/shard_map/ppermute | solution.py:279
  54.7 3.2 %collective-permute-done.15.refs_0_ = bf16[256,1024]{1,0:T(8,128)(2,1)S(1)} collective-permute-done((bf16[256,1024]{1,0:T(8,128)(2,1)S(1)}, bf16[256,1024]{1,0:T(8,128)(2,1)S(1)}, u32[]{:S(2)}, u32[]{:S(2)}) %collective-permute-start.15) | collective-permute-done | bytes 524320 | tf_op jit(solution)/shard_map/ppermute | solution.py:276
  57.9 1.3 %collective-permute-start.16 = (bf16[64,1024]{1,0:T(8,128)(2,1)S(1)}, bf16[64,1024]{1,0:T(8,128)(2,1)S(1)}, u32[]{:S(2)}, u32[]{:S(2)}) collective-permute-start(bf16[64,1024]{1,0:T(8,128)(2,1)S(1)} %get-tuple-element.107), channel_id=1, source_target_pairs={{0,2},{2,0},{4,6},{6,4},{8,10},{10,8},{12,14},{14,12},{16,18},{18,... | collective-permute-start | bytes 393224 | tf_op jit(solution)/shard_map/ppermute | solution.py:270
  61.3 1.7 %shard_map.70 = (bf16[132,1024]{1,0:T(8,128)(2,1)S(1)}, bf16[256,128]{1,0:T(8,128)(2,1)S(1)}) custom-call(bf16[256,1024]{1,0:T(8,128)(2,1)S(1)} %collective-permute-done.15.refs_0_, bf16[256,1024]{1,0:T(8,128)(2,1)S(1)} %pad_maximum_fusion.5.refs_1_, bf16[1024,1792]{1,0:T(8,128)(2,1)S(1)} %bitcast.9), custom_call_target="tpu_custom_call" | custom-call | tf_op jit(solution)/shard_map/pallas_call | solution.py:282
  63.0 1.3 %collective-permute-start.20 = (bf16[132,1024]{1,0:T(8,128)(2,1)S(1)}, bf16[132,1024]{1,0:T(8,128)(2,1)S(1)}, u32[]{:S(2)}, u32[]{:S(2)}) collective-permute-start(bf16[132,1024]{1,0:T(8,128)(2,1)S(1)} %get-tuple-element.66.refs_0_), channel_id=1, source_target_pairs={{0,1},{1,0},{2,3},{3,2},{4,5},{5,4},{6,7},{7,6},{8,9},{9,8},{10,11... | collective-permute-start | bytes 811016 | tf_op jit(solution)/shard_map/ppermute | solution.py:279
  64.3 5.8 %collective-permute-done.20.refs_1_ = bf16[132,1024]{1,0:T(8,128)(2,1)S(1)} collective-permute-done((bf16[132,1024]{1,0:T(8,128)(2,1)S(1)}, bf16[132,1024]{1,0:T(8,128)(2,1)S(1)}, u32[]{:S(2)}, u32[]{:S(2)}) %collective-permute-start.20) | collective-permute-done | bytes 270368 | tf_op jit(solution)/shard_map/ppermute | solution.py:279
  71.2 2.1 %shard_map.71 = (bf16[256,896]{1,0:T(8,128)(2,1)S(1)}, bf16[256,896]{1,0:T(8,128)(2,1)S(1)}) custom-call(bf16[256,128]{1,0:T(8,128)(2,1)S(1)} %get-tuple-element.68.table_ref, bf16[132,1024]{1,0:T(8,128)(2,1)S(1)} %get-tuple-element.66.refs_0_, bf16[132,1024]{1,0:T(8,128)(2,1)S(1)} %collective-permute-done.20.refs_1_, ...), custom_call_target="tpu_custom_call" | custom-call | tf_op jit(solution)/shard_map/pallas_call | solution.py:282
  73.4 2.5 %collective-permute-start.25 = (bf16[64,896]{1,0:T(8,128)(2,1)S(1)}, bf16[64,896]{1,0:T(8,128)(2,1)S(1)}, u32[]{:S(2)}, u32[]{:S(2)}) collective-permute-start(bf16[64,896]{1,0:T(8,128)(2,1)S(1)} %get-tuple-element.113), channel_id=1, source_target_pairs={{0,2},{2,0},{4,6},{6,4},{8,10},{10,8},{12,14},{14,12},{16,18},{18,... | collective-permute-start | bytes 344072 | tf_op jit(solution)/shard_map/ppermute | solution.py:270
  77.8 1.5 %collective-permute-start.28 = (bf16[256,896]{1,0:T(8,128)(2,1)S(1)}, bf16[256,896]{1,0:T(8,128)(2,1)S(1)}, u32[]{:S(2)}, u32[]{:S(2)}) collective-permute-start(bf16[256,896]{1,0:T(8,128)(2,1)S(1)} %shard_map.72), channel_id=1, source_target_pairs={{0,8},{2,6},{4,0},{6,14},{8,16},{10,2},{12,4},{14,22},{16,24},{18,... | collective-permute-start | bytes 1376264 | tf_op jit(solution)/shard_map/ppermute | solution.py:276
  79.3 1.9 %shard_map.73 = (bf16[256,1792]{1,0:T(8,128)(2,1)S(1)}, bf16[256,1792]{1,0:T(8,128)(2,1)S(1)}) custom-call(bf16[512,128]{1,0:T(8,128)(2,1)S(1)} %get-tuple-element.74.table_ref, bf16[264,512]{1,0:T(8,128)(2,1)S(1)} %multiply_convert_fusion.2.refs_0_, bf16[264,512]{1,0:T(8,128)(2,1)S(1)} %collective-permute-done.21.refs_1_, bf16[1792,1024]{1,0:T(8,128)(2,1)S(1)} %bitcast.11), custom_call_target="tpu_custom_call" | custom-call | tf_op jit(solution)/shard_map/pallas_call | solution.py:282
  83.3 2.3 %collective-permute-done.28 = bf16[256,896]{1,0:T(8,128)(2,1)S(1)} collective-permute-done((bf16[256,896]{1,0:T(8,128)(2,1)S(1)}, bf16[256,896]{1,0:T(8,128)(2,1)S(1)}, u32[]{:S(2)}, u32[]{:S(2)}) %collective-permute-start.28) | collective-permute-done | bytes 458784 | tf_op jit(solution)/shard_map/ppermute | solution.py:276
  85.9 1.4 %collective-permute-start.39 = (bf16[128,1792]{1,0:T(8,128)(2,1)S(1)}, bf16[128,1792]{1,0:T(8,128)(2,1)S(1)}, u32[]{:S(2)}, u32[]{:S(2)}) collective-permute-start(bf16[128,1792]{1,0:T(8,128)(2,1)S(1)} %shard_map.80), channel_id=1, source_target_pairs={{0,8},{2,6},{4,0},{6,14},{8,16},{10,2},{12,4},{14,22},{16,24},{18,... | collective-permute-start | bytes 1376264 | tf_op jit(solution)/shard_map/ppermute | solution.py:276
  87.4 1.4 %collective-permute-start.31 = (bf16[128,1792]{1,0:T(8,128)(2,1)S(1)}, bf16[128,1792]{1,0:T(8,128)(2,1)S(1)}, u32[]{:S(2)}, u32[]{:S(2)}) collective-permute-start(bf16[128,1792]{1,0:T(8,128)(2,1)S(1)} %shard_map.74), channel_id=1, source_target_pairs={{0,8},{2,6},{4,0},{6,14},{8,16},{10,2},{12,4},{14,22},{16,24},{18,... | collective-permute-start | bytes 1376264 | tf_op jit(solution)/shard_map/ppermute | solution.py:276
  88.7 2.3 %collective-permute-done.26.refs_1_ = bf16[264,512]{1,0:T(8,128)(2,1)S(1)} collective-permute-done((bf16[264,512]{1,0:T(8,128)(2,1)S(1)}, bf16[264,512]{1,0:T(8,128)(2,1)S(1)}, u32[]{:S(2)}, u32[]{:S(2)}) %collective-permute-start.26) | collective-permute-done | bytes 270368 | tf_op jit(solution)/shard_map/ppermute | solution.py:279
  91.0 1.9 %shard_map.75 = (bf16[256,1792]{1,0:T(8,128)(2,1)S(1)}, bf16[256,1792]{1,0:T(8,128)(2,1)S(1)}) custom-call(bf16[512,128]{1,0:T(8,128)(2,1)S(1)} %copy-done.14, bf16[264,512]{1,0:T(8,128)(2,1)S(1)} %multiply_convert_fusion.1.refs_0_, bf16[264,512]{1,0:T(8,128)(2,1)S(1)} %collective-permute-done.26.refs_1_, bf16[1792,1024]{1,0:T(8,128)(2,1)S(1)} %bitcast.12), custom_call_target="tpu_custom_call" | custom-call | tf_op jit(solution)/shard_map/pallas_call | solution.py:282
  95.5 1.4 %collective-permute-start.40 = (bf16[128,1792]{1,0:T(8,128)(2,1)S(1)}, bf16[128,1792]{1,0:T(8,128)(2,1)S(1)}, u32[]{:S(2)}, u32[]{:S(2)}) collective-permute-start(bf16[128,1792]{1,0:T(8,128)(2,1)S(1)} %shard_map.81), channel_id=1, source_target_pairs={{0,8},{2,6},{4,0},{6,14},{8,16},{10,2},{12,4},{14,22},{16,24},{18,... | collective-permute-start | bytes 1376264 | tf_op jit(solution)/shard_map/ppermute | solution.py:276
  96.9 1.6 %collective-permute-done.31.refs_1_ = bf16[128,1792]{1,0:T(8,128)(2,1)S(1)} collective-permute-done((bf16[128,1792]{1,0:T(8,128)(2,1)S(1)}, bf16[128,1792]{1,0:T(8,128)(2,1)S(1)}, u32[]{:S(2)}, u32[]{:S(2)}) %collective-permute-start.31) | collective-permute-done | bytes 458784 | tf_op jit(solution)/shard_map/ppermute | solution.py:276
  98.6 2.8 %collective-permute-done.29.refs_1_ = bf16[264,512]{1,0:T(8,128)(2,1)S(1)} collective-permute-done((bf16[264,512]{1,0:T(8,128)(2,1)S(1)}, bf16[264,512]{1,0:T(8,128)(2,1)S(1)}, u32[]{:S(2)}, u32[]{:S(2)}) %collective-permute-start.29) | collective-permute-done | bytes 270368 | tf_op jit(solution)/shard_map/ppermute | solution.py:279
  101.4 1.9 %shard_map.77 = (bf16[256,1792]{1,0:T(8,128)(2,1)S(1)}, bf16[256,1792]{1,0:T(8,128)(2,1)S(1)}) custom-call(bf16[512,128]{1,0:T(8,128)(2,1)S(1)} %copy-done.12, bf16[264,512]{1,0:T(8,128)(2,1)S(1)} %multiply_convert_fusion.refs_0_, bf16[264,512]{1,0:T(8,128)(2,1)S(1)} %collective-permute-done.29.refs_1_, bf16[1792,1024]{1,0:T(8,128)(2,1)S(1)} %bitcast.13), custom_call_target="tpu_custom_call" | custom-call | tf_op jit(solution)/shard_map/pallas_call | solution.py:282
  103.4 1.7 %collective-permute-start.36 = (bf16[128,1792]{1,0:T(8,128)(2,1)S(1)}, bf16[128,1792]{1,0:T(8,128)(2,1)S(1)}, u32[]{:S(2)}, u32[]{:S(2)}) collective-permute-start(bf16[128,1792]{1,0:T(8,128)(2,1)S(1)} %get-tuple-element.105), channel_id=1, source_target_pairs={{0,2},{2,0},{4,6},{6,4},{8,10},{10,8},{12,14},{14,12},{16,18},{18,... | collective-permute-start | bytes 1376264 | tf_op jit(solution)/shard_map/ppermute | solution.py:270
  105.1 1.3 %collective-permute-start.33 = (bf16[128,1792]{1,0:T(8,128)(2,1)S(1)}, bf16[128,1792]{1,0:T(8,128)(2,1)S(1)}, u32[]{:S(2)}, u32[]{:S(2)}) collective-permute-start(bf16[128,1792]{1,0:T(8,128)(2,1)S(1)} %shard_map.76), channel_id=1, source_target_pairs={{0,8},{2,6},{4,0},{6,14},{8,16},{10,2},{12,4},{14,22},{16,24},{18,... | collective-permute-start | bytes 1376264 | tf_op jit(solution)/shard_map/ppermute | solution.py:276
  106.7 1.4 %collective-permute-start.41 = (bf16[128,1792]{1,0:T(8,128)(2,1)S(1)}, bf16[128,1792]{1,0:T(8,128)(2,1)S(1)}, u32[]{:S(2)}, u32[]{:S(2)}) collective-permute-start(bf16[128,1792]{1,0:T(8,128)(2,1)S(1)} %shard_map.82), channel_id=1, source_target_pairs={{0,8},{2,6},{4,0},{6,14},{8,16},{10,2},{12,4},{14,22},{16,24},{18,... | collective-permute-start | bytes 1376264 | tf_op jit(solution)/shard_map/ppermute | solution.py:276
  108.5 4.2 %collective-permute-done.33.refs_1_ = bf16[128,1792]{1,0:T(8,128)(2,1)S(1)} collective-permute-done((bf16[128,1792]{1,0:T(8,128)(2,1)S(1)}, bf16[128,1792]{1,0:T(8,128)(2,1)S(1)}, u32[]{:S(2)}, u32[]{:S(2)}) %collective-permute-start.33) | collective-permute-done | bytes 458784 | tf_op jit(solution)/shard_map/ppermute | solution.py:276
  112.9 1.4 %collective-permute-start.34 = (bf16[128,1792]{1,0:T(8,128)(2,1)S(1)}, bf16[128,1792]{1,0:T(8,128)(2,1)S(1)}, u32[]{:S(2)}, u32[]{:S(2)}) collective-permute-start(bf16[128,1792]{1,0:T(8,128)(2,1)S(1)} %shard_map.78), channel_id=1, source_target_pairs={{0,8},{2,6},{4,0},{6,14},{8,16},{10,2},{12,4},{14,22},{16,24},{18,... | collective-permute-start | bytes 1376264 | tf_op jit(solution)/shard_map/ppermute | solution.py:276
  114.2 1.7 %shard_map.79 = (bf16[128,1792]{1,0:T(8,128)(2,1)S(1)}, bf16[128,1792]{1,0:T(8,128)(2,1)S(1)}) custom-call(bf16[256,128]{1,0:T(8,128)(2,1)S(1)} %get-tuple-element.86.table_ref, bf16[132,512]{1,0:T(8,128)(2,1)S(1)} %multiply_convert_fusion.3.refs_0_, bf16[132,512]{1,0:T(8,128)(2,1)S(1)} %collective-permute-done.35.refs_1_, bf16[1792,1024]{1,0:T(8,128)(2,1)S(1)} %bitcast.14), custom_call_target="tpu_custom_call" | custom-call | tf_op jit(solution)/shard_map/pallas_call | solution.py:282
  116.0 1.6 %collective-permute-done.41 = bf16[128,1792]{1,0:T(8,128)(2,1)S(1)} collective-permute-done((bf16[128,1792]{1,0:T(8,128)(2,1)S(1)}, bf16[128,1792]{1,0:T(8,128)(2,1)S(1)}, u32[]{:S(2)}, u32[]{:S(2)}) %collective-permute-start.41) | collective-permute-done | bytes 458784 | tf_op jit(solution)/shard_map/ppermute | solution.py:276
  118.7 3.8 %collective-permute-done.34 = bf16[128,1792]{1,0:T(8,128)(2,1)S(1)} collective-permute-done((bf16[128,1792]{1,0:T(8,128)(2,1)S(1)}, bf16[128,1792]{1,0:T(8,128)(2,1)S(1)}, u32[]{:S(2)}, u32[]{:S(2)}) %collective-permute-start.34) | collective-permute-done | bytes 458784 | tf_op jit(solution)/shard_map/ppermute | solution.py:276
  (122 shorter events, 23.0 us)
Async XLA Ops:
  2.4 8.7 %copy-start = (bf16[1,1024,1792]{2,1,0:T(8,128)(2,1)S(1)}, bf16[1,1024,1792]{2,1,0:T(8,128)(2,1)}, u32[]{:S(2)}) copy-start(bf16[1,1024,1792]{2,1,0:T(8,128)(2,1)} %param.10) | copy-start | bytes 11010052
  2.7 2.2 %collective-permute-start = (bf16[128,1920]{1,0:T(8,128)(2,1)S(1)}, bf16[128,1920]{1,0:T(8,128)(2,1)S(1)}, u32[]{:S(2)}, u32[]{:S(2)}) collective-permute-start(bf16[128,1920]{1,0:T(8,128)(2,1)S(1)} %shard_map.64.refs_0_), channel_id=1, source_target_pairs={{0,2},{2,0},{4,6},{6,4},{8,10},{10,8},{12,14},{14,12},{16,18},{18,... | collective-permute-start | bytes 1474568 | tf_op jit(solution)/shard_map/ppermute | solution.py:270
  5.0 13.4 %collective-permute-start.1 = (bf16[256,1920]{1,0:T(8,128)(2,1)S(1)}, bf16[256,1920]{1,0:T(8,128)(2,1)S(1)}, u32[]{:S(2)}, u32[]{:S(2)}) collective-permute-start(bf16[256,1920]{1,0:T(8,128)(2,1)S(1)} %pad_maximum_fusion), channel_id=1, source_target_pairs={{0,8},{2,6},{4,0},{6,14},{8,16},{10,2},{12,4},{14,22},{16,24},{18,... | collective-permute-start | bytes 2949128 | tf_op jit(solution)/shard_map/ppermute | solution.py:276
  9.9 5.7 %collective-permute-start.3 = (bf16[132,512]{1,0:T(8,128)(2,1)S(1)}, bf16[132,512]{1,0:T(8,128)(2,1)S(1)}, u32[]{:S(2)}, u32[]{:S(2)}) collective-permute-start(bf16[132,512]{1,0:T(8,128)(2,1)S(1)} %get-tuple-element.52.refs_2_), channel_id=1, source_target_pairs={{0,1},{1,0},{2,3},{3,2},{4,5},{5,4},{6,7},{7,6},{8,9},{9,8},{10,11... | collective-permute-start | bytes 405512 | tf_op jit(solution)/shard_map/ppermute | solution.py:279
  12.9 9.1 %copy-start.9 = (bf16[132,512]{1,0:T(8,128)(2,1)}, bf16[132,512]{1,0:T(8,128)(2,1)S(1)}, u32[]{:S(2)}) copy-start(bf16[132,512]{1,0:T(8,128)(2,1)S(1)} %get-tuple-element.50) | copy-start | bytes 405508
  12.9 5.5 %collective-permute-start.2 = (bf16[132,512]{1,0:T(8,128)(2,1)S(1)}, bf16[132,512]{1,0:T(8,128)(2,1)S(1)}, u32[]{:S(2)}, u32[]{:S(2)}) collective-permute-start(bf16[132,512]{1,0:T(8,128)(2,1)S(1)} %get-tuple-element.51), channel_id=1, source_target_pairs={{0,1},{1,0},{2,3},{3,2},{4,5},{5,4},{6,7},{7,6},{8,9},{9,8},{10,11... | collective-permute-start | bytes 405512 | tf_op jit(solution)/shard_map/ppermute | solution.py:279
  18.5 2.7 %collective-permute-start.4 = (bf16[128,1920]{1,0:T(8,128)(2,1)S(1)}, bf16[128,1920]{1,0:T(8,128)(2,1)S(1)}, u32[]{:S(2)}, u32[]{:S(2)}) collective-permute-start(bf16[128,1920]{1,0:T(8,128)(2,1)S(1)} %get-tuple-element.99), channel_id=1, source_target_pairs={{0,2},{2,0},{4,6},{6,4},{8,10},{10,8},{12,14},{14,12},{16,18},{18,... | collective-permute-start | bytes 1474568 | tf_op jit(solution)/shard_map/ppermute | solution.py:270
  19.7 2.2 %collective-permute-start.5 = (bf16[128,1920]{1,0:T(8,128)(2,1)S(1)}, bf16[128,1920]{1,0:T(8,128)(2,1)S(1)}, u32[]{:S(2)}, u32[]{:S(2)}) collective-permute-start(bf16[128,1920]{1,0:T(8,128)(2,1)S(1)} %get-tuple-element.100), channel_id=1, source_target_pairs={{0,2},{2,0},{4,6},{6,4},{8,10},{10,8},{12,14},{14,12},{16,18},{18,... | collective-permute-start | bytes 1474568 | tf_op jit(solution)/shard_map/ppermute | solution.py:270
  19.8 13.2 %collective-permute-start.7 = (bf16[256,1920]{1,0:T(8,128)(2,1)S(1)}, bf16[256,1920]{1,0:T(8,128)(2,1)S(1)}, u32[]{:S(2)}, u32[]{:S(2)}) collective-permute-start(bf16[256,1920]{1,0:T(8,128)(2,1)S(1)} %collective-permute-done.1.refs_0_), channel_id=1, source_target_pairs={{0,8},{2,6},{4,0},{6,14},{8,16},{10,2},{12,4},{14,22},{16,24},{18,... | collective-permute-start | bytes 2949128 | tf_op jit(solution)/shard_map/ppermute | solution.py:276
  23.8 12.8 %copy-start.11 = (bf16[512,128]{1,0:T(8,128)(2,1)}, bf16[512,128]{1,0:T(8,128)(2,1)S(1)}, u32[]{:S(2)}) copy-start(bf16[512,128]{1,0:T(8,128)(2,1)S(1)} %get-tuple-element.54.table_ref) | copy-start | bytes 393220
  23.8 7.8 %collective-permute-start.6 = (bf16[264,512]{1,0:T(8,128)(2,1)S(1)}, bf16[264,512]{1,0:T(8,128)(2,1)S(1)}, u32[]{:S(2)}, u32[]{:S(2)}) collective-permute-start(bf16[264,512]{1,0:T(8,128)(2,1)S(1)} %get-tuple-element.56), channel_id=1, source_target_pairs={{0,1},{1,0},{2,3},{3,2},{4,5},{5,4},{6,7},{7,6},{8,9},{9,8},{10,11... | collective-permute-start | bytes 811016 | tf_op jit(solution)/shard_map/ppermute | solution.py:279
  33.1 2.8 %collective-permute-start.8 = (bf16[128,1920]{1,0:T(8,128)(2,1)S(1)}, bf16[128,1920]{1,0:T(8,128)(2,1)S(1)}, u32[]{:S(2)}, u32[]{:S(2)}) collective-permute-start(bf16[128,1920]{1,0:T(8,128)(2,1)S(1)} %get-tuple-element.97), channel_id=1, source_target_pairs={{0,2},{2,0},{4,6},{6,4},{8,10},{10,8},{12,14},{14,12},{16,18},{18,... | collective-permute-start | bytes 1474568 | tf_op jit(solution)/shard_map/ppermute | solution.py:270
  34.4 2.2 %collective-permute-start.9 = (bf16[128,1920]{1,0:T(8,128)(2,1)S(1)}, bf16[128,1920]{1,0:T(8,128)(2,1)S(1)}, u32[]{:S(2)}, u32[]{:S(2)}) collective-permute-start(bf16[128,1920]{1,0:T(8,128)(2,1)S(1)} %get-tuple-element.98), channel_id=1, source_target_pairs={{0,2},{2,0},{4,6},{6,4},{8,10},{10,8},{12,14},{14,12},{16,18},{18,... | collective-permute-start | bytes 1474568 | tf_op jit(solution)/shard_map/ppermute | solution.py:270
  34.5 13.4 %collective-permute-start.11 = (bf16[256,1920]{1,0:T(8,128)(2,1)S(1)}, bf16[256,1920]{1,0:T(8,128)(2,1)S(1)}, u32[]{:S(2)}, u32[]{:S(2)}) collective-permute-start(bf16[256,1920]{1,0:T(8,128)(2,1)S(1)} %collective-permute-done.7.refs_0_), channel_id=1, source_target_pairs={{0,8},{2,6},{4,0},{6,14},{8,16},{10,2},{12,4},{14,22},{16,24},{18,... | collective-permute-start | bytes 2949128 | tf_op jit(solution)/shard_map/ppermute | solution.py:276
  39.9 8.0 %collective-permute-start.10 = (bf16[264,512]{1,0:T(8,128)(2,1)}, bf16[264,512]{1,0:T(8,128)(2,1)}, u32[]{:S(2)}, u32[]{:S(2)}) collective-permute-start(bf16[264,512]{1,0:T(8,128)(2,1)} %get-tuple-element.59), channel_id=1, source_target_pairs={{0,1},{1,0},{2,3},{3,2},{4,5},{5,4},{6,7},{7,6},{8,9},{9,8},{10,11... | collective-permute-start | bytes 811016 | tf_op jit(solution)/shard_map/ppermute | solution.py:279
  48.0 2.8 %collective-permute-start.12 = (bf16[128,1920]{1,0:T(8,128)(2,1)S(1)}, bf16[128,1920]{1,0:T(8,128)(2,1)S(1)}, u32[]{:S(2)}, u32[]{:S(2)}) collective-permute-start(bf16[128,1920]{1,0:T(8,128)(2,1)S(1)} %get-tuple-element.95), channel_id=1, source_target_pairs={{0,2},{2,0},{4,6},{6,4},{8,10},{10,8},{12,14},{14,12},{16,18},{18,... | collective-permute-start | bytes 1474568 | tf_op jit(solution)/shard_map/ppermute | solution.py:270
  49.3 2.2 %collective-permute-start.13 = (bf16[128,1920]{1,0:T(8,128)(2,1)S(1)}, bf16[128,1920]{1,0:T(8,128)(2,1)S(1)}, u32[]{:S(2)}, u32[]{:S(2)}) collective-permute-start(bf16[128,1920]{1,0:T(8,128)(2,1)S(1)} %get-tuple-element.96), channel_id=1, source_target_pairs={{0,2},{2,0},{4,6},{6,4},{8,10},{10,8},{12,14},{14,12},{16,18},{18,... | collective-permute-start | bytes 1474568 | tf_op jit(solution)/shard_map/ppermute | solution.py:270
  49.5 8.4 %collective-permute-start.15 = (bf16[256,1024]{1,0:T(8,128)(2,1)S(1)}, bf16[256,1024]{1,0:T(8,128)(2,1)S(1)}, u32[]{:S(2)}, u32[]{:S(2)}) collective-permute-start(bf16[256,1024]{1,0:T(8,128)(2,1)S(1)} %pad_maximum_fusion.4), channel_id=1, source_target_pairs={{0,8},{2,6},{4,0},{6,14},{8,16},{10,2},{12,4},{14,22},{16,24},{18,... | collective-permute-start | bytes 1572872 | tf_op jit(solution)/shard_map/ppermute | solution.py:276
  53.4 7.8 %collective-permute-start.14 = (bf16[264,512]{1,0:T(8,128)(2,1)S(1)}, bf16[264,512]{1,0:T(8,128)(2,1)S(1)}, u32[]{:S(2)}, u32[]{:S(2)}) collective-permute-start(bf16[264,512]{1,0:T(8,128)(2,1)S(1)} %get-tuple-element.62), channel_id=1, source_target_pairs={{0,1},{1,0},{2,3},{3,2},{4,5},{5,4},{6,7},{7,6},{8,9},{9,8},{10,11... | collective-permute-start | bytes 811016 | tf_op jit(solution)/shard_map/ppermute | solution.py:279
  57.9 2.3 %collective-permute-start.16 = (bf16[64,1024]{1,0:T(8,128)(2,1)S(1)}, bf16[64,1024]{1,0:T(8,128)(2,1)S(1)}, u32[]{:S(2)}, u32[]{:S(2)}) collective-permute-start(bf16[64,1024]{1,0:T(8,128)(2,1)S(1)} %get-tuple-element.107), channel_id=1, source_target_pairs={{0,2},{2,0},{4,6},{6,4},{8,10},{10,8},{12,14},{14,12},{16,18},{18,... | collective-permute-start | bytes 393224 | tf_op jit(solution)/shard_map/ppermute | solution.py:270
  59.2 1.3 %collective-permute-start.19 = (bf16[64,1024]{1,0:T(8,128)(2,1)S(1)}, bf16[64,1024]{1,0:T(8,128)(2,1)S(1)}, u32[]{:S(2)}, u32[]{:S(2)}) collective-permute-start(bf16[64,1024]{1,0:T(8,128)(2,1)S(1)} %get-tuple-element.108), channel_id=1, source_target_pairs={{0,2},{2,0},{4,6},{6,4},{8,10},{10,8},{12,14},{14,12},{16,18},{18,... | collective-permute-start | bytes 393224 | tf_op jit(solution)/shard_map/ppermute | solution.py:270
  59.3 1.5 %collective-permute-start.18 = (bf16[64,1024]{1,0:T(8,128)(2,1)S(1)}, bf16[64,1024]{1,0:T(8,128)(2,1)S(1)}, u32[]{:S(2)}, u32[]{:S(2)}) collective-permute-start(bf16[64,1024]{1,0:T(8,128)(2,1)S(1)} %get-tuple-element.109), channel_id=1, source_target_pairs={{0,2},{2,0},{4,6},{6,4},{8,10},{10,8},{12,14},{14,12},{16,18},{18,... | collective-permute-start | bytes 393224 | tf_op jit(solution)/shard_map/ppermute | solution.py:270
  59.8 1.3 %collective-permute-start.17 = (bf16[64,1024]{1,0:T(8,128)(2,1)S(1)}, bf16[64,1024]{1,0:T(8,128)(2,1)S(1)}, u32[]{:S(2)}, u32[]{:S(2)}) collective-permute-start(bf16[64,1024]{1,0:T(8,128)(2,1)S(1)} %get-tuple-element.110), channel_id=1, source_target_pairs={{0,2},{2,0},{4,6},{6,4},{8,10},{10,8},{12,14},{14,12},{16,18},{18,... | collective-permute-start | bytes 393224 | tf_op jit(solution)/shard_map/ppermute | solution.py:270
  61.3 9.9 %copy-start.2 = (bf16[1,1792,1024]{2,1,0:T(8,128)(2,1)S(1)}, bf16[1,1792,1024]{2,1,0:T(8,128)(2,1)}, u32[]{:S(2)}) copy-start(bf16[1,1792,1024]{2,1,0:T(8,128)(2,1)} %param.11) | copy-start | bytes 11010052
  61.3 9.9 %copy-start.6 = (bf16[132,512]{1,0:T(8,128)(2,1)S(1)}, bf16[132,512]{1,0:T(8,128)(2,1)}, u32[]{:S(2)}) copy-start(bf16[132,512]{1,0:T(8,128)(2,1)} %copy-done.5) | copy-start | bytes 405508
  63.0 7.0 %collective-permute-start.20 = (bf16[132,1024]{1,0:T(8,128)(2,1)S(1)}, bf16[132,1024]{1,0:T(8,128)(2,1)S(1)}, u32[]{:S(2)}, u32[]{:S(2)}) collective-permute-start(bf16[132,1024]{1,0:T(8,128)(2,1)S(1)} %get-tuple-element.66.refs_0_), channel_id=1, source_target_pairs={{0,1},{1,0},{2,3},{3,2},{4,5},{5,4},{6,7},{7,6},{8,9},{9,8},{10,11... | collective-permute-start | bytes 811016 | tf_op jit(solution)/shard_map/ppermute | solution.py:279
  70.0 9.3 %collective-permute-start.21 = (bf16[264,512]{1,0:T(8,128)(2,1)S(1)}, bf16[264,512]{1,0:T(8,128)(2,1)S(1)}, u32[]{:S(2)}, u32[]{:S(2)}) collective-permute-start(bf16[264,512]{1,0:T(8,128)(2,1)S(1)} %multiply_convert_fusion.2.refs_0_), channel_id=1, source_target_pairs={{0,1},{1,0},{2,3},{3,2},{4,5},{5,4},{6,7},{7,6},{8,9},{9,8},{10,11... | collective-permute-start | bytes 811016 | tf_op jit(solution)/shard_map/ppermute | solution.py:279
  73.4 3.4 %collective-permute-start.25 = (bf16[64,896]{1,0:T(8,128)(2,1)S(1)}, bf16[64,896]{1,0:T(8,128)(2,1)S(1)}, u32[]{:S(2)}, u32[]{:S(2)}) collective-permute-start(bf16[64,896]{1,0:T(8,128)(2,1)S(1)} %get-tuple-element.113), channel_id=1, source_target_pairs={{0,2},{2,0},{4,6},{6,4},{8,10},{10,8},{12,14},{14,12},{16,18},{18,... | collective-permute-start | bytes 344072 | tf_op jit(solution)/shard_map/ppermute | solution.py:270
  75.8 1.3 %collective-permute-start.24 = (bf16[64,896]{1,0:T(8,128)(2,1)S(1)}, bf16[64,896]{1,0:T(8,128)(2,1)S(1)}, u32[]{:S(2)}, u32[]{:S(2)}) collective-permute-start(bf16[64,896]{1,0:T(8,128)(2,1)S(1)} %get-tuple-element.114), channel_id=1, source_target_pairs={{0,2},{2,0},{4,6},{6,4},{8,10},{10,8},{12,14},{14,12},{16,18},{18,... | collective-permute-start | bytes 344072 | tf_op jit(solution)/shard_map/ppermute | solution.py:270
  75.9 1.4 %collective-permute-start.23 = (bf16[64,896]{1,0:T(8,128)(2,1)S(1)}, bf16[64,896]{1,0:T(8,128)(2,1)S(1)}, u32[]{:S(2)}, u32[]{:S(2)}) collective-permute-start(bf16[64,896]{1,0:T(8,128)(2,1)S(1)} %get-tuple-element.115), channel_id=1, source_target_pairs={{0,2},{2,0},{4,6},{6,4},{8,10},{10,8},{12,14},{14,12},{16,18},{18,... | collective-permute-start | bytes 344072 | tf_op jit(solution)/shard_map/ppermute | solution.py:270
  76.4 1.3 %collective-permute-start.22 = (bf16[64,896]{1,0:T(8,128)(2,1)S(1)}, bf16[64,896]{1,0:T(8,128)(2,1)S(1)}, u32[]{:S(2)}, u32[]{:S(2)}) collective-permute-start(bf16[64,896]{1,0:T(8,128)(2,1)S(1)} %get-tuple-element.116), channel_id=1, source_target_pairs={{0,2},{2,0},{4,6},{6,4},{8,10},{10,8},{12,14},{14,12},{16,18},{18,... | collective-permute-start | bytes 344072 | tf_op jit(solution)/shard_map/ppermute | solution.py:270
  77.8 7.9 %collective-permute-start.28 = (bf16[256,896]{1,0:T(8,128)(2,1)S(1)}, bf16[256,896]{1,0:T(8,128)(2,1)S(1)}, u32[]{:S(2)}, u32[]{:S(2)}) collective-permute-start(bf16[256,896]{1,0:T(8,128)(2,1)S(1)} %shard_map.72), channel_id=1, source_target_pairs={{0,8},{2,6},{4,0},{6,14},{8,16},{10,2},{12,4},{14,22},{16,24},{18,... | collective-permute-start | bytes 1376264 | tf_op jit(solution)/shard_map/ppermute | solution.py:276
  81.3 4.4 %collective-permute-start.38 = (bf16[128,1792]{1,0:T(8,128)(2,1)S(1)}, bf16[128,1792]{1,0:T(8,128)(2,1)S(1)}, u32[]{:S(2)}, u32[]{:S(2)}) collective-permute-start(bf16[128,1792]{1,0:T(8,128)(2,1)S(1)} %get-tuple-element.101), channel_id=1, source_target_pairs={{0,2},{2,0},{4,6},{6,4},{8,10},{10,8},{12,14},{14,12},{16,18},{18,... | collective-permute-start | bytes 1376264 | tf_op jit(solution)/shard_map/ppermute | solution.py:270
  81.4 5.9 %collective-permute-start.27 = (bf16[128,1792]{1,0:T(8,128)(2,1)S(1)}, bf16[128,1792]{1,0:T(8,128)(2,1)S(1)}, u32[]{:S(2)}, u32[]{:S(2)}) collective-permute-start(bf16[128,1792]{1,0:T(8,128)(2,1)S(1)} %get-tuple-element.102), channel_id=1, source_target_pairs={{0,2},{2,0},{4,6},{6,4},{8,10},{10,8},{12,14},{14,12},{16,18},{18,... | collective-permute-start | bytes 1376264 | tf_op jit(solution)/shard_map/ppermute | solution.py:270
  82.9 8.1 %collective-permute-start.26 = (bf16[264,512]{1,0:T(8,128)(2,1)S(1)}, bf16[264,512]{1,0:T(8,128)(2,1)S(1)}, u32[]{:S(2)}, u32[]{:S(2)}) collective-permute-start(bf16[264,512]{1,0:T(8,128)(2,1)S(1)} %multiply_convert_fusion.1.refs_0_), channel_id=1, source_target_pairs={{0,1},{1,0},{2,3},{3,2},{4,5},{5,4},{6,7},{7,6},{8,9},{9,8},{10,11... | collective-permute-start | bytes 811016 | tf_op jit(solution)/shard_map/ppermute | solution.py:279
  85.9 8.6 %collective-permute-start.39 = (bf16[128,1792]{1,0:T(8,128)(2,1)S(1)}, bf16[128,1792]{1,0:T(8,128)(2,1)S(1)}, u32[]{:S(2)}, u32[]{:S(2)}) collective-permute-start(bf16[128,1792]{1,0:T(8,128)(2,1)S(1)} %shard_map.80), channel_id=1, source_target_pairs={{0,8},{2,6},{4,0},{6,14},{8,16},{10,2},{12,4},{14,22},{16,24},{18,... | collective-permute-start | bytes 1376264 | tf_op jit(solution)/shard_map/ppermute | solution.py:276
  87.4 11.1 %collective-permute-start.31 = (bf16[128,1792]{1,0:T(8,128)(2,1)S(1)}, bf16[128,1792]{1,0:T(8,128)(2,1)S(1)}, u32[]{:S(2)}, u32[]{:S(2)}) collective-permute-start(bf16[128,1792]{1,0:T(8,128)(2,1)S(1)} %shard_map.74), channel_id=1, source_target_pairs={{0,8},{2,6},{4,0},{6,14},{8,16},{10,2},{12,4},{14,22},{16,24},{18,... | collective-permute-start | bytes 1376264 | tf_op jit(solution)/shard_map/ppermute | solution.py:276
  93.0 2.4 %collective-permute-start.37 = (bf16[128,1792]{1,0:T(8,128)(2,1)S(1)}, bf16[128,1792]{1,0:T(8,128)(2,1)S(1)}, u32[]{:S(2)}, u32[]{:S(2)}) collective-permute-start(bf16[128,1792]{1,0:T(8,128)(2,1)S(1)} %get-tuple-element.103), channel_id=1, source_target_pairs={{0,2},{2,0},{4,6},{6,4},{8,10},{10,8},{12,14},{14,12},{16,18},{18,... | collective-permute-start | bytes 1376264 | tf_op jit(solution)/shard_map/ppermute | solution.py:270
  93.9 4.6 %collective-permute-start.30 = (bf16[128,1792]{1,0:T(8,128)(2,1)S(1)}, bf16[128,1792]{1,0:T(8,128)(2,1)S(1)}, u32[]{:S(2)}, u32[]{:S(2)}) collective-permute-start(bf16[128,1792]{1,0:T(8,128)(2,1)S(1)} %get-tuple-element.104), channel_id=1, source_target_pairs={{0,2},{2,0},{4,6},{6,4},{8,10},{10,8},{12,14},{14,12},{16,18},{18,... | collective-permute-start | bytes 1376264 | tf_op jit(solution)/shard_map/ppermute | solution.py:270
  94.1 7.4 %collective-permute-start.29 = (bf16[264,512]{1,0:T(8,128)(2,1)S(1)}, bf16[264,512]{1,0:T(8,128)(2,1)S(1)}, u32[]{:S(2)}, u32[]{:S(2)}) collective-permute-start(bf16[264,512]{1,0:T(8,128)(2,1)S(1)} %multiply_convert_fusion.refs_0_), channel_id=1, source_target_pairs={{0,1},{1,0},{2,3},{3,2},{4,5},{5,4},{6,7},{7,6},{8,9},{9,8},{10,11... | collective-permute-start | bytes 811016 | tf_op jit(solution)/shard_map/ppermute | solution.py:279
  95.5 10.9 %collective-permute-start.40 = (bf16[128,1792]{1,0:T(8,128)(2,1)S(1)}, bf16[128,1792]{1,0:T(8,128)(2,1)S(1)}, u32[]{:S(2)}, u32[]{:S(2)}) collective-permute-start(bf16[128,1792]{1,0:T(8,128)(2,1)S(1)} %shard_map.81), channel_id=1, source_target_pairs={{0,8},{2,6},{4,0},{6,14},{8,16},{10,2},{12,4},{14,22},{16,24},{18,... | collective-permute-start | bytes 1376264 | tf_op jit(solution)/shard_map/ppermute | solution.py:276
  103.4 3.1 %collective-permute-start.36 = (bf16[128,1792]{1,0:T(8,128)(2,1)S(1)}, bf16[128,1792]{1,0:T(8,128)(2,1)S(1)}, u32[]{:S(2)}, u32[]{:S(2)}) collective-permute-start(bf16[128,1792]{1,0:T(8,128)(2,1)S(1)} %get-tuple-element.105), channel_id=1, source_target_pairs={{0,2},{2,0},{4,6},{6,4},{8,10},{10,8},{12,14},{14,12},{16,18},{18,... | collective-permute-start | bytes 1376264 | tf_op jit(solution)/shard_map/ppermute | solution.py:270
  105.1 7.6 %collective-permute-start.33 = (bf16[128,1792]{1,0:T(8,128)(2,1)S(1)}, bf16[128,1792]{1,0:T(8,128)(2,1)S(1)}, u32[]{:S(2)}, u32[]{:S(2)}) collective-permute-start(bf16[128,1792]{1,0:T(8,128)(2,1)S(1)} %shard_map.76), channel_id=1, source_target_pairs={{0,8},{2,6},{4,0},{6,14},{8,16},{10,2},{12,4},{14,22},{16,24},{18,... | collective-permute-start | bytes 1376264 | tf_op jit(solution)/shard_map/ppermute | solution.py:276
  106.4 6.3 %collective-permute-start.32 = (bf16[128,1792]{1,0:T(8,128)(2,1)S(1)}, bf16[128,1792]{1,0:T(8,128)(2,1)S(1)}, u32[]{:S(2)}, u32[]{:S(2)}) collective-permute-start(bf16[128,1792]{1,0:T(8,128)(2,1)S(1)} %get-tuple-element.106), channel_id=1, source_target_pairs={{0,2},{2,0},{4,6},{6,4},{8,10},{10,8},{12,14},{14,12},{16,18},{18,... | collective-permute-start | bytes 1376264 | tf_op jit(solution)/shard_map/ppermute | solution.py:270
  106.7 10.9 %collective-permute-start.41 = (bf16[128,1792]{1,0:T(8,128)(2,1)S(1)}, bf16[128,1792]{1,0:T(8,128)(2,1)S(1)}, u32[]{:S(2)}, u32[]{:S(2)}) collective-permute-start(bf16[128,1792]{1,0:T(8,128)(2,1)S(1)} %shard_map.82), channel_id=1, source_target_pairs={{0,8},{2,6},{4,0},{6,14},{8,16},{10,2},{12,4},{14,22},{16,24},{18,... | collective-permute-start | bytes 1376264 | tf_op jit(solution)/shard_map/ppermute | solution.py:276
  108.1 6.1 %collective-permute-start.35 = (bf16[132,512]{1,0:T(8,128)(2,1)S(1)}, bf16[132,512]{1,0:T(8,128)(2,1)S(1)}, u32[]{:S(2)}, u32[]{:S(2)}) collective-permute-start(bf16[132,512]{1,0:T(8,128)(2,1)S(1)} %multiply_convert_fusion.3.refs_0_), channel_id=1, source_target_pairs={{0,1},{1,0},{2,3},{3,2},{4,5},{5,4},{6,7},{7,6},{8,9},{9,8},{10,11... | collective-permute-start | bytes 405512 | tf_op jit(solution)/shard_map/ppermute | solution.py:279
  112.9 9.7 %collective-permute-start.34 = (bf16[128,1792]{1,0:T(8,128)(2,1)S(1)}, bf16[128,1792]{1,0:T(8,128)(2,1)S(1)}, u32[]{:S(2)}, u32[]{:S(2)}) collective-permute-start(bf16[128,1792]{1,0:T(8,128)(2,1)S(1)} %shard_map.78), channel_id=1, source_target_pairs={{0,8},{2,6},{4,0},{6,14},{8,16},{10,2},{12,4},{14,22},{16,24},{18,... | collective-permute-start | bytes 1376264 | tf_op jit(solution)/shard_map/ppermute | solution.py:276
  117.7 4.8 %collective-permute-start.42 = (bf16[128,1792]{1,0:T(8,128)(2,1)S(1)}, bf16[128,1792]{1,0:T(8,128)(2,1)S(1)}, u32[]{:S(2)}, u32[]{:S(2)}) collective-permute-start(bf16[128,1792]{1,0:T(8,128)(2,1)S(1)} %add_convert_fusion.1), channel_id=1, source_target_pairs={{0,2},{2,0},{4,6},{6,4},{8,10},{10,8},{12,14},{14,12},{16,18},{18,... | collective-permute-start | bytes 1376264 | tf_op jit(solution)/shard_map/ppermute | solution.py:270
  (16 other events, 48.7 us)

commit v4 on v3

--- a/solution.py
+++ b/solution.py
@@ -10,7 +10,6 @@
 BF16 = jnp.bfloat16
 F32 = jnp.float32
 VMEM = pl.BlockSpec(memory_space=pltpu.VMEM)
-HBM = pl.BlockSpec(memory_space=pltpu.HBM)
 TABLE = 128
 LIMIT = pltpu.CompilerParams(vmem_limit_bytes=16 * 1024 * 1024)
 
@@ -19,18 +18,8 @@
     return lax.dot_general(a, b, (((1,), (1,)), ((), ())), preferred_element_type=F32)
 
 
-def prepare_kernel(rows_hbm, routes_hbm, gates_hbm, block_ref, routes_ref, gates_ref, sems):
-    token_n, feat_n = rows_hbm.shape
-    copies = [
-        pltpu.make_async_copy(routes_hbm, routes_ref, sems.at[0]),
-        pltpu.make_async_copy(gates_hbm, gates_ref, sems.at[1]),
-        pltpu.make_async_copy(rows_hbm, block_ref.at[:, pl.ds(0, feat_n)], sems.at[2]),
-    ]
-    for copy in copies:
-        copy.start()
-    copies[0].wait()
-    copies[1].wait()
-    choose_n = routes_ref.shape[0]
+def table_kernel(routes_ref, gates_ref, table_ref):
+    choose_n, token_n = routes_ref.shape
     expert_n = lax.axis_size("ep")
     expert = lax.broadcasted_iota(jnp.int32, (expert_n, token_n), 0)
     chosen = jnp.zeros((expert_n, token_n), F32)
@@ -47,8 +36,7 @@
     high = weight.astype(BF16).astype(F32)
     parts = [slot, high, weight - high]
     rest = jnp.zeros((TABLE - len(parts) * expert_n, token_n), F32)
-    block_ref[:, feat_n:] = jnp.transpose(jnp.concatenate(parts + [rest], axis=0)).astype(BF16)
-    copies[2].wait()
+    table_ref[...] = jnp.transpose(jnp.concatenate(parts + [rest], axis=0)).astype(BF16)
 
 
 class Ring:
@@ -262,12 +250,20 @@
     unit_n = gate_act.shape[2]
     ring = Ring(experts_n, slot_n, token_n)
     far, pieces = ring.far, ring.pieces
+    split = 7 * token_n // 8
+    streams = ((0, split), (split, 2 * token_n))
     swap = [(i, i ^ 1) for i in range(experts_n)]
     ring_pairs = ring.pairs()
     core = lax.axis_index("ep") % 2
 
     def parts_to_core(x, rows):
         return [lax.ppermute(p, "ep", swap) for p in jnp.split(x, x.shape[0] // rows)]
+
+    def streams_to_core(x, *parts):
+        return [
+            [to_core(x[i:j], j - i) for i, j in zip(range(a, b, n), (*range(a + n, b, n), b))]
+            for (a, b), n in zip(streams, parts)
+        ]
 
     def to_core(x, rows=128):
         return jnp.concatenate(parts_to_core(x, rows), axis=0)
@@ -314,25 +310,16 @@
             scratch=[pltpu.VMEM((pieces[k] * slot_n, n), BF16) for n in (2 * unit_n, feat_n)],
         )
 
-    def join(first, width, *args):
-        rows_n = 2 * token_n if width == half else token_n
-        return call(functools.partial(join_kernel, first), [(rows_n, width)], *args)[0]
-
-    own = pl.pallas_call(
-        prepare_kernel,
-        out_shape=jax.ShapeDtypeStruct((token_n, feat_n + TABLE), BF16),
-        in_specs=[HBM] * 3,
-        out_specs=VMEM,
-        scratch_shapes=[
-            pltpu.VMEM(routes.shape[::-1], jnp.int32),
-            pltpu.VMEM(routes.shape[::-1], F32),
-            pltpu.SemaphoreType.DMA((3,)),
-        ],
-        compiler_params=LIMIT,
-    )(grad_out, routes.T, gate_weights.T)
-    sibling = to_core(own)
-    blocks = [[own, sibling]]
-    moving = to_ring(jnp.concatenate(blocks[0], axis=0))
+    def join(rows, width, *args):
+        out = [(rows[1] - rows[0], width)]
+        return call(functools.partial(join_kernel, rows[0]), out, *args)[0]
+
+    sibling = to_core(grad_out)
+    moving = to_ring(jnp.concatenate([grad_out, sibling], axis=0))
+    (table,) = call(table_kernel, [(token_n, TABLE)], routes.T, gate_weights.T)
+    tables = [table, to_core(table)]
+    blocks = [[jnp.concatenate(x, axis=1) for x in zip([grad_out, sibling], tables)]]
+    moving = jnp.concatenate([moving, to_ring(jnp.concatenate(tables, axis=0))], axis=1)
     acts = call(
         functools.partial(act_kernel, ring),
         [(p * slot_n, unit_n) for p in pieces],
@@ -340,17 +327,23 @@
     )
     act_peer = to_side(acts[far])
     partials, mines, ups = [down(0)], {}, {}
-    sents = [to_side(partials[0][1])]
+    sents = [None]
     for k in range(1, far + 1):
         ended = [partials[k - 1][0]]
         if k < far:
-            ended += [sents[k - 1]] + ([act_peer] if k == 1 else [])
+            ended += [act_peer if k == 1 else sents[k - 1]]
+        if k == far - 1:
+            ended += [early]
         here = after(moving, *ended)
         if k < far - 1:
             moving = to_ring(here)
         elif k == far - 1:
             part = lax.dynamic_slice_in_dim(here, core * half, half, 1)
             moving = to_ring(jnp.concatenate([part, here[:, feat_n:]], axis=1))
+        if k == far - 2:
+            mines[k - 1] = middle(k - 1, sents[k - 1])
+            early = to_side(mines[k - 1])
+            here = after(here, mines[k - 1])
         blocks.append([here, to_core(here, 64 if k == far else 128)])
         if k == far:
             mines[k - 1] = middle(k - 1, sents[k - 1])
@@ -358,27 +351,37 @@
         partials.append(down(k))
         sents.append(to_side(partials[k][-2]))
 
-    keep, give = up(far, partials[far][0], sents[far], acts[far], act_peer)
-    peer = to_side(after(mines[far - 1], sents[far]))
-    total = join(0, half, keep, *parts_to_core(give, 64))
+    ups[far - 3] = up(far - 3, mines[far - 3], after(early, partials[far][0]))
+    swapped = streams_to_core(ups[far - 3][1], 64, 80)
+    full = after(sents[far], ups[far - 3][0], *swapped[0], *swapped[1])
+    keep, give = up(far, partials[far][0], full, acts[far], act_peer)
+    peer = to_side(after(mines[far - 1], full))
+    total = join((0, 2 * token_n), half, keep, *parts_to_core(give, 64))
     came = to_ring(total)
-    came = [came[:token_n], came[token_n:]]
+    came = [came[a:b] for a, b in streams]
     peer = after(peer, total)
     for k in range(far - 1, 0, -1):
-        keep, give = up(k, mines[k], peer)
-        mines[k - 1] = middle(k - 1, after(sents[k - 1], peer))
-        peer = to_side(mines[k - 1])
-        rows = 128
-        given = parts_to_core(give, rows)
+        keep, give = ups[k] if k in ups else up(k, mines[k], peer)
+        if k == far - 1:
+            mines[k - 1] = middle(k - 1, after(sents[k - 1], peer))
+            peer = to_side(mines[k - 1])
+        elif k == far - 2:
+            mines[0] = middle(0, to_side(after(partials[0][1], peer)))
+            peer = to_side(mines[0])
+        given = swapped if k in ups else streams_to_core(give, split if k == far - 1 else 64, 2 * token_n - split)
+        totals = []
         for i in range(2):
-            parts = given[i * (token_n // rows) : (i + 1) * (token_n // rows)]
-            total = join(i * token_n, feat_n, keep, *parts, came[i])
-            came[i] = to_ring(total)
-        came[0] = after(came[0], total)
-        peer = after(peer, total)
+            totals.append(join(streams[i], feat_n, keep, *given[i], came[i]))
+            came[i] = to_ring(totals[i])
+        came[0] = after(came[0], *totals)
+        peer = after(peer, *totals)
     keep, give = up(0, mines[0], peer)
-    total = to_core((came[0].astype(F32) + keep.astype(F32)).astype(BF16))
-    return (came[1].astype(F32) + give.astype(F32) + total.astype(F32)).astype(BF16)
+    total = [
+        parts_to_core((x.astype(F32) + y.astype(F32)).astype(BF16), x.shape[0])[0]
+        for x, y in ((came[0], keep[:split]), (came[1][: token_n - split], keep[split:]))
+    ]
+    total = jnp.concatenate(total, axis=0).astype(F32)
+    return (came[1][token_n - split :].astype(F32) + give.astype(F32) + total).astype(BF16)
 
 
 def spread_on_device(grad_out, routes, gate_weights, gate_act, w_down, w_up):

time: 125 us -> 123 us (0.984)
  waiting for transfers between devices: 54.7 us -> 51.6 us
  local copies, waits for them, and re-layouts: 5.56 us -> 2.65 us
  other arithmetic: 2.76 us -> 5.09 us
  starting transfers between devices: 37.9 us -> 40.1 us
    ppermute x10, waiting for transfers between devices: 29.4 us -> 19.4 us  [to_side(): return lax.ppermute(x, 'tp', [(0, 1), (1, 0)])]
    ppermute x11 -> x12, waiting for transfers between devices: 18.1 us -> 23 us  [to_ring(): return lax.ppermute(x, 'ep', ring_pairs)]
    unnamed x42 -> x36, local copies, waits for them, and re-layouts: 5.01 us -> 2.09 us
    concatenate x1 -> x5, other arithmetic: 0.07 us -> 2.39 us  [the longest x1 1.23 us: ring_on_device(): moving = to_ring(jnp.concatenate([grad_out, sibling], axis=0))]
    ppermute x22 -> x27, waiting for transfers between devices: 7.26 us -> 9.17 us  [parts_to_core(): lax.ppermute(p, 'ep', swap)]
    ppermute x22 -> x27, starting transfers between devices: 14 us -> 15.8 us  [parts_to_core(): lax.ppermute(p, 'ep', swap)]
    ppermute x10, starting transfers between devices: 9.01 us -> 10.6 us  [to_side(): return lax.ppermute(x, 'tp', [(0, 1), (1, 0)])]
    ppermute x11 -> x12, starting transfers between devices: 14.9 us -> 13.7 us  [to_ring(): return lax.ppermute(x, 'ep', ring_pairs)]
  transfers between devices with their start and end apart: 43 -> 49, of which waited for: 31 -> 29; matrix products, arithmetic and copies ran while one was open for 2% -> 3% of each run, Pallas kernels for 16% -> 17%
where the time goes in v4:
time: 123 us; the launch traced here: 122 us
  waiting for transfers between devices  51.6 us (42%)
  starting transfers between devices  40.1 us (33%)
  Pallas kernels  22.1 us (18%)
  other arithmetic  5.09 us (4%)
  local copies, waits for them, and re-layouts  2.65 us (2%)
    ppermute x12, waiting for transfers between devices, to_ring(): return lax.ppermute(x, 'ep', ring_pairs)  23 us
    pallas_call x19, Pallas kernels, call(): pl.pallas_call(kernel, out_shape=[jax.ShapeDtypeStruct(shape, BF16) for s...  22.1 us
    ppermute x10, waiting for transfers between devices, to_side(): return lax.ppermute(x, 'tp', [(0, 1), (1, 0)])  19.4 us
    ppermute x27, starting transfers between devices, parts_to_core(): lax.ppermute(p, 'ep', swap)  15.8 us
    ppermute x12, starting transfers between devices, to_ring(): return lax.ppermute(x, 'ep', ring_pairs)  13.7 us
    ppermute x10, starting transfers between devices, to_side(): return lax.ppermute(x, 'tp', [(0, 1), (1, 0)])  10.6 us
    ppermute x27, waiting for transfers between devices, parts_to_core(): lax.ppermute(p, 'ep', swap)  9.17 us
  transfers between devices with their start and end apart: 49, of which 29 were waited for; matrix products, arithmetic and copies ran while one was open for 3% of the time, Pallas kernels for 17%

profile of v4, /device:TPU:13, one launch (start us, length us, event | category | flops | bytes accessed | tf_op | source)
XLA Modules:
  0.0 122.1 jit_solution(11702856817407908498)
XLA Ops:
  0.7 1.7 %collective-permute-done = bf16[128,1792]{1,0:T(8,128)(2,1)S(1)} collective-permute-done((bf16[128,1792]{1,0:T(8,128)(2,1)}, bf16[128,1792]{1,0:T(8,128)(2,1)S(1)}, u32[]{:S(2)}, u32[]{:S(2)}) %collective-permute-start) | collective-permute-done | bytes 458784 | tf_op jit(solution)/shard_map/ppermute | solution.py:260
  2.3 1.2 %pad_maximum_fusion.4 = bf16[256,1792]{1,0:T(8,128)(2,1)S(1)} fusion(bf16[128,1792]{1,0:T(8,128)(2,1)S(1)} %collective-permute-done, bf16[128,1792]{1,0:T(8,128)(2,1)} %param.6), kind=kLoop, calls=%fused_computation.4 | loop fusion | flops 1835008 | bytes 1835008 | tf_op jit(solution)/shard_map/concatenate | solution.py:318
  3.6 1.3 %collective-permute-start.1 = (bf16[256,1792]{1,0:T(8,128)(2,1)S(1)}, bf16[256,1792]{1,0:T(8,128)(2,1)S(1)}, u32[]{:S(2)}, u32[]{:S(2)}) collective-permute-start(bf16[256,1792]{1,0:T(8,128)(2,1)S(1)} %pad_maximum_fusion.4), channel_id=1, source_target_pairs={{0,8},{2,6},{4,0},{6,14},{8,16},{10,2},{12,4},{14,22},{16,24},{18,... | collective-permute-start | bytes 2752520 | tf_op jit(solution)/shard_map/ppermute | solution.py:272
  6.6 1.6 %shard_map.66 = (bf16[132,512]{1,0:T(8,128)(2,1)S(1)}, bf16[264,512]{1,0:T(8,128)(2,1)S(1)}, bf16[264,512]{1,0:T(8,128)(2,1)S(1)}, bf16[264,512]{1,0:T(8,128)(2,1)S(1)}, bf16[132,512]{1,0:T(8,128)(2,1)S(1)}) custom-call(bf16[1056,512]{1,0:T(8,128)(2,1)S(1)} %bitcast.15), custom_call_target="tpu_custom_call" | custom-call | tf_op jit(solution)/shard_map/pallas_call | solution.py:278
  8.3 1.3 %collective-permute-start.4 = (bf16[132,512]{1,0:T(8,128)(2,1)S(1)}, bf16[132,512]{1,0:T(8,128)(2,1)S(1)}, u32[]{:S(2)}, u32[]{:S(2)}) collective-permute-start(bf16[132,512]{1,0:T(8,128)(2,1)S(1)} %get-tuple-element.53.refs_2_), channel_id=1, source_target_pairs={{0,1},{1,0},{2,3},{3,2},{4,5},{5,4},{6,7},{7,6},{8,9},{9,8},{10,11... | collective-permute-start | bytes 405512 | tf_op jit(solution)/shard_map/ppermute | solution.py:275
  10.6 1.3 %collective-permute-start.3 = (bf16[256,128]{1,0:T(8,128)(2,1)S(1)}, bf16[256,128]{1,0:T(8,128)(2,1)S(1)}, u32[]{:S(2)}, u32[]{:S(2)}) collective-permute-start(bf16[256,128]{1,0:T(8,128)(2,1)S(1)} %pad_maximum_fusion.9), channel_id=1, source_target_pairs={{0,8},{2,6},{4,0},{6,14},{8,16},{10,2},{12,4},{14,22},{16,24},{18,... | collective-permute-start | bytes 196616 | tf_op jit(solution)/shard_map/ppermute | solution.py:272
  12.0 1.7 %shard_map.65 = (bf16[132,512]{1,0:T(8,128)(2,1)S(1)}, bf16[132,512]{1,0:T(8,128)(2,1)S(1)}, bf16[256,128]{1,0:T(8,128)(2,1)S(1)}) custom-call(bf16[128,1920]{1,0:T(8,128)(2,1)S(1)} %pad_maximum_fusion.7.refs_0_, bf16[128,1920]{1,0:T(8,128)(2,1)S(1)} %pad_maximum_fusion.8.refs_1_, bf16[1024,1792]{1,0:T(8,128)(2,1)S(1)} %bitcast.5), custom_call_target="tpu_custom_call" | custom-call | tf_op jit(solution)/shard_map/pallas_call | solution.py:278
  13.8 3.1 %collective-permute-done.3 = bf16[256,128]{1,0:T(8,128)(2,1)S(1)} collective-permute-done((bf16[256,128]{1,0:T(8,128)(2,1)S(1)}, bf16[256,128]{1,0:T(8,128)(2,1)S(1)}, u32[]{:S(2)}, u32[]{:S(2)}) %collective-permute-start.3) | collective-permute-done | bytes 65568 | tf_op jit(solution)/shard_map/ppermute | solution.py:272
  17.1 1.3 %collective-permute-start.5 = (bf16[128,1920]{1,0:T(8,128)(2,1)S(1)}, bf16[128,1920]{1,0:T(8,128)(2,1)S(1)}, u32[]{:S(2)}, u32[]{:S(2)}) collective-permute-start(bf16[128,1920]{1,0:T(8,128)(2,1)S(1)} %get-tuple-element.103), channel_id=1, source_target_pairs={{0,2},{2,0},{4,6},{6,4},{8,10},{10,8},{12,14},{14,12},{16,18},{18,... | collective-permute-start | bytes 1474568 | tf_op jit(solution)/shard_map/ppermute | solution.py:260
  18.4 1.3 %collective-permute-start.9 = (bf16[256,1920]{1,0:T(8,128)(2,1)S(1)}, bf16[256,1920]{1,0:T(8,128)(2,1)S(1)}, u32[]{:S(2)}, u32[]{:S(2)}) collective-permute-start(bf16[256,1920]{1,0:T(8,128)(2,1)S(1)} %pad_maximum_fusion.refs_0_), channel_id=1, source_target_pairs={{0,8},{2,6},{4,0},{6,14},{8,16},{10,2},{12,4},{14,22},{16,24},{18,... | collective-permute-start | bytes 2949128 | tf_op jit(solution)/shard_map/ppermute | solution.py:272
  20.6 1.9 %shard_map.67 = (bf16[264,512]{1,0:T(8,128)(2,1)S(1)}, bf16[264,512]{1,0:T(8,128)(2,1)S(1)}, bf16[512,128]{1,0:T(8,128)(2,1)S(1)}) custom-call(bf16[256,1920]{1,0:T(8,128)(2,1)S(1)} %pad_maximum_fusion.refs_0_, bf16[256,1920]{1,0:T(8,128)(2,1)S(1)} %pad_maximum_fusion.1.refs_1_, bf16[1024,1792]{1,0:T(8,128)(2,1)S(1)} %bitcast.6), custom_call_target="tpu_custom_call" | custom-call | tf_op jit(solution)/shard_map/pallas_call | solution.py:278
  22.5 1.3 %collective-permute-start.7 = (bf16[264,512]{1,0:T(8,128)(2,1)S(1)}, bf16[264,512]{1,0:T(8,128)(2,1)S(1)}, u32[]{:S(2)}, u32[]{:S(2)}) collective-permute-start(bf16[264,512]{1,0:T(8,128)(2,1)S(1)} %get-tuple-element.57), channel_id=1, source_target_pairs={{0,1},{1,0},{2,3},{3,2},{4,5},{5,4},{6,7},{7,6},{8,9},{9,8},{10,11... | collective-permute-start | bytes 811016 | tf_op jit(solution)/shard_map/ppermute | solution.py:275
  23.8 6.5 %collective-permute-done.7 = bf16[264,512]{1,0:T(8,128)(2,1)S(1)} collective-permute-done((bf16[264,512]{1,0:T(8,128)(2,1)S(1)}, bf16[264,512]{1,0:T(8,128)(2,1)S(1)}, u32[]{:S(2)}, u32[]{:S(2)}) %collective-permute-start.7) | collective-permute-done | bytes 270368 | tf_op jit(solution)/shard_map/ppermute | solution.py:275
  30.4 1.3 %collective-permute-done.9.refs_0_ = bf16[256,1920]{1,0:T(8,128)(2,1)S(1)} collective-permute-done((bf16[256,1920]{1,0:T(8,128)(2,1)S(1)}, bf16[256,1920]{1,0:T(8,128)(2,1)S(1)}, u32[]{:S(2)}, u32[]{:S(2)}) %collective-permute-start.9) | collective-permute-done | bytes 983072 | tf_op jit(solution)/shard_map/ppermute | solution.py:272
  31.8 1.4 %collective-permute-start.11 = (bf16[128,1920]{1,0:T(8,128)(2,1)S(1)}, bf16[128,1920]{1,0:T(8,128)(2,1)S(1)}, u32[]{:S(2)}, u32[]{:S(2)}) collective-permute-start(bf16[128,1920]{1,0:T(8,128)(2,1)S(1)} %get-tuple-element.101), channel_id=1, source_target_pairs={{0,2},{2,0},{4,6},{6,4},{8,10},{10,8},{12,14},{14,12},{16,18},{18,... | collective-permute-start | bytes 1474568 | tf_op jit(solution)/shard_map/ppermute | solution.py:260
  33.2 1.3 %collective-permute-start.10 = (bf16[256,1920]{1,0:T(8,128)(2,1)S(1)}, bf16[256,1920]{1,0:T(8,128)(2,1)S(1)}, u32[]{:S(2)}, u32[]{:S(2)}) collective-permute-start(bf16[256,1920]{1,0:T(8,128)(2,1)S(1)} %collective-permute-done.9.refs_0_), channel_id=1, source_target_pairs={{0,8},{2,6},{4,0},{6,14},{8,16},{10,2},{12,4},{14,22},{16,24},{18,... | collective-permute-start | bytes 2949128 | tf_op jit(solution)/shard_map/ppermute | solution.py:272
  35.8 2.6 %shard_map.68 = (bf16[264,512]{1,0:T(8,128)(2,1)S(1)}, bf16[264,512]{1,0:T(8,128)(2,1)}, bf16[512,128]{1,0:T(8,128)(2,1)S(1)}) custom-call(bf16[256,1920]{1,0:T(8,128)(2,1)S(1)} %collective-permute-done.9.refs_0_, bf16[256,1920]{1,0:T(8,128)(2,1)S(1)} %pad_maximum_fusion.2.refs_1_, bf16[1024,1792]{1,0:T(8,128)(2,1)S(1)} %bitcast.7), custom_call_target="tpu_custom_call" | custom-call | tf_op jit(solution)/shard_map/pallas_call | solution.py:278
  39.8 3.1 %collective-permute-done.8.refs_1_ = bf16[264,512]{1,0:T(8,128)(2,1)S(1)} collective-permute-done((bf16[264,512]{1,0:T(8,128)(2,1)S(1)}, bf16[264,512]{1,0:T(8,128)(2,1)S(1)}, u32[]{:S(2)}, u32[]{:S(2)}) %collective-permute-start.8) | collective-permute-done | bytes 270368 | tf_op jit(solution)/shard_map/ppermute | solution.py:275
  42.9 5.9 %collective-permute-done.13 = bf16[264,512]{1,0:T(8,128)(2,1)} collective-permute-done((bf16[264,512]{1,0:T(8,128)(2,1)}, bf16[264,512]{1,0:T(8,128)(2,1)}, u32[]{:S(2)}, u32[]{:S(2)}) %collective-permute-start.13) | collective-permute-done | bytes 270368 | tf_op jit(solution)/shard_map/ppermute | solution.py:275
  49.6 1.5 %collective-permute-start.14 = (bf16[256,1024]{1,0:T(8,128)(2,1)S(1)}, bf16[256,1024]{1,0:T(8,128)(2,1)S(1)}, u32[]{:S(2)}, u32[]{:S(2)}) collective-permute-start(bf16[256,1024]{1,0:T(8,128)(2,1)S(1)} %pad_maximum_fusion.5), channel_id=1, source_target_pairs={{0,8},{2,6},{4,0},{6,14},{8,16},{10,2},{12,4},{14,22},{16,24},{18,... | collective-permute-start | bytes 1572872 | tf_op jit(solution)/shard_map/ppermute | solution.py:272
  51.7 1.9 %shard_map.69 = (bf16[264,512]{1,0:T(8,128)(2,1)S(1)}, bf16[264,512]{1,0:T(8,128)(2,1)S(1)}, bf16[512,128]{1,0:T(8,128)(2,1)S(1)}) custom-call(bf16[256,1920]{1,0:T(8,128)(2,1)S(1)} %collective-permute-done.10.refs_0_, bf16[256,1920]{1,0:T(8,128)(2,1)S(1)} %pad_maximum_fusion.3.refs_1_, bf16[1024,1792]{1,0:T(8,128)(2,1)S(1)} %bitcast.8), custom_call_target="tpu_custom_call" | custom-call | tf_op jit(solution)/shard_map/pallas_call | solution.py:278
  53.6 1.3 %collective-permute-start.21 = (bf16[264,512]{1,0:T(8,128)(2,1)S(1)}, bf16[264,512]{1,0:T(8,128)(2,1)S(1)}, u32[]{:S(2)}, u32[]{:S(2)}) collective-permute-start(bf16[264,512]{1,0:T(8,128)(2,1)S(1)} %get-tuple-element.66), channel_id=1, source_target_pairs={{0,1},{1,0},{2,3},{3,2},{4,5},{5,4},{6,7},{7,6},{8,9},{9,8},{10,11... | collective-permute-start | bytes 811016 | tf_op jit(solution)/shard_map/ppermute | solution.py:275
  54.9 3.3 %collective-permute-done.14.refs_0_ = bf16[256,1024]{1,0:T(8,128)(2,1)S(1)} collective-permute-done((bf16[256,1024]{1,0:T(8,128)(2,1)S(1)}, bf16[256,1024]{1,0:T(8,128)(2,1)S(1)}, u32[]{:S(2)}, u32[]{:S(2)}) %collective-permute-start.14) | collective-permute-done | bytes 524320 | tf_op jit(solution)/shard_map/ppermute | solution.py:272
  58.2 1.3 %collective-permute-start.17 = (bf16[64,1024]{1,0:T(8,128)(2,1)S(1)}, bf16[64,1024]{1,0:T(8,128)(2,1)S(1)}, u32[]{:S(2)}, u32[]{:S(2)}) collective-permute-start(bf16[64,1024]{1,0:T(8,128)(2,1)S(1)} %get-tuple-element.107), channel_id=1, source_target_pairs={{0,2},{2,0},{4,6},{6,4},{8,10},{10,8},{12,14},{14,12},{16,18},{18,... | collective-permute-start | bytes 393224 | tf_op jit(solution)/shard_map/ppermute | solution.py:260
  61.6 1.7 %shard_map.70 = (bf16[132,1024]{1,0:T(8,128)(2,1)S(1)}, bf16[256,128]{1,0:T(8,128)(2,1)S(1)}) custom-call(bf16[256,1024]{1,0:T(8,128)(2,1)S(1)} %collective-permute-done.14.refs_0_, bf16[256,1024]{1,0:T(8,128)(2,1)S(1)} %pad_maximum_fusion.6.refs_1_, bf16[1024,1792]{1,0:T(8,128)(2,1)S(1)} %bitcast.9), custom_call_target="tpu_custom_call" | custom-call | tf_op jit(solution)/shard_map/pallas_call | solution.py:278
  63.3 1.3 %collective-permute-start.24 = (bf16[132,1024]{1,0:T(8,128)(2,1)S(1)}, bf16[132,1024]{1,0:T(8,128)(2,1)S(1)}, u32[]{:S(2)}, u32[]{:S(2)}) collective-permute-start(bf16[132,1024]{1,0:T(8,128)(2,1)S(1)} %get-tuple-element.69.refs_0_), channel_id=1, source_target_pairs={{0,1},{1,0},{2,3},{3,2},{4,5},{5,4},{6,7},{7,6},{8,9},{9,8},{10,11... | collective-permute-start | bytes 811016 | tf_op jit(solution)/shard_map/ppermute | solution.py:275
  64.6 1.9 %shard_map.71 = (bf16[256,1792]{1,0:T(8,128)(2,1)S(1)}, bf16[256,1792]{1,0:T(8,128)(2,1)S(1)}) custom-call(bf16[512,128]{1,0:T(8,128)(2,1)S(1)} %copy-done.13, bf16[264,512]{1,0:T(8,128)(2,1)S(1)} %multiply_convert_fusion.2.refs_0_, bf16[264,512]{1,0:T(8,128)(2,1)S(1)} %collective-permute-done.8.refs_1_, bf16[1792,1024]{1,0:T(8,128)(2,1)S(1)} %bitcast.10), custom_call_target="tpu_custom_call" | custom-call | tf_op jit(solution)/shard_map/pallas_call | solution.py:278
  66.5 1.4 %collective-permute-start.22 = (bf16[80,1792]{1,0:T(8,128)(2,1)S(1)}, bf16[80,1792]{1,0:T(8,128)(2,1)S(1)}, u32[]{:S(2)}, u32[]{:S(2)}) collective-permute-start(bf16[80,1792]{1,0:T(8,128)(2,1)S(1)} %slice.49), channel_id=1, source_target_pairs={{0,2},{2,0},{4,6},{6,4},{8,10},{10,8},{12,14},{14,12},{16,18},{18,... | collective-permute-start | bytes 860168 | tf_op jit(solution)/shard_map/ppermute | solution.py:260
  68.6 1.4 %collective-permute-done.26.refs_1_ = bf16[48,1792]{1,0:T(8,128)(2,1)S(1)} collective-permute-done((bf16[48,1792]{1,0:T(8,128)(2,1)S(1)}, bf16[48,1792]{1,0:T(8,128)(2,1)S(1)}, u32[]{:S(2)}, u32[]{:S(2)}) %collective-permute-start.26) | collective-permute-done | bytes 172064 | tf_op jit(solution)/shard_map/ppermute | solution.py:260
  70.5 1.2 %collective-permute-start.27 = (bf16[264,512]{1,0:T(8,128)(2,1)S(1)}, bf16[264,512]{1,0:T(8,128)(2,1)S(1)}, u32[]{:S(2)}, u32[]{:S(2)}) collective-permute-start(bf16[264,512]{1,0:T(8,128)(2,1)S(1)} %multiply_convert_fusion.1.refs_0_), channel_id=1, source_target_pairs={{0,1},{1,0},{2,3},{3,2},{4,5},{5,4},{6,7},{7,6},{8,9},{9,8},{10,11... | collective-permute-start | bytes 811016 | tf_op jit(solution)/shard_map/ppermute | solution.py:275
  71.7 2.1 %shard_map.72 = (bf16[256,896]{1,0:T(8,128)(2,1)S(1)}, bf16[256,896]{1,0:T(8,128)(2,1)S(1)}) custom-call(bf16[256,128]{1,0:T(8,128)(2,1)S(1)} %get-tuple-element.76.table_ref, bf16[132,1024]{1,0:T(8,128)(2,1)S(1)} %get-tuple-element.69.refs_0_, bf16[132,1024]{1,0:T(8,128)(2,1)S(1)} %collective-permute-done.24.refs_1_, ...), custom_call_target="tpu_custom_call" | custom-call | tf_op jit(solution)/shard_map/pallas_call | solution.py:278
  73.8 2.3 %collective-permute-start.31 = (bf16[64,896]{1,0:T(8,128)(2,1)S(1)}, bf16[64,896]{1,0:T(8,128)(2,1)S(1)}, u32[]{:S(2)}, u32[]{:S(2)}) collective-permute-start(bf16[64,896]{1,0:T(8,128)(2,1)S(1)} %get-tuple-element.111), channel_id=1, source_target_pairs={{0,2},{2,0},{4,6},{6,4},{8,10},{10,8},{12,14},{14,12},{16,18},{18,... | collective-permute-start | bytes 344072 | tf_op jit(solution)/shard_map/ppermute | solution.py:260
  78.1 1.4 %collective-permute-start.34 = (bf16[256,896]{1,0:T(8,128)(2,1)S(1)}, bf16[256,896]{1,0:T(8,128)(2,1)S(1)}, u32[]{:S(2)}, u32[]{:S(2)}) collective-permute-start(bf16[256,896]{1,0:T(8,128)(2,1)S(1)} %shard_map.73), channel_id=1, source_target_pairs={{0,8},{2,6},{4,0},{6,14},{8,16},{10,2},{12,4},{14,22},{16,24},{18,... | collective-permute-start | bytes 1376264 | tf_op jit(solution)/shard_map/ppermute | solution.py:272
  79.4 1.9 %shard_map.74 = (bf16[256,1792]{1,0:T(8,128)(2,1)S(1)}, bf16[256,1792]{1,0:T(8,128)(2,1)S(1)}) custom-call(bf16[512,128]{1,0:T(8,128)(2,1)S(1)} %get-tuple-element.82.table_ref, bf16[264,512]{1,0:T(8,128)(2,1)S(1)} %multiply_convert_fusion.1.refs_0_, bf16[264,512]{1,0:T(8,128)(2,1)S(1)} %collective-permute-done.27.refs_1_, bf16[1792,1024]{1,0:T(8,128)(2,1)S(1)} %bitcast.12), custom_call_target="tpu_custom_call" | custom-call | tf_op jit(solution)/shard_map/pallas_call | solution.py:278
  83.8 1.9 %collective-permute-done.34 = bf16[256,896]{1,0:T(8,128)(2,1)S(1)} collective-permute-done((bf16[256,896]{1,0:T(8,128)(2,1)S(1)}, bf16[256,896]{1,0:T(8,128)(2,1)S(1)}, u32[]{:S(2)}, u32[]{:S(2)}) %collective-permute-start.34) | collective-permute-done | bytes 458784 | tf_op jit(solution)/shard_map/ppermute | solution.py:272
  85.9 1.4 %collective-permute-start.44 = (bf16[112,1792]{1,0:T(8,128)(2,1)S(1)}, bf16[112,1792]{1,0:T(8,128)(2,1)S(1)}, u32[]{:S(2)}, u32[]{:S(2)}) collective-permute-start(bf16[112,1792]{1,0:T(8,128)(2,1)S(1)} %shard_map.75), channel_id=1, source_target_pairs={{0,8},{2,6},{4,0},{6,14},{8,16},{10,2},{12,4},{14,22},{16,24},{18,... | collective-permute-start | bytes 1204232 | tf_op jit(solution)/shard_map/ppermute | solution.py:272
  87.8 3.5 %collective-permute-done.32.refs_1_ = bf16[264,512]{1,0:T(8,128)(2,1)S(1)} collective-permute-done((bf16[264,512]{1,0:T(8,128)(2,1)S(1)}, bf16[264,512]{1,0:T(8,128)(2,1)S(1)}, u32[]{:S(2)}, u32[]{:S(2)}) %collective-permute-start.32) | collective-permute-done | bytes 270368 | tf_op jit(solution)/shard_map/ppermute | solution.py:275
  91.2 1.9 %shard_map.77 = (bf16[256,1792]{1,0:T(8,128)(2,1)S(1)}, bf16[256,1792]{1,0:T(8,128)(2,1)S(1)}) custom-call(bf16[512,128]{1,0:T(8,128)(2,1)S(1)} %copy-done.11, bf16[264,512]{1,0:T(8,128)(2,1)S(1)} %multiply_convert_fusion.refs_0_, bf16[264,512]{1,0:T(8,128)(2,1)S(1)} %collective-permute-done.32.refs_1_, bf16[1792,1024]{1,0:T(8,128)(2,1)S(1)} %bitcast.13), custom_call_target="tpu_custom_call" | custom-call | tf_op jit(solution)/shard_map/pallas_call | solution.py:278
  94.7 1.4 %collective-permute-done.43.refs_1_ = bf16[48,1792]{1,0:T(8,128)(2,1)S(1)} collective-permute-done((bf16[48,1792]{1,0:T(8,128)(2,1)S(1)}, bf16[48,1792]{1,0:T(8,128)(2,1)S(1)}, u32[]{:S(2)}, u32[]{:S(2)}) %collective-permute-start.43) | collective-permute-done | bytes 172064 | tf_op jit(solution)/shard_map/ppermute | solution.py:260
  98.7 1.4 %collective-permute-start.38 = (bf16[144,1792]{1,0:T(8,128)(2,1)S(1)}, bf16[144,1792]{1,0:T(8,128)(2,1)S(1)}, u32[]{:S(2)}, u32[]{:S(2)}) collective-permute-start(bf16[144,1792]{1,0:T(8,128)(2,1)S(1)} %shard_map.78), channel_id=1, source_target_pairs={{0,8},{2,6},{4,0},{6,14},{8,16},{10,2},{12,4},{14,22},{16,24},{18,... | collective-permute-start | bytes 1548296 | tf_op jit(solution)/shard_map/ppermute | solution.py:272
  100.3 3.2 %collective-permute-done.45.refs_2_ = bf16[112,1792]{1,0:T(8,128)(2,1)S(1)} collective-permute-done((bf16[112,1792]{1,0:T(8,128)(2,1)S(1)}, bf16[112,1792]{1,0:T(8,128)(2,1)S(1)}, u32[]{:S(2)}, u32[]{:S(2)}) %collective-permute-start.45) | collective-permute-done | bytes 401440 | tf_op jit(solution)/shard_map/ppermute | solution.py:272
  104.6 1.3 %collective-permute-start.41 = (bf16[132,512]{1,0:T(8,128)(2,1)S(1)}, bf16[132,512]{1,0:T(8,128)(2,1)S(1)}, u32[]{:S(2)}, u32[]{:S(2)}) collective-permute-start(bf16[132,512]{1,0:T(8,128)(2,1)S(1)} %multiply_convert_fusion.3.refs_0_), channel_id=1, source_target_pairs={{0,1},{1,0},{2,3},{3,2},{4,5},{5,4},{6,7},{7,6},{8,9},{9,8},{10,11... | collective-permute-start | bytes 405512 | tf_op jit(solution)/shard_map/ppermute | solution.py:275
  105.9 3.2 %collective-permute-done.38.refs_2_ = bf16[144,1792]{1,0:T(8,128)(2,1)S(1)} collective-permute-done((bf16[144,1792]{1,0:T(8,128)(2,1)S(1)}, bf16[144,1792]{1,0:T(8,128)(2,1)S(1)}, u32[]{:S(2)}, u32[]{:S(2)}) %collective-permute-start.38) | collective-permute-done | bytes 516128 | tf_op jit(solution)/shard_map/ppermute | solution.py:272
  110.1 1.7 %shard_map.82 = (bf16[128,1792]{1,0:T(8,128)(2,1)S(1)}, bf16[128,1792]{1,0:T(8,128)(2,1)S(1)}) custom-call(bf16[256,128]{1,0:T(8,128)(2,1)S(1)} %get-tuple-element.88.table_ref, bf16[132,512]{1,0:T(8,128)(2,1)S(1)} %multiply_convert_fusion.3.refs_0_, bf16[132,512]{1,0:T(8,128)(2,1)S(1)} %collective-permute-done.41.refs_1_, bf16[1792,1024]{1,0:T(8,128)(2,1)S(1)} %bitcast.14), custom_call_target="tpu_custom_call" | custom-call | tf_op jit(solution)/shard_map/pallas_call | solution.py:278
  111.9 1.6 %collective-permute-done.46 = bf16[112,1792]{1,0:T(8,128)(2,1)S(1)} collective-permute-done((bf16[112,1792]{1,0:T(8,128)(2,1)S(1)}, bf16[112,1792]{1,0:T(8,128)(2,1)S(1)}, u32[]{:S(2)}, u32[]{:S(2)}) %collective-permute-start.46) | collective-permute-done | bytes 401440 | tf_op jit(solution)/shard_map/ppermute | solution.py:272
  113.5 1.3 %collective-permute-start.47 = (bf16[112,1792]{1,0:T(8,128)(2,1)S(1)}, bf16[112,1792]{1,0:T(8,128)(2,1)S(1)}, u32[]{:S(2)}, u32[]{:S(2)}) collective-permute-start(bf16[112,1792]{1,0:T(8,128)(2,1)S(1)} %add_convert_fusion.1), channel_id=1, source_target_pairs={{0,2},{2,0},{4,6},{6,4},{8,10},{10,8},{12,14},{14,12},{16,18},{18,... | collective-permute-start | bytes 1204232 | tf_op jit(solution)/shard_map/ppermute | solution.py:260
  114.8 4.1 %collective-permute-done.39 = bf16[144,1792]{1,0:T(8,128)(2,1)S(1)} collective-permute-done((bf16[144,1792]{1,0:T(8,128)(2,1)S(1)}, bf16[144,1792]{1,0:T(8,128)(2,1)S(1)}, u32[]{:S(2)}, u32[]{:S(2)}) %collective-permute-start.39) | collective-permute-done | bytes 516128 | tf_op jit(solution)/shard_map/ppermute | solution.py:272
  119.0 1.3 %collective-permute-start.48 = (bf16[16,1792]{1,0:T(8,128)(2,1)S(1)}, bf16[16,1792]{1,0:T(8,128)(2,1)S(1)}, u32[]{:S(2)}, u32[]{:S(2)}) collective-permute-start(bf16[16,1792]{1,0:T(8,128)(2,1)S(1)} %add_convert_fusion.2), channel_id=1, source_target_pairs={{0,2},{2,0},{4,6},{6,4},{8,10},{10,8},{12,14},{14,12},{16,18},{18,... | collective-permute-start | bytes 172040 | tf_op jit(solution)/shard_map/ppermute | solution.py:260
  (139 shorter events, 25.6 us)
Async XLA Ops:
  0.0 2.3 %collective-permute-start = (bf16[128,1792]{1,0:T(8,128)(2,1)}, bf16[128,1792]{1,0:T(8,128)(2,1)S(1)}, u32[]{:S(2)}, u32[]{:S(2)}) collective-permute-start(bf16[128,1792]{1,0:T(8,128)(2,1)} %param.6), channel_id=1, source_target_pairs={{0,2},{2,0},{4,6},{6,4},{8,10},{10,8},{12,14},{14,12},{16,18},{18,... | collective-permute-start | bytes 1376264 | tf_op jit(solution)/shard_map/ppermute | solution.py:260
  3.6 13.3 %collective-permute-start.1 = (bf16[256,1792]{1,0:T(8,128)(2,1)S(1)}, bf16[256,1792]{1,0:T(8,128)(2,1)S(1)}, u32[]{:S(2)}, u32[]{:S(2)}) collective-permute-start(bf16[256,1792]{1,0:T(8,128)(2,1)S(1)} %pad_maximum_fusion.4), channel_id=1, source_target_pairs={{0,8},{2,6},{4,0},{6,14},{8,16},{10,2},{12,4},{14,22},{16,24},{18,... | collective-permute-start | bytes 2752520 | tf_op jit(solution)/shard_map/ppermute | solution.py:272
  6.5 4.1 %collective-permute-start.2 = (bf16[128,128]{1,0:T(8,128)(2,1)S(1)}, bf16[128,128]{1,0:T(8,128)(2,1)S(1)}, u32[]{:S(2)}, u32[]{:S(2)}) collective-permute-start(bf16[128,128]{1,0:T(8,128)(2,1)S(1)} %shard_map.64), channel_id=1, source_target_pairs={{0,2},{2,0},{4,6},{6,4},{8,10},{10,8},{12,14},{14,12},{16,18},{18,... | collective-permute-start | bytes 98312 | tf_op jit(solution)/shard_map/ppermute | solution.py:260
  8.3 8.7 %collective-permute-start.4 = (bf16[132,512]{1,0:T(8,128)(2,1)S(1)}, bf16[132,512]{1,0:T(8,128)(2,1)S(1)}, u32[]{:S(2)}, u32[]{:S(2)}) collective-permute-start(bf16[132,512]{1,0:T(8,128)(2,1)S(1)} %get-tuple-element.53.refs_2_), channel_id=1, source_target_pairs={{0,1},{1,0},{2,3},{3,2},{4,5},{5,4},{6,7},{7,6},{8,9},{9,8},{10,11... | collective-permute-start | bytes 405512 | tf_op jit(solution)/shard_map/ppermute | solution.py:275
  10.6 6.2 %collective-permute-start.3 = (bf16[256,128]{1,0:T(8,128)(2,1)S(1)}, bf16[256,128]{1,0:T(8,128)(2,1)S(1)}, u32[]{:S(2)}, u32[]{:S(2)}) collective-permute-start(bf16[256,128]{1,0:T(8,128)(2,1)S(1)} %pad_maximum_fusion.9), channel_id=1, source_target_pairs={{0,8},{2,6},{4,0},{6,14},{8,16},{10,2},{12,4},{14,22},{16,24},{18,... | collective-permute-start | bytes 196616 | tf_op jit(solution)/shard_map/ppermute | solution.py:272
  17.1 2.8 %collective-permute-start.5 = (bf16[128,1920]{1,0:T(8,128)(2,1)S(1)}, bf16[128,1920]{1,0:T(8,128)(2,1)S(1)}, u32[]{:S(2)}, u32[]{:S(2)}) collective-permute-start(bf16[128,1920]{1,0:T(8,128)(2,1)S(1)} %get-tuple-element.103), channel_id=1, source_target_pairs={{0,2},{2,0},{4,6},{6,4},{8,10},{10,8},{12,14},{14,12},{16,18},{18,... | collective-permute-start | bytes 1474568 | tf_op jit(solution)/shard_map/ppermute | solution.py:260
  18.4 2.2 %collective-permute-start.6 = (bf16[128,1920]{1,0:T(8,128)(2,1)S(1)}, bf16[128,1920]{1,0:T(8,128)(2,1)S(1)}, u32[]{:S(2)}, u32[]{:S(2)}) collective-permute-start(bf16[128,1920]{1,0:T(8,128)(2,1)S(1)} %get-tuple-element.104), channel_id=1, source_target_pairs={{0,2},{2,0},{4,6},{6,4},{8,10},{10,8},{12,14},{14,12},{16,18},{18,... | collective-permute-start | bytes 1474568 | tf_op jit(solution)/shard_map/ppermute | solution.py:260
  18.4 13.2 %collective-permute-start.9 = (bf16[256,1920]{1,0:T(8,128)(2,1)S(1)}, bf16[256,1920]{1,0:T(8,128)(2,1)S(1)}, u32[]{:S(2)}, u32[]{:S(2)}) collective-permute-start(bf16[256,1920]{1,0:T(8,128)(2,1)S(1)} %pad_maximum_fusion.refs_0_), channel_id=1, source_target_pairs={{0,8},{2,6},{4,0},{6,14},{8,16},{10,2},{12,4},{14,22},{16,24},{18,... | collective-permute-start | bytes 2949128 | tf_op jit(solution)/shard_map/ppermute | solution.py:272
  22.5 7.8 %collective-permute-start.7 = (bf16[264,512]{1,0:T(8,128)(2,1)S(1)}, bf16[264,512]{1,0:T(8,128)(2,1)S(1)}, u32[]{:S(2)}, u32[]{:S(2)}) collective-permute-start(bf16[264,512]{1,0:T(8,128)(2,1)S(1)} %get-tuple-element.57), channel_id=1, source_target_pairs={{0,1},{1,0},{2,3},{3,2},{4,5},{5,4},{6,7},{7,6},{8,9},{9,8},{10,11... | collective-permute-start | bytes 811016 | tf_op jit(solution)/shard_map/ppermute | solution.py:275
  31.8 3.9 %collective-permute-start.11 = (bf16[128,1920]{1,0:T(8,128)(2,1)S(1)}, bf16[128,1920]{1,0:T(8,128)(2,1)S(1)}, u32[]{:S(2)}, u32[]{:S(2)}) collective-permute-start(bf16[128,1920]{1,0:T(8,128)(2,1)S(1)} %get-tuple-element.101), channel_id=1, source_target_pairs={{0,2},{2,0},{4,6},{6,4},{8,10},{10,8},{12,14},{14,12},{16,18},{18,... | collective-permute-start | bytes 1474568 | tf_op jit(solution)/shard_map/ppermute | solution.py:260
  33.1 2.6 %collective-permute-start.12 = (bf16[128,1920]{1,0:T(8,128)(2,1)S(1)}, bf16[128,1920]{1,0:T(8,128)(2,1)S(1)}, u32[]{:S(2)}, u32[]{:S(2)}) collective-permute-start(bf16[128,1920]{1,0:T(8,128)(2,1)S(1)} %get-tuple-element.102), channel_id=1, source_target_pairs={{0,2},{2,0},{4,6},{6,4},{8,10},{10,8},{12,14},{14,12},{16,18},{18,... | collective-permute-start | bytes 1474568 | tf_op jit(solution)/shard_map/ppermute | solution.py:260
  33.2 15.7 %collective-permute-start.10 = (bf16[256,1920]{1,0:T(8,128)(2,1)S(1)}, bf16[256,1920]{1,0:T(8,128)(2,1)S(1)}, u32[]{:S(2)}, u32[]{:S(2)}) collective-permute-start(bf16[256,1920]{1,0:T(8,128)(2,1)S(1)} %collective-permute-done.9.refs_0_), channel_id=1, source_target_pairs={{0,8},{2,6},{4,0},{6,14},{8,16},{10,2},{12,4},{14,22},{16,24},{18,... | collective-permute-start | bytes 2949128 | tf_op jit(solution)/shard_map/ppermute | solution.py:272
  34.5 8.5 %collective-permute-start.8 = (bf16[264,512]{1,0:T(8,128)(2,1)S(1)}, bf16[264,512]{1,0:T(8,128)(2,1)S(1)}, u32[]{:S(2)}, u32[]{:S(2)}) collective-permute-start(bf16[264,512]{1,0:T(8,128)(2,1)S(1)} %multiply_convert_fusion.2.refs_0_), channel_id=1, source_target_pairs={{0,1},{1,0},{2,3},{3,2},{4,5},{5,4},{6,7},{7,6},{8,9},{9,8},{10,11... | collective-permute-start | bytes 811016 | tf_op jit(solution)/shard_map/ppermute | solution.py:275
  39.0 9.8 %collective-permute-start.13 = (bf16[264,512]{1,0:T(8,128)(2,1)}, bf16[264,512]{1,0:T(8,128)(2,1)}, u32[]{:S(2)}, u32[]{:S(2)}) collective-permute-start(bf16[264,512]{1,0:T(8,128)(2,1)} %get-tuple-element.62), channel_id=1, source_target_pairs={{0,1},{1,0},{2,3},{3,2},{4,5},{5,4},{6,7},{7,6},{8,9},{9,8},{10,11... | collective-permute-start | bytes 811016 | tf_op jit(solution)/shard_map/ppermute | solution.py:275
  48.9 2.2 %collective-permute-start.15 = (bf16[128,1920]{1,0:T(8,128)(2,1)S(1)}, bf16[128,1920]{1,0:T(8,128)(2,1)S(1)}, u32[]{:S(2)}, u32[]{:S(2)}) collective-permute-start(bf16[128,1920]{1,0:T(8,128)(2,1)S(1)} %get-tuple-element.99), channel_id=1, source_target_pairs={{0,2},{2,0},{4,6},{6,4},{8,10},{10,8},{12,14},{14,12},{16,18},{18,... | collective-permute-start | bytes 1474568 | tf_op jit(solution)/shard_map/ppermute | solution.py:260
  49.4 2.2 %collective-permute-start.16 = (bf16[128,1920]{1,0:T(8,128)(2,1)S(1)}, bf16[128,1920]{1,0:T(8,128)(2,1)S(1)}, u32[]{:S(2)}, u32[]{:S(2)}) collective-permute-start(bf16[128,1920]{1,0:T(8,128)(2,1)S(1)} %get-tuple-element.100), channel_id=1, source_target_pairs={{0,2},{2,0},{4,6},{6,4},{8,10},{10,8},{12,14},{14,12},{16,18},{18,... | collective-permute-start | bytes 1474568 | tf_op jit(solution)/shard_map/ppermute | solution.py:260
  49.6 8.6 %collective-permute-start.14 = (bf16[256,1024]{1,0:T(8,128)(2,1)S(1)}, bf16[256,1024]{1,0:T(8,128)(2,1)S(1)}, u32[]{:S(2)}, u32[]{:S(2)}) collective-permute-start(bf16[256,1024]{1,0:T(8,128)(2,1)S(1)} %pad_maximum_fusion.5), channel_id=1, source_target_pairs={{0,8},{2,6},{4,0},{6,14},{8,16},{10,2},{12,4},{14,22},{16,24},{18,... | collective-permute-start | bytes 1572872 | tf_op jit(solution)/shard_map/ppermute | solution.py:272
  53.6 7.9 %collective-permute-start.21 = (bf16[264,512]{1,0:T(8,128)(2,1)S(1)}, bf16[264,512]{1,0:T(8,128)(2,1)S(1)}, u32[]{:S(2)}, u32[]{:S(2)}) collective-permute-start(bf16[264,512]{1,0:T(8,128)(2,1)S(1)} %get-tuple-element.66), channel_id=1, source_target_pairs={{0,1},{1,0},{2,3},{3,2},{4,5},{5,4},{6,7},{7,6},{8,9},{9,8},{10,11... | collective-permute-start | bytes 811016 | tf_op jit(solution)/shard_map/ppermute | solution.py:275
  58.2 2.3 %collective-permute-start.17 = (bf16[64,1024]{1,0:T(8,128)(2,1)S(1)}, bf16[64,1024]{1,0:T(8,128)(2,1)S(1)}, u32[]{:S(2)}, u32[]{:S(2)}) collective-permute-start(bf16[64,1024]{1,0:T(8,128)(2,1)S(1)} %get-tuple-element.107), channel_id=1, source_target_pairs={{0,2},{2,0},{4,6},{6,4},{8,10},{10,8},{12,14},{14,12},{16,18},{18,... | collective-permute-start | bytes 393224 | tf_op jit(solution)/shard_map/ppermute | solution.py:260
  59.6 1.3 %collective-permute-start.20 = (bf16[64,1024]{1,0:T(8,128)(2,1)S(1)}, bf16[64,1024]{1,0:T(8,128)(2,1)S(1)}, u32[]{:S(2)}, u32[]{:S(2)}) collective-permute-start(bf16[64,1024]{1,0:T(8,128)(2,1)S(1)} %get-tuple-element.108), channel_id=1, source_target_pairs={{0,2},{2,0},{4,6},{6,4},{8,10},{10,8},{12,14},{14,12},{16,18},{18,... | collective-permute-start | bytes 393224 | tf_op jit(solution)/shard_map/ppermute | solution.py:260
  59.7 1.5 %collective-permute-start.19 = (bf16[64,1024]{1,0:T(8,128)(2,1)S(1)}, bf16[64,1024]{1,0:T(8,128)(2,1)S(1)}, u32[]{:S(2)}, u32[]{:S(2)}) collective-permute-start(bf16[64,1024]{1,0:T(8,128)(2,1)S(1)} %get-tuple-element.109), channel_id=1, source_target_pairs={{0,2},{2,0},{4,6},{6,4},{8,10},{10,8},{12,14},{14,12},{16,18},{18,... | collective-permute-start | bytes 393224 | tf_op jit(solution)/shard_map/ppermute | solution.py:260
  60.1 1.3 %collective-permute-start.18 = (bf16[64,1024]{1,0:T(8,128)(2,1)S(1)}, bf16[64,1024]{1,0:T(8,128)(2,1)S(1)}, u32[]{:S(2)}, u32[]{:S(2)}) collective-permute-start(bf16[64,1024]{1,0:T(8,128)(2,1)S(1)} %get-tuple-element.110), channel_id=1, source_target_pairs={{0,2},{2,0},{4,6},{6,4},{8,10},{10,8},{12,14},{14,12},{16,18},{18,... | collective-permute-start | bytes 393224 | tf_op jit(solution)/shard_map/ppermute | solution.py:260
  63.3 7.2 %collective-permute-start.24 = (bf16[132,1024]{1,0:T(8,128)(2,1)S(1)}, bf16[132,1024]{1,0:T(8,128)(2,1)S(1)}, u32[]{:S(2)}, u32[]{:S(2)}) collective-permute-start(bf16[132,1024]{1,0:T(8,128)(2,1)S(1)} %get-tuple-element.69.refs_0_), channel_id=1, source_target_pairs={{0,1},{1,0},{2,3},{3,2},{4,5},{5,4},{6,7},{7,6},{8,9},{9,8},{10,11... | collective-permute-start | bytes 811016 | tf_op jit(solution)/shard_map/ppermute | solution.py:275
  66.5 4.0 %collective-permute-start.22 = (bf16[80,1792]{1,0:T(8,128)(2,1)S(1)}, bf16[80,1792]{1,0:T(8,128)(2,1)S(1)}, u32[]{:S(2)}, u32[]{:S(2)}) collective-permute-start(bf16[80,1792]{1,0:T(8,128)(2,1)S(1)} %slice.49), channel_id=1, source_target_pairs={{0,2},{2,0},{4,6},{6,4},{8,10},{10,8},{12,14},{14,12},{16,18},{18,... | collective-permute-start | bytes 860168 | tf_op jit(solution)/shard_map/ppermute | solution.py:260
  67.9 2.1 %collective-permute-start.23 = (bf16[64,1792]{1,0:T(8,128)(2,1)S(1)}, bf16[64,1792]{1,0:T(8,128)(2,1)S(1)}, u32[]{:S(2)}, u32[]{:S(2)}) collective-permute-start(bf16[64,1792]{1,0:T(8,128)(2,1)S(1)} %get-tuple-element.105), channel_id=1, source_target_pairs={{0,2},{2,0},{4,6},{6,4},{8,10},{10,8},{12,14},{14,12},{16,18},{18,... | collective-permute-start | bytes 688136 | tf_op jit(solution)/shard_map/ppermute | solution.py:260
  68.0 2.0 %collective-permute-start.25 = (bf16[64,1792]{1,0:T(8,128)(2,1)S(1)}, bf16[64,1792]{1,0:T(8,128)(2,1)S(1)}, u32[]{:S(2)}, u32[]{:S(2)}) collective-permute-start(bf16[64,1792]{1,0:T(8,128)(2,1)S(1)} %get-tuple-element.106), channel_id=1, source_target_pairs={{0,2},{2,0},{4,6},{6,4},{8,10},{10,8},{12,14},{14,12},{16,18},{18,... | collective-permute-start | bytes 688136 | tf_op jit(solution)/shard_map/ppermute | solution.py:260
  68.5 1.5 %collective-permute-start.26 = (bf16[48,1792]{1,0:T(8,128)(2,1)S(1)}, bf16[48,1792]{1,0:T(8,128)(2,1)S(1)}, u32[]{:S(2)}, u32[]{:S(2)}) collective-permute-start(bf16[48,1792]{1,0:T(8,128)(2,1)S(1)} %slice.52), channel_id=1, source_target_pairs={{0,2},{2,0},{4,6},{6,4},{8,10},{10,8},{12,14},{14,12},{16,18},{18,... | collective-permute-start | bytes 516104 | tf_op jit(solution)/shard_map/ppermute | solution.py:260
  70.5 9.0 %collective-permute-start.27 = (bf16[264,512]{1,0:T(8,128)(2,1)S(1)}, bf16[264,512]{1,0:T(8,128)(2,1)S(1)}, u32[]{:S(2)}, u32[]{:S(2)}) collective-permute-start(bf16[264,512]{1,0:T(8,128)(2,1)S(1)} %multiply_convert_fusion.1.refs_0_), channel_id=1, source_target_pairs={{0,1},{1,0},{2,3},{3,2},{4,5},{5,4},{6,7},{7,6},{8,9},{9,8},{10,11... | collective-permute-start | bytes 811016 | tf_op jit(solution)/shard_map/ppermute | solution.py:275
  73.8 3.3 %collective-permute-start.31 = (bf16[64,896]{1,0:T(8,128)(2,1)S(1)}, bf16[64,896]{1,0:T(8,128)(2,1)S(1)}, u32[]{:S(2)}, u32[]{:S(2)}) collective-permute-start(bf16[64,896]{1,0:T(8,128)(2,1)S(1)} %get-tuple-element.111), channel_id=1, source_target_pairs={{0,2},{2,0},{4,6},{6,4},{8,10},{10,8},{12,14},{14,12},{16,18},{18,... | collective-permute-start | bytes 344072 | tf_op jit(solution)/shard_map/ppermute | solution.py:260
  76.1 1.3 %collective-permute-start.30 = (bf16[64,896]{1,0:T(8,128)(2,1)S(1)}, bf16[64,896]{1,0:T(8,128)(2,1)S(1)}, u32[]{:S(2)}, u32[]{:S(2)}) collective-permute-start(bf16[64,896]{1,0:T(8,128)(2,1)S(1)} %get-tuple-element.112), channel_id=1, source_target_pairs={{0,2},{2,0},{4,6},{6,4},{8,10},{10,8},{12,14},{14,12},{16,18},{18,... | collective-permute-start | bytes 344072 | tf_op jit(solution)/shard_map/ppermute | solution.py:260
  76.2 1.4 %collective-permute-start.29 = (bf16[64,896]{1,0:T(8,128)(2,1)S(1)}, bf16[64,896]{1,0:T(8,128)(2,1)S(1)}, u32[]{:S(2)}, u32[]{:S(2)}) collective-permute-start(bf16[64,896]{1,0:T(8,128)(2,1)S(1)} %get-tuple-element.113), channel_id=1, source_target_pairs={{0,2},{2,0},{4,6},{6,4},{8,10},{10,8},{12,14},{14,12},{16,18},{18,... | collective-permute-start | bytes 344072 | tf_op jit(solution)/shard_map/ppermute | solution.py:260
  78.1 7.7 %collective-permute-start.34 = (bf16[256,896]{1,0:T(8,128)(2,1)S(1)}, bf16[256,896]{1,0:T(8,128)(2,1)S(1)}, u32[]{:S(2)}, u32[]{:S(2)}) collective-permute-start(bf16[256,896]{1,0:T(8,128)(2,1)S(1)} %shard_map.73), channel_id=1, source_target_pairs={{0,8},{2,6},{4,0},{6,14},{8,16},{10,2},{12,4},{14,22},{16,24},{18,... | collective-permute-start | bytes 1376264 | tf_op jit(solution)/shard_map/ppermute | solution.py:272
  81.3 4.4 %collective-permute-start.33 = (bf16[112,1792]{1,0:T(8,128)(2,1)S(1)}, bf16[112,1792]{1,0:T(8,128)(2,1)S(1)}, u32[]{:S(2)}, u32[]{:S(2)}) collective-permute-start(bf16[112,1792]{1,0:T(8,128)(2,1)S(1)} %slice.53), channel_id=1, source_target_pairs={{0,2},{2,0},{4,6},{6,4},{8,10},{10,8},{12,14},{14,12},{16,18},{18,... | collective-permute-start | bytes 1204232 | tf_op jit(solution)/shard_map/ppermute | solution.py:260
  81.5 5.9 %collective-permute-start.35 = (bf16[144,1792]{1,0:T(8,128)(2,1)S(1)}, bf16[144,1792]{1,0:T(8,128)(2,1)S(1)}, u32[]{:S(2)}, u32[]{:S(2)}) collective-permute-start(bf16[144,1792]{1,0:T(8,128)(2,1)S(1)} %slice.55), channel_id=1, source_target_pairs={{0,2},{2,0},{4,6},{6,4},{8,10},{10,8},{12,14},{14,12},{16,18},{18,... | collective-permute-start | bytes 1548296 | tf_op jit(solution)/shard_map/ppermute | solution.py:260
  83.1 8.2 %collective-permute-start.32 = (bf16[264,512]{1,0:T(8,128)(2,1)S(1)}, bf16[264,512]{1,0:T(8,128)(2,1)S(1)}, u32[]{:S(2)}, u32[]{:S(2)}) collective-permute-start(bf16[264,512]{1,0:T(8,128)(2,1)S(1)} %multiply_convert_fusion.refs_0_), channel_id=1, source_target_pairs={{0,1},{1,0},{2,3},{3,2},{4,5},{5,4},{6,7},{7,6},{8,9},{9,8},{10,11... | collective-permute-start | bytes 811016 | tf_op jit(solution)/shard_map/ppermute | solution.py:275
  85.9 8.8 %collective-permute-start.44 = (bf16[112,1792]{1,0:T(8,128)(2,1)S(1)}, bf16[112,1792]{1,0:T(8,128)(2,1)S(1)}, u32[]{:S(2)}, u32[]{:S(2)}) collective-permute-start(bf16[112,1792]{1,0:T(8,128)(2,1)S(1)} %shard_map.75), channel_id=1, source_target_pairs={{0,8},{2,6},{4,0},{6,14},{8,16},{10,2},{12,4},{14,22},{16,24},{18,... | collective-permute-start | bytes 1204232 | tf_op jit(solution)/shard_map/ppermute | solution.py:272
  87.5 11.0 %collective-permute-start.37 = (bf16[144,1792]{1,0:T(8,128)(2,1)S(1)}, bf16[144,1792]{1,0:T(8,128)(2,1)S(1)}, u32[]{:S(2)}, u32[]{:S(2)}) collective-permute-start(bf16[144,1792]{1,0:T(8,128)(2,1)S(1)} %shard_map.76), channel_id=1, source_target_pairs={{0,8},{2,6},{4,0},{6,14},{8,16},{10,2},{12,4},{14,22},{16,24},{18,... | collective-permute-start | bytes 1548296 | tf_op jit(solution)/shard_map/ppermute | solution.py:272
  93.2 5.4 %collective-permute-start.36 = (bf16[144,1792]{1,0:T(8,128)(2,1)S(1)}, bf16[144,1792]{1,0:T(8,128)(2,1)S(1)}, u32[]{:S(2)}, u32[]{:S(2)}) collective-permute-start(bf16[144,1792]{1,0:T(8,128)(2,1)S(1)} %slice.57), channel_id=1, source_target_pairs={{0,2},{2,0},{4,6},{6,4},{8,10},{10,8},{12,14},{14,12},{16,18},{18,... | collective-permute-start | bytes 1548296 | tf_op jit(solution)/shard_map/ppermute | solution.py:260
  94.0 2.1 %collective-permute-start.42 = (bf16[64,1792]{1,0:T(8,128)(2,1)S(1)}, bf16[64,1792]{1,0:T(8,128)(2,1)S(1)}, u32[]{:S(2)}, u32[]{:S(2)}) collective-permute-start(bf16[64,1792]{1,0:T(8,128)(2,1)S(1)} %slice.59), channel_id=1, source_target_pairs={{0,2},{2,0},{4,6},{6,4},{8,10},{10,8},{12,14},{14,12},{16,18},{18,... | collective-permute-start | bytes 688136 | tf_op jit(solution)/shard_map/ppermute | solution.py:260
  94.1 2.0 %collective-permute-start.43 = (bf16[48,1792]{1,0:T(8,128)(2,1)S(1)}, bf16[48,1792]{1,0:T(8,128)(2,1)S(1)}, u32[]{:S(2)}, u32[]{:S(2)}) collective-permute-start(bf16[48,1792]{1,0:T(8,128)(2,1)S(1)} %slice.60), channel_id=1, source_target_pairs={{0,2},{2,0},{4,6},{6,4},{8,10},{10,8},{12,14},{14,12},{16,18},{18,... | collective-permute-start | bytes 516104 | tf_op jit(solution)/shard_map/ppermute | solution.py:260
  96.3 7.3 %collective-permute-start.45 = (bf16[112,1792]{1,0:T(8,128)(2,1)S(1)}, bf16[112,1792]{1,0:T(8,128)(2,1)S(1)}, u32[]{:S(2)}, u32[]{:S(2)}) collective-permute-start(bf16[112,1792]{1,0:T(8,128)(2,1)S(1)} %shard_map.80), channel_id=1, source_target_pairs={{0,8},{2,6},{4,0},{6,14},{8,16},{10,2},{12,4},{14,22},{16,24},{18,... | collective-permute-start | bytes 1204232 | tf_op jit(solution)/shard_map/ppermute | solution.py:272
  98.7 10.4 %collective-permute-start.38 = (bf16[144,1792]{1,0:T(8,128)(2,1)S(1)}, bf16[144,1792]{1,0:T(8,128)(2,1)S(1)}, u32[]{:S(2)}, u32[]{:S(2)}) collective-permute-start(bf16[144,1792]{1,0:T(8,128)(2,1)S(1)} %shard_map.78), channel_id=1, source_target_pairs={{0,8},{2,6},{4,0},{6,14},{8,16},{10,2},{12,4},{14,22},{16,24},{18,... | collective-permute-start | bytes 1548296 | tf_op jit(solution)/shard_map/ppermute | solution.py:272
  100.1 4.4 %collective-permute-start.40 = (bf16[132,512]{1,0:T(8,128)(2,1)S(1)}, bf16[132,512]{1,0:T(8,128)(2,1)S(1)}, u32[]{:S(2)}, u32[]{:S(2)}) collective-permute-start(bf16[132,512]{1,0:T(8,128)(2,1)S(1)} %copy-done.17), channel_id=1, source_target_pairs={{0,1},{1,0},{2,3},{3,2},{4,5},{5,4},{6,7},{7,6},{8,9},{9,8},{10,11... | collective-permute-start | bytes 405512 | tf_op jit(solution)/shard_map/ppermute | solution.py:275
  103.7 9.7 %collective-permute-start.46 = (bf16[112,1792]{1,0:T(8,128)(2,1)S(1)}, bf16[112,1792]{1,0:T(8,128)(2,1)S(1)}, u32[]{:S(2)}, u32[]{:S(2)}) collective-permute-start(bf16[112,1792]{1,0:T(8,128)(2,1)S(1)} %shard_map.81), channel_id=1, source_target_pairs={{0,8},{2,6},{4,0},{6,14},{8,16},{10,2},{12,4},{14,22},{16,24},{18,... | collective-permute-start | bytes 1204232 | tf_op jit(solution)/shard_map/ppermute | solution.py:272
  104.6 5.5 %collective-permute-start.41 = (bf16[132,512]{1,0:T(8,128)(2,1)S(1)}, bf16[132,512]{1,0:T(8,128)(2,1)S(1)}, u32[]{:S(2)}, u32[]{:S(2)}) collective-permute-start(bf16[132,512]{1,0:T(8,128)(2,1)S(1)} %multiply_convert_fusion.3.refs_0_), channel_id=1, source_target_pairs={{0,1},{1,0},{2,3},{3,2},{4,5},{5,4},{6,7},{7,6},{8,9},{9,8},{10,11... | collective-permute-start | bytes 405512 | tf_op jit(solution)/shard_map/ppermute | solution.py:275
  109.3 9.6 %collective-permute-start.39 = (bf16[144,1792]{1,0:T(8,128)(2,1)S(1)}, bf16[144,1792]{1,0:T(8,128)(2,1)S(1)}, u32[]{:S(2)}, u32[]{:S(2)}) collective-permute-start(bf16[144,1792]{1,0:T(8,128)(2,1)S(1)} %shard_map.79), channel_id=1, source_target_pairs={{0,8},{2,6},{4,0},{6,14},{8,16},{10,2},{12,4},{14,22},{16,24},{18,... | collective-permute-start | bytes 1548296 | tf_op jit(solution)/shard_map/ppermute | solution.py:272
  113.5 6.7 %collective-permute-start.47 = (bf16[112,1792]{1,0:T(8,128)(2,1)S(1)}, bf16[112,1792]{1,0:T(8,128)(2,1)S(1)}, u32[]{:S(2)}, u32[]{:S(2)}) collective-permute-start(bf16[112,1792]{1,0:T(8,128)(2,1)S(1)} %add_convert_fusion.1), channel_id=1, source_target_pairs={{0,2},{2,0},{4,6},{6,4},{8,10},{10,8},{12,14},{14,12},{16,18},{18,... | collective-permute-start | bytes 1204232 | tf_op jit(solution)/shard_map/ppermute | solution.py:260
  119.0 2.2 %collective-permute-start.48 = (bf16[16,1792]{1,0:T(8,128)(2,1)S(1)}, bf16[16,1792]{1,0:T(8,128)(2,1)S(1)}, u32[]{:S(2)}, u32[]{:S(2)}) collective-permute-start(bf16[16,1792]{1,0:T(8,128)(2,1)S(1)} %add_convert_fusion.2), channel_id=1, source_target_pairs={{0,2},{2,0},{4,6},{6,4},{8,10},{10,8},{12,14},{14,12},{16,18},{18,... | collective-permute-start | bytes 172040 | tf_op jit(solution)/shard_map/ppermute | solution.py:260
  (19 other events, 89.0 us)

commit v5 on v4

--- a/solution.py
+++ b/solution.py
@@ -315,7 +315,7 @@
         return call(functools.partial(join_kernel, rows[0]), out, *args)[0]
 
     sibling = to_core(grad_out)
-    moving = to_ring(jnp.concatenate([grad_out, sibling], axis=0))
+    moving = jnp.concatenate([to_ring(grad_out), to_ring(sibling)], axis=0)
     (table,) = call(table_kernel, [(token_n, TABLE)], routes.T, gate_weights.T)
     tables = [table, to_core(table)]
     blocks = [[jnp.concatenate(x, axis=1) for x in zip([grad_out, sibling], tables)]]
@@ -329,9 +329,11 @@
     partials, mines, ups = [down(0)], {}, {}
     sents = [None]
     for k in range(1, far + 1):
-        ended = [partials[k - 1][0]]
+        ended = [partials[k - 1][0]] if k > 1 else []
+        if k == 2:
+            ended += [partials[0][0], act_peer]
         if k < far:
-            ended += [act_peer if k == 1 else sents[k - 1]]
+            ended += [acts[0] if k == 1 else sents[k - 1]]
         if k == far - 1:
             ended += [early]
         here = after(moving, *ended)
@@ -356,14 +358,16 @@
     full = after(sents[far], ups[far - 3][0], *swapped[0], *swapped[1])
     keep, give = up(far, partials[far][0], full, acts[far], act_peer)
     peer = to_side(after(mines[far - 1], full))
-    total = join((0, 2 * token_n), half, keep, *parts_to_core(give, 64))
+    total = join((0, 2 * token_n), half, keep, *parts_to_core(give, 128))
     came = to_ring(total)
     came = [came[a:b] for a, b in streams]
     peer = after(peer, total)
     for k in range(far - 1, 0, -1):
+        if k == far - 1:
+            mines[k - 1] = middle(k - 1, after(sents[k - 1], peer))
+            mines[k] = after(mines[k], mines[k - 1])
         keep, give = ups[k] if k in ups else up(k, mines[k], peer)
         if k == far - 1:
-            mines[k - 1] = middle(k - 1, after(sents[k - 1], peer))
             peer = to_side(mines[k - 1])
         elif k == far - 2:
             mines[0] = middle(0, to_side(after(partials[0][1], peer)))

time: 123 us -> 120 us (0.976)
  waiting for transfers between devices: 51.6 us -> 46.3 us
  starting transfers between devices: 40.1 us -> 42.5 us
  other arithmetic: 5.09 us -> 2.85 us
  local copies, waits for them, and re-layouts: 2.65 us -> 4.54 us
    ppermute x12 -> x13, waiting for transfers between devices: 23 us -> 20.5 us  [to_ring(): return lax.ppermute(x, 'ep', ring_pairs)]
    ppermute x12 -> x13, starting transfers between devices: 13.7 us -> 16.1 us  [to_ring(): return lax.ppermute(x, 'ep', ring_pairs)]
    ppermute x10, waiting for transfers between devices: 19.4 us -> 17.4 us  [to_side(): return lax.ppermute(x, 'tp', [(0, 1), (1, 0)])]
    unnamed x36 -> x38, local copies, waits for them, and re-layouts: 2.09 us -> 3.98 us
    ppermute x27 -> x25, waiting for transfers between devices: 9.17 us -> 8.42 us  [parts_to_core(): lax.ppermute(p, 'ep', swap)]
    ppermute x27 -> x25, starting transfers between devices: 15.8 us -> 15.9 us  [parts_to_core(): lax.ppermute(p, 'ep', swap)]
  transfers between devices with their start and end apart: 49 -> 48, of which waited for: 29 -> 26; matrix products, arithmetic and copies ran while one was open for 3% -> 2% of each run, Pallas kernels for 17% -> 17%
where the time goes in v5:
time: 120 us; the launch traced here: 119 us
  waiting for transfers between devices  46.3 us (39%)
  starting transfers between devices  42.5 us (35%)
  Pallas kernels  22.1 us (18%)
  local copies, waits for them, and re-layouts  4.54 us (4%)
  other arithmetic  2.85 us (2%)
    pallas_call x19, Pallas kernels, call(): pl.pallas_call(kernel, out_shape=[jax.ShapeDtypeStruct(shape, BF16) for s...  22.1 us
    ppermute x13, waiting for transfers between devices, to_ring(): return lax.ppermute(x, 'ep', ring_pairs)  20.5 us
    ppermute x10, waiting for transfers between devices, to_side(): return lax.ppermute(x, 'tp', [(0, 1), (1, 0)])  17.4 us
    ppermute x13, starting transfers between devices, to_ring(): return lax.ppermute(x, 'ep', ring_pairs)  16.1 us
    ppermute x25, starting transfers between devices, parts_to_core(): lax.ppermute(p, 'ep', swap)  15.9 us
    ppermute x10, starting transfers between devices, to_side(): return lax.ppermute(x, 'tp', [(0, 1), (1, 0)])  10.5 us
    ppermute x25, waiting for transfers between devices, parts_to_core(): lax.ppermute(p, 'ep', swap)  8.42 us
    unnamed x38, local copies, waits for them, and re-layouts  3.98 us
  transfers between devices with their start and end apart: 48, of which 26 were waited for; matrix products, arithmetic and copies ran while one was open for 2% of the time, Pallas kernels for 17%

profile of v5, /device:TPU:13, one launch (start us, length us, event | category | flops | bytes accessed | tf_op | source)
XLA Modules:
  0.0 118.7 jit_solution(7201084426797313827)
XLA Ops:
  0.7 1.3 %collective-permute-start = (bf16[128,1792]{1,0:T(8,128)(2,1)}, bf16[128,1792]{1,0:T(8,128)(2,1)S(1)}, u32[]{:S(2)}, u32[]{:S(2)}) collective-permute-start(bf16[128,1792]{1,0:T(8,128)(2,1)} %param.6), channel_id=1, source_target_pairs={{0,8},{2,6},{4,0},{6,14},{8,16},{10,2},{12,4},{14,22},{16,24},{18,... | collective-permute-start | bytes 1376264 | tf_op jit(solution)/shard_map/ppermute | solution.py:272
  2.3 1.3 %collective-permute-start.2 = (bf16[128,1792]{1,0:T(8,128)(2,1)S(1)}, bf16[128,1792]{1,0:T(8,128)(2,1)S(1)}, u32[]{:S(2)}, u32[]{:S(2)}) collective-permute-start(bf16[128,1792]{1,0:T(8,128)(2,1)S(1)} %collective-permute-done.1), channel_id=1, source_target_pairs={{0,8},{2,6},{4,0},{6,14},{8,16},{10,2},{12,4},{14,22},{16,24},{18,... | collective-permute-start | bytes 1376264 | tf_op jit(solution)/shard_map/ppermute | solution.py:272
  5.3 1.2 %collective-permute-done.3 = bf16[128,128]{1,0:T(8,128)(2,1)S(1)} collective-permute-done((bf16[128,128]{1,0:T(8,128)(2,1)S(1)}, bf16[128,128]{1,0:T(8,128)(2,1)S(1)}, u32[]{:S(2)}, u32[]{:S(2)}) %collective-permute-start.3) | collective-permute-done | bytes 32800 | tf_op jit(solution)/shard_map/ppermute | solution.py:260
  6.5 1.3 %collective-permute-start.4 = (bf16[256,128]{1,0:T(8,128)(2,1)S(1)}, bf16[256,128]{1,0:T(8,128)(2,1)S(1)}, u32[]{:S(2)}, u32[]{:S(2)}) collective-permute-start(bf16[256,128]{1,0:T(8,128)(2,1)S(1)} %pad_maximum_fusion.8), channel_id=1, source_target_pairs={{0,8},{2,6},{4,0},{6,14},{8,16},{10,2},{12,4},{14,22},{16,24},{18,... | collective-permute-start | bytes 196616 | tf_op jit(solution)/shard_map/ppermute | solution.py:272
  7.8 1.2 %copy-done.3 = bf16[1,1056,512]{2,1,0:T(8,128)(2,1)S(1)} copy-done((bf16[1,1056,512]{2,1,0:T(8,128)(2,1)S(1)}, bf16[1,1056,512]{2,1,0:T(8,128)(2,1)}, u32[]{:S(2)}) %copy-start.3) | copy-done | bytes 1081368
  9.0 1.6 %shard_map.65 = (bf16[132,512]{1,0:T(8,128)(2,1)S(1)}, bf16[264,512]{1,0:T(8,128)(2,1)S(1)}, bf16[264,512]{1,0:T(8,128)(2,1)S(1)}, bf16[264,512]{1,0:T(8,128)(2,1)S(1)}, bf16[132,512]{1,0:T(8,128)(2,1)S(1)}) custom-call(bf16[1056,512]{1,0:T(8,128)(2,1)S(1)} %bitcast.15), custom_call_target="tpu_custom_call" | custom-call | tf_op jit(solution)/shard_map/pallas_call | solution.py:278
  10.7 3.4 %collective-permute-done.4 = bf16[256,128]{1,0:T(8,128)(2,1)S(1)} collective-permute-done((bf16[256,128]{1,0:T(8,128)(2,1)S(1)}, bf16[256,128]{1,0:T(8,128)(2,1)S(1)}, u32[]{:S(2)}, u32[]{:S(2)}) %collective-permute-start.4) | collective-permute-done | bytes 65568 | tf_op jit(solution)/shard_map/ppermute | solution.py:272
  15.3 1.3 %collective-permute-start.9 = (bf16[256,1920]{1,0:T(8,128)(2,1)S(1)}, bf16[256,1920]{1,0:T(8,128)(2,1)S(1)}, u32[]{:S(2)}, u32[]{:S(2)}) collective-permute-start(bf16[256,1920]{1,0:T(8,128)(2,1)S(1)} %pad_maximum_fusion.refs_0_), channel_id=1, source_target_pairs={{0,8},{2,6},{4,0},{6,14},{8,16},{10,2},{12,4},{14,22},{16,24},{18,... | collective-permute-start | bytes 2949128 | tf_op jit(solution)/shard_map/ppermute | solution.py:272
  16.6 1.2 %collective-permute-start.10 = (bf16[132,512]{1,0:T(8,128)(2,1)S(1)}, bf16[132,512]{1,0:T(8,128)(2,1)S(1)}, u32[]{:S(2)}, u32[]{:S(2)}) collective-permute-start(bf16[132,512]{1,0:T(8,128)(2,1)S(1)} %get-tuple-element.60.refs_2_), channel_id=1, source_target_pairs={{0,1},{1,0},{2,3},{3,2},{4,5},{5,4},{6,7},{7,6},{8,9},{9,8},{10,11... | collective-permute-start | bytes 405512 | tf_op jit(solution)/shard_map/ppermute | solution.py:275
  17.9 1.8 %shard_map.66 = (bf16[264,512]{1,0:T(8,128)(2,1)S(1)}, bf16[264,512]{1,0:T(8,128)(2,1)S(1)}, bf16[512,128]{1,0:T(8,128)(2,1)S(1)}) custom-call(bf16[256,1920]{1,0:T(8,128)(2,1)S(1)} %pad_maximum_fusion.refs_0_, bf16[256,1920]{1,0:T(8,128)(2,1)S(1)} %pad_maximum_fusion.1.refs_1_, bf16[1024,1792]{1,0:T(8,128)(2,1)S(1)} %bitcast.5), custom_call_target="tpu_custom_call" | custom-call | tf_op jit(solution)/shard_map/pallas_call | solution.py:278
  20.8 1.7 %shard_map.67 = (bf16[132,512]{1,0:T(8,128)(2,1)S(1)}, bf16[132,512]{1,0:T(8,128)(2,1)S(1)}, bf16[256,128]{1,0:T(8,128)(2,1)S(1)}) custom-call(bf16[128,1920]{1,0:T(8,128)(2,1)S(1)} %pad_maximum_fusion.6.refs_0_, bf16[128,1920]{1,0:T(8,128)(2,1)S(1)} %pad_maximum_fusion.7.refs_1_, bf16[1024,1792]{1,0:T(8,128)(2,1)S(1)} %bitcast.6), custom_call_target="tpu_custom_call" | custom-call | tf_op jit(solution)/shard_map/pallas_call | solution.py:278
  23.2 4.8 %collective-permute-done.7 = bf16[264,512]{1,0:T(8,128)(2,1)S(1)} collective-permute-done((bf16[264,512]{1,0:T(8,128)(2,1)S(1)}, bf16[264,512]{1,0:T(8,128)(2,1)S(1)}, u32[]{:S(2)}, u32[]{:S(2)}) %collective-permute-start.7) | collective-permute-done | bytes 270368 | tf_op jit(solution)/shard_map/ppermute | solution.py:275
  28.6 1.4 %collective-permute-start.12 = (bf16[128,1920]{1,0:T(8,128)(2,1)S(1)}, bf16[128,1920]{1,0:T(8,128)(2,1)S(1)}, u32[]{:S(2)}, u32[]{:S(2)}) collective-permute-start(bf16[128,1920]{1,0:T(8,128)(2,1)S(1)} %get-tuple-element.103), channel_id=1, source_target_pairs={{0,2},{2,0},{4,6},{6,4},{8,10},{10,8},{12,14},{14,12},{16,18},{18,... | collective-permute-start | bytes 1474568 | tf_op jit(solution)/shard_map/ppermute | solution.py:260
  30.1 1.3 %collective-permute-start.11 = (bf16[256,1920]{1,0:T(8,128)(2,1)S(1)}, bf16[256,1920]{1,0:T(8,128)(2,1)S(1)}, u32[]{:S(2)}, u32[]{:S(2)}) collective-permute-start(bf16[256,1920]{1,0:T(8,128)(2,1)S(1)} %collective-permute-done.9.refs_0_), channel_id=1, source_target_pairs={{0,8},{2,6},{4,0},{6,14},{8,16},{10,2},{12,4},{14,22},{16,24},{18,... | collective-permute-start | bytes 2949128 | tf_op jit(solution)/shard_map/ppermute | solution.py:272
  31.4 1.2 %collective-permute-start.8 = (bf16[264,512]{1,0:T(8,128)(2,1)S(1)}, bf16[264,512]{1,0:T(8,128)(2,1)S(1)}, u32[]{:S(2)}, u32[]{:S(2)}) collective-permute-start(bf16[264,512]{1,0:T(8,128)(2,1)S(1)} %multiply_convert_fusion.2.refs_0_), channel_id=1, source_target_pairs={{0,1},{1,0},{2,3},{3,2},{4,5},{5,4},{6,7},{7,6},{8,9},{9,8},{10,11... | collective-permute-start | bytes 811016 | tf_op jit(solution)/shard_map/ppermute | solution.py:275
  32.7 2.6 %shard_map.68 = (bf16[264,512]{1,0:T(8,128)(2,1)S(1)}, bf16[264,512]{1,0:T(8,128)(2,1)}, bf16[512,128]{1,0:T(8,128)(2,1)S(1)}) custom-call(bf16[256,1920]{1,0:T(8,128)(2,1)S(1)} %collective-permute-done.9.refs_0_, bf16[256,1920]{1,0:T(8,128)(2,1)S(1)} %pad_maximum_fusion.2.refs_1_, bf16[1024,1792]{1,0:T(8,128)(2,1)S(1)} %bitcast.7), custom_call_target="tpu_custom_call" | custom-call | tf_op jit(solution)/shard_map/pallas_call | solution.py:278
  36.7 3.1 %collective-permute-done.8.refs_1_ = bf16[264,512]{1,0:T(8,128)(2,1)S(1)} collective-permute-done((bf16[264,512]{1,0:T(8,128)(2,1)S(1)}, bf16[264,512]{1,0:T(8,128)(2,1)S(1)}, u32[]{:S(2)}, u32[]{:S(2)}) %collective-permute-start.8) | collective-permute-done | bytes 270368 | tf_op jit(solution)/shard_map/ppermute | solution.py:275
  39.8 5.9 %collective-permute-done.14 = bf16[264,512]{1,0:T(8,128)(2,1)} collective-permute-done((bf16[264,512]{1,0:T(8,128)(2,1)}, bf16[264,512]{1,0:T(8,128)(2,1)}, u32[]{:S(2)}, u32[]{:S(2)}) %collective-permute-start.14) | collective-permute-done | bytes 270368 | tf_op jit(solution)/shard_map/ppermute | solution.py:275
  46.5 1.5 %collective-permute-start.15 = (bf16[256,1024]{1,0:T(8,128)(2,1)S(1)}, bf16[256,1024]{1,0:T(8,128)(2,1)S(1)}, u32[]{:S(2)}, u32[]{:S(2)}) collective-permute-start(bf16[256,1024]{1,0:T(8,128)(2,1)S(1)} %pad_maximum_fusion.4), channel_id=1, source_target_pairs={{0,8},{2,6},{4,0},{6,14},{8,16},{10,2},{12,4},{14,22},{16,24},{18,... | collective-permute-start | bytes 1572872 | tf_op jit(solution)/shard_map/ppermute | solution.py:272
  48.6 1.9 %shard_map.69 = (bf16[264,512]{1,0:T(8,128)(2,1)S(1)}, bf16[264,512]{1,0:T(8,128)(2,1)S(1)}, bf16[512,128]{1,0:T(8,128)(2,1)S(1)}) custom-call(bf16[256,1920]{1,0:T(8,128)(2,1)S(1)} %collective-permute-done.11.refs_0_, bf16[256,1920]{1,0:T(8,128)(2,1)S(1)} %pad_maximum_fusion.3.refs_1_, bf16[1024,1792]{1,0:T(8,128)(2,1)S(1)} %bitcast.8), custom_call_target="tpu_custom_call" | custom-call | tf_op jit(solution)/shard_map/pallas_call | solution.py:278
  50.5 1.3 %collective-permute-start.22 = (bf16[264,512]{1,0:T(8,128)(2,1)S(1)}, bf16[264,512]{1,0:T(8,128)(2,1)S(1)}, u32[]{:S(2)}, u32[]{:S(2)}) collective-permute-start(bf16[264,512]{1,0:T(8,128)(2,1)S(1)} %get-tuple-element.68), channel_id=1, source_target_pairs={{0,1},{1,0},{2,3},{3,2},{4,5},{5,4},{6,7},{7,6},{8,9},{9,8},{10,11... | collective-permute-start | bytes 811016 | tf_op jit(solution)/shard_map/ppermute | solution.py:275
  51.7 3.3 %collective-permute-done.15.refs_0_ = bf16[256,1024]{1,0:T(8,128)(2,1)S(1)} collective-permute-done((bf16[256,1024]{1,0:T(8,128)(2,1)S(1)}, bf16[256,1024]{1,0:T(8,128)(2,1)S(1)}, u32[]{:S(2)}, u32[]{:S(2)}) %collective-permute-start.15) | collective-permute-done | bytes 524320 | tf_op jit(solution)/shard_map/ppermute | solution.py:272
  55.1 1.3 %collective-permute-start.18 = (bf16[64,1024]{1,0:T(8,128)(2,1)S(1)}, bf16[64,1024]{1,0:T(8,128)(2,1)S(1)}, u32[]{:S(2)}, u32[]{:S(2)}) collective-permute-start(bf16[64,1024]{1,0:T(8,128)(2,1)S(1)} %get-tuple-element.109), channel_id=1, source_target_pairs={{0,2},{2,0},{4,6},{6,4},{8,10},{10,8},{12,14},{14,12},{16,18},{18,... | collective-permute-start | bytes 393224 | tf_op jit(solution)/shard_map/ppermute | solution.py:260
  58.5 1.7 %shard_map.70 = (bf16[132,1024]{1,0:T(8,128)(2,1)S(1)}, bf16[256,128]{1,0:T(8,128)(2,1)S(1)}) custom-call(bf16[256,1024]{1,0:T(8,128)(2,1)S(1)} %collective-permute-done.15.refs_0_, bf16[256,1024]{1,0:T(8,128)(2,1)S(1)} %pad_maximum_fusion.5.refs_1_, bf16[1024,1792]{1,0:T(8,128)(2,1)S(1)} %bitcast.9), custom_call_target="tpu_custom_call" | custom-call | tf_op jit(solution)/shard_map/pallas_call | solution.py:278
  60.2 1.3 %collective-permute-start.25 = (bf16[132,1024]{1,0:T(8,128)(2,1)S(1)}, bf16[132,1024]{1,0:T(8,128)(2,1)S(1)}, u32[]{:S(2)}, u32[]{:S(2)}) collective-permute-start(bf16[132,1024]{1,0:T(8,128)(2,1)S(1)} %get-tuple-element.71.refs_0_), channel_id=1, source_target_pairs={{0,1},{1,0},{2,3},{3,2},{4,5},{5,4},{6,7},{7,6},{8,9},{9,8},{10,11... | collective-permute-start | bytes 811016 | tf_op jit(solution)/shard_map/ppermute | solution.py:275
  61.5 1.9 %shard_map.71 = (bf16[256,1792]{1,0:T(8,128)(2,1)S(1)}, bf16[256,1792]{1,0:T(8,128)(2,1)S(1)}) custom-call(bf16[512,128]{1,0:T(8,128)(2,1)S(1)} %copy-done.13, bf16[264,512]{1,0:T(8,128)(2,1)S(1)} %multiply_convert_fusion.2.refs_0_, bf16[264,512]{1,0:T(8,128)(2,1)S(1)} %collective-permute-done.8.refs_1_, bf16[1792,1024]{1,0:T(8,128)(2,1)S(1)} %bitcast.10), custom_call_target="tpu_custom_call" | custom-call | tf_op jit(solution)/shard_map/pallas_call | solution.py:278
  63.4 1.4 %collective-permute-start.23 = (bf16[80,1792]{1,0:T(8,128)(2,1)S(1)}, bf16[80,1792]{1,0:T(8,128)(2,1)S(1)}, u32[]{:S(2)}, u32[]{:S(2)}) collective-permute-start(bf16[80,1792]{1,0:T(8,128)(2,1)S(1)} %slice.49), channel_id=1, source_target_pairs={{0,2},{2,0},{4,6},{6,4},{8,10},{10,8},{12,14},{14,12},{16,18},{18,... | collective-permute-start | bytes 860168 | tf_op jit(solution)/shard_map/ppermute | solution.py:260
  65.5 1.4 %collective-permute-done.27.refs_1_ = bf16[48,1792]{1,0:T(8,128)(2,1)S(1)} collective-permute-done((bf16[48,1792]{1,0:T(8,128)(2,1)S(1)}, bf16[48,1792]{1,0:T(8,128)(2,1)S(1)}, u32[]{:S(2)}, u32[]{:S(2)}) %collective-permute-start.27) | collective-permute-done | bytes 172064 | tf_op jit(solution)/shard_map/ppermute | solution.py:260
  67.3 1.2 %collective-permute-start.28 = (bf16[264,512]{1,0:T(8,128)(2,1)S(1)}, bf16[264,512]{1,0:T(8,128)(2,1)S(1)}, u32[]{:S(2)}, u32[]{:S(2)}) collective-permute-start(bf16[264,512]{1,0:T(8,128)(2,1)S(1)} %multiply_convert_fusion.1.refs_0_), channel_id=1, source_target_pairs={{0,1},{1,0},{2,3},{3,2},{4,5},{5,4},{6,7},{7,6},{8,9},{9,8},{10,11... | collective-permute-start | bytes 811016 | tf_op jit(solution)/shard_map/ppermute | solution.py:275
  68.6 2.1 %shard_map.72 = (bf16[256,896]{1,0:T(8,128)(2,1)S(1)}, bf16[256,896]{1,0:T(8,128)(2,1)S(1)}) custom-call(bf16[256,128]{1,0:T(8,128)(2,1)S(1)} %get-tuple-element.78.table_ref, bf16[132,1024]{1,0:T(8,128)(2,1)S(1)} %get-tuple-element.71.refs_0_, bf16[132,1024]{1,0:T(8,128)(2,1)S(1)} %collective-permute-done.25.refs_1_, ...), custom_call_target="tpu_custom_call" | custom-call | tf_op jit(solution)/shard_map/pallas_call | solution.py:278
  70.7 2.3 %collective-permute-start.30 = (bf16[128,896]{1,0:T(8,128)(2,1)S(1)}, bf16[128,896]{1,0:T(8,128)(2,1)S(1)}, u32[]{:S(2)}, u32[]{:S(2)}) collective-permute-start(bf16[128,896]{1,0:T(8,128)(2,1)S(1)} %get-tuple-element.113), channel_id=1, source_target_pairs={{0,2},{2,0},{4,6},{6,4},{8,10},{10,8},{12,14},{14,12},{16,18},{18,... | collective-permute-start | bytes 688136 | tf_op jit(solution)/shard_map/ppermute | solution.py:260
  74.6 1.4 %collective-permute-start.33 = (bf16[256,896]{1,0:T(8,128)(2,1)S(1)}, bf16[256,896]{1,0:T(8,128)(2,1)S(1)}, u32[]{:S(2)}, u32[]{:S(2)}) collective-permute-start(bf16[256,896]{1,0:T(8,128)(2,1)S(1)} %shard_map.73), channel_id=1, source_target_pairs={{0,8},{2,6},{4,0},{6,14},{8,16},{10,2},{12,4},{14,22},{16,24},{18,... | collective-permute-start | bytes 1376264 | tf_op jit(solution)/shard_map/ppermute | solution.py:272
  77.0 1.9 %shard_map.74 = (bf16[256,1792]{1,0:T(8,128)(2,1)S(1)}, bf16[256,1792]{1,0:T(8,128)(2,1)S(1)}) custom-call(bf16[512,128]{1,0:T(8,128)(2,1)S(1)} %get-tuple-element.84.table_ref, bf16[264,512]{1,0:T(8,128)(2,1)S(1)} %multiply_convert_fusion.1.refs_0_, bf16[264,512]{1,0:T(8,128)(2,1)S(1)} %collective-permute-done.28.refs_1_, bf16[1792,1024]{1,0:T(8,128)(2,1)S(1)} %bitcast.12), custom_call_target="tpu_custom_call" | custom-call | tf_op jit(solution)/shard_map/pallas_call | solution.py:278
  80.7 1.6 %collective-permute-done.33 = bf16[256,896]{1,0:T(8,128)(2,1)S(1)} collective-permute-done((bf16[256,896]{1,0:T(8,128)(2,1)S(1)}, bf16[256,896]{1,0:T(8,128)(2,1)S(1)}, u32[]{:S(2)}, u32[]{:S(2)}) %collective-permute-start.33) | collective-permute-done | bytes 458784 | tf_op jit(solution)/shard_map/ppermute | solution.py:272
  82.5 1.4 %collective-permute-start.43 = (bf16[112,1792]{1,0:T(8,128)(2,1)S(1)}, bf16[112,1792]{1,0:T(8,128)(2,1)S(1)}, u32[]{:S(2)}, u32[]{:S(2)}) collective-permute-start(bf16[112,1792]{1,0:T(8,128)(2,1)S(1)} %shard_map.75), channel_id=1, source_target_pairs={{0,8},{2,6},{4,0},{6,14},{8,16},{10,2},{12,4},{14,22},{16,24},{18,... | collective-permute-start | bytes 1204232 | tf_op jit(solution)/shard_map/ppermute | solution.py:272
  84.3 3.1 %collective-permute-done.31.refs_1_ = bf16[264,512]{1,0:T(8,128)(2,1)S(1)} collective-permute-done((bf16[264,512]{1,0:T(8,128)(2,1)S(1)}, bf16[264,512]{1,0:T(8,128)(2,1)S(1)}, u32[]{:S(2)}, u32[]{:S(2)}) %collective-permute-start.31) | collective-permute-done | bytes 270368 | tf_op jit(solution)/shard_map/ppermute | solution.py:275
  87.5 1.9 %shard_map.77 = (bf16[256,1792]{1,0:T(8,128)(2,1)S(1)}, bf16[256,1792]{1,0:T(8,128)(2,1)S(1)}) custom-call(bf16[512,128]{1,0:T(8,128)(2,1)S(1)} %copy-done.11, bf16[264,512]{1,0:T(8,128)(2,1)S(1)} %multiply_convert_fusion.refs_0_, bf16[264,512]{1,0:T(8,128)(2,1)S(1)} %collective-permute-done.31.refs_1_, bf16[1792,1024]{1,0:T(8,128)(2,1)S(1)} %bitcast.13), custom_call_target="tpu_custom_call" | custom-call | tf_op jit(solution)/shard_map/pallas_call | solution.py:278
  91.2 1.4 %collective-permute-done.42.refs_1_ = bf16[48,1792]{1,0:T(8,128)(2,1)S(1)} collective-permute-done((bf16[48,1792]{1,0:T(8,128)(2,1)S(1)}, bf16[48,1792]{1,0:T(8,128)(2,1)S(1)}, u32[]{:S(2)}, u32[]{:S(2)}) %collective-permute-start.42) | collective-permute-done | bytes 172064 | tf_op jit(solution)/shard_map/ppermute | solution.py:260
  95.3 1.6 %collective-permute-start.37 = (bf16[144,1792]{1,0:T(8,128)(2,1)S(1)}, bf16[144,1792]{1,0:T(8,128)(2,1)S(1)}, u32[]{:S(2)}, u32[]{:S(2)}) collective-permute-start(bf16[144,1792]{1,0:T(8,128)(2,1)S(1)} %shard_map.78), channel_id=1, source_target_pairs={{0,8},{2,6},{4,0},{6,14},{8,16},{10,2},{12,4},{14,22},{16,24},{18,... | collective-permute-start | bytes 1548296 | tf_op jit(solution)/shard_map/ppermute | solution.py:272
  97.1 2.7 %collective-permute-done.44.refs_2_ = bf16[112,1792]{1,0:T(8,128)(2,1)S(1)} collective-permute-done((bf16[112,1792]{1,0:T(8,128)(2,1)S(1)}, bf16[112,1792]{1,0:T(8,128)(2,1)S(1)}, u32[]{:S(2)}, u32[]{:S(2)}) %collective-permute-start.44) | collective-permute-done | bytes 401440 | tf_op jit(solution)/shard_map/ppermute | solution.py:272
  100.0 1.2 collective-permute-start.45
  101.2 1.3 %collective-permute-start.40 = (bf16[132,512]{1,0:T(8,128)(2,1)S(1)}, bf16[132,512]{1,0:T(8,128)(2,1)S(1)}, u32[]{:S(2)}, u32[]{:S(2)}) collective-permute-start(bf16[132,512]{1,0:T(8,128)(2,1)S(1)} %multiply_convert_fusion.3.refs_0_), channel_id=1, source_target_pairs={{0,1},{1,0},{2,3},{3,2},{4,5},{5,4},{6,7},{7,6},{8,9},{9,8},{10,11... | collective-permute-start | bytes 405512 | tf_op jit(solution)/shard_map/ppermute | solution.py:275
  102.5 2.8 %collective-permute-done.37.refs_2_ = bf16[144,1792]{1,0:T(8,128)(2,1)S(1)} collective-permute-done((bf16[144,1792]{1,0:T(8,128)(2,1)S(1)}, bf16[144,1792]{1,0:T(8,128)(2,1)S(1)}, u32[]{:S(2)}, u32[]{:S(2)}) %collective-permute-start.37) | collective-permute-done | bytes 516128 | tf_op jit(solution)/shard_map/ppermute | solution.py:272
  105.6 1.2 collective-permute-start.38
  106.7 1.7 %shard_map.82 = (bf16[128,1792]{1,0:T(8,128)(2,1)S(1)}, bf16[128,1792]{1,0:T(8,128)(2,1)S(1)}) custom-call(bf16[256,128]{1,0:T(8,128)(2,1)S(1)} %get-tuple-element.91.table_ref, bf16[132,512]{1,0:T(8,128)(2,1)S(1)} %multiply_convert_fusion.3.refs_0_, bf16[132,512]{1,0:T(8,128)(2,1)S(1)} %collective-permute-done.40.refs_1_, bf16[1792,1024]{1,0:T(8,128)(2,1)S(1)} %bitcast.14), custom_call_target="tpu_custom_call" | custom-call | tf_op jit(solution)/shard_map/pallas_call | solution.py:278
  109.8 1.6 %collective-permute-start.46 = (bf16[112,1792]{1,0:T(8,128)(2,1)S(1)}, bf16[112,1792]{1,0:T(8,128)(2,1)S(1)}, u32[]{:S(2)}, u32[]{:S(2)}) collective-permute-start(bf16[112,1792]{1,0:T(8,128)(2,1)S(1)} %add_convert_fusion.1), channel_id=1, source_target_pairs={{0,2},{2,0},{4,6},{6,4},{8,10},{10,8},{12,14},{14,12},{16,18},{18,... | collective-permute-start | bytes 1204232 | tf_op jit(solution)/shard_map/ppermute | solution.py:260
  111.4 3.8 %collective-permute-done.38 = bf16[144,1792]{1,0:T(8,128)(2,1)S(1)} collective-permute-done((bf16[144,1792]{1,0:T(8,128)(2,1)S(1)}, bf16[144,1792]{1,0:T(8,128)(2,1)S(1)}, u32[]{:S(2)}, u32[]{:S(2)}) %collective-permute-start.38) | collective-permute-done | bytes 516128 | tf_op jit(solution)/shard_map/ppermute | solution.py:272
  115.2 1.6 %collective-permute-start.47 = (bf16[16,1792]{1,0:T(8,128)(2,1)S(1)}, bf16[16,1792]{1,0:T(8,128)(2,1)S(1)}, u32[]{:S(2)}, u32[]{:S(2)}) collective-permute-start(bf16[16,1792]{1,0:T(8,128)(2,1)S(1)} %add_convert_fusion.2), channel_id=1, source_target_pairs={{0,2},{2,0},{4,6},{6,4},{8,10},{10,8},{12,14},{14,12},{16,18},{18,... | collective-permute-start | bytes 172040 | tf_op jit(solution)/shard_map/ppermute | solution.py:260
  (138 shorter events, 25.7 us)
Async XLA Ops:
  0.0 2.3 %collective-permute-start.1 = (bf16[128,1792]{1,0:T(8,128)(2,1)}, bf16[128,1792]{1,0:T(8,128)(2,1)S(1)}, u32[]{:S(2)}, u32[]{:S(2)}) collective-permute-start(bf16[128,1792]{1,0:T(8,128)(2,1)} %param.6), channel_id=1, source_target_pairs={{0,2},{2,0},{4,6},{6,4},{8,10},{10,8},{12,14},{14,12},{16,18},{18,... | collective-permute-start | bytes 1376264 | tf_op jit(solution)/shard_map/ppermute | solution.py:260
  0.7 13.5 %collective-permute-start = (bf16[128,1792]{1,0:T(8,128)(2,1)}, bf16[128,1792]{1,0:T(8,128)(2,1)S(1)}, u32[]{:S(2)}, u32[]{:S(2)}) collective-permute-start(bf16[128,1792]{1,0:T(8,128)(2,1)} %param.6), channel_id=1, source_target_pairs={{0,8},{2,6},{4,0},{6,14},{8,16},{10,2},{12,4},{14,22},{16,24},{18,... | collective-permute-start | bytes 1376264 | tf_op jit(solution)/shard_map/ppermute | solution.py:272
  2.3 11.8 %collective-permute-start.2 = (bf16[128,1792]{1,0:T(8,128)(2,1)S(1)}, bf16[128,1792]{1,0:T(8,128)(2,1)S(1)}, u32[]{:S(2)}, u32[]{:S(2)}) collective-permute-start(bf16[128,1792]{1,0:T(8,128)(2,1)S(1)} %collective-permute-done.1), channel_id=1, source_target_pairs={{0,8},{2,6},{4,0},{6,14},{8,16},{10,2},{12,4},{14,22},{16,24},{18,... | collective-permute-start | bytes 1376264 | tf_op jit(solution)/shard_map/ppermute | solution.py:272
  5.2 1.3 %collective-permute-start.3 = (bf16[128,128]{1,0:T(8,128)(2,1)S(1)}, bf16[128,128]{1,0:T(8,128)(2,1)S(1)}, u32[]{:S(2)}, u32[]{:S(2)}) collective-permute-start(bf16[128,128]{1,0:T(8,128)(2,1)S(1)} %shard_map.64), channel_id=1, source_target_pairs={{0,2},{2,0},{4,6},{6,4},{8,10},{10,8},{12,14},{14,12},{16,18},{18,... | collective-permute-start | bytes 98312 | tf_op jit(solution)/shard_map/ppermute | solution.py:260
  6.5 7.6 %collective-permute-start.4 = (bf16[256,128]{1,0:T(8,128)(2,1)S(1)}, bf16[256,128]{1,0:T(8,128)(2,1)S(1)}, u32[]{:S(2)}, u32[]{:S(2)}) collective-permute-start(bf16[256,128]{1,0:T(8,128)(2,1)S(1)} %pad_maximum_fusion.8), channel_id=1, source_target_pairs={{0,8},{2,6},{4,0},{6,14},{8,16},{10,2},{12,4},{14,22},{16,24},{18,... | collective-permute-start | bytes 196616 | tf_op jit(solution)/shard_map/ppermute | solution.py:272
  14.3 3.5 %collective-permute-start.5 = (bf16[128,1920]{1,0:T(8,128)(2,1)S(1)}, bf16[128,1920]{1,0:T(8,128)(2,1)S(1)}, u32[]{:S(2)}, u32[]{:S(2)}) collective-permute-start(bf16[128,1920]{1,0:T(8,128)(2,1)S(1)} %get-tuple-element.105), channel_id=1, source_target_pairs={{0,2},{2,0},{4,6},{6,4},{8,10},{10,8},{12,14},{14,12},{16,18},{18,... | collective-permute-start | bytes 1474568 | tf_op jit(solution)/shard_map/ppermute | solution.py:260
  15.2 2.6 %collective-permute-start.6 = (bf16[128,1920]{1,0:T(8,128)(2,1)S(1)}, bf16[128,1920]{1,0:T(8,128)(2,1)S(1)}, u32[]{:S(2)}, u32[]{:S(2)}) collective-permute-start(bf16[128,1920]{1,0:T(8,128)(2,1)S(1)} %get-tuple-element.106), channel_id=1, source_target_pairs={{0,2},{2,0},{4,6},{6,4},{8,10},{10,8},{12,14},{14,12},{16,18},{18,... | collective-permute-start | bytes 1474568 | tf_op jit(solution)/shard_map/ppermute | solution.py:260
  15.3 13.2 %collective-permute-start.9 = (bf16[256,1920]{1,0:T(8,128)(2,1)S(1)}, bf16[256,1920]{1,0:T(8,128)(2,1)S(1)}, u32[]{:S(2)}, u32[]{:S(2)}) collective-permute-start(bf16[256,1920]{1,0:T(8,128)(2,1)S(1)} %pad_maximum_fusion.refs_0_), channel_id=1, source_target_pairs={{0,8},{2,6},{4,0},{6,14},{8,16},{10,2},{12,4},{14,22},{16,24},{18,... | collective-permute-start | bytes 2949128 | tf_op jit(solution)/shard_map/ppermute | solution.py:272
  16.6 11.5 %collective-permute-start.10 = (bf16[132,512]{1,0:T(8,128)(2,1)S(1)}, bf16[132,512]{1,0:T(8,128)(2,1)S(1)}, u32[]{:S(2)}, u32[]{:S(2)}) collective-permute-start(bf16[132,512]{1,0:T(8,128)(2,1)S(1)} %get-tuple-element.60.refs_2_), channel_id=1, source_target_pairs={{0,1},{1,0},{2,3},{3,2},{4,5},{5,4},{6,7},{7,6},{8,9},{9,8},{10,11... | collective-permute-start | bytes 405512 | tf_op jit(solution)/shard_map/ppermute | solution.py:275
  19.8 8.2 %collective-permute-start.7 = (bf16[264,512]{1,0:T(8,128)(2,1)S(1)}, bf16[264,512]{1,0:T(8,128)(2,1)S(1)}, u32[]{:S(2)}, u32[]{:S(2)}) collective-permute-start(bf16[264,512]{1,0:T(8,128)(2,1)S(1)} %get-tuple-element.57), channel_id=1, source_target_pairs={{0,1},{1,0},{2,3},{3,2},{4,5},{5,4},{6,7},{7,6},{8,9},{9,8},{10,11... | collective-permute-start | bytes 811016 | tf_op jit(solution)/shard_map/ppermute | solution.py:275
  28.6 3.9 %collective-permute-start.12 = (bf16[128,1920]{1,0:T(8,128)(2,1)S(1)}, bf16[128,1920]{1,0:T(8,128)(2,1)S(1)}, u32[]{:S(2)}, u32[]{:S(2)}) collective-permute-start(bf16[128,1920]{1,0:T(8,128)(2,1)S(1)} %get-tuple-element.103), channel_id=1, source_target_pairs={{0,2},{2,0},{4,6},{6,4},{8,10},{10,8},{12,14},{14,12},{16,18},{18,... | collective-permute-start | bytes 1474568 | tf_op jit(solution)/shard_map/ppermute | solution.py:260
  30.0 2.6 %collective-permute-start.13 = (bf16[128,1920]{1,0:T(8,128)(2,1)S(1)}, bf16[128,1920]{1,0:T(8,128)(2,1)S(1)}, u32[]{:S(2)}, u32[]{:S(2)}) collective-permute-start(bf16[128,1920]{1,0:T(8,128)(2,1)S(1)} %get-tuple-element.104), channel_id=1, source_target_pairs={{0,2},{2,0},{4,6},{6,4},{8,10},{10,8},{12,14},{14,12},{16,18},{18,... | collective-permute-start | bytes 1474568 | tf_op jit(solution)/shard_map/ppermute | solution.py:260
  30.1 15.7 %collective-permute-start.11 = (bf16[256,1920]{1,0:T(8,128)(2,1)S(1)}, bf16[256,1920]{1,0:T(8,128)(2,1)S(1)}, u32[]{:S(2)}, u32[]{:S(2)}) collective-permute-start(bf16[256,1920]{1,0:T(8,128)(2,1)S(1)} %collective-permute-done.9.refs_0_), channel_id=1, source_target_pairs={{0,8},{2,6},{4,0},{6,14},{8,16},{10,2},{12,4},{14,22},{16,24},{18,... | collective-permute-start | bytes 2949128 | tf_op jit(solution)/shard_map/ppermute | solution.py:272
  31.4 8.5 %collective-permute-start.8 = (bf16[264,512]{1,0:T(8,128)(2,1)S(1)}, bf16[264,512]{1,0:T(8,128)(2,1)S(1)}, u32[]{:S(2)}, u32[]{:S(2)}) collective-permute-start(bf16[264,512]{1,0:T(8,128)(2,1)S(1)} %multiply_convert_fusion.2.refs_0_), channel_id=1, source_target_pairs={{0,1},{1,0},{2,3},{3,2},{4,5},{5,4},{6,7},{7,6},{8,9},{9,8},{10,11... | collective-permute-start | bytes 811016 | tf_op jit(solution)/shard_map/ppermute | solution.py:275
  35.9 9.8 %collective-permute-start.14 = (bf16[264,512]{1,0:T(8,128)(2,1)}, bf16[264,512]{1,0:T(8,128)(2,1)}, u32[]{:S(2)}, u32[]{:S(2)}) collective-permute-start(bf16[264,512]{1,0:T(8,128)(2,1)} %get-tuple-element.64), channel_id=1, source_target_pairs={{0,1},{1,0},{2,3},{3,2},{4,5},{5,4},{6,7},{7,6},{8,9},{9,8},{10,11... | collective-permute-start | bytes 811016 | tf_op jit(solution)/shard_map/ppermute | solution.py:275
  45.8 2.2 %collective-permute-start.16 = (bf16[128,1920]{1,0:T(8,128)(2,1)S(1)}, bf16[128,1920]{1,0:T(8,128)(2,1)S(1)}, u32[]{:S(2)}, u32[]{:S(2)}) collective-permute-start(bf16[128,1920]{1,0:T(8,128)(2,1)S(1)} %get-tuple-element.101), channel_id=1, source_target_pairs={{0,2},{2,0},{4,6},{6,4},{8,10},{10,8},{12,14},{14,12},{16,18},{18,... | collective-permute-start | bytes 1474568 | tf_op jit(solution)/shard_map/ppermute | solution.py:260
  46.3 2.2 %collective-permute-start.17 = (bf16[128,1920]{1,0:T(8,128)(2,1)S(1)}, bf16[128,1920]{1,0:T(8,128)(2,1)S(1)}, u32[]{:S(2)}, u32[]{:S(2)}) collective-permute-start(bf16[128,1920]{1,0:T(8,128)(2,1)S(1)} %get-tuple-element.102), channel_id=1, source_target_pairs={{0,2},{2,0},{4,6},{6,4},{8,10},{10,8},{12,14},{14,12},{16,18},{18,... | collective-permute-start | bytes 1474568 | tf_op jit(solution)/shard_map/ppermute | solution.py:260
  46.5 8.6 %collective-permute-start.15 = (bf16[256,1024]{1,0:T(8,128)(2,1)S(1)}, bf16[256,1024]{1,0:T(8,128)(2,1)S(1)}, u32[]{:S(2)}, u32[]{:S(2)}) collective-permute-start(bf16[256,1024]{1,0:T(8,128)(2,1)S(1)} %pad_maximum_fusion.4), channel_id=1, source_target_pairs={{0,8},{2,6},{4,0},{6,14},{8,16},{10,2},{12,4},{14,22},{16,24},{18,... | collective-permute-start | bytes 1572872 | tf_op jit(solution)/shard_map/ppermute | solution.py:272
  50.5 7.9 %collective-permute-start.22 = (bf16[264,512]{1,0:T(8,128)(2,1)S(1)}, bf16[264,512]{1,0:T(8,128)(2,1)S(1)}, u32[]{:S(2)}, u32[]{:S(2)}) collective-permute-start(bf16[264,512]{1,0:T(8,128)(2,1)S(1)} %get-tuple-element.68), channel_id=1, source_target_pairs={{0,1},{1,0},{2,3},{3,2},{4,5},{5,4},{6,7},{7,6},{8,9},{9,8},{10,11... | collective-permute-start | bytes 811016 | tf_op jit(solution)/shard_map/ppermute | solution.py:275
  55.1 2.3 %collective-permute-start.18 = (bf16[64,1024]{1,0:T(8,128)(2,1)S(1)}, bf16[64,1024]{1,0:T(8,128)(2,1)S(1)}, u32[]{:S(2)}, u32[]{:S(2)}) collective-permute-start(bf16[64,1024]{1,0:T(8,128)(2,1)S(1)} %get-tuple-element.109), channel_id=1, source_target_pairs={{0,2},{2,0},{4,6},{6,4},{8,10},{10,8},{12,14},{14,12},{16,18},{18,... | collective-permute-start | bytes 393224 | tf_op jit(solution)/shard_map/ppermute | solution.py:260
  56.5 1.3 %collective-permute-start.21 = (bf16[64,1024]{1,0:T(8,128)(2,1)S(1)}, bf16[64,1024]{1,0:T(8,128)(2,1)S(1)}, u32[]{:S(2)}, u32[]{:S(2)}) collective-permute-start(bf16[64,1024]{1,0:T(8,128)(2,1)S(1)} %get-tuple-element.110), channel_id=1, source_target_pairs={{0,2},{2,0},{4,6},{6,4},{8,10},{10,8},{12,14},{14,12},{16,18},{18,... | collective-permute-start | bytes 393224 | tf_op jit(solution)/shard_map/ppermute | solution.py:260
  56.5 1.5 %collective-permute-start.20 = (bf16[64,1024]{1,0:T(8,128)(2,1)S(1)}, bf16[64,1024]{1,0:T(8,128)(2,1)S(1)}, u32[]{:S(2)}, u32[]{:S(2)}) collective-permute-start(bf16[64,1024]{1,0:T(8,128)(2,1)S(1)} %get-tuple-element.111), channel_id=1, source_target_pairs={{0,2},{2,0},{4,6},{6,4},{8,10},{10,8},{12,14},{14,12},{16,18},{18,... | collective-permute-start | bytes 393224 | tf_op jit(solution)/shard_map/ppermute | solution.py:260
  57.0 1.3 %collective-permute-start.19 = (bf16[64,1024]{1,0:T(8,128)(2,1)S(1)}, bf16[64,1024]{1,0:T(8,128)(2,1)S(1)}, u32[]{:S(2)}, u32[]{:S(2)}) collective-permute-start(bf16[64,1024]{1,0:T(8,128)(2,1)S(1)} %get-tuple-element.112), channel_id=1, source_target_pairs={{0,2},{2,0},{4,6},{6,4},{8,10},{10,8},{12,14},{14,12},{16,18},{18,... | collective-permute-start | bytes 393224 | tf_op jit(solution)/shard_map/ppermute | solution.py:260
  60.2 7.2 %collective-permute-start.25 = (bf16[132,1024]{1,0:T(8,128)(2,1)S(1)}, bf16[132,1024]{1,0:T(8,128)(2,1)S(1)}, u32[]{:S(2)}, u32[]{:S(2)}) collective-permute-start(bf16[132,1024]{1,0:T(8,128)(2,1)S(1)} %get-tuple-element.71.refs_0_), channel_id=1, source_target_pairs={{0,1},{1,0},{2,3},{3,2},{4,5},{5,4},{6,7},{7,6},{8,9},{9,8},{10,11... | collective-permute-start | bytes 811016 | tf_op jit(solution)/shard_map/ppermute | solution.py:275
  63.4 4.0 %collective-permute-start.23 = (bf16[80,1792]{1,0:T(8,128)(2,1)S(1)}, bf16[80,1792]{1,0:T(8,128)(2,1)S(1)}, u32[]{:S(2)}, u32[]{:S(2)}) collective-permute-start(bf16[80,1792]{1,0:T(8,128)(2,1)S(1)} %slice.49), channel_id=1, source_target_pairs={{0,2},{2,0},{4,6},{6,4},{8,10},{10,8},{12,14},{14,12},{16,18},{18,... | collective-permute-start | bytes 860168 | tf_op jit(solution)/shard_map/ppermute | solution.py:260
  64.8 2.1 %collective-permute-start.24 = (bf16[64,1792]{1,0:T(8,128)(2,1)S(1)}, bf16[64,1792]{1,0:T(8,128)(2,1)S(1)}, u32[]{:S(2)}, u32[]{:S(2)}) collective-permute-start(bf16[64,1792]{1,0:T(8,128)(2,1)S(1)} %get-tuple-element.107), channel_id=1, source_target_pairs={{0,2},{2,0},{4,6},{6,4},{8,10},{10,8},{12,14},{14,12},{16,18},{18,... | collective-permute-start | bytes 688136 | tf_op jit(solution)/shard_map/ppermute | solution.py:260
  64.9 2.0 %collective-permute-start.26 = (bf16[64,1792]{1,0:T(8,128)(2,1)S(1)}, bf16[64,1792]{1,0:T(8,128)(2,1)S(1)}, u32[]{:S(2)}, u32[]{:S(2)}) collective-permute-start(bf16[64,1792]{1,0:T(8,128)(2,1)S(1)} %get-tuple-element.108), channel_id=1, source_target_pairs={{0,2},{2,0},{4,6},{6,4},{8,10},{10,8},{12,14},{14,12},{16,18},{18,... | collective-permute-start | bytes 688136 | tf_op jit(solution)/shard_map/ppermute | solution.py:260
  65.4 1.5 %collective-permute-start.27 = (bf16[48,1792]{1,0:T(8,128)(2,1)S(1)}, bf16[48,1792]{1,0:T(8,128)(2,1)S(1)}, u32[]{:S(2)}, u32[]{:S(2)}) collective-permute-start(bf16[48,1792]{1,0:T(8,128)(2,1)S(1)} %slice.52), channel_id=1, source_target_pairs={{0,2},{2,0},{4,6},{6,4},{8,10},{10,8},{12,14},{14,12},{16,18},{18,... | collective-permute-start | bytes 516104 | tf_op jit(solution)/shard_map/ppermute | solution.py:260
  67.3 8.6 %collective-permute-start.28 = (bf16[264,512]{1,0:T(8,128)(2,1)S(1)}, bf16[264,512]{1,0:T(8,128)(2,1)S(1)}, u32[]{:S(2)}, u32[]{:S(2)}) collective-permute-start(bf16[264,512]{1,0:T(8,128)(2,1)S(1)} %multiply_convert_fusion.1.refs_0_), channel_id=1, source_target_pairs={{0,1},{1,0},{2,3},{3,2},{4,5},{5,4},{6,7},{7,6},{8,9},{9,8},{10,11... | collective-permute-start | bytes 811016 | tf_op jit(solution)/shard_map/ppermute | solution.py:275
  70.7 3.4 %collective-permute-start.30 = (bf16[128,896]{1,0:T(8,128)(2,1)S(1)}, bf16[128,896]{1,0:T(8,128)(2,1)S(1)}, u32[]{:S(2)}, u32[]{:S(2)}) collective-permute-start(bf16[128,896]{1,0:T(8,128)(2,1)S(1)} %get-tuple-element.113), channel_id=1, source_target_pairs={{0,2},{2,0},{4,6},{6,4},{8,10},{10,8},{12,14},{14,12},{16,18},{18,... | collective-permute-start | bytes 688136 | tf_op jit(solution)/shard_map/ppermute | solution.py:260
  73.0 1.5 %collective-permute-start.29 = (bf16[128,896]{1,0:T(8,128)(2,1)S(1)}, bf16[128,896]{1,0:T(8,128)(2,1)S(1)}, u32[]{:S(2)}, u32[]{:S(2)}) collective-permute-start(bf16[128,896]{1,0:T(8,128)(2,1)S(1)} %get-tuple-element.114), channel_id=1, source_target_pairs={{0,2},{2,0},{4,6},{6,4},{8,10},{10,8},{12,14},{14,12},{16,18},{18,... | collective-permute-start | bytes 688136 | tf_op jit(solution)/shard_map/ppermute | solution.py:260
  74.6 7.7 %collective-permute-start.33 = (bf16[256,896]{1,0:T(8,128)(2,1)S(1)}, bf16[256,896]{1,0:T(8,128)(2,1)S(1)}, u32[]{:S(2)}, u32[]{:S(2)}) collective-permute-start(bf16[256,896]{1,0:T(8,128)(2,1)S(1)} %shard_map.73), channel_id=1, source_target_pairs={{0,8},{2,6},{4,0},{6,14},{8,16},{10,2},{12,4},{14,22},{16,24},{18,... | collective-permute-start | bytes 1376264 | tf_op jit(solution)/shard_map/ppermute | solution.py:272
  79.0 3.4 %collective-permute-start.32 = (bf16[112,1792]{1,0:T(8,128)(2,1)S(1)}, bf16[112,1792]{1,0:T(8,128)(2,1)S(1)}, u32[]{:S(2)}, u32[]{:S(2)}) collective-permute-start(bf16[112,1792]{1,0:T(8,128)(2,1)S(1)} %slice.53), channel_id=1, source_target_pairs={{0,2},{2,0},{4,6},{6,4},{8,10},{10,8},{12,14},{14,12},{16,18},{18,... | collective-permute-start | bytes 1204232 | tf_op jit(solution)/shard_map/ppermute | solution.py:260
  79.3 4.5 %collective-permute-start.34 = (bf16[144,1792]{1,0:T(8,128)(2,1)S(1)}, bf16[144,1792]{1,0:T(8,128)(2,1)S(1)}, u32[]{:S(2)}, u32[]{:S(2)}) collective-permute-start(bf16[144,1792]{1,0:T(8,128)(2,1)S(1)} %slice.55), channel_id=1, source_target_pairs={{0,2},{2,0},{4,6},{6,4},{8,10},{10,8},{12,14},{14,12},{16,18},{18,... | collective-permute-start | bytes 1548296 | tf_op jit(solution)/shard_map/ppermute | solution.py:260
  79.6 7.8 %collective-permute-start.31 = (bf16[264,512]{1,0:T(8,128)(2,1)S(1)}, bf16[264,512]{1,0:T(8,128)(2,1)S(1)}, u32[]{:S(2)}, u32[]{:S(2)}) collective-permute-start(bf16[264,512]{1,0:T(8,128)(2,1)S(1)} %multiply_convert_fusion.refs_0_), channel_id=1, source_target_pairs={{0,1},{1,0},{2,3},{3,2},{4,5},{5,4},{6,7},{7,6},{8,9},{9,8},{10,11... | collective-permute-start | bytes 811016 | tf_op jit(solution)/shard_map/ppermute | solution.py:275
  82.5 8.7 %collective-permute-start.43 = (bf16[112,1792]{1,0:T(8,128)(2,1)S(1)}, bf16[112,1792]{1,0:T(8,128)(2,1)S(1)}, u32[]{:S(2)}, u32[]{:S(2)}) collective-permute-start(bf16[112,1792]{1,0:T(8,128)(2,1)S(1)} %shard_map.75), channel_id=1, source_target_pairs={{0,8},{2,6},{4,0},{6,14},{8,16},{10,2},{12,4},{14,22},{16,24},{18,... | collective-permute-start | bytes 1204232 | tf_op jit(solution)/shard_map/ppermute | solution.py:272
  84.0 11.0 %collective-permute-start.36 = (bf16[144,1792]{1,0:T(8,128)(2,1)S(1)}, bf16[144,1792]{1,0:T(8,128)(2,1)S(1)}, u32[]{:S(2)}, u32[]{:S(2)}) collective-permute-start(bf16[144,1792]{1,0:T(8,128)(2,1)S(1)} %shard_map.76), channel_id=1, source_target_pairs={{0,8},{2,6},{4,0},{6,14},{8,16},{10,2},{12,4},{14,22},{16,24},{18,... | collective-permute-start | bytes 1548296 | tf_op jit(solution)/shard_map/ppermute | solution.py:272
  89.4 5.7 %collective-permute-start.35 = (bf16[144,1792]{1,0:T(8,128)(2,1)S(1)}, bf16[144,1792]{1,0:T(8,128)(2,1)S(1)}, u32[]{:S(2)}, u32[]{:S(2)}) collective-permute-start(bf16[144,1792]{1,0:T(8,128)(2,1)S(1)} %slice.57), channel_id=1, source_target_pairs={{0,2},{2,0},{4,6},{6,4},{8,10},{10,8},{12,14},{14,12},{16,18},{18,... | collective-permute-start | bytes 1548296 | tf_op jit(solution)/shard_map/ppermute | solution.py:260
  90.5 2.1 %collective-permute-start.41 = (bf16[64,1792]{1,0:T(8,128)(2,1)S(1)}, bf16[64,1792]{1,0:T(8,128)(2,1)S(1)}, u32[]{:S(2)}, u32[]{:S(2)}) collective-permute-start(bf16[64,1792]{1,0:T(8,128)(2,1)S(1)} %slice.59), channel_id=1, source_target_pairs={{0,2},{2,0},{4,6},{6,4},{8,10},{10,8},{12,14},{14,12},{16,18},{18,... | collective-permute-start | bytes 688136 | tf_op jit(solution)/shard_map/ppermute | solution.py:260
  90.6 2.0 %collective-permute-start.42 = (bf16[48,1792]{1,0:T(8,128)(2,1)S(1)}, bf16[48,1792]{1,0:T(8,128)(2,1)S(1)}, u32[]{:S(2)}, u32[]{:S(2)}) collective-permute-start(bf16[48,1792]{1,0:T(8,128)(2,1)S(1)} %slice.60), channel_id=1, source_target_pairs={{0,2},{2,0},{4,6},{6,4},{8,10},{10,8},{12,14},{14,12},{16,18},{18,... | collective-permute-start | bytes 516104 | tf_op jit(solution)/shard_map/ppermute | solution.py:260
  92.8 7.1 %collective-permute-start.44 = (bf16[112,1792]{1,0:T(8,128)(2,1)S(1)}, bf16[112,1792]{1,0:T(8,128)(2,1)S(1)}, u32[]{:S(2)}, u32[]{:S(2)}) collective-permute-start(bf16[112,1792]{1,0:T(8,128)(2,1)S(1)} %shard_map.80), channel_id=1, source_target_pairs={{0,8},{2,6},{4,0},{6,14},{8,16},{10,2},{12,4},{14,22},{16,24},{18,... | collective-permute-start | bytes 1204232 | tf_op jit(solution)/shard_map/ppermute | solution.py:272
  95.3 10.1 %collective-permute-start.37 = (bf16[144,1792]{1,0:T(8,128)(2,1)S(1)}, bf16[144,1792]{1,0:T(8,128)(2,1)S(1)}, u32[]{:S(2)}, u32[]{:S(2)}) collective-permute-start(bf16[144,1792]{1,0:T(8,128)(2,1)S(1)} %shard_map.78), channel_id=1, source_target_pairs={{0,8},{2,6},{4,0},{6,14},{8,16},{10,2},{12,4},{14,22},{16,24},{18,... | collective-permute-start | bytes 1548296 | tf_op jit(solution)/shard_map/ppermute | solution.py:272
  96.8 4.3 %collective-permute-start.39 = (bf16[132,512]{1,0:T(8,128)(2,1)S(1)}, bf16[132,512]{1,0:T(8,128)(2,1)S(1)}, u32[]{:S(2)}, u32[]{:S(2)}) collective-permute-start(bf16[132,512]{1,0:T(8,128)(2,1)S(1)} %copy-done.17), channel_id=1, source_target_pairs={{0,1},{1,0},{2,3},{3,2},{4,5},{5,4},{6,7},{7,6},{8,9},{9,8},{10,11... | collective-permute-start | bytes 405512 | tf_op jit(solution)/shard_map/ppermute | solution.py:275
  100.0 9.7 %collective-permute-start.45 = (bf16[112,1792]{1,0:T(8,128)(2,1)S(1)}, bf16[112,1792]{1,0:T(8,128)(2,1)S(1)}, u32[]{:S(2)}, u32[]{:S(2)}) collective-permute-start(bf16[112,1792]{1,0:T(8,128)(2,1)S(1)} %shard_map.81), channel_id=1, source_target_pairs={{0,8},{2,6},{4,0},{6,14},{8,16},{10,2},{12,4},{14,22},{16,24},{18,... | collective-permute-start | bytes 1204232 | tf_op jit(solution)/shard_map/ppermute | solution.py:272
  101.2 5.5 %collective-permute-start.40 = (bf16[132,512]{1,0:T(8,128)(2,1)S(1)}, bf16[132,512]{1,0:T(8,128)(2,1)S(1)}, u32[]{:S(2)}, u32[]{:S(2)}) collective-permute-start(bf16[132,512]{1,0:T(8,128)(2,1)S(1)} %multiply_convert_fusion.3.refs_0_), channel_id=1, source_target_pairs={{0,1},{1,0},{2,3},{3,2},{4,5},{5,4},{6,7},{7,6},{8,9},{9,8},{10,11... | collective-permute-start | bytes 405512 | tf_op jit(solution)/shard_map/ppermute | solution.py:275
  105.6 9.6 %collective-permute-start.38 = (bf16[144,1792]{1,0:T(8,128)(2,1)S(1)}, bf16[144,1792]{1,0:T(8,128)(2,1)S(1)}, u32[]{:S(2)}, u32[]{:S(2)}) collective-permute-start(bf16[144,1792]{1,0:T(8,128)(2,1)S(1)} %shard_map.79), channel_id=1, source_target_pairs={{0,8},{2,6},{4,0},{6,14},{8,16},{10,2},{12,4},{14,22},{16,24},{18,... | collective-permute-start | bytes 1548296 | tf_op jit(solution)/shard_map/ppermute | solution.py:272
  109.8 7.1 %collective-permute-start.46 = (bf16[112,1792]{1,0:T(8,128)(2,1)S(1)}, bf16[112,1792]{1,0:T(8,128)(2,1)S(1)}, u32[]{:S(2)}, u32[]{:S(2)}) collective-permute-start(bf16[112,1792]{1,0:T(8,128)(2,1)S(1)} %add_convert_fusion.1), channel_id=1, source_target_pairs={{0,2},{2,0},{4,6},{6,4},{8,10},{10,8},{12,14},{14,12},{16,18},{18,... | collective-permute-start | bytes 1204232 | tf_op jit(solution)/shard_map/ppermute | solution.py:260
  115.2 2.5 %collective-permute-start.47 = (bf16[16,1792]{1,0:T(8,128)(2,1)S(1)}, bf16[16,1792]{1,0:T(8,128)(2,1)S(1)}, u32[]{:S(2)}, u32[]{:S(2)}) collective-permute-start(bf16[16,1792]{1,0:T(8,128)(2,1)S(1)} %add_convert_fusion.2), channel_id=1, source_target_pairs={{0,2},{2,0},{4,6},{6,4},{8,10},{10,8},{12,14},{14,12},{16,18},{18,... | collective-permute-start | bytes 172040 | tf_op jit(solution)/shard_map/ppermute | solution.py:260
  (19 other events, 72.2 us)

commit v6 on v5

--- a/solution.py
+++ b/solution.py
@@ -176,21 +176,24 @@
     tile = 256
     for t in range(0, feat_n, tile):
         row_ref[:, t : t + tile] = dot_t(up_ref[...], w_ref[t : t + tile, :]).astype(BF16)
-    window = rows_n if rows_n <= 2 * slot_n else 2 * slot_n + (-2 * slot_n) % 16
-    lane = lax.broadcasted_iota(jnp.int32, (token_n, window), 1)
+    if rows_n <= 2 * slot_n:
+        windows = [(0, rows_n)]
+    else:
+        windows = [(0, 2 * slot_n + (-2 * slot_n) % 16), (2 * slot_n // 16 * 16, rows_n)]
     mine = mine_of((0,))
-    selects, starts = [], []
+    selects = []
     for b in range(ring.pieces[chunk]):
-        start = 0 if b < 2 else rows_n - window
+        start, end = windows[b // 2]
+        lane = lax.broadcasted_iota(jnp.int32, (token_n, end - start), 1)
         table = table_ref[b * token_n : (b + 1) * token_n, :]
         slot = dot_t(table, mine)[:, 0:1].astype(jnp.int32)
         slot = jnp.where(slot >= 0, slot + (b * slot_n - start), -1)
         selects.append(jnp.where(lane == slot, 1.0, 0.0).astype(BF16))
-        starts.append(start)
 
     def placed(b, sources_n, columns):
         select = jnp.concatenate(selects[b : b + sources_n], axis=0)
-        rows = row_ref[starts[b] : starts[b] + window, columns]
+        start, end = windows[b // 2]
+        rows = row_ref[start:end, columns]
         return jnp.dot(select, rows, preferred_element_type=F32).astype(BF16)
 
     if chunk == ring.far:

time: 120 us -> 120 us (level)
  no operation moved by 1% of the time
where the time goes in v6:
time: 120 us; the launch traced here: 119 us
  waiting for transfers between devices  46.3 us (39%)
  starting transfers between devices  42.5 us (35%)
  Pallas kernels  22.1 us (18%)
  local copies, waits for them, and re-layouts  4.54 us (4%)
  other arithmetic  2.85 us (2%)
    pallas_call x19, Pallas kernels, call(): pl.pallas_call(kernel, out_shape=[jax.ShapeDtypeStruct(shape, BF16) for s...  22.1 us
    ppermute x13, waiting for transfers between devices, to_ring(): return lax.ppermute(x, 'ep', ring_pairs)  20.5 us
    ppermute x10, waiting for transfers between devices, to_side(): return lax.ppermute(x, 'tp', [(0, 1), (1, 0)])  17.4 us
    ppermute x13, starting transfers between devices, to_ring(): return lax.ppermute(x, 'ep', ring_pairs)  16.1 us
    ppermute x25, starting transfers between devices, parts_to_core(): lax.ppermute(p, 'ep', swap)  15.9 us
    ppermute x10, starting transfers between devices, to_side(): return lax.ppermute(x, 'tp', [(0, 1), (1, 0)])  10.5 us
    ppermute x25, waiting for transfers between devices, parts_to_core(): lax.ppermute(p, 'ep', swap)  8.42 us
    unnamed x38, local copies, waits for them, and re-layouts  3.98 us
  transfers between devices with their start and end apart: 48, of which 26 were waited for; matrix products, arithmetic and copies ran while one was open for 2% of the time, Pallas kernels for 17%

profile of v6, /device:TPU:13, one launch (start us, length us, event | category | flops | bytes accessed | tf_op | source)
XLA Modules:
  0.0 118.7 jit_solution(8064543776482572396)
XLA Ops:
  0.7 1.3 %collective-permute-start = (bf16[128,1792]{1,0:T(8,128)(2,1)}, bf16[128,1792]{1,0:T(8,128)(2,1)S(1)}, u32[]{:S(2)}, u32[]{:S(2)}) collective-permute-start(bf16[128,1792]{1,0:T(8,128)(2,1)} %param.6), channel_id=1, source_target_pairs={{0,8},{2,6},{4,0},{6,14},{8,16},{10,2},{12,4},{14,22},{16,24},{18,... | collective-permute-start | bytes 1376264 | tf_op jit(solution)/shard_map/ppermute | solution.py:275
  2.3 1.3 %collective-permute-start.2 = (bf16[128,1792]{1,0:T(8,128)(2,1)S(1)}, bf16[128,1792]{1,0:T(8,128)(2,1)S(1)}, u32[]{:S(2)}, u32[]{:S(2)}) collective-permute-start(bf16[128,1792]{1,0:T(8,128)(2,1)S(1)} %collective-permute-done.1), channel_id=1, source_target_pairs={{0,8},{2,6},{4,0},{6,14},{8,16},{10,2},{12,4},{14,22},{16,24},{18,... | collective-permute-start | bytes 1376264 | tf_op jit(solution)/shard_map/ppermute | solution.py:275
  5.3 1.2 %collective-permute-done.3 = bf16[128,128]{1,0:T(8,128)(2,1)S(1)} collective-permute-done((bf16[128,128]{1,0:T(8,128)(2,1)S(1)}, bf16[128,128]{1,0:T(8,128)(2,1)S(1)}, u32[]{:S(2)}, u32[]{:S(2)}) %collective-permute-start.3) | collective-permute-done | bytes 32800 | tf_op jit(solution)/shard_map/ppermute | solution.py:263
  6.5 1.3 %collective-permute-start.4 = (bf16[256,128]{1,0:T(8,128)(2,1)S(1)}, bf16[256,128]{1,0:T(8,128)(2,1)S(1)}, u32[]{:S(2)}, u32[]{:S(2)}) collective-permute-start(bf16[256,128]{1,0:T(8,128)(2,1)S(1)} %pad_maximum_fusion.8), channel_id=1, source_target_pairs={{0,8},{2,6},{4,0},{6,14},{8,16},{10,2},{12,4},{14,22},{16,24},{18,... | collective-permute-start | bytes 196616 | tf_op jit(solution)/shard_map/ppermute | solution.py:275
  7.8 1.2 %copy-done.3 = bf16[1,1056,512]{2,1,0:T(8,128)(2,1)S(1)} copy-done((bf16[1,1056,512]{2,1,0:T(8,128)(2,1)S(1)}, bf16[1,1056,512]{2,1,0:T(8,128)(2,1)}, u32[]{:S(2)}) %copy-start.3) | copy-done | bytes 1081368
  9.0 1.6 %shard_map.65 = (bf16[132,512]{1,0:T(8,128)(2,1)S(1)}, bf16[264,512]{1,0:T(8,128)(2,1)S(1)}, bf16[264,512]{1,0:T(8,128)(2,1)S(1)}, bf16[264,512]{1,0:T(8,128)(2,1)S(1)}, bf16[132,512]{1,0:T(8,128)(2,1)S(1)}) custom-call(bf16[1056,512]{1,0:T(8,128)(2,1)S(1)} %bitcast.15), custom_call_target="tpu_custom_call" | custom-call | tf_op jit(solution)/shard_map/pallas_call | solution.py:281
  10.7 3.4 %collective-permute-done.4 = bf16[256,128]{1,0:T(8,128)(2,1)S(1)} collective-permute-done((bf16[256,128]{1,0:T(8,128)(2,1)S(1)}, bf16[256,128]{1,0:T(8,128)(2,1)S(1)}, u32[]{:S(2)}, u32[]{:S(2)}) %collective-permute-start.4) | collective-permute-done | bytes 65568 | tf_op jit(solution)/shard_map/ppermute | solution.py:275
  15.3 1.3 %collective-permute-start.9 = (bf16[256,1920]{1,0:T(8,128)(2,1)S(1)}, bf16[256,1920]{1,0:T(8,128)(2,1)S(1)}, u32[]{:S(2)}, u32[]{:S(2)}) collective-permute-start(bf16[256,1920]{1,0:T(8,128)(2,1)S(1)} %pad_maximum_fusion.refs_0_), channel_id=1, source_target_pairs={{0,8},{2,6},{4,0},{6,14},{8,16},{10,2},{12,4},{14,22},{16,24},{18,... | collective-permute-start | bytes 2949128 | tf_op jit(solution)/shard_map/ppermute | solution.py:275
  16.6 1.2 %collective-permute-start.10 = (bf16[132,512]{1,0:T(8,128)(2,1)S(1)}, bf16[132,512]{1,0:T(8,128)(2,1)S(1)}, u32[]{:S(2)}, u32[]{:S(2)}) collective-permute-start(bf16[132,512]{1,0:T(8,128)(2,1)S(1)} %get-tuple-element.60.refs_2_), channel_id=1, source_target_pairs={{0,1},{1,0},{2,3},{3,2},{4,5},{5,4},{6,7},{7,6},{8,9},{9,8},{10,11... | collective-permute-start | bytes 405512 | tf_op jit(solution)/shard_map/ppermute | solution.py:278
  17.9 1.8 %shard_map.66 = (bf16[264,512]{1,0:T(8,128)(2,1)S(1)}, bf16[264,512]{1,0:T(8,128)(2,1)S(1)}, bf16[512,128]{1,0:T(8,128)(2,1)S(1)}) custom-call(bf16[256,1920]{1,0:T(8,128)(2,1)S(1)} %pad_maximum_fusion.refs_0_, bf16[256,1920]{1,0:T(8,128)(2,1)S(1)} %pad_maximum_fusion.1.refs_1_, bf16[1024,1792]{1,0:T(8,128)(2,1)S(1)} %bitcast.5), custom_call_target="tpu_custom_call" | custom-call | tf_op jit(solution)/shard_map/pallas_call | solution.py:281
  20.8 1.7 %shard_map.67 = (bf16[132,512]{1,0:T(8,128)(2,1)S(1)}, bf16[132,512]{1,0:T(8,128)(2,1)S(1)}, bf16[256,128]{1,0:T(8,128)(2,1)S(1)}) custom-call(bf16[128,1920]{1,0:T(8,128)(2,1)S(1)} %pad_maximum_fusion.6.refs_0_, bf16[128,1920]{1,0:T(8,128)(2,1)S(1)} %pad_maximum_fusion.7.refs_1_, bf16[1024,1792]{1,0:T(8,128)(2,1)S(1)} %bitcast.6), custom_call_target="tpu_custom_call" | custom-call | tf_op jit(solution)/shard_map/pallas_call | solution.py:281
  23.2 4.8 %collective-permute-done.7 = bf16[264,512]{1,0:T(8,128)(2,1)S(1)} collective-permute-done((bf16[264,512]{1,0:T(8,128)(2,1)S(1)}, bf16[264,512]{1,0:T(8,128)(2,1)S(1)}, u32[]{:S(2)}, u32[]{:S(2)}) %collective-permute-start.7) | collective-permute-done | bytes 270368 | tf_op jit(solution)/shard_map/ppermute | solution.py:278
  28.6 1.4 %collective-permute-start.12 = (bf16[128,1920]{1,0:T(8,128)(2,1)S(1)}, bf16[128,1920]{1,0:T(8,128)(2,1)S(1)}, u32[]{:S(2)}, u32[]{:S(2)}) collective-permute-start(bf16[128,1920]{1,0:T(8,128)(2,1)S(1)} %get-tuple-element.103), channel_id=1, source_target_pairs={{0,2},{2,0},{4,6},{6,4},{8,10},{10,8},{12,14},{14,12},{16,18},{18,... | collective-permute-start | bytes 1474568 | tf_op jit(solution)/shard_map/ppermute | solution.py:263
  30.1 1.3 %collective-permute-start.11 = (bf16[256,1920]{1,0:T(8,128)(2,1)S(1)}, bf16[256,1920]{1,0:T(8,128)(2,1)S(1)}, u32[]{:S(2)}, u32[]{:S(2)}) collective-permute-start(bf16[256,1920]{1,0:T(8,128)(2,1)S(1)} %collective-permute-done.9.refs_0_), channel_id=1, source_target_pairs={{0,8},{2,6},{4,0},{6,14},{8,16},{10,2},{12,4},{14,22},{16,24},{18,... | collective-permute-start | bytes 2949128 | tf_op jit(solution)/shard_map/ppermute | solution.py:275
  31.4 1.2 %collective-permute-start.8 = (bf16[264,512]{1,0:T(8,128)(2,1)S(1)}, bf16[264,512]{1,0:T(8,128)(2,1)S(1)}, u32[]{:S(2)}, u32[]{:S(2)}) collective-permute-start(bf16[264,512]{1,0:T(8,128)(2,1)S(1)} %multiply_convert_fusion.2.refs_0_), channel_id=1, source_target_pairs={{0,1},{1,0},{2,3},{3,2},{4,5},{5,4},{6,7},{7,6},{8,9},{9,8},{10,11... | collective-permute-start | bytes 811016 | tf_op jit(solution)/shard_map/ppermute | solution.py:278
  32.7 2.6 %shard_map.68 = (bf16[264,512]{1,0:T(8,128)(2,1)S(1)}, bf16[264,512]{1,0:T(8,128)(2,1)}, bf16[512,128]{1,0:T(8,128)(2,1)S(1)}) custom-call(bf16[256,1920]{1,0:T(8,128)(2,1)S(1)} %collective-permute-done.9.refs_0_, bf16[256,1920]{1,0:T(8,128)(2,1)S(1)} %pad_maximum_fusion.2.refs_1_, bf16[1024,1792]{1,0:T(8,128)(2,1)S(1)} %bitcast.7), custom_call_target="tpu_custom_call" | custom-call | tf_op jit(solution)/shard_map/pallas_call | solution.py:281
  36.7 3.1 %collective-permute-done.8.refs_1_ = bf16[264,512]{1,0:T(8,128)(2,1)S(1)} collective-permute-done((bf16[264,512]{1,0:T(8,128)(2,1)S(1)}, bf16[264,512]{1,0:T(8,128)(2,1)S(1)}, u32[]{:S(2)}, u32[]{:S(2)}) %collective-permute-start.8) | collective-permute-done | bytes 270368 | tf_op jit(solution)/shard_map/ppermute | solution.py:278
  39.8 5.9 %collective-permute-done.14 = bf16[264,512]{1,0:T(8,128)(2,1)} collective-permute-done((bf16[264,512]{1,0:T(8,128)(2,1)}, bf16[264,512]{1,0:T(8,128)(2,1)}, u32[]{:S(2)}, u32[]{:S(2)}) %collective-permute-start.14) | collective-permute-done | bytes 270368 | tf_op jit(solution)/shard_map/ppermute | solution.py:278
  46.5 1.5 %collective-permute-start.15 = (bf16[256,1024]{1,0:T(8,128)(2,1)S(1)}, bf16[256,1024]{1,0:T(8,128)(2,1)S(1)}, u32[]{:S(2)}, u32[]{:S(2)}) collective-permute-start(bf16[256,1024]{1,0:T(8,128)(2,1)S(1)} %pad_maximum_fusion.4), channel_id=1, source_target_pairs={{0,8},{2,6},{4,0},{6,14},{8,16},{10,2},{12,4},{14,22},{16,24},{18,... | collective-permute-start | bytes 1572872 | tf_op jit(solution)/shard_map/ppermute | solution.py:275
  48.6 1.9 %shard_map.69 = (bf16[264,512]{1,0:T(8,128)(2,1)S(1)}, bf16[264,512]{1,0:T(8,128)(2,1)S(1)}, bf16[512,128]{1,0:T(8,128)(2,1)S(1)}) custom-call(bf16[256,1920]{1,0:T(8,128)(2,1)S(1)} %collective-permute-done.11.refs_0_, bf16[256,1920]{1,0:T(8,128)(2,1)S(1)} %pad_maximum_fusion.3.refs_1_, bf16[1024,1792]{1,0:T(8,128)(2,1)S(1)} %bitcast.8), custom_call_target="tpu_custom_call" | custom-call | tf_op jit(solution)/shard_map/pallas_call | solution.py:281
  50.5 1.3 %collective-permute-start.22 = (bf16[264,512]{1,0:T(8,128)(2,1)S(1)}, bf16[264,512]{1,0:T(8,128)(2,1)S(1)}, u32[]{:S(2)}, u32[]{:S(2)}) collective-permute-start(bf16[264,512]{1,0:T(8,128)(2,1)S(1)} %get-tuple-element.68), channel_id=1, source_target_pairs={{0,1},{1,0},{2,3},{3,2},{4,5},{5,4},{6,7},{7,6},{8,9},{9,8},{10,11... | collective-permute-start | bytes 811016 | tf_op jit(solution)/shard_map/ppermute | solution.py:278
  51.7 3.3 %collective-permute-done.15.refs_0_ = bf16[256,1024]{1,0:T(8,128)(2,1)S(1)} collective-permute-done((bf16[256,1024]{1,0:T(8,128)(2,1)S(1)}, bf16[256,1024]{1,0:T(8,128)(2,1)S(1)}, u32[]{:S(2)}, u32[]{:S(2)}) %collective-permute-start.15) | collective-permute-done | bytes 524320 | tf_op jit(solution)/shard_map/ppermute | solution.py:275
  55.1 1.3 %collective-permute-start.18 = (bf16[64,1024]{1,0:T(8,128)(2,1)S(1)}, bf16[64,1024]{1,0:T(8,128)(2,1)S(1)}, u32[]{:S(2)}, u32[]{:S(2)}) collective-permute-start(bf16[64,1024]{1,0:T(8,128)(2,1)S(1)} %get-tuple-element.109), channel_id=1, source_target_pairs={{0,2},{2,0},{4,6},{6,4},{8,10},{10,8},{12,14},{14,12},{16,18},{18,... | collective-permute-start | bytes 393224 | tf_op jit(solution)/shard_map/ppermute | solution.py:263
  58.5 1.7 %shard_map.70 = (bf16[132,1024]{1,0:T(8,128)(2,1)S(1)}, bf16[256,128]{1,0:T(8,128)(2,1)S(1)}) custom-call(bf16[256,1024]{1,0:T(8,128)(2,1)S(1)} %collective-permute-done.15.refs_0_, bf16[256,1024]{1,0:T(8,128)(2,1)S(1)} %pad_maximum_fusion.5.refs_1_, bf16[1024,1792]{1,0:T(8,128)(2,1)S(1)} %bitcast.9), custom_call_target="tpu_custom_call" | custom-call | tf_op jit(solution)/shard_map/pallas_call | solution.py:281
  60.2 1.3 %collective-permute-start.25 = (bf16[132,1024]{1,0:T(8,128)(2,1)S(1)}, bf16[132,1024]{1,0:T(8,128)(2,1)S(1)}, u32[]{:S(2)}, u32[]{:S(2)}) collective-permute-start(bf16[132,1024]{1,0:T(8,128)(2,1)S(1)} %get-tuple-element.71.refs_0_), channel_id=1, source_target_pairs={{0,1},{1,0},{2,3},{3,2},{4,5},{5,4},{6,7},{7,6},{8,9},{9,8},{10,11... | collective-permute-start | bytes 811016 | tf_op jit(solution)/shard_map/ppermute | solution.py:278
  61.5 1.9 %shard_map.71 = (bf16[256,1792]{1,0:T(8,128)(2,1)S(1)}, bf16[256,1792]{1,0:T(8,128)(2,1)S(1)}) custom-call(bf16[512,128]{1,0:T(8,128)(2,1)S(1)} %copy-done.13, bf16[264,512]{1,0:T(8,128)(2,1)S(1)} %multiply_convert_fusion.2.refs_0_, bf16[264,512]{1,0:T(8,128)(2,1)S(1)} %collective-permute-done.8.refs_1_, bf16[1792,1024]{1,0:T(8,128)(2,1)S(1)} %bitcast.10), custom_call_target="tpu_custom_call" | custom-call | tf_op jit(solution)/shard_map/pallas_call | solution.py:281
  63.4 1.4 %collective-permute-start.23 = (bf16[80,1792]{1,0:T(8,128)(2,1)S(1)}, bf16[80,1792]{1,0:T(8,128)(2,1)S(1)}, u32[]{:S(2)}, u32[]{:S(2)}) collective-permute-start(bf16[80,1792]{1,0:T(8,128)(2,1)S(1)} %slice.49), channel_id=1, source_target_pairs={{0,2},{2,0},{4,6},{6,4},{8,10},{10,8},{12,14},{14,12},{16,18},{18,... | collective-permute-start | bytes 860168 | tf_op jit(solution)/shard_map/ppermute | solution.py:263
  65.5 1.4 %collective-permute-done.27.refs_1_ = bf16[48,1792]{1,0:T(8,128)(2,1)S(1)} collective-permute-done((bf16[48,1792]{1,0:T(8,128)(2,1)S(1)}, bf16[48,1792]{1,0:T(8,128)(2,1)S(1)}, u32[]{:S(2)}, u32[]{:S(2)}) %collective-permute-start.27) | collective-permute-done | bytes 172064 | tf_op jit(solution)/shard_map/ppermute | solution.py:263
  67.3 1.2 %collective-permute-start.28 = (bf16[264,512]{1,0:T(8,128)(2,1)S(1)}, bf16[264,512]{1,0:T(8,128)(2,1)S(1)}, u32[]{:S(2)}, u32[]{:S(2)}) collective-permute-start(bf16[264,512]{1,0:T(8,128)(2,1)S(1)} %multiply_convert_fusion.1.refs_0_), channel_id=1, source_target_pairs={{0,1},{1,0},{2,3},{3,2},{4,5},{5,4},{6,7},{7,6},{8,9},{9,8},{10,11... | collective-permute-start | bytes 811016 | tf_op jit(solution)/shard_map/ppermute | solution.py:278
  68.6 2.1 %shard_map.72 = (bf16[256,896]{1,0:T(8,128)(2,1)S(1)}, bf16[256,896]{1,0:T(8,128)(2,1)S(1)}) custom-call(bf16[256,128]{1,0:T(8,128)(2,1)S(1)} %get-tuple-element.78.table_ref, bf16[132,1024]{1,0:T(8,128)(2,1)S(1)} %get-tuple-element.71.refs_0_, bf16[132,1024]{1,0:T(8,128)(2,1)S(1)} %collective-permute-done.25.refs_1_, ...), custom_call_target="tpu_custom_call" | custom-call | tf_op jit(solution)/shard_map/pallas_call | solution.py:281
  70.7 2.3 %collective-permute-start.30 = (bf16[128,896]{1,0:T(8,128)(2,1)S(1)}, bf16[128,896]{1,0:T(8,128)(2,1)S(1)}, u32[]{:S(2)}, u32[]{:S(2)}) collective-permute-start(bf16[128,896]{1,0:T(8,128)(2,1)S(1)} %get-tuple-element.113), channel_id=1, source_target_pairs={{0,2},{2,0},{4,6},{6,4},{8,10},{10,8},{12,14},{14,12},{16,18},{18,... | collective-permute-start | bytes 688136 | tf_op jit(solution)/shard_map/ppermute | solution.py:263
  74.6 1.4 %collective-permute-start.33 = (bf16[256,896]{1,0:T(8,128)(2,1)S(1)}, bf16[256,896]{1,0:T(8,128)(2,1)S(1)}, u32[]{:S(2)}, u32[]{:S(2)}) collective-permute-start(bf16[256,896]{1,0:T(8,128)(2,1)S(1)} %shard_map.73), channel_id=1, source_target_pairs={{0,8},{2,6},{4,0},{6,14},{8,16},{10,2},{12,4},{14,22},{16,24},{18,... | collective-permute-start | bytes 1376264 | tf_op jit(solution)/shard_map/ppermute | solution.py:275
  77.0 1.9 %shard_map.74 = (bf16[256,1792]{1,0:T(8,128)(2,1)S(1)}, bf16[256,1792]{1,0:T(8,128)(2,1)S(1)}) custom-call(bf16[512,128]{1,0:T(8,128)(2,1)S(1)} %get-tuple-element.84.table_ref, bf16[264,512]{1,0:T(8,128)(2,1)S(1)} %multiply_convert_fusion.1.refs_0_, bf16[264,512]{1,0:T(8,128)(2,1)S(1)} %collective-permute-done.28.refs_1_, bf16[1792,1024]{1,0:T(8,128)(2,1)S(1)} %bitcast.12), custom_call_target="tpu_custom_call" | custom-call | tf_op jit(solution)/shard_map/pallas_call | solution.py:281
  80.7 1.6 %collective-permute-done.33 = bf16[256,896]{1,0:T(8,128)(2,1)S(1)} collective-permute-done((bf16[256,896]{1,0:T(8,128)(2,1)S(1)}, bf16[256,896]{1,0:T(8,128)(2,1)S(1)}, u32[]{:S(2)}, u32[]{:S(2)}) %collective-permute-start.33) | collective-permute-done | bytes 458784 | tf_op jit(solution)/shard_map/ppermute | solution.py:275
  82.5 1.4 %collective-permute-start.43 = (bf16[112,1792]{1,0:T(8,128)(2,1)S(1)}, bf16[112,1792]{1,0:T(8,128)(2,1)S(1)}, u32[]{:S(2)}, u32[]{:S(2)}) collective-permute-start(bf16[112,1792]{1,0:T(8,128)(2,1)S(1)} %shard_map.75), channel_id=1, source_target_pairs={{0,8},{2,6},{4,0},{6,14},{8,16},{10,2},{12,4},{14,22},{16,24},{18,... | collective-permute-start | bytes 1204232 | tf_op jit(solution)/shard_map/ppermute | solution.py:275
  84.3 3.1 %collective-permute-done.31.refs_1_ = bf16[264,512]{1,0:T(8,128)(2,1)S(1)} collective-permute-done((bf16[264,512]{1,0:T(8,128)(2,1)S(1)}, bf16[264,512]{1,0:T(8,128)(2,1)S(1)}, u32[]{:S(2)}, u32[]{:S(2)}) %collective-permute-start.31) | collective-permute-done | bytes 270368 | tf_op jit(solution)/shard_map/ppermute | solution.py:278
  87.5 1.9 %shard_map.77 = (bf16[256,1792]{1,0:T(8,128)(2,1)S(1)}, bf16[256,1792]{1,0:T(8,128)(2,1)S(1)}) custom-call(bf16[512,128]{1,0:T(8,128)(2,1)S(1)} %copy-done.11, bf16[264,512]{1,0:T(8,128)(2,1)S(1)} %multiply_convert_fusion.refs_0_, bf16[264,512]{1,0:T(8,128)(2,1)S(1)} %collective-permute-done.31.refs_1_, bf16[1792,1024]{1,0:T(8,128)(2,1)S(1)} %bitcast.13), custom_call_target="tpu_custom_call" | custom-call | tf_op jit(solution)/shard_map/pallas_call | solution.py:281
  91.2 1.4 %collective-permute-done.42.refs_1_ = bf16[48,1792]{1,0:T(8,128)(2,1)S(1)} collective-permute-done((bf16[48,1792]{1,0:T(8,128)(2,1)S(1)}, bf16[48,1792]{1,0:T(8,128)(2,1)S(1)}, u32[]{:S(2)}, u32[]{:S(2)}) %collective-permute-start.42) | collective-permute-done | bytes 172064 | tf_op jit(solution)/shard_map/ppermute | solution.py:263
  95.3 1.6 %collective-permute-start.37 = (bf16[144,1792]{1,0:T(8,128)(2,1)S(1)}, bf16[144,1792]{1,0:T(8,128)(2,1)S(1)}, u32[]{:S(2)}, u32[]{:S(2)}) collective-permute-start(bf16[144,1792]{1,0:T(8,128)(2,1)S(1)} %shard_map.78), channel_id=1, source_target_pairs={{0,8},{2,6},{4,0},{6,14},{8,16},{10,2},{12,4},{14,22},{16,24},{18,... | collective-permute-start | bytes 1548296 | tf_op jit(solution)/shard_map/ppermute | solution.py:275
  97.1 2.7 %collective-permute-done.44.refs_2_ = bf16[112,1792]{1,0:T(8,128)(2,1)S(1)} collective-permute-done((bf16[112,1792]{1,0:T(8,128)(2,1)S(1)}, bf16[112,1792]{1,0:T(8,128)(2,1)S(1)}, u32[]{:S(2)}, u32[]{:S(2)}) %collective-permute-start.44) | collective-permute-done | bytes 401440 | tf_op jit(solution)/shard_map/ppermute | solution.py:275
  100.0 1.2 collective-permute-start.45
  101.2 1.3 %collective-permute-start.40 = (bf16[132,512]{1,0:T(8,128)(2,1)S(1)}, bf16[132,512]{1,0:T(8,128)(2,1)S(1)}, u32[]{:S(2)}, u32[]{:S(2)}) collective-permute-start(bf16[132,512]{1,0:T(8,128)(2,1)S(1)} %multiply_convert_fusion.3.refs_0_), channel_id=1, source_target_pairs={{0,1},{1,0},{2,3},{3,2},{4,5},{5,4},{6,7},{7,6},{8,9},{9,8},{10,11... | collective-permute-start | bytes 405512 | tf_op jit(solution)/shard_map/ppermute | solution.py:278
  102.5 2.8 %collective-permute-done.37.refs_2_ = bf16[144,1792]{1,0:T(8,128)(2,1)S(1)} collective-permute-done((bf16[144,1792]{1,0:T(8,128)(2,1)S(1)}, bf16[144,1792]{1,0:T(8,128)(2,1)S(1)}, u32[]{:S(2)}, u32[]{:S(2)}) %collective-permute-start.37) | collective-permute-done | bytes 516128 | tf_op jit(solution)/shard_map/ppermute | solution.py:275
  105.6 1.2 collective-permute-start.38
  106.7 1.7 %shard_map.82 = (bf16[128,1792]{1,0:T(8,128)(2,1)S(1)}, bf16[128,1792]{1,0:T(8,128)(2,1)S(1)}) custom-call(bf16[256,128]{1,0:T(8,128)(2,1)S(1)} %get-tuple-element.91.table_ref, bf16[132,512]{1,0:T(8,128)(2,1)S(1)} %multiply_convert_fusion.3.refs_0_, bf16[132,512]{1,0:T(8,128)(2,1)S(1)} %collective-permute-done.40.refs_1_, bf16[1792,1024]{1,0:T(8,128)(2,1)S(1)} %bitcast.14), custom_call_target="tpu_custom_call" | custom-call | tf_op jit(solution)/shard_map/pallas_call | solution.py:281
  109.8 1.6 %collective-permute-start.46 = (bf16[112,1792]{1,0:T(8,128)(2,1)S(1)}, bf16[112,1792]{1,0:T(8,128)(2,1)S(1)}, u32[]{:S(2)}, u32[]{:S(2)}) collective-permute-start(bf16[112,1792]{1,0:T(8,128)(2,1)S(1)} %add_convert_fusion.1), channel_id=1, source_target_pairs={{0,2},{2,0},{4,6},{6,4},{8,10},{10,8},{12,14},{14,12},{16,18},{18,... | collective-permute-start | bytes 1204232 | tf_op jit(solution)/shard_map/ppermute | solution.py:263
  111.4 3.8 %collective-permute-done.38 = bf16[144,1792]{1,0:T(8,128)(2,1)S(1)} collective-permute-done((bf16[144,1792]{1,0:T(8,128)(2,1)S(1)}, bf16[144,1792]{1,0:T(8,128)(2,1)S(1)}, u32[]{:S(2)}, u32[]{:S(2)}) %collective-permute-start.38) | collective-permute-done | bytes 516128 | tf_op jit(solution)/shard_map/ppermute | solution.py:275
  115.2 1.6 %collective-permute-start.47 = (bf16[16,1792]{1,0:T(8,128)(2,1)S(1)}, bf16[16,1792]{1,0:T(8,128)(2,1)S(1)}, u32[]{:S(2)}, u32[]{:S(2)}) collective-permute-start(bf16[16,1792]{1,0:T(8,128)(2,1)S(1)} %add_convert_fusion.2), channel_id=1, source_target_pairs={{0,2},{2,0},{4,6},{6,4},{8,10},{10,8},{12,14},{14,12},{16,18},{18,... | collective-permute-start | bytes 172040 | tf_op jit(solution)/shard_map/ppermute | solution.py:263
  (138 shorter events, 25.7 us)
Async XLA Ops:
  0.0 2.3 %collective-permute-start.1 = (bf16[128,1792]{1,0:T(8,128)(2,1)}, bf16[128,1792]{1,0:T(8,128)(2,1)S(1)}, u32[]{:S(2)}, u32[]{:S(2)}) collective-permute-start(bf16[128,1792]{1,0:T(8,128)(2,1)} %param.6), channel_id=1, source_target_pairs={{0,2},{2,0},{4,6},{6,4},{8,10},{10,8},{12,14},{14,12},{16,18},{18,... | collective-permute-start | bytes 1376264 | tf_op jit(solution)/shard_map/ppermute | solution.py:263
  0.7 13.5 %collective-permute-start = (bf16[128,1792]{1,0:T(8,128)(2,1)}, bf16[128,1792]{1,0:T(8,128)(2,1)S(1)}, u32[]{:S(2)}, u32[]{:S(2)}) collective-permute-start(bf16[128,1792]{1,0:T(8,128)(2,1)} %param.6), channel_id=1, source_target_pairs={{0,8},{2,6},{4,0},{6,14},{8,16},{10,2},{12,4},{14,22},{16,24},{18,... | collective-permute-start | bytes 1376264 | tf_op jit(solution)/shard_map/ppermute | solution.py:275
  2.3 11.8 %collective-permute-start.2 = (bf16[128,1792]{1,0:T(8,128)(2,1)S(1)}, bf16[128,1792]{1,0:T(8,128)(2,1)S(1)}, u32[]{:S(2)}, u32[]{:S(2)}) collective-permute-start(bf16[128,1792]{1,0:T(8,128)(2,1)S(1)} %collective-permute-done.1), channel_id=1, source_target_pairs={{0,8},{2,6},{4,0},{6,14},{8,16},{10,2},{12,4},{14,22},{16,24},{18,... | collective-permute-start | bytes 1376264 | tf_op jit(solution)/shard_map/ppermute | solution.py:275
  5.2 1.3 %collective-permute-start.3 = (bf16[128,128]{1,0:T(8,128)(2,1)S(1)}, bf16[128,128]{1,0:T(8,128)(2,1)S(1)}, u32[]{:S(2)}, u32[]{:S(2)}) collective-permute-start(bf16[128,128]{1,0:T(8,128)(2,1)S(1)} %shard_map.64), channel_id=1, source_target_pairs={{0,2},{2,0},{4,6},{6,4},{8,10},{10,8},{12,14},{14,12},{16,18},{18,... | collective-permute-start | bytes 98312 | tf_op jit(solution)/shard_map/ppermute | solution.py:263
  6.5 7.6 %collective-permute-start.4 = (bf16[256,128]{1,0:T(8,128)(2,1)S(1)}, bf16[256,128]{1,0:T(8,128)(2,1)S(1)}, u32[]{:S(2)}, u32[]{:S(2)}) collective-permute-start(bf16[256,128]{1,0:T(8,128)(2,1)S(1)} %pad_maximum_fusion.8), channel_id=1, source_target_pairs={{0,8},{2,6},{4,0},{6,14},{8,16},{10,2},{12,4},{14,22},{16,24},{18,... | collective-permute-start | bytes 196616 | tf_op jit(solution)/shard_map/ppermute | solution.py:275
  14.3 3.5 %collective-permute-start.5 = (bf16[128,1920]{1,0:T(8,128)(2,1)S(1)}, bf16[128,1920]{1,0:T(8,128)(2,1)S(1)}, u32[]{:S(2)}, u32[]{:S(2)}) collective-permute-start(bf16[128,1920]{1,0:T(8,128)(2,1)S(1)} %get-tuple-element.105), channel_id=1, source_target_pairs={{0,2},{2,0},{4,6},{6,4},{8,10},{10,8},{12,14},{14,12},{16,18},{18,... | collective-permute-start | bytes 1474568 | tf_op jit(solution)/shard_map/ppermute | solution.py:263
  15.2 2.6 %collective-permute-start.6 = (bf16[128,1920]{1,0:T(8,128)(2,1)S(1)}, bf16[128,1920]{1,0:T(8,128)(2,1)S(1)}, u32[]{:S(2)}, u32[]{:S(2)}) collective-permute-start(bf16[128,1920]{1,0:T(8,128)(2,1)S(1)} %get-tuple-element.106), channel_id=1, source_target_pairs={{0,2},{2,0},{4,6},{6,4},{8,10},{10,8},{12,14},{14,12},{16,18},{18,... | collective-permute-start | bytes 1474568 | tf_op jit(solution)/shard_map/ppermute | solution.py:263
  15.3 13.2 %collective-permute-start.9 = (bf16[256,1920]{1,0:T(8,128)(2,1)S(1)}, bf16[256,1920]{1,0:T(8,128)(2,1)S(1)}, u32[]{:S(2)}, u32[]{:S(2)}) collective-permute-start(bf16[256,1920]{1,0:T(8,128)(2,1)S(1)} %pad_maximum_fusion.refs_0_), channel_id=1, source_target_pairs={{0,8},{2,6},{4,0},{6,14},{8,16},{10,2},{12,4},{14,22},{16,24},{18,... | collective-permute-start | bytes 2949128 | tf_op jit(solution)/shard_map/ppermute | solution.py:275
  16.6 11.5 %collective-permute-start.10 = (bf16[132,512]{1,0:T(8,128)(2,1)S(1)}, bf16[132,512]{1,0:T(8,128)(2,1)S(1)}, u32[]{:S(2)}, u32[]{:S(2)}) collective-permute-start(bf16[132,512]{1,0:T(8,128)(2,1)S(1)} %get-tuple-element.60.refs_2_), channel_id=1, source_target_pairs={{0,1},{1,0},{2,3},{3,2},{4,5},{5,4},{6,7},{7,6},{8,9},{9,8},{10,11... | collective-permute-start | bytes 405512 | tf_op jit(solution)/shard_map/ppermute | solution.py:278
  19.8 8.2 %collective-permute-start.7 = (bf16[264,512]{1,0:T(8,128)(2,1)S(1)}, bf16[264,512]{1,0:T(8,128)(2,1)S(1)}, u32[]{:S(2)}, u32[]{:S(2)}) collective-permute-start(bf16[264,512]{1,0:T(8,128)(2,1)S(1)} %get-tuple-element.57), channel_id=1, source_target_pairs={{0,1},{1,0},{2,3},{3,2},{4,5},{5,4},{6,7},{7,6},{8,9},{9,8},{10,11... | collective-permute-start | bytes 811016 | tf_op jit(solution)/shard_map/ppermute | solution.py:278
  28.6 3.9 %collective-permute-start.12 = (bf16[128,1920]{1,0:T(8,128)(2,1)S(1)}, bf16[128,1920]{1,0:T(8,128)(2,1)S(1)}, u32[]{:S(2)}, u32[]{:S(2)}) collective-permute-start(bf16[128,1920]{1,0:T(8,128)(2,1)S(1)} %get-tuple-element.103), channel_id=1, source_target_pairs={{0,2},{2,0},{4,6},{6,4},{8,10},{10,8},{12,14},{14,12},{16,18},{18,... | collective-permute-start | bytes 1474568 | tf_op jit(solution)/shard_map/ppermute | solution.py:263
  30.0 2.6 %collective-permute-start.13 = (bf16[128,1920]{1,0:T(8,128)(2,1)S(1)}, bf16[128,1920]{1,0:T(8,128)(2,1)S(1)}, u32[]{:S(2)}, u32[]{:S(2)}) collective-permute-start(bf16[128,1920]{1,0:T(8,128)(2,1)S(1)} %get-tuple-element.104), channel_id=1, source_target_pairs={{0,2},{2,0},{4,6},{6,4},{8,10},{10,8},{12,14},{14,12},{16,18},{18,... | collective-permute-start | bytes 1474568 | tf_op jit(solution)/shard_map/ppermute | solution.py:263
  30.1 15.7 %collective-permute-start.11 = (bf16[256,1920]{1,0:T(8,128)(2,1)S(1)}, bf16[256,1920]{1,0:T(8,128)(2,1)S(1)}, u32[]{:S(2)}, u32[]{:S(2)}) collective-permute-start(bf16[256,1920]{1,0:T(8,128)(2,1)S(1)} %collective-permute-done.9.refs_0_), channel_id=1, source_target_pairs={{0,8},{2,6},{4,0},{6,14},{8,16},{10,2},{12,4},{14,22},{16,24},{18,... | collective-permute-start | bytes 2949128 | tf_op jit(solution)/shard_map/ppermute | solution.py:275
  31.4 8.5 %collective-permute-start.8 = (bf16[264,512]{1,0:T(8,128)(2,1)S(1)}, bf16[264,512]{1,0:T(8,128)(2,1)S(1)}, u32[]{:S(2)}, u32[]{:S(2)}) collective-permute-start(bf16[264,512]{1,0:T(8,128)(2,1)S(1)} %multiply_convert_fusion.2.refs_0_), channel_id=1, source_target_pairs={{0,1},{1,0},{2,3},{3,2},{4,5},{5,4},{6,7},{7,6},{8,9},{9,8},{10,11... | collective-permute-start | bytes 811016 | tf_op jit(solution)/shard_map/ppermute | solution.py:278
  35.9 9.8 %collective-permute-start.14 = (bf16[264,512]{1,0:T(8,128)(2,1)}, bf16[264,512]{1,0:T(8,128)(2,1)}, u32[]{:S(2)}, u32[]{:S(2)}) collective-permute-start(bf16[264,512]{1,0:T(8,128)(2,1)} %get-tuple-element.64), channel_id=1, source_target_pairs={{0,1},{1,0},{2,3},{3,2},{4,5},{5,4},{6,7},{7,6},{8,9},{9,8},{10,11... | collective-permute-start | bytes 811016 | tf_op jit(solution)/shard_map/ppermute | solution.py:278
  45.8 2.2 %collective-permute-start.16 = (bf16[128,1920]{1,0:T(8,128)(2,1)S(1)}, bf16[128,1920]{1,0:T(8,128)(2,1)S(1)}, u32[]{:S(2)}, u32[]{:S(2)}) collective-permute-start(bf16[128,1920]{1,0:T(8,128)(2,1)S(1)} %get-tuple-element.101), channel_id=1, source_target_pairs={{0,2},{2,0},{4,6},{6,4},{8,10},{10,8},{12,14},{14,12},{16,18},{18,... | collective-permute-start | bytes 1474568 | tf_op jit(solution)/shard_map/ppermute | solution.py:263
  46.3 2.2 %collective-permute-start.17 = (bf16[128,1920]{1,0:T(8,128)(2,1)S(1)}, bf16[128,1920]{1,0:T(8,128)(2,1)S(1)}, u32[]{:S(2)}, u32[]{:S(2)}) collective-permute-start(bf16[128,1920]{1,0:T(8,128)(2,1)S(1)} %get-tuple-element.102), channel_id=1, source_target_pairs={{0,2},{2,0},{4,6},{6,4},{8,10},{10,8},{12,14},{14,12},{16,18},{18,... | collective-permute-start | bytes 1474568 | tf_op jit(solution)/shard_map/ppermute | solution.py:263
  46.5 8.6 %collective-permute-start.15 = (bf16[256,1024]{1,0:T(8,128)(2,1)S(1)}, bf16[256,1024]{1,0:T(8,128)(2,1)S(1)}, u32[]{:S(2)}, u32[]{:S(2)}) collective-permute-start(bf16[256,1024]{1,0:T(8,128)(2,1)S(1)} %pad_maximum_fusion.4), channel_id=1, source_target_pairs={{0,8},{2,6},{4,0},{6,14},{8,16},{10,2},{12,4},{14,22},{16,24},{18,... | collective-permute-start | bytes 1572872 | tf_op jit(solution)/shard_map/ppermute | solution.py:275
  50.5 7.9 %collective-permute-start.22 = (bf16[264,512]{1,0:T(8,128)(2,1)S(1)}, bf16[264,512]{1,0:T(8,128)(2,1)S(1)}, u32[]{:S(2)}, u32[]{:S(2)}) collective-permute-start(bf16[264,512]{1,0:T(8,128)(2,1)S(1)} %get-tuple-element.68), channel_id=1, source_target_pairs={{0,1},{1,0},{2,3},{3,2},{4,5},{5,4},{6,7},{7,6},{8,9},{9,8},{10,11... | collective-permute-start | bytes 811016 | tf_op jit(solution)/shard_map/ppermute | solution.py:278
  55.1 2.3 %collective-permute-start.18 = (bf16[64,1024]{1,0:T(8,128)(2,1)S(1)}, bf16[64,1024]{1,0:T(8,128)(2,1)S(1)}, u32[]{:S(2)}, u32[]{:S(2)}) collective-permute-start(bf16[64,1024]{1,0:T(8,128)(2,1)S(1)} %get-tuple-element.109), channel_id=1, source_target_pairs={{0,2},{2,0},{4,6},{6,4},{8,10},{10,8},{12,14},{14,12},{16,18},{18,... | collective-permute-start | bytes 393224 | tf_op jit(solution)/shard_map/ppermute | solution.py:263
  56.5 1.3 %collective-permute-start.21 = (bf16[64,1024]{1,0:T(8,128)(2,1)S(1)}, bf16[64,1024]{1,0:T(8,128)(2,1)S(1)}, u32[]{:S(2)}, u32[]{:S(2)}) collective-permute-start(bf16[64,1024]{1,0:T(8,128)(2,1)S(1)} %get-tuple-element.110), channel_id=1, source_target_pairs={{0,2},{2,0},{4,6},{6,4},{8,10},{10,8},{12,14},{14,12},{16,18},{18,... | collective-permute-start | bytes 393224 | tf_op jit(solution)/shard_map/ppermute | solution.py:263
  56.5 1.5 %collective-permute-start.20 = (bf16[64,1024]{1,0:T(8,128)(2,1)S(1)}, bf16[64,1024]{1,0:T(8,128)(2,1)S(1)}, u32[]{:S(2)}, u32[]{:S(2)}) collective-permute-start(bf16[64,1024]{1,0:T(8,128)(2,1)S(1)} %get-tuple-element.111), channel_id=1, source_target_pairs={{0,2},{2,0},{4,6},{6,4},{8,10},{10,8},{12,14},{14,12},{16,18},{18,... | collective-permute-start | bytes 393224 | tf_op jit(solution)/shard_map/ppermute | solution.py:263
  57.0 1.3 %collective-permute-start.19 = (bf16[64,1024]{1,0:T(8,128)(2,1)S(1)}, bf16[64,1024]{1,0:T(8,128)(2,1)S(1)}, u32[]{:S(2)}, u32[]{:S(2)}) collective-permute-start(bf16[64,1024]{1,0:T(8,128)(2,1)S(1)} %get-tuple-element.112), channel_id=1, source_target_pairs={{0,2},{2,0},{4,6},{6,4},{8,10},{10,8},{12,14},{14,12},{16,18},{18,... | collective-permute-start | bytes 393224 | tf_op jit(solution)/shard_map/ppermute | solution.py:263
  60.2 7.2 %collective-permute-start.25 = (bf16[132,1024]{1,0:T(8,128)(2,1)S(1)}, bf16[132,1024]{1,0:T(8,128)(2,1)S(1)}, u32[]{:S(2)}, u32[]{:S(2)}) collective-permute-start(bf16[132,1024]{1,0:T(8,128)(2,1)S(1)} %get-tuple-element.71.refs_0_), channel_id=1, source_target_pairs={{0,1},{1,0},{2,3},{3,2},{4,5},{5,4},{6,7},{7,6},{8,9},{9,8},{10,11... | collective-permute-start | bytes 811016 | tf_op jit(solution)/shard_map/ppermute | solution.py:278
  63.4 4.0 %collective-permute-start.23 = (bf16[80,1792]{1,0:T(8,128)(2,1)S(1)}, bf16[80,1792]{1,0:T(8,128)(2,1)S(1)}, u32[]{:S(2)}, u32[]{:S(2)}) collective-permute-start(bf16[80,1792]{1,0:T(8,128)(2,1)S(1)} %slice.49), channel_id=1, source_target_pairs={{0,2},{2,0},{4,6},{6,4},{8,10},{10,8},{12,14},{14,12},{16,18},{18,... | collective-permute-start | bytes 860168 | tf_op jit(solution)/shard_map/ppermute | solution.py:263
  64.8 2.1 %collective-permute-start.24 = (bf16[64,1792]{1,0:T(8,128)(2,1)S(1)}, bf16[64,1792]{1,0:T(8,128)(2,1)S(1)}, u32[]{:S(2)}, u32[]{:S(2)}) collective-permute-start(bf16[64,1792]{1,0:T(8,128)(2,1)S(1)} %get-tuple-element.107), channel_id=1, source_target_pairs={{0,2},{2,0},{4,6},{6,4},{8,10},{10,8},{12,14},{14,12},{16,18},{18,... | collective-permute-start | bytes 688136 | tf_op jit(solution)/shard_map/ppermute | solution.py:263
  64.9 2.0 %collective-permute-start.26 = (bf16[64,1792]{1,0:T(8,128)(2,1)S(1)}, bf16[64,1792]{1,0:T(8,128)(2,1)S(1)}, u32[]{:S(2)}, u32[]{:S(2)}) collective-permute-start(bf16[64,1792]{1,0:T(8,128)(2,1)S(1)} %get-tuple-element.108), channel_id=1, source_target_pairs={{0,2},{2,0},{4,6},{6,4},{8,10},{10,8},{12,14},{14,12},{16,18},{18,... | collective-permute-start | bytes 688136 | tf_op jit(solution)/shard_map/ppermute | solution.py:263
  65.4 1.5 %collective-permute-start.27 = (bf16[48,1792]{1,0:T(8,128)(2,1)S(1)}, bf16[48,1792]{1,0:T(8,128)(2,1)S(1)}, u32[]{:S(2)}, u32[]{:S(2)}) collective-permute-start(bf16[48,1792]{1,0:T(8,128)(2,1)S(1)} %slice.52), channel_id=1, source_target_pairs={{0,2},{2,0},{4,6},{6,4},{8,10},{10,8},{12,14},{14,12},{16,18},{18,... | collective-permute-start | bytes 516104 | tf_op jit(solution)/shard_map/ppermute | solution.py:263
  67.3 8.6 %collective-permute-start.28 = (bf16[264,512]{1,0:T(8,128)(2,1)S(1)}, bf16[264,512]{1,0:T(8,128)(2,1)S(1)}, u32[]{:S(2)}, u32[]{:S(2)}) collective-permute-start(bf16[264,512]{1,0:T(8,128)(2,1)S(1)} %multiply_convert_fusion.1.refs_0_), channel_id=1, source_target_pairs={{0,1},{1,0},{2,3},{3,2},{4,5},{5,4},{6,7},{7,6},{8,9},{9,8},{10,11... | collective-permute-start | bytes 811016 | tf_op jit(solution)/shard_map/ppermute | solution.py:278
  70.7 3.4 %collective-permute-start.30 = (bf16[128,896]{1,0:T(8,128)(2,1)S(1)}, bf16[128,896]{1,0:T(8,128)(2,1)S(1)}, u32[]{:S(2)}, u32[]{:S(2)}) collective-permute-start(bf16[128,896]{1,0:T(8,128)(2,1)S(1)} %get-tuple-element.113), channel_id=1, source_target_pairs={{0,2},{2,0},{4,6},{6,4},{8,10},{10,8},{12,14},{14,12},{16,18},{18,... | collective-permute-start | bytes 688136 | tf_op jit(solution)/shard_map/ppermute | solution.py:263
  73.0 1.5 %collective-permute-start.29 = (bf16[128,896]{1,0:T(8,128)(2,1)S(1)}, bf16[128,896]{1,0:T(8,128)(2,1)S(1)}, u32[]{:S(2)}, u32[]{:S(2)}) collective-permute-start(bf16[128,896]{1,0:T(8,128)(2,1)S(1)} %get-tuple-element.114), channel_id=1, source_target_pairs={{0,2},{2,0},{4,6},{6,4},{8,10},{10,8},{12,14},{14,12},{16,18},{18,... | collective-permute-start | bytes 688136 | tf_op jit(solution)/shard_map/ppermute | solution.py:263
  74.6 7.7 %collective-permute-start.33 = (bf16[256,896]{1,0:T(8,128)(2,1)S(1)}, bf16[256,896]{1,0:T(8,128)(2,1)S(1)}, u32[]{:S(2)}, u32[]{:S(2)}) collective-permute-start(bf16[256,896]{1,0:T(8,128)(2,1)S(1)} %shard_map.73), channel_id=1, source_target_pairs={{0,8},{2,6},{4,0},{6,14},{8,16},{10,2},{12,4},{14,22},{16,24},{18,... | collective-permute-start | bytes 1376264 | tf_op jit(solution)/shard_map/ppermute | solution.py:275
  79.0 3.4 %collective-permute-start.32 = (bf16[112,1792]{1,0:T(8,128)(2,1)S(1)}, bf16[112,1792]{1,0:T(8,128)(2,1)S(1)}, u32[]{:S(2)}, u32[]{:S(2)}) collective-permute-start(bf16[112,1792]{1,0:T(8,128)(2,1)S(1)} %slice.53), channel_id=1, source_target_pairs={{0,2},{2,0},{4,6},{6,4},{8,10},{10,8},{12,14},{14,12},{16,18},{18,... | collective-permute-start | bytes 1204232 | tf_op jit(solution)/shard_map/ppermute | solution.py:263
  79.3 4.5 %collective-permute-start.34 = (bf16[144,1792]{1,0:T(8,128)(2,1)S(1)}, bf16[144,1792]{1,0:T(8,128)(2,1)S(1)}, u32[]{:S(2)}, u32[]{:S(2)}) collective-permute-start(bf16[144,1792]{1,0:T(8,128)(2,1)S(1)} %slice.55), channel_id=1, source_target_pairs={{0,2},{2,0},{4,6},{6,4},{8,10},{10,8},{12,14},{14,12},{16,18},{18,... | collective-permute-start | bytes 1548296 | tf_op jit(solution)/shard_map/ppermute | solution.py:263
  79.6 7.8 %collective-permute-start.31 = (bf16[264,512]{1,0:T(8,128)(2,1)S(1)}, bf16[264,512]{1,0:T(8,128)(2,1)S(1)}, u32[]{:S(2)}, u32[]{:S(2)}) collective-permute-start(bf16[264,512]{1,0:T(8,128)(2,1)S(1)} %multiply_convert_fusion.refs_0_), channel_id=1, source_target_pairs={{0,1},{1,0},{2,3},{3,2},{4,5},{5,4},{6,7},{7,6},{8,9},{9,8},{10,11... | collective-permute-start | bytes 811016 | tf_op jit(solution)/shard_map/ppermute | solution.py:278
  82.5 8.7 %collective-permute-start.43 = (bf16[112,1792]{1,0:T(8,128)(2,1)S(1)}, bf16[112,1792]{1,0:T(8,128)(2,1)S(1)}, u32[]{:S(2)}, u32[]{:S(2)}) collective-permute-start(bf16[112,1792]{1,0:T(8,128)(2,1)S(1)} %shard_map.75), channel_id=1, source_target_pairs={{0,8},{2,6},{4,0},{6,14},{8,16},{10,2},{12,4},{14,22},{16,24},{18,... | collective-permute-start | bytes 1204232 | tf_op jit(solution)/shard_map/ppermute | solution.py:275
  84.0 11.0 %collective-permute-start.36 = (bf16[144,1792]{1,0:T(8,128)(2,1)S(1)}, bf16[144,1792]{1,0:T(8,128)(2,1)S(1)}, u32[]{:S(2)}, u32[]{:S(2)}) collective-permute-start(bf16[144,1792]{1,0:T(8,128)(2,1)S(1)} %shard_map.76), channel_id=1, source_target_pairs={{0,8},{2,6},{4,0},{6,14},{8,16},{10,2},{12,4},{14,22},{16,24},{18,... | collective-permute-start | bytes 1548296 | tf_op jit(solution)/shard_map/ppermute | solution.py:275
  89.4 5.7 %collective-permute-start.35 = (bf16[144,1792]{1,0:T(8,128)(2,1)S(1)}, bf16[144,1792]{1,0:T(8,128)(2,1)S(1)}, u32[]{:S(2)}, u32[]{:S(2)}) collective-permute-start(bf16[144,1792]{1,0:T(8,128)(2,1)S(1)} %slice.57), channel_id=1, source_target_pairs={{0,2},{2,0},{4,6},{6,4},{8,10},{10,8},{12,14},{14,12},{16,18},{18,... | collective-permute-start | bytes 1548296 | tf_op jit(solution)/shard_map/ppermute | solution.py:263
  90.5 2.1 %collective-permute-start.41 = (bf16[64,1792]{1,0:T(8,128)(2,1)S(1)}, bf16[64,1792]{1,0:T(8,128)(2,1)S(1)}, u32[]{:S(2)}, u32[]{:S(2)}) collective-permute-start(bf16[64,1792]{1,0:T(8,128)(2,1)S(1)} %slice.59), channel_id=1, source_target_pairs={{0,2},{2,0},{4,6},{6,4},{8,10},{10,8},{12,14},{14,12},{16,18},{18,... | collective-permute-start | bytes 688136 | tf_op jit(solution)/shard_map/ppermute | solution.py:263
  90.6 2.0 %collective-permute-start.42 = (bf16[48,1792]{1,0:T(8,128)(2,1)S(1)}, bf16[48,1792]{1,0:T(8,128)(2,1)S(1)}, u32[]{:S(2)}, u32[]{:S(2)}) collective-permute-start(bf16[48,1792]{1,0:T(8,128)(2,1)S(1)} %slice.60), channel_id=1, source_target_pairs={{0,2},{2,0},{4,6},{6,4},{8,10},{10,8},{12,14},{14,12},{16,18},{18,... | collective-permute-start | bytes 516104 | tf_op jit(solution)/shard_map/ppermute | solution.py:263
  92.8 7.1 %collective-permute-start.44 = (bf16[112,1792]{1,0:T(8,128)(2,1)S(1)}, bf16[112,1792]{1,0:T(8,128)(2,1)S(1)}, u32[]{:S(2)}, u32[]{:S(2)}) collective-permute-start(bf16[112,1792]{1,0:T(8,128)(2,1)S(1)} %shard_map.80), channel_id=1, source_target_pairs={{0,8},{2,6},{4,0},{6,14},{8,16},{10,2},{12,4},{14,22},{16,24},{18,... | collective-permute-start | bytes 1204232 | tf_op jit(solution)/shard_map/ppermute | solution.py:275
  95.3 10.1 %collective-permute-start.37 = (bf16[144,1792]{1,0:T(8,128)(2,1)S(1)}, bf16[144,1792]{1,0:T(8,128)(2,1)S(1)}, u32[]{:S(2)}, u32[]{:S(2)}) collective-permute-start(bf16[144,1792]{1,0:T(8,128)(2,1)S(1)} %shard_map.78), channel_id=1, source_target_pairs={{0,8},{2,6},{4,0},{6,14},{8,16},{10,2},{12,4},{14,22},{16,24},{18,... | collective-permute-start | bytes 1548296 | tf_op jit(solution)/shard_map/ppermute | solution.py:275
  96.8 4.3 %collective-permute-start.39 = (bf16[132,512]{1,0:T(8,128)(2,1)S(1)}, bf16[132,512]{1,0:T(8,128)(2,1)S(1)}, u32[]{:S(2)}, u32[]{:S(2)}) collective-permute-start(bf16[132,512]{1,0:T(8,128)(2,1)S(1)} %copy-done.17), channel_id=1, source_target_pairs={{0,1},{1,0},{2,3},{3,2},{4,5},{5,4},{6,7},{7,6},{8,9},{9,8},{10,11... | collective-permute-start | bytes 405512 | tf_op jit(solution)/shard_map/ppermute | solution.py:278
  100.0 9.7 %collective-permute-start.45 = (bf16[112,1792]{1,0:T(8,128)(2,1)S(1)}, bf16[112,1792]{1,0:T(8,128)(2,1)S(1)}, u32[]{:S(2)}, u32[]{:S(2)}) collective-permute-start(bf16[112,1792]{1,0:T(8,128)(2,1)S(1)} %shard_map.81), channel_id=1, source_target_pairs={{0,8},{2,6},{4,0},{6,14},{8,16},{10,2},{12,4},{14,22},{16,24},{18,... | collective-permute-start | bytes 1204232 | tf_op jit(solution)/shard_map/ppermute | solution.py:275
  101.2 5.5 %collective-permute-start.40 = (bf16[132,512]{1,0:T(8,128)(2,1)S(1)}, bf16[132,512]{1,0:T(8,128)(2,1)S(1)}, u32[]{:S(2)}, u32[]{:S(2)}) collective-permute-start(bf16[132,512]{1,0:T(8,128)(2,1)S(1)} %multiply_convert_fusion.3.refs_0_), channel_id=1, source_target_pairs={{0,1},{1,0},{2,3},{3,2},{4,5},{5,4},{6,7},{7,6},{8,9},{9,8},{10,11... | collective-permute-start | bytes 405512 | tf_op jit(solution)/shard_map/ppermute | solution.py:278
  105.6 9.6 %collective-permute-start.38 = (bf16[144,1792]{1,0:T(8,128)(2,1)S(1)}, bf16[144,1792]{1,0:T(8,128)(2,1)S(1)}, u32[]{:S(2)}, u32[]{:S(2)}) collective-permute-start(bf16[144,1792]{1,0:T(8,128)(2,1)S(1)} %shard_map.79), channel_id=1, source_target_pairs={{0,8},{2,6},{4,0},{6,14},{8,16},{10,2},{12,4},{14,22},{16,24},{18,... | collective-permute-start | bytes 1548296 | tf_op jit(solution)/shard_map/ppermute | solution.py:275
  109.8 7.1 %collective-permute-start.46 = (bf16[112,1792]{1,0:T(8,128)(2,1)S(1)}, bf16[112,1792]{1,0:T(8,128)(2,1)S(1)}, u32[]{:S(2)}, u32[]{:S(2)}) collective-permute-start(bf16[112,1792]{1,0:T(8,128)(2,1)S(1)} %add_convert_fusion.1), channel_id=1, source_target_pairs={{0,2},{2,0},{4,6},{6,4},{8,10},{10,8},{12,14},{14,12},{16,18},{18,... | collective-permute-start | bytes 1204232 | tf_op jit(solution)/shard_map/ppermute | solution.py:263
  115.2 2.5 %collective-permute-start.47 = (bf16[16,1792]{1,0:T(8,128)(2,1)S(1)}, bf16[16,1792]{1,0:T(8,128)(2,1)S(1)}, u32[]{:S(2)}, u32[]{:S(2)}) collective-permute-start(bf16[16,1792]{1,0:T(8,128)(2,1)S(1)} %add_convert_fusion.2), channel_id=1, source_target_pairs={{0,2},{2,0},{4,6},{6,4},{8,10},{10,8},{12,14},{14,12},{16,18},{18,... | collective-permute-start | bytes 172040 | tf_op jit(solution)/shard_map/ppermute | solution.py:263
  (19 other events, 72.2 us)
